TPU v7x, 32 devices: a whole 2x2x4 slice. The times are simulated.
32 devices in a mesh: dam: 16 (over z, y, x), sec: 2 (over core).
Axes of the slice: x: 2, y: 2, z: 4, core: 2. Of those that a mesh axis runs over, the one named last changes fastest.
Arguments:
- segment_load: float32 [16, 2, 16, 1024], P('dam', 'sec')
- segment_mask: int32 [16, 2, 16, 16], P('dam', 'sec'), may hold values 0 or 1
- stiffness: float32 [16, 2, 16, 64, 448], P('dam', 'sec'), may hold values from -2 to 3, as said below
- block_cols: int32 [16, 2, 16, 7], P('dam', 'sec'), may hold values from 0 to 15, as said below
- capillary: float32 [16, 2, 16, 64], P('dam', 'sec'), may hold values from 0.25 to 2
- dirichlet_blocks: float32 [16, 2, 16, 64, 64], P('dam', 'sec'), may hold values from -1 to 1, as said below
- face_map: int32 [16, 2, 4, 8], P('dam', 'sec'), may hold values from 0 to 15, as said below
- face_weight: float32 [16, 2, 4, 512], P('dam', 'sec'), may hold values from 0 to 2, as said below
- corner_map: int32 [16, 2, 4], P('dam', 'sec'), may hold values from 0 to 15, as said below
- coarse_inverse: float32 [16, 512, 512], P('dam', 'sec'), may hold values from -1 to 1, as said below
Outputs:
- solution: float32 [16, 2, 16, 1024], P('dam', 'sec')
- residual: float32 [16, 2, 16, 1024], P('dam', 'sec')
Inputs may be any that keep to these rules, and one draw needn't show every extreme that they name: `block_cols`: in each subdomain block b stores blocks b, b + o1, b - o1, b + o2, b - o2, b + o3, b - o3 (mod 16), for 3 distinct offsets o1, o2, o3 from 1 to 7 drawn per subdomain, in that order. The stiffness is symmetric, its off-diagonal entries of a row sum in magnitude to under 1.5, and its diagonal entries are 2 to 3. `dirichlet_blocks`: each block is symmetric and positive definite. `coarse_inverse`: each cross-section's matrix is symmetric and positive definite. `face_map`: the 8 blocks of a face are distinct; position p of a face meets position p of the neighbour's opposite face. `face_weight`: equal on the two sides of an interface, zero on faces with no neighbour. `corner_map`: distinct within a subdomain.
All inputs are finite; a program needn't handle non-finite values. No bound on the sum of `segment_mask` on one device may be relied on, other than what follows from the above.
Results may differ from a plain program's by a relative error of at most 0.00075.
Values sent between devices are 32-bit elements; how exact they have to be, the bound alone decides.
No kernel may reach another device: no remote copies, remote signals or barrier semaphores. Data moves between devices by JAX's collectives and lax.ppermute only.
A program may use at most 64 MiB of HBM per device.

v0:
```python
import jax
import jax.numpy as jnp
from jax import lax
from jax.sharding import PartitionSpec as P

ITERS = 2


HIGH = lax.Precision.HIGHEST


def with_halo(array, sides, width):
    for axis, dim in sides:
        peers, length = (lax.axis_size(axis), array.shape[dim])
        up = [(i, (i + 1) % peers) for i in range(peers - 1)]
        down = [(j, i) for i, j in up]
        last = lax.slice_in_dim(array, length - width, length, axis=dim)
        first = lax.slice_in_dim(array, 0, width, axis=dim)
        before = lax.ppermute(last, axis, up)
        after = lax.ppermute(first, axis, down)
        array = jnp.concatenate([before, array, after], axis=dim)
    return array


def local_product(stiff, cols, tang, field):
    nblk, bdof = tang.shape
    ncol = field.shape[1] // bdof
    gathered = field[cols].reshape(nblk, cols.shape[1] * bdof, ncol)
    prod = jnp.einsum("bde,bes->bds", stiff, gathered, precision=HIGH)
    prod = prod + tang[:, :, None] * field.reshape(nblk, bdof, ncol)
    return prod.reshape(nblk, bdof * ncol)


def shards(
    segment_load,
    segment_mask,
    stiffness,
    block_cols,
    capillary,
    dirichlet_blocks,
    face_map,
    face_weight,
    corner_map,
    coarse_inverse,
):
    stiff = stiffness[0, 0]
    cols = block_cols[0, 0]
    tang = capillary[0, 0]
    blocks_pre = dirichlet_blocks[0, 0]
    fmap = face_map[0, 0]
    cmap = corner_map[0, 0]
    own_rows = coarse_inverse[0]
    nblk, bdof = tang.shape
    width = segment_load.shape[-1]
    ncol = width // bdof
    nface = fmap.shape[1]
    ncorner = cmap.shape[0]
    weights = face_weight[0, 0].reshape(4, nface, bdof, 1)
    flat_faces = fmap.reshape(4 * nface)
    masked = (
        segment_load[0, 0].reshape(nblk, bdof, ncol)
        * segment_mask[0, 0].astype(jnp.float32)[:, None, :]
    )
    resid = masked.reshape(nblk, width)

    def precondition(field):
        outz = jnp.einsum(
            "bde,bes->bds", blocks_pre, field.reshape(nblk, bdof, ncol), precision=HIGH
        ).reshape(nblk, width)
        corners = field[cmap]
        piece = lax.all_gather(corners, "sec", axis=0, tiled=True)
        correct = jnp.dot(
            own_rows, piece.reshape(piece.shape[0] * bdof, ncol), precision=HIGH
        ).reshape(ncorner, width)
        return outz.at[cmap].add(correct)

    def inner(first, second):
        return (first * second).reshape(nblk, bdof, ncol).sum(axis=(0, 1))

    def spread(coef):
        return jnp.tile(coef, bdof)

    def global_inner(first, second):
        return lax.psum(inner(first, second), ("dam", "sec"))

    solution = jnp.zeros_like(resid)
    zvec = precondition(resid)
    direction = zvec
    gamma = global_inner(resid, zvec)
    for step in range(ITERS):
        local = local_product(stiff, cols, tang, direction)
        faces = direction[fmap]
        dam_side = with_halo(faces[0:2], (("dam", 0),), 1)
        sec_side = with_halo(faces[2:4], (("sec", 0),), 1)
        beside = jnp.stack([dam_side[0], dam_side[3], sec_side[0], sec_side[3]])
        term = (weights * (faces - beside).reshape(4, nface, bdof, ncol)).reshape(4 * nface, width)
        image = local.at[flat_faces].add(term)
        delta = global_inner(direction, image)
        alpha = spread(gamma / delta)
        solution = solution + alpha * direction
        resid = resid - alpha * image
        if step + 1 < ITERS:
            zvec = precondition(resid)
            gnew = global_inner(resid, zvec)
            direction = zvec + spread(gnew / gamma) * direction
            gamma = gnew
    return (solution[None, None], resid[None, None])


def solution(mesh):
    placed = (
        P("dam", "sec", None, None),
        P("dam", "sec", None, None),
        P("dam", "sec", None, None, None),
        P("dam", "sec", None, None),
        P("dam", "sec", None, None),
        P("dam", "sec", None, None, None),
        P("dam", "sec", None, None),
        P("dam", "sec", None, None),
        P("dam", "sec", None),
        P("dam", "sec", None),
    )
    return jax.shard_map(
        shards,
        mesh=mesh,
        in_specs=placed,
        out_specs=(P("dam", "sec", None, None), P("dam", "sec", None, None)),
        check_vma=False,
    )
```

profile of v0, /device:TPU:0, one launch (start us, length us, event | category | flops | bytes accessed | tf_op | source)
XLA Modules:
  0.0 219.1 jit_solution(17807767833007039431)
XLA Ops:
  0.7 0.8 convert_bitcast_fusion
  1.8 1.0 reshape_squeeze.10
  2.9 0.9 bitcast_multiply_fusion
  3.8 2.0 convolution_bitcast_fusion.1
  6.9 1.9 all-gather.2
  9.9 0.7 scatter_fusion
  11.2 0.7 slice_bitcast_fusion.7
  11.9 1.3 collective-permute-start.3
  13.1 4.2 %collective-permute-start.2 = (f32[1,8,1024]{2,1,0:T(8,128)}, f32[1,8,1024]{2,1,0:T(8,128)}, u32[]{:S(2)}, u32[]{:S(2)}) collective-permute-start(f32[1,8,1024]{2,1,0:T(8,128)} %get-tuple-element.11), channel_id=1, source_target_pairs={{0,1},{2,3},{4,5},{6,7},{8,9},{10,11},{12,13},{14,15},{16,17},{18,... | collective-permute-start | bytes 98312 | tf_op jit(solution)/shard_map/ppermute | solution.py:19
  17.4 1.3 collective-permute-start.1
  18.6 6.0 %collective-permute-start = (f32[1,8,1024]{2,1,0:T(8,128)}, f32[1,8,1024]{2,1,0:T(8,128)}, u32[]{:S(2)}, u32[]{:S(2)}) collective-permute-start(f32[1,8,1024]{2,1,0:T(8,128)} %get-tuple-element.10), channel_id=1, source_target_pairs={{0,2},{2,4},{4,6},{6,8},{8,10},{10,12},{12,14},{14,16},{16,18},{18... | collective-permute-start | bytes 98312 | tf_op jit(solution)/shard_map/ppermute | solution.py:19
  25.1 0.8 gather_fusion.1
  25.9 3.0 %reshape.203 = f32[16,448,16]{2,1,0:T(8,128)} reshape(f32[112,1024]{1,0:T(8,128)S(1)} %gather_fusion.1) | data formatting | bytes 917504 | tf_op jit(solution)/shard_map/reshape | solution.py:28
  29.1 7.9 %fusion.7 = f32[16,64,16]{1,2,0:T(8,128)S(1)} fusion(f32[16,448,16]{2,1,0:T(8,128)} %reshape.203, f32[1,1,16,64,448]{4,3,2,1,0:T(8,128)S(1)} %copy-done, f32[16,64,16]{1,2,0:T(8,128)S(1)} %copy.59, f32[16,64]{1,0:T(8,128)S(1)} %bitcast.95), kind=kOutput, calls=%fused_computation.17 | convolution fusion | flops 88113152 | bytes 2428928 | tf_op jit(solution)/shard_map/bde,bes->bds/dot_general | solution.py:29
  37.2 0.9 reshape.205
  39.2 1.6 stack.29
  40.8 1.6 stack.28
  42.3 1.6 stack.27
  43.9 1.6 stack.26
  45.5 1.3 pad_maximum_fusion
  46.8 1.3 stack.31
  48.1 2.7 %scatter_custom_fusion.1 = f32[16,1024]{1,0:T(8,128)} fusion(f32[16,1024]{1,0:T(8,128)} %reshape.205, s32[32]{0:T(128)S(1)} %fusion.29, f32[32,1024]{1,0:T(8,128)S(1)} %mul.113, f32[32,1024]{1,0:T(8,128)S(1)} %gather_fusion.2, f32[32,1024]{1,0:T(8,128)} %stack.31), kind=kCustom, calls=%fused_computation.33 | custom fusion | flops 98304 | bytes 458752 | tf_op jit(solution)/shard_map/scatter-add | solution.py:97
  50.8 0.9 multiply_reduce_fusion.2
  51.9 42.3 %all-reduce = (f32[16]{0:T(128)S(1)}, f32[16]{0:T(128)S(1)}) all-reduce(f32[16]{0:T(128)S(1)} %reduce_sum.51, f32[16]{0:T(128)S(1)} %reduce_sum.54), channel_id=1, replica_groups=mesh['dam'=16,'sec'=2] {'dam','sec'}, use_global_device_ids=true, to_apply=%region_3.0 | all-reduce | flops 32 | bytes 256 | tf_op jit(solution)/shard_map/psum | solution.py:84
  94.8 0.9 multiply_subtract_fusion
  95.8 0.7 gather_fusion.3
  96.5 2.7 %convolution_bitcast_fusion = f32[16,64,16]{1,2,0:T(8,128)} fusion(f32[16,64,16]{2,1,0:T(8,128)S(1)} %reshape.206, f32[1,1,16,64,64]{4,3,2,1,0:T(8,128)} %param.15), kind=kOutput, calls=%fused_computation.14 | convolution fusion | flops 12582912 | bytes 393216 | tf_op jit(solution)/shard_map/bde,bes->bds/dot_general | solution.py:67
  99.2 1.1 copy.62
  100.6 1.8 all-gather.3
  103.3 0.8 scatter_fusion.1
  104.3 39.1 %psum.30 = f32[16]{0:T(128)S(1)} all-reduce(f32[16]{0:T(128)S(1)} %reduce_sum.72), channel_id=1, replica_groups=mesh['dam'=16,'sec'=2] {'dam','sec'}, use_global_device_ids=true, to_apply=%region_11.0 | all-reduce | flops 16 | bytes 128 | tf_op jit(solution)/shard_map/psum | solution.py:84
  144.1 0.8 gather_fusion.4
  145.0 0.7 gather_fusion.5
  145.8 3.0 %reshape.210 = f32[16,448,16]{2,1,0:T(8,128)} reshape(f32[112,1024]{1,0:T(8,128)S(1)} %gather_fusion.4) | data formatting | bytes 917504 | tf_op jit(solution)/shard_map/reshape | solution.py:28
  149.6 1.3 collective-permute-start.7
  150.9 3.0 %collective-permute-start.6 = (f32[1,8,1024]{2,1,0:T(8,128)}, f32[1,8,1024]{2,1,0:T(8,128)S(1)}, u32[]{:S(2)}, u32[]{:S(2)}) collective-permute-start(f32[1,8,1024]{2,1,0:T(8,128)} %get-tuple-element.7), channel_id=1, source_target_pairs={{0,1},{2,3},{4,5},{6,7},{8,9},{10,11},{12,13},{14,15},{16,17},{18,... | collective-permute-start | bytes 98312 | tf_op jit(solution)/shard_map/ppermute | solution.py:19
  154.0 1.3 collective-permute-start.5
  155.3 4.8 %collective-permute-start.4 = (f32[1,8,1024]{2,1,0:T(8,128)S(1)}, f32[1,8,1024]{2,1,0:T(8,128)S(1)}, u32[]{:S(2)}, u32[]{:S(2)}) collective-permute-start(f32[1,8,1024]{2,1,0:T(8,128)S(1)} %get-tuple-element.6), channel_id=1, source_target_pairs={{0,2},{2,4},{4,6},{6,8},{8,10},{10,12},{12,14},{14,16},{16,18},{18... | collective-permute-start | bytes 98312 | tf_op jit(solution)/shard_map/ppermute | solution.py:19
  160.1 7.9 %fusion.13 = f32[16,64,16]{1,2,0:T(8,128)S(1)} fusion(f32[16,448,16]{2,1,0:T(8,128)} %reshape.210, f32[1,1,16,64,448]{4,3,2,1,0:T(8,128)S(1)} %copy-done, f32[16,64,16]{1,2,0:T(8,128)S(1)} %copy.65, f32[16,64]{1,0:T(8,128)S(1)} %bitcast.96), kind=kOutput, calls=%fused_computation.19 | convolution fusion | flops 88113152 | bytes 2428928 | tf_op jit(solution)/shard_map/bde,bes->bds/dot_general | solution.py:29
  168.5 0.8 stack.35
  169.3 0.8 stack.34
  170.1 0.8 stack.33
  170.9 0.8 stack.32
  171.8 1.3 pad_maximum_fusion.1
  173.1 1.3 stack.37
  174.3 1.3 scatter_custom_fusion.3
  175.8 42.5 %psum.31 = f32[16]{0:T(128)S(1)} all-reduce(f32[16]{0:T(128)S(1)} %reduce_sum.75), channel_id=1, replica_groups=mesh['dam'=16,'sec'=2] {'dam','sec'}, use_global_device_ids=true, to_apply=%region_15.16 | all-reduce | flops 16 | bytes 128 | tf_op jit(solution)/shard_map/psum | solution.py:84
  218.4 0.7 subtract_bitcast_fusion
  (100 shorter events, 9.6 us)
Async XLA Ops:
  0.6 28.5 %copy-start = (f32[1,1,16,64,448]{4,3,2,1,0:T(8,128)S(1)}, f32[1,1,16,64,448]{4,3,2,1,0:T(8,128)}, u32[]{:S(2)}) copy-start(f32[1,1,16,64,448]{4,3,2,1,0:T(8,128)} %param.12) | copy-start | bytes 5505028
  0.6 5.6 %copy-start.11 = (s32[1,1,4]{2,1,0:T(1,128)S(1)}, s32[1,1,4]{2,1,0:T(1,128)}, u32[]{:S(2)}) copy-start(s32[1,1,4]{2,1,0:T(1,128)} %param.18) | copy-start | bytes 52
  0.7 8.3 %copy-start.1 = (f32[1,256,512]{2,1,0:T(8,128)S(1)}, f32[1,256,512]{2,1,0:T(8,128)}, u32[]{:S(2)}) copy-start(f32[1,256,512]{2,1,0:T(8,128)} %param.19) | copy-start | bytes 1572868
  0.7 9.1 %copy-start.7 = (s32[1,1,4,8]{3,2,1,0:T(4,128)S(1)}, s32[1,1,4,8]{3,2,1,0:T(4,128)}, u32[]{:S(2)}) copy-start(s32[1,1,4,8]{3,2,1,0:T(4,128)} %param.16) | copy-start | bytes 388
  1.8 23.1 %copy-start.10 = (s32[1,1,16,7]{2,1,3,0:T(1,128)S(1)}, s32[1,1,16,7]{2,1,3,0:T(1,128)}, u32[]{:S(2)}) copy-start(s32[1,1,16,7]{2,1,3,0:T(1,128)} %param.13) | copy-start | bytes 1348
  6.3 18.8 %copy-start.9 = (s32[4]{0:T(128)}, s32[4]{0:T(128)S(1)}, u32[]{:S(2)}) copy-start(s32[4]{0:T(128)S(1)} %fusion.28) | copy-start | bytes 52
  6.3 0.6 copy-start.8
  9.9 15.0 %copy-start.5 = (s32[1024]{0:T(1024)}, s32[1024]{0:T(1024)S(1)}, u32[]{:S(2)}) copy-start(s32[1024]{0:T(1024)S(1)} %pad_clamp_fusion) | copy-start | bytes 12292
  11.9 27.3 %collective-permute-start.3 = (f32[1,8,1024]{2,1,0:T(8,128)}, f32[1,8,1024]{2,1,0:T(8,128)}, u32[]{:S(2)}, u32[]{:S(2)}) collective-permute-start(f32[1,8,1024]{2,1,0:T(8,128)} %get-tuple-element.13), channel_id=1, source_target_pairs={{1,0},{3,2},{5,4},{7,6},{9,8},{11,10},{13,12},{15,14},{17,16},{19,... | collective-permute-start | bytes 98312 | tf_op jit(solution)/shard_map/ppermute | solution.py:20
  13.1 27.6 %collective-permute-start.2 = (f32[1,8,1024]{2,1,0:T(8,128)}, f32[1,8,1024]{2,1,0:T(8,128)}, u32[]{:S(2)}, u32[]{:S(2)}) collective-permute-start(f32[1,8,1024]{2,1,0:T(8,128)} %get-tuple-element.11), channel_id=1, source_target_pairs={{0,1},{2,3},{4,5},{6,7},{8,9},{10,11},{12,13},{14,15},{16,17},{18,... | collective-permute-start | bytes 98312 | tf_op jit(solution)/shard_map/ppermute | solution.py:19
  17.4 25.0 %collective-permute-start.1 = (f32[1,8,1024]{2,1,0:T(8,128)}, f32[1,8,1024]{2,1,0:T(8,128)}, u32[]{:S(2)}, u32[]{:S(2)}) collective-permute-start(f32[1,8,1024]{2,1,0:T(8,128)} %get-tuple-element.12), channel_id=1, source_target_pairs={{2,0},{4,2},{6,4},{8,6},{10,8},{12,10},{14,12},{16,14},{18,16},{20... | collective-permute-start | bytes 98312 | tf_op jit(solution)/shard_map/ppermute | solution.py:20
  18.6 25.3 %collective-permute-start = (f32[1,8,1024]{2,1,0:T(8,128)}, f32[1,8,1024]{2,1,0:T(8,128)}, u32[]{:S(2)}, u32[]{:S(2)}) collective-permute-start(f32[1,8,1024]{2,1,0:T(8,128)} %get-tuple-element.10), channel_id=1, source_target_pairs={{0,2},{2,4},{4,6},{6,8},{8,10},{10,12},{12,14},{14,16},{16,18},{18... | collective-permute-start | bytes 98312 | tf_op jit(solution)/shard_map/ppermute | solution.py:19
  25.1 4.0 %copy-start.4 = (f32[1,1,16,64]{3,2,1,0:T(8,128)S(1)}, f32[1,1,16,64]{3,2,1,0:T(8,128)}, u32[]{:S(2)}) copy-start(f32[1,1,16,64]{3,2,1,0:T(8,128)} %param.14) | copy-start | bytes 12292
  29.1 9.0 %copy-start.6 = (f32[1,1,4,512]{3,2,1,0:T(4,128)S(1)}, f32[1,1,4,512]{3,2,1,0:T(4,128)}, u32[]{:S(2)}) copy-start(f32[1,1,4,512]{3,2,1,0:T(4,128)} %param.17) | copy-start | bytes 24580
  37.0 11.1 %copy-start.12 = (s32[32]{0:T(128)}, s32[32]{0:T(128)S(1)}, u32[]{:S(2)}) copy-start(s32[32]{0:T(128)S(1)} %fusion.29) | copy-start | bytes 388
  48.1 54.5 %copy-start.2 = (f32[1,256,512]{2,1,0:T(8,128)S(1)}, f32[1,256,512]{2,1,0:T(8,128)}, u32[]{:S(2)}) copy-start(f32[1,256,512]{2,1,0:T(8,128)} %param.19) | copy-start | bytes 1572868
  94.2 0.5 copy-start.15
  95.6 47.8 %copy-start.16 = (f32[16]{0:T(128)S(1)}, f32[16]{0:T(128)}, u32[]{:S(2)}) copy-start(f32[16]{0:T(128)} %copy-done.15) | copy-start | bytes 196
  143.4 0.6 copy-start.13
  145.8 22.2 %copy-start.3 = (f32[32,1024]{1,0:T(8,128)}, f32[32,1024]{1,0:T(8,128)S(1)}, u32[]{:S(2)}) copy-start(f32[32,1024]{1,0:T(8,128)S(1)} %gather_fusion.5) | copy-start | bytes 393220
  149.6 18.8 %collective-permute-start.7 = (f32[1,8,1024]{2,1,0:T(8,128)}, f32[1,8,1024]{2,1,0:T(8,128)S(1)}, u32[]{:S(2)}, u32[]{:S(2)}) collective-permute-start(f32[1,8,1024]{2,1,0:T(8,128)} %get-tuple-element.9), channel_id=1, source_target_pairs={{1,0},{3,2},{5,4},{7,6},{9,8},{11,10},{13,12},{15,14},{17,16},{19,... | collective-permute-start | bytes 98312 | tf_op jit(solution)/shard_map/ppermute | solution.py:20
  150.9 18.3 %collective-permute-start.6 = (f32[1,8,1024]{2,1,0:T(8,128)}, f32[1,8,1024]{2,1,0:T(8,128)S(1)}, u32[]{:S(2)}, u32[]{:S(2)}) collective-permute-start(f32[1,8,1024]{2,1,0:T(8,128)} %get-tuple-element.7), channel_id=1, source_target_pairs={{0,1},{2,3},{4,5},{6,7},{8,9},{10,11},{12,13},{14,15},{16,17},{18,... | collective-permute-start | bytes 98312 | tf_op jit(solution)/shard_map/ppermute | solution.py:19
  154.0 16.1 %collective-permute-start.5 = (f32[1,8,1024]{2,1,0:T(8,128)S(1)}, f32[1,8,1024]{2,1,0:T(8,128)S(1)}, u32[]{:S(2)}, u32[]{:S(2)}) collective-permute-start(f32[1,8,1024]{2,1,0:T(8,128)S(1)} %get-tuple-element.8), channel_id=1, source_target_pairs={{2,0},{4,2},{6,4},{8,6},{10,8},{12,10},{14,12},{16,14},{18,16},{20... | collective-permute-start | bytes 98312 | tf_op jit(solution)/shard_map/ppermute | solution.py:20
  155.3 15.7 %collective-permute-start.4 = (f32[1,8,1024]{2,1,0:T(8,128)S(1)}, f32[1,8,1024]{2,1,0:T(8,128)S(1)}, u32[]{:S(2)}, u32[]{:S(2)}) collective-permute-start(f32[1,8,1024]{2,1,0:T(8,128)S(1)} %get-tuple-element.6), channel_id=1, source_target_pairs={{0,2},{2,4},{4,6},{6,8},{8,10},{10,12},{12,14},{14,16},{16,18},{18... | collective-permute-start | bytes 98312 | tf_op jit(solution)/shard_map/ppermute | solution.py:19
  168.0 50.4 %copy-start.14 = (f32[16]{0:T(128)S(1)}, f32[16]{0:T(128)}, u32[]{:S(2)}) copy-start(f32[16]{0:T(128)} %copy-done.13) | copy-start | bytes 196
where the time goes:
time: 220 us; the launch traced here: 219 us
  blocking collectives  128 us (58%)
  local copies, waits for them, and re-layouts  33.2 us (15%)
  starting transfers between devices  23.1 us (10%)
  matrix products  21.5 us (10%)
  other arithmetic  12.4 us (6%)
    psum x3, blocking collectives, global_inner(): return lax.psum(inner(first, second), ('dam', 'sec'))  124 us
    ppermute x4, starting transfers between devices, with_halo(): before = lax.ppermute(last, axis, up)  18 us
    dot_general x2, matrix products, local_product(): prod = jnp.einsum('bde,bes->bds', stiff, gathered, precision=HIGH)  15.7 us
    another operation x10, local copies, waits for them, and re-layouts, shards(): beside = jnp.stack([dam_side[0], dam_side[3], sec_side[0], sec_side[3]])  12.2 us
    reshape x2, local copies, waits for them, and re-layouts, local_product(): gathered = field[cols].reshape(nblk, cols.shape[1] * bdof, ncol)  6.06 us
    ppermute x4, starting transfers between devices, with_halo(): after = lax.ppermute(first, axis, down)  5.13 us
    dot_general x2, matrix products, precondition(): jnp.einsum('bde,bes->bds', blocks_pre, field.reshape(nblk, bdof, ncol), p...  4.68 us
  transfers between devices with their start and end apart: 8, of which 0 were waited for; matrix products, arithmetic and copies ran while one was open for 14% of the time, Pallas kernels for 0%

commit v1 on v0

--- a/solution.py
+++ b/solution.py
@@ -3,10 +3,21 @@
 from jax import lax
 from jax.sharding import PartitionSpec as P
 
-ITERS = 2
+HIGH = lax.Precision.HIGHEST
 
 
-HIGH = lax.Precision.HIGHEST
+def swap_gather(values, axis):
+    size = lax.axis_size(axis)
+    if size & (size - 1):
+        return lax.all_gather(values, axis, axis=0, tiled=True)
+    hop = 1
+    while hop < size:
+        pairs = [[i, i + hop] for i in range(size) if not i & hop]
+        values = lax.all_gather(
+            values, axis, axis=0, tiled=True, axis_index_groups=pairs
+        )
+        hop *= 2
+    return values
 
 
 def with_halo(array, sides, width):
@@ -74,37 +85,42 @@
         ).reshape(ncorner, width)
         return outz.at[cmap].add(correct)
 
+    def operate(field):
+        local = local_product(stiff, cols, tang, field)
+        faces = field[fmap]
+        dam_side = with_halo(faces[0:2], (("dam", 0),), 1)
+        sec_side = with_halo(faces[2:4], (("sec", 0),), 1)
+        beside = jnp.stack([dam_side[0], dam_side[3], sec_side[0], sec_side[3]])
+        term = (weights * (faces - beside).reshape(4, nface, bdof, ncol)).reshape(4 * nface, width)
+        return local.at[flat_faces].add(term)
+
     def inner(first, second):
         return (first * second).reshape(nblk, bdof, ncol).sum(axis=(0, 1))
 
     def spread(coef):
         return jnp.tile(coef, bdof)
 
-    def global_inner(first, second):
-        return lax.psum(inner(first, second), ("dam", "sec"))
-
-    solution = jnp.zeros_like(resid)
     zvec = precondition(resid)
-    direction = zvec
-    gamma = global_inner(resid, zvec)
-    for step in range(ITERS):
-        local = local_product(stiff, cols, tang, direction)
-        faces = direction[fmap]
-        dam_side = with_halo(faces[0:2], (("dam", 0),), 1)
-        sec_side = with_halo(faces[2:4], (("sec", 0),), 1)
-        beside = jnp.stack([dam_side[0], dam_side[3], sec_side[0], sec_side[3]])
-        term = (weights * (faces - beside).reshape(4, nface, bdof, ncol)).reshape(4 * nface, width)
-        image = local.at[flat_faces].add(term)
-        delta = global_inner(direction, image)
-        alpha = spread(gamma / delta)
-        solution = solution + alpha * direction
-        resid = resid - alpha * image
-        if step + 1 < ITERS:
-            zvec = precondition(resid)
-            gnew = global_inner(resid, zvec)
-            direction = zvec + spread(gnew / gamma) * direction
-            gamma = gnew
-    return (solution[None, None], resid[None, None])
+    image = operate(zvec)
+    mvec = precondition(image)
+    nvec = operate(mvec)
+    parts = jnp.concatenate(
+        [inner(resid, zvec), inner(zvec, image), inner(image, mvec), inner(mvec, nvec)]
+    )
+    stacked = swap_gather(swap_gather(parts[None], "sec"), "dam")
+    sums = stacked.sum(axis=0).reshape(4, ncol)
+    gamma, delta, mu, nu = sums[0], sums[1], sums[2], sums[3]
+    alpha = gamma / delta
+    gnew = gamma - 2.0 * alpha * delta + alpha * alpha * mu
+    grow = 1.0 + gnew / gamma
+    dnew = grow * grow * delta - 2.0 * alpha * grow * mu + alpha * alpha * nu
+    anew = gnew / dnew
+    both = spread(alpha + anew * grow)
+    second = spread(anew * alpha)
+    return (
+        (both * zvec - second * mvec)[None, None],
+        (resid - both * image + second * nvec)[None, None],
+    )
 
 
 def solution(mesh):

time: 220 us -> 122 us (0.55)
  blocking collectives: 128 us -> 26.7 us
    psum x3 -> x0, blocking collectives: 124 us -> none  [global_inner(): return lax.psum(inner(first, second), ('dam', 'sec'))]
    all_gather x0 -> x4, blocking collectives: none -> 20.3 us  [swap_gather(): lax.all_gather(values, axis, axis=0, tiled=True, axis_index_groups=pairs)]
    unnamed x0 -> x1, blocking collectives: none -> 2.45 us
  transfers between devices with their start and end apart: 8 -> 8, of which waited for: 0 -> 0; matrix products, arithmetic and copies ran while one was open for 14% -> 26% of each run, Pallas kernels for 0% -> 0%
where the time goes in v1:
time: 122 us; the launch traced here: 121 us
  local copies, waits for them, and re-layouts  34.9 us (29%)
  blocking collectives  26.7 us (22%)
  starting transfers between devices  23.2 us (19%)
  matrix products  21.5 us (18%)
  other arithmetic  13.2 us (11%)
  between operations  1.68 us (1%)
    all_gather x4, blocking collectives, swap_gather(): lax.all_gather(values, axis, axis=0, tiled=True, axis_index_groups=pairs)  20.3 us
    ppermute x4, starting transfers between devices, with_halo(): before = lax.ppermute(last, axis, up)  18.1 us
    dot_general x2, matrix products, local_product(): prod = jnp.einsum('bde,bes->bds', stiff, gathered, precision=HIGH)  15.7 us
    another operation x10, local copies, waits for them, and re-layouts, operate(): beside = jnp.stack([dam_side[0], dam_side[3], sec_side[0], sec_side[3]])  12.2 us
    reshape x2, local copies, waits for them, and re-layouts, local_product(): gathered = field[cols].reshape(nblk, cols.shape[1] * bdof, ncol)  6.06 us
    ppermute x4, starting transfers between devices, with_halo(): after = lax.ppermute(first, axis, down)  5.14 us
    dot_general x2, matrix products, precondition(): jnp.einsum('bde,bes->bds', blocks_pre, field.reshape(nblk, bdof, ncol), p...  4.69 us
    scatter-add x2, other arithmetic, operate(): return local.at[flat_faces].add(term)  4.3 us
  transfers between devices with their start and end apart: 8, of which 0 were waited for; matrix products, arithmetic and copies ran while one was open for 26% of the time, Pallas kernels for 0%

profile of v1, /device:TPU:0, one launch (start us, length us, event | category | flops | bytes accessed | tf_op | source)
XLA Modules:
  0.0 121.2 jit_solution(28599262615286470)
XLA Ops:
  0.7 1.2 reshape_squeeze.10
  1.9 0.7 convert_bitcast_fusion
  2.6 2.0 %convolution_bitcast_fusion.1 = f32[16,64,16]{1,2,0:T(8,128)S(1)} fusion(f32[1,1,16,64,64]{4,3,2,1,0:T(8,128)} %param.15, f32[16,64,16]{2,1,0:T(8,128)S(1)} %reshape_squeeze.10, f32[16,16]{1,0:T(8,128)S(1)} %convert_bitcast_fusion), kind=kOutput, calls=%fused_computation.15 | convolution fusion | flops 12599296 | bytes 394240 | tf_op jit(solution)/shard_map/bde,bes->bds/dot_general | solution.py:78
  6.7 1.9 %all-gather.3 = f32[2,4,1024]{2,1,0:T(4,128)S(1)} all-gather(f32[1,4,1024]{2,1,0:T(4,128)S(1)} %bitcast.97), channel_id=2, replica_groups=mesh['dam'=16,'sec'=2] {'sec'}, dimensions={0}, use_global_device_ids=true | all-gather | bytes 49152 | tf_op jit(solution)/shard_map/all_gather | solution.py:82
  11.7 1.3 %collective-permute-start.3 = (f32[1,8,1024]{2,1,0:T(8,128)}, f32[1,8,1024]{2,1,0:T(8,128)}, u32[]{:S(2)}, u32[]{:S(2)}) collective-permute-start(f32[1,8,1024]{2,1,0:T(8,128)} %get-tuple-element.18), channel_id=1, source_target_pairs={{1,0},{3,2},{5,4},{7,6},{9,8},{11,10},{13,12},{15,14},{17,16},{19,... | collective-permute-start | bytes 98312 | tf_op jit(solution)/shard_map/ppermute | solution.py:31
  13.0 4.2 %collective-permute-start.2 = (f32[1,8,1024]{2,1,0:T(8,128)}, f32[1,8,1024]{2,1,0:T(8,128)}, u32[]{:S(2)}, u32[]{:S(2)}) collective-permute-start(f32[1,8,1024]{2,1,0:T(8,128)} %get-tuple-element.16), channel_id=1, source_target_pairs={{0,1},{2,3},{4,5},{6,7},{8,9},{10,11},{12,13},{14,15},{16,17},{18,... | collective-permute-start | bytes 98312 | tf_op jit(solution)/shard_map/ppermute | solution.py:30
  17.2 1.3 %collective-permute-start.1 = (f32[1,8,1024]{2,1,0:T(8,128)}, f32[1,8,1024]{2,1,0:T(8,128)}, u32[]{:S(2)}, u32[]{:S(2)}) collective-permute-start(f32[1,8,1024]{2,1,0:T(8,128)} %get-tuple-element.17), channel_id=1, source_target_pairs={{2,0},{4,2},{6,4},{8,6},{10,8},{12,10},{14,12},{16,14},{18,16},{20... | collective-permute-start | bytes 98312 | tf_op jit(solution)/shard_map/ppermute | solution.py:31
  18.5 6.0 %collective-permute-start = (f32[1,8,1024]{2,1,0:T(8,128)}, f32[1,8,1024]{2,1,0:T(8,128)}, u32[]{:S(2)}, u32[]{:S(2)}) collective-permute-start(f32[1,8,1024]{2,1,0:T(8,128)} %get-tuple-element.15), channel_id=1, source_target_pairs={{0,2},{2,4},{4,6},{6,8},{8,10},{10,12},{12,14},{14,16},{16,18},{18... | collective-permute-start | bytes 98312 | tf_op jit(solution)/shard_map/ppermute | solution.py:30
  24.9 0.8 gather_fusion.1
  25.7 3.0 %reshape.210 = f32[16,448,16]{2,1,0:T(8,128)} reshape(f32[112,1024]{1,0:T(8,128)S(1)} %gather_fusion.1) | data formatting | bytes 917504 | tf_op jit(solution)/shard_map/reshape | solution.py:39
  29.0 7.9 %fusion.7 = f32[16,64,16]{1,2,0:T(8,128)S(1)} fusion(f32[16,448,16]{2,1,0:T(8,128)} %reshape.210, f32[1,1,16,64,448]{4,3,2,1,0:T(8,128)S(1)} %copy-done, f32[16,64,16]{1,2,0:T(8,128)S(1)} %copy.59, f32[16,64]{1,0:T(8,128)S(1)} %bitcast.98), kind=kOutput, calls=%fused_computation.17 | convolution fusion | flops 88113152 | bytes 2428928 | tf_op jit(solution)/shard_map/bde,bes->bds/dot_general | solution.py:40
  39.0 1.3 %dynamic-slice = u32[1]{0:T(128)} dynamic-slice(u32[32]{0:T(128)} %constant.28, u32[]{:T(128)S(6)} %add.86), dynamic_slice_sizes={1} | dynamic-slice | bytes 12
  40.9 1.6 %stack.29 = f32[1,8,64,16]{3,2,1,0:T(8,128)} reshape(f32[1,8,1024]{2,1,0:T(8,128)} %collective-permute-done.3) | data formatting | bytes 65536 | tf_op jit(solution)/shard_map/stack | solution.py:93
  42.5 1.6 %stack.28 = f32[1,8,64,16]{3,2,1,0:T(8,128)} reshape(f32[1,8,1024]{2,1,0:T(8,128)} %collective-permute-done.2) | data formatting | bytes 65536 | tf_op jit(solution)/shard_map/stack | solution.py:93
  44.1 1.6 %stack.27 = f32[1,8,64,16]{3,2,1,0:T(8,128)} reshape(f32[1,8,1024]{2,1,0:T(8,128)} %collective-permute-done.1) | data formatting | bytes 65536 | tf_op jit(solution)/shard_map/stack | solution.py:93
  45.6 1.6 %stack.26 = f32[1,8,64,16]{3,2,1,0:T(8,128)} reshape(f32[1,8,1024]{2,1,0:T(8,128)} %collective-permute-done) | data formatting | bytes 65536 | tf_op jit(solution)/shard_map/stack | solution.py:93
  47.2 1.3 %pad_maximum_fusion = f32[4,8,64,16]{3,2,1,0:T(8,128)S(1)} fusion(f32[1,8,64,16]{3,2,1,0:T(8,128)} %stack.29, f32[1,8,64,16]{3,2,1,0:T(8,128)} %stack.28, f32[1,8,64,16]{3,2,1,0:T(8,128)} %stack.27, f32[1,8,64,16]{3,2,1,0:T(8,128)} %stack.26), kind=kLoop, calls=%fused_computation.22 | loop fusion | flops 98304 | bytes 262144 | tf_op jit(solution)/shard_map/stack | solution.py:93
  48.5 1.3 %stack.31 = f32[32,1024]{1,0:T(8,128)} reshape(f32[4,8,64,16]{3,2,1,0:T(8,128)S(1)} %pad_maximum_fusion) | data formatting | bytes 262144 | tf_op jit(solution)/shard_map/stack | solution.py:93
  49.8 1.6 %scatter_custom_fusion.1 = f32[16,1024]{1,0:T(8,128)S(1)} fusion(f32[16,1024]{1,0:T(8,128)S(1)} %reshape.212, s32[32]{0:T(128)} %fusion.29, f32[32,1024]{1,0:T(8,128)S(1)} %mul.138, f32[32,1024]{1,0:T(8,128)} %copy-done.3, f32[32,1024]{1,0:T(8,128)} %stack.31), kind=kCustom, calls=%fused_computation.33 | custom fusion | flops 98304 | bytes 458752 | tf_op jit(solution)/shard_map/scatter-add | solution.py:95
  51.6 1.3 %gather_fusion.3 = f32[4,1024]{1,0:T(4,128)} fusion(f32[16,1024]{1,0:T(8,128)S(1)} %scatter_custom_fusion.1, s32[1024]{0:T(1024)} %copy-done.8), kind=kCustom, calls=%fused_computation.3 | custom fusion | bytes 32784 | tf_op jit(solution)/shard_map/gather | solution.py:81
  52.9 2.7 %convolution_bitcast_fusion = f32[16,64,16]{1,2,0:T(8,128)} fusion(f32[16,64,16]{2,1,0:T(8,128)S(1)} %reshape.213, f32[1,1,16,64,64]{4,3,2,1,0:T(8,128)} %param.15), kind=kOutput, calls=%fused_computation.14 | convolution fusion | flops 12582912 | bytes 393216 | tf_op jit(solution)/shard_map/bde,bes->bds/dot_general | solution.py:78
  55.5 1.1 copy.62
  56.9 2.0 %all-gather.4 = f32[2,4,1024]{2,1,0:T(4,128)S(1)} all-gather(f32[1,4,1024]{2,1,0:T(4,128)} %bitcast.96), channel_id=3, replica_groups=mesh['dam'=16,'sec'=2] {'sec'}, dimensions={0}, use_global_device_ids=true | all-gather | bytes 49152 | tf_op jit(solution)/shard_map/all_gather | solution.py:82
  59.9 0.8 scatter_fusion.1
  60.7 0.8 gather_fusion.4
  61.7 1.2 %gather_fusion.5 = f32[32,1024]{1,0:T(8,128)} fusion(f32[16,1024]{1,0:T(8,128)S(1)} %scatter_fusion.1, s32[1024]{0:T(1024)S(1)} %pad_clamp_fusion), kind=kCustom, calls=%fused_computation.5 | custom fusion | bytes 262272 | tf_op jit(solution)/shard_map/gather | solution.py:90
  62.9 3.0 %reshape.217 = f32[16,448,16]{2,1,0:T(8,128)} reshape(f32[112,1024]{1,0:T(8,128)S(1)} %gather_fusion.4) | data formatting | bytes 917504 | tf_op jit(solution)/shard_map/reshape | solution.py:39
  66.1 0.8 slice_bitcast_fusion.3
  67.0 1.3 %collective-permute-start.7 = (f32[1,8,1024]{2,1,0:T(8,128)S(1)}, f32[1,8,1024]{2,1,0:T(8,128)S(1)}, u32[]{:S(2)}, u32[]{:S(2)}) collective-permute-start(f32[1,8,1024]{2,1,0:T(8,128)S(1)} %get-tuple-element.14), channel_id=1, source_target_pairs={{1,0},{3,2},{5,4},{7,6},{9,8},{11,10},{13,12},{15,14},{17,16},{19,... | collective-permute-start | bytes 98312 | tf_op jit(solution)/shard_map/ppermute | solution.py:31
  68.3 3.0 %collective-permute-start.6 = (f32[1,8,1024]{2,1,0:T(8,128)S(1)}, f32[1,8,1024]{2,1,0:T(8,128)S(1)}, u32[]{:S(2)}, u32[]{:S(2)}) collective-permute-start(f32[1,8,1024]{2,1,0:T(8,128)S(1)} %get-tuple-element.12), channel_id=1, source_target_pairs={{0,1},{2,3},{4,5},{6,7},{8,9},{10,11},{12,13},{14,15},{16,17},{18,... | collective-permute-start | bytes 98312 | tf_op jit(solution)/shard_map/ppermute | solution.py:30
  71.3 1.3 %collective-permute-start.5 = (f32[1,8,1024]{2,1,0:T(8,128)S(1)}, f32[1,8,1024]{2,1,0:T(8,128)S(1)}, u32[]{:S(2)}, u32[]{:S(2)}) collective-permute-start(f32[1,8,1024]{2,1,0:T(8,128)S(1)} %get-tuple-element.13), channel_id=1, source_target_pairs={{2,0},{4,2},{6,4},{8,6},{10,8},{12,10},{14,12},{16,14},{18,16},{20... | collective-permute-start | bytes 98312 | tf_op jit(solution)/shard_map/ppermute | solution.py:31
  72.6 4.8 %collective-permute-start.4 = (f32[1,8,1024]{2,1,0:T(8,128)S(1)}, f32[1,8,1024]{2,1,0:T(8,128)S(1)}, u32[]{:S(2)}, u32[]{:S(2)}) collective-permute-start(f32[1,8,1024]{2,1,0:T(8,128)S(1)} %get-tuple-element.11), channel_id=1, source_target_pairs={{0,2},{2,4},{4,6},{6,8},{8,10},{10,12},{12,14},{14,16},{16,18},{18... | collective-permute-start | bytes 98312 | tf_op jit(solution)/shard_map/ppermute | solution.py:30
  77.5 7.9 %fusion.13 = f32[16,64,16]{1,2,0:T(8,128)S(1)} fusion(f32[16,448,16]{2,1,0:T(8,128)} %reshape.217, f32[1,1,16,64,448]{4,3,2,1,0:T(8,128)S(1)} %copy-done, f32[16,64,16]{1,2,0:T(8,128)S(1)} %copy.65, f32[16,64]{1,0:T(8,128)S(1)} %bitcast.99), kind=kOutput, calls=%fused_computation.19 | convolution fusion | flops 88113152 | bytes 2428928 | tf_op jit(solution)/shard_map/bde,bes->bds/dot_general | solution.py:40
  85.5 0.9 reshape.219
  86.5 0.8 stack.35
  87.3 0.8 stack.34
  88.1 0.8 stack.33
  88.9 0.8 stack.32
  89.8 1.3 %pad_maximum_fusion.1 = f32[4,8,64,16]{3,2,1,0:T(8,128)S(1)} fusion(f32[1,8,64,16]{3,2,1,0:T(8,128)} %stack.35, f32[1,8,64,16]{3,2,1,0:T(8,128)} %stack.34, f32[1,8,64,16]{3,2,1,0:T(8,128)} %stack.33, f32[1,8,64,16]{3,2,1,0:T(8,128)} %stack.32), kind=kLoop, calls=%fused_computation.23 | loop fusion | flops 98304 | bytes 262144 | tf_op jit(solution)/shard_map/stack | solution.py:93
  91.1 1.3 %stack.37 = f32[32,1024]{1,0:T(8,128)} reshape(f32[4,8,64,16]{3,2,1,0:T(8,128)S(1)} %pad_maximum_fusion.1) | data formatting | bytes 262144 | tf_op jit(solution)/shard_map/stack | solution.py:93
  92.3 2.7 %scatter_custom_fusion.3 = f32[16,1024]{1,0:T(8,128)} fusion(f32[16,1024]{1,0:T(8,128)} %reshape.219, s32[32]{0:T(128)} %fusion.29, f32[32,1024]{1,0:T(8,128)S(1)} %mul.138, f32[32,1024]{1,0:T(8,128)} %gather_fusion.5, f32[32,1024]{1,0:T(8,128)} %stack.37), kind=kCustom, calls=%fused_computation.30 | custom fusion | flops 98304 | bytes 458752 | tf_op jit(solution)/shard_map/scatter-add | solution.py:95
  95.0 0.9 multiply_reduce_fusion.3
  96.5 2.4 %all-reduce = f32[128]{0:T(128)S(1)} all-reduce(f32[128]{0:T(128)S(1)} %maximum_dynamic-update-slice_fusion), channel_id=4, replica_groups={{0,1},{2,3},{4,5},{6,7},{8,9},{10,11},{12,13},{14,15},{16,17},{18,19},{..., use_global_device_ids=true, to_apply=%add | all-reduce | flops 128 | bytes 1024
  99.0 5.1 %all-gather.5 = f32[2,2,64]{2,1,0:T(2,128)S(1)} all-gather(f32[1,2,64]{2,1,0:T(2,128)S(1)} %reshape.326), channel_id=1, replica_groups={{0,2},{4,6},{8,10},{12,14},{16,18},{20,22},{24,26},{28,30},{1,3},{5,7},..., dimensions={0}, use_global_device_ids=true | all-gather | bytes 1536 | tf_op jit(solution)/shard_map/all_gather | solution.py:16
  104.1 5.6 %all-gather.6 = f32[2,4,64]{2,1,0:T(4,128)S(1)} all-gather(f32[1,4,64]{2,1,0:T(4,128)S(1)} %bitcast.101), channel_id=1, replica_groups={{0,4},{2,6},{8,12},{10,14},{16,20},{18,22},{24,28},{26,30},{1,5},{3,7},..., dimensions={0}, use_global_device_ids=true | all-gather | bytes 3072 | tf_op jit(solution)/shard_map/all_gather | solution.py:16
  109.7 4.3 %all_gather.26 = f32[16,64]{1,0:T(8,128)S(1)} all-gather(f32[8,64]{1,0:T(8,128)S(1)} %bitcast.100), channel_id=1, replica_groups={{0,8},{2,10},{4,12},{6,14},{16,24},{18,26},{20,28},{22,30},{1,9},{3,11}..., dimensions={0}, use_global_device_ids=true | all-gather | bytes 6144 | tf_op jit(solution)/shard_map/all_gather | solution.py:16
  114.1 5.3 %all_gather.27 = f32[32,64]{1,0:T(8,128)S(1)} all-gather(f32[16,64]{1,0:T(8,128)S(1)} %all_gather.26), channel_id=1, replica_groups={{0,16},{2,18},{4,20},{6,22},{8,24},{10,26},{12,28},{14,30},{1,17},{3,19..., dimensions={0}, use_global_device_ids=true | all-gather | bytes 12288 | tf_op jit(solution)/shard_map/all_gather | solution.py:16
  119.7 1.5 %add_bitcast_fusion = (f32[1,1,16,1024]{3,2,1,0:T(8,128)}, f32[1,1,16,1024]{3,2,1,0:T(8,128)}) fusion(f32[16,1024]{1,0:T(8,128)} %scatter_custom_fusion.3, f32[16,1024]{1,0:T(8,128)S(1)} %bitcast_multiply_fusion, f32[16,1024]{1,0:T(8,128)S(1)} %scatter_custom_fusion.1, f32[1024]{0:T(1024)S(1)} %mul.159, f32[1024]{0:T(1024)S(1)} %mul.155, ...), kind=kLoop, calls=%fused_computation.37 | loop fusion | flops 114688 | bytes 466944 | tf_op jit(solution)/shard_map/broadcast_in_dim | solution.py:122
  (89 shorter events, 10.8 us)
Async XLA Ops:
  0.6 28.3 %copy-start = (f32[1,1,16,64,448]{4,3,2,1,0:T(8,128)S(1)}, f32[1,1,16,64,448]{4,3,2,1,0:T(8,128)}, u32[]{:S(2)}) copy-start(f32[1,1,16,64,448]{4,3,2,1,0:T(8,128)} %param.12) | copy-start | bytes 5505028
  0.6 5.4 %copy-start.4 = (f32[1,1,16,1024]{3,2,1,0:T(8,128)S(1)}, f32[1,1,16,1024]{3,2,1,0:T(8,128)}, u32[]{:S(2)}) copy-start(f32[1,1,16,1024]{3,2,1,0:T(8,128)} %param.10) | copy-start | bytes 196612
  0.7 8.1 %copy-start.1 = (f32[1,256,512]{2,1,0:T(8,128)S(1)}, f32[1,256,512]{2,1,0:T(8,128)}, u32[]{:S(2)}) copy-start(f32[1,256,512]{2,1,0:T(8,128)} %param.19) | copy-start | bytes 1572868
  0.7 8.9 %copy-start.7 = (s32[1,1,4,8]{3,2,1,0:T(4,128)S(1)}, s32[1,1,4,8]{3,2,1,0:T(4,128)}, u32[]{:S(2)}) copy-start(s32[1,1,4,8]{3,2,1,0:T(4,128)} %param.16) | copy-start | bytes 388
  2.6 22.2 %copy-start.10 = (s32[1,1,16,7]{2,1,3,0:T(1,128)S(1)}, s32[1,1,16,7]{2,1,3,0:T(1,128)}, u32[]{:S(2)}) copy-start(s32[1,1,16,7]{2,1,3,0:T(1,128)} %param.13) | copy-start | bytes 1348
  5.8 20.0 %copy-start.9 = (s32[4]{0:T(128)}, s32[4]{0:T(128)S(1)}, u32[]{:S(2)}) copy-start(s32[4]{0:T(128)S(1)} %fusion.28) | copy-start | bytes 52
  6.1 19.6 %copy-start.8 = (s32[1024]{0:T(1024)}, s32[1024]{0:T(1024)S(1)}, u32[]{:S(2)}) copy-start(s32[1024]{0:T(1024)S(1)} %pad_clamp_fusion.2) | copy-start | bytes 12292
  11.0 7.5 %copy-start.3 = (f32[32,1024]{1,0:T(8,128)}, f32[32,1024]{1,0:T(8,128)S(1)}, u32[]{:S(2)}) copy-start(f32[32,1024]{1,0:T(8,128)S(1)} %gather_fusion.2) | copy-start | bytes 393220
  11.7 29.2 %collective-permute-start.3 = (f32[1,8,1024]{2,1,0:T(8,128)}, f32[1,8,1024]{2,1,0:T(8,128)}, u32[]{:S(2)}, u32[]{:S(2)}) collective-permute-start(f32[1,8,1024]{2,1,0:T(8,128)} %get-tuple-element.18), channel_id=1, source_target_pairs={{1,0},{3,2},{5,4},{7,6},{9,8},{11,10},{13,12},{15,14},{17,16},{19,... | collective-permute-start | bytes 98312 | tf_op jit(solution)/shard_map/ppermute | solution.py:31
  13.0 29.5 %collective-permute-start.2 = (f32[1,8,1024]{2,1,0:T(8,128)}, f32[1,8,1024]{2,1,0:T(8,128)}, u32[]{:S(2)}, u32[]{:S(2)}) collective-permute-start(f32[1,8,1024]{2,1,0:T(8,128)} %get-tuple-element.16), channel_id=1, source_target_pairs={{0,1},{2,3},{4,5},{6,7},{8,9},{10,11},{12,13},{14,15},{16,17},{18,... | collective-permute-start | bytes 98312 | tf_op jit(solution)/shard_map/ppermute | solution.py:30
  17.2 26.9 %collective-permute-start.1 = (f32[1,8,1024]{2,1,0:T(8,128)}, f32[1,8,1024]{2,1,0:T(8,128)}, u32[]{:S(2)}, u32[]{:S(2)}) collective-permute-start(f32[1,8,1024]{2,1,0:T(8,128)} %get-tuple-element.17), channel_id=1, source_target_pairs={{2,0},{4,2},{6,4},{8,6},{10,8},{12,10},{14,12},{16,14},{18,16},{20... | collective-permute-start | bytes 98312 | tf_op jit(solution)/shard_map/ppermute | solution.py:31
  18.5 27.2 %collective-permute-start = (f32[1,8,1024]{2,1,0:T(8,128)}, f32[1,8,1024]{2,1,0:T(8,128)}, u32[]{:S(2)}, u32[]{:S(2)}) collective-permute-start(f32[1,8,1024]{2,1,0:T(8,128)} %get-tuple-element.15), channel_id=1, source_target_pairs={{0,2},{2,4},{4,6},{6,8},{8,10},{10,12},{12,14},{14,16},{16,18},{18... | collective-permute-start | bytes 98312 | tf_op jit(solution)/shard_map/ppermute | solution.py:30
  24.9 4.0 %copy-start.5 = (f32[1,1,16,64]{3,2,1,0:T(8,128)S(1)}, f32[1,1,16,64]{3,2,1,0:T(8,128)}, u32[]{:S(2)}) copy-start(f32[1,1,16,64]{3,2,1,0:T(8,128)} %param.14) | copy-start | bytes 12292
  29.0 9.0 %copy-start.6 = (f32[1,1,4,512]{3,2,1,0:T(4,128)S(1)}, f32[1,1,4,512]{3,2,1,0:T(4,128)}, u32[]{:S(2)}) copy-start(f32[1,1,4,512]{3,2,1,0:T(4,128)} %param.17) | copy-start | bytes 24580
  49.8 9.3 %copy-start.2 = (f32[1,256,512]{2,1,0:T(8,128)S(1)}, f32[1,256,512]{2,1,0:T(8,128)}, u32[]{:S(2)}) copy-start(f32[1,256,512]{2,1,0:T(8,128)} %param.19) | copy-start | bytes 1572868
  67.0 19.5 %collective-permute-start.7 = (f32[1,8,1024]{2,1,0:T(8,128)S(1)}, f32[1,8,1024]{2,1,0:T(8,128)S(1)}, u32[]{:S(2)}, u32[]{:S(2)}) collective-permute-start(f32[1,8,1024]{2,1,0:T(8,128)S(1)} %get-tuple-element.14), channel_id=1, source_target_pairs={{1,0},{3,2},{5,4},{7,6},{9,8},{11,10},{13,12},{15,14},{17,16},{19,... | collective-permute-start | bytes 98312 | tf_op jit(solution)/shard_map/ppermute | solution.py:31
  68.3 19.0 %collective-permute-start.6 = (f32[1,8,1024]{2,1,0:T(8,128)S(1)}, f32[1,8,1024]{2,1,0:T(8,128)S(1)}, u32[]{:S(2)}, u32[]{:S(2)}) collective-permute-start(f32[1,8,1024]{2,1,0:T(8,128)S(1)} %get-tuple-element.12), channel_id=1, source_target_pairs={{0,1},{2,3},{4,5},{6,7},{8,9},{10,11},{12,13},{14,15},{16,17},{18,... | collective-permute-start | bytes 98312 | tf_op jit(solution)/shard_map/ppermute | solution.py:30
  71.3 16.8 %collective-permute-start.5 = (f32[1,8,1024]{2,1,0:T(8,128)S(1)}, f32[1,8,1024]{2,1,0:T(8,128)S(1)}, u32[]{:S(2)}, u32[]{:S(2)}) collective-permute-start(f32[1,8,1024]{2,1,0:T(8,128)S(1)} %get-tuple-element.13), channel_id=1, source_target_pairs={{2,0},{4,2},{6,4},{8,6},{10,8},{12,10},{14,12},{16,14},{18,16},{20... | collective-permute-start | bytes 98312 | tf_op jit(solution)/shard_map/ppermute | solution.py:31
  72.6 16.3 %collective-permute-start.4 = (f32[1,8,1024]{2,1,0:T(8,128)S(1)}, f32[1,8,1024]{2,1,0:T(8,128)S(1)}, u32[]{:S(2)}, u32[]{:S(2)}) collective-permute-start(f32[1,8,1024]{2,1,0:T(8,128)S(1)} %get-tuple-element.11), channel_id=1, source_target_pairs={{0,2},{2,4},{4,6},{6,8},{8,10},{10,12},{12,14},{14,16},{16,18},{18... | collective-permute-start | bytes 98312 | tf_op jit(solution)/shard_map/ppermute | solution.py:30

commit v2 on v1

--- a/solution.py
+++ b/solution.py
@@ -6,31 +6,30 @@
 HIGH = lax.Precision.HIGHEST
 
 
-def swap_gather(values, axis):
-    size = lax.axis_size(axis)
-    if size & (size - 1):
-        return lax.all_gather(values, axis, axis=0, tiled=True)
-    hop = 1
-    while hop < size:
-        pairs = [[i, i + hop] for i in range(size) if not i & hop]
-        values = lax.all_gather(
-            values, axis, axis=0, tiled=True, axis_index_groups=pairs
-        )
-        hop *= 2
-    return values
+def everywhere(values):
+    total = lax.axis_size("dam") * lax.axis_size("sec")
+    copies = jnp.broadcast_to(values[None], (total,) + values.shape)
+    return lax.all_to_all(copies, ("dam", "sec"), split_axis=0, concat_axis=0)
 
 
-def with_halo(array, sides, width):
-    for axis, dim in sides:
-        peers, length = (lax.axis_size(axis), array.shape[dim])
-        up = [(i, (i + 1) % peers) for i in range(peers - 1)]
+def from_sides(lower, upper, axis):
+    size = lax.axis_size(axis)
+    if size & 1:
+        up = [(i, i + 1) for i in range(size - 1)]
         down = [(j, i) for i, j in up]
-        last = lax.slice_in_dim(array, length - width, length, axis=dim)
-        first = lax.slice_in_dim(array, 0, width, axis=dim)
-        before = lax.ppermute(last, axis, up)
-        after = lax.ppermute(first, axis, down)
-        array = jnp.concatenate([before, array, after], axis=dim)
-    return array
+        return lax.ppermute(upper, axis, up), lax.ppermute(lower, axis, down)
+    even = lax.axis_index(axis) % 2 == 0
+    if size == 2:
+        both = lax.all_gather(jnp.where(even, upper, lower), axis)
+        other = jnp.where(even, both[1], both[0])
+        zero = jnp.zeros_like(other)
+        return jnp.where(even, zero, other), jnp.where(even, other, zero)
+    first = [(i, i ^ 1) for i in range(size)]
+    second = [(i, i + 1) for i in range(1, size - 1, 2)]
+    second = second + [(j, i) for i, j in second]
+    near = lax.ppermute(jnp.where(even, upper, lower), axis, first)
+    far = lax.ppermute(jnp.where(even, lower, upper), axis, second)
+    return jnp.where(even, far, near), jnp.where(even, near, far)
 
 
 def local_product(stiff, cols, tang, field):
@@ -88,9 +87,9 @@
     def operate(field):
         local = local_product(stiff, cols, tang, field)
         faces = field[fmap]
-        dam_side = with_halo(faces[0:2], (("dam", 0),), 1)
-        sec_side = with_halo(faces[2:4], (("sec", 0),), 1)
-        beside = jnp.stack([dam_side[0], dam_side[3], sec_side[0], sec_side[3]])
+        sec_side = from_sides(faces[2], faces[3], "sec")
+        dam_side = from_sides(faces[0], faces[1], "dam")
+        beside = jnp.stack(dam_side + sec_side)
         term = (weights * (faces - beside).reshape(4, nface, bdof, ncol)).reshape(4 * nface, width)
         return local.at[flat_faces].add(term)
 
@@ -107,8 +106,7 @@
     parts = jnp.concatenate(
         [inner(resid, zvec), inner(zvec, image), inner(image, mvec), inner(mvec, nvec)]
     )
-    stacked = swap_gather(swap_gather(parts[None], "sec"), "dam")
-    sums = stacked.sum(axis=0).reshape(4, ncol)
+    sums = everywhere(parts).sum(axis=0).reshape(4, ncol)
     gamma, delta, mu, nu = sums[0], sums[1], sums[2], sums[3]
     alpha = gamma / delta
     gnew = gamma - 2.0 * alpha * delta + alpha * alpha * mu

time: 122 us -> 101 us (0.83)
  starting transfers between devices: 23.2 us -> 11.2 us
  blocking collectives: 26.7 us -> 19.4 us
  local copies, waits for them, and re-layouts: 34.9 us -> 30.5 us
  other arithmetic: 13.2 us -> 16 us
    all_gather x4 -> x2, blocking collectives: 20.3 us -> 3.7 us  [from_sides(): both = lax.all_gather(jnp.where(even, upper, lower), axis)]
    ppermute x8 -> x4, starting transfers between devices: 23.2 us -> 11.2 us  [the longest x2 9.34 us: from_sides(): near = lax.ppermute(jnp.where(even, upper, lower), axis, first)]
    all_to_all x0 -> x1, blocking collectives: none -> 11.7 us  [everywhere(): return lax.all_to_all(copies, ('dam', 'sec'), split_axis=0, concat_axis=0)]
    select_n x0 -> x6, other arithmetic: none -> 2.92 us  [the longest x2 1.49 us: from_sides(): far = lax.ppermute(jnp.where(even, lower, upper), axis, second)]
    unnamed x1 -> x0, blocking collectives: 2.45 us -> none
    another operation x10, local copies, waits for them, and re-layouts: 12.2 us -> 10.7 us  [operate(): beside = jnp.stack(dam_side + sec_side)]
    slice x2 -> x0, local copies, waits for them, and re-layouts: 1.49 us -> none  [with_halo(): last = lax.slice_in_dim(array, length - width, length, axis=dim)]
    unnamed x25 -> x22, local copies, waits for them, and re-layouts: 1.44 us -> 0.05 us
  transfers between devices with their start and end apart: 8 -> 4, of which waited for: 0 -> 0; matrix products, arithmetic and copies ran while one was open for 26% -> 29% of each run, Pallas kernels for 0% -> 0%
where the time goes in v2:
time: 101 us; the launch traced here: 99.6 us
  local copies, waits for them, and re-layouts  30.5 us (30%)
  matrix products  21.5 us (21%)
  blocking collectives  19.4 us (19%)
  other arithmetic  16 us (16%)
  starting transfers between devices  11.2 us (11%)
  between operations  1.02 us (1%)
    dot_general x2, matrix products, local_product(): prod = jnp.einsum('bde,bes->bds', stiff, gathered, precision=HIGH)  15.7 us
    all_to_all x1, blocking collectives, everywhere(): return lax.all_to_all(copies, ('dam', 'sec'), split_axis=0, concat_axis=0)  11.7 us
    another operation x10, local copies, waits for them, and re-layouts, operate(): beside = jnp.stack(dam_side + sec_side)  10.7 us
    ppermute x2, starting transfers between devices, from_sides(): near = lax.ppermute(jnp.where(even, upper, lower), axis, first)  9.34 us
    reshape x2, local copies, waits for them, and re-layouts, local_product(): gathered = field[cols].reshape(nblk, cols.shape[1] * bdof, ncol)  6.06 us
    dot_general x2, matrix products, precondition(): jnp.einsum('bde,bes->bds', blocks_pre, field.reshape(nblk, bdof, ncol), p...  4.69 us
    scatter-add x2, other arithmetic, operate(): return local.at[flat_faces].add(term)  4.3 us
    all_gather x2, blocking collectives, precondition(): piece = lax.all_gather(corners, 'sec', axis=0, tiled=True)  3.99 us
  transfers between devices with their start and end apart: 4, of which 0 were waited for; matrix products, arithmetic and copies ran while one was open for 29% of the time, Pallas kernels for 0%

profile of v2, /device:TPU:0, one launch (start us, length us, event | category | flops | bytes accessed | tf_op | source)
XLA Modules:
  0.0 99.6 jit_solution(18117813441687582811)
XLA Ops:
  0.7 1.2 %reshape_squeeze.10 = f32[16,64,16]{2,1,0:T(8,128)S(1)} reshape(f32[1,1,16,1024]{3,2,1,0:T(8,128)} %param.10) | data formatting | bytes 131072 | tf_op jit(solution)/shard_map/reshape;squeeze | solution.py:71
  1.9 0.7 convert_bitcast_fusion
  2.6 2.0 %convolution_bitcast_fusion.1 = f32[16,64,16]{1,2,0:T(8,128)S(1)} fusion(f32[1,1,16,64,64]{4,3,2,1,0:T(8,128)} %param.15, f32[16,64,16]{2,1,0:T(8,128)S(1)} %reshape_squeeze.10, f32[16,16]{1,0:T(8,128)S(1)} %convert_bitcast_fusion), kind=kOutput, calls=%fused_computation.15 | convolution fusion | flops 12599296 | bytes 394240 | tf_op jit(solution)/shard_map/bde,bes->bds/dot_general | solution.py:77
  5.1 0.7 fusion.28
  6.7 1.9 %all-gather.4 = f32[2,4,1024]{2,1,0:T(4,128)S(1)} all-gather(f32[1,4,1024]{2,1,0:T(4,128)S(1)} %bitcast.79), channel_id=2, replica_groups=mesh['dam'=16,'sec'=2] {'sec'}, dimensions={0}, use_global_device_ids=true | all-gather | bytes 49152 | tf_op jit(solution)/shard_map/all_gather | solution.py:81
  9.7 0.7 scatter_fusion
  10.4 0.6 gather_fusion.2
  11.0 0.7 slice_select_fusion.6
  11.7 1.3 %collective-permute-start = (f32[8,1024]{1,0:T(8,128)}, f32[8,1024]{1,0:T(8,128)}, u32[]{:S(2)}, u32[]{:S(2)}) collective-permute-start(f32[8,1024]{1,0:T(8,128)} %get-tuple-element.14), channel_id=1, source_target_pairs={{2,4},{6,8},{10,12},{14,16},{18,20},{22,24},{26,28},{4,2},{8,6},{1... | collective-permute-start | bytes 98312 | tf_op jit(solution)/shard_map/ppermute | solution.py:31
  12.9 5.0 %collective-permute-start.1 = (f32[8,1024]{1,0:T(8,128)}, f32[8,1024]{1,0:T(8,128)}, u32[]{:S(2)}, u32[]{:S(2)}) collective-permute-start(f32[8,1024]{1,0:T(8,128)} %get-tuple-element.15), channel_id=1, source_target_pairs={{0,2},{2,0},{4,6},{6,4},{8,10},{10,8},{12,14},{14,12},{16,18},{18,... | collective-permute-start | bytes 98312 | tf_op jit(solution)/shard_map/ppermute | solution.py:30
  18.5 0.8 gather_fusion.1
  19.3 3.0 %reshape.228 = f32[16,448,16]{2,1,0:T(8,128)} reshape(f32[112,1024]{1,0:T(8,128)S(1)} %gather_fusion.1) | data formatting | bytes 917504 | tf_op jit(solution)/shard_map/reshape | solution.py:38
  22.5 1.9 %all-gather.2 = f32[16,1024]{1,0:T(8,128)S(1)} all-gather(f32[8,1024]{1,0:T(8,128)S(1)} %get-tuple-element.16), channel_id=4, replica_groups=mesh['dam'=16,'sec'=2] {'sec'}, dimensions={0}, use_global_device_ids=true | all-gather | bytes 98304 | tf_op jit(solution)/shard_map/all_gather | solution.py:23
  24.3 0.6 broadcast_select_fusion.3
  25.0 7.9 %fusion.7 = f32[16,64,16]{1,2,0:T(8,128)S(1)} fusion(f32[16,448,16]{2,1,0:T(8,128)} %reshape.228, f32[1,1,16,64,448]{4,3,2,1,0:T(8,128)S(1)} %copy-done, f32[16,64,16]{1,2,0:T(8,128)S(1)} %copy.72, f32[16,64]{1,0:T(8,128)S(1)} %bitcast.81), kind=kOutput, calls=%fused_computation.17 | convolution fusion | flops 88113152 | bytes 2428928 | tf_op jit(solution)/shard_map/bde,bes->bds/dot_general | solution.py:39
  34.3 0.6 mul.138
  34.9 1.6 %stack.37 = f32[1,8,64,16]{3,2,1,0:T(8,128)} reshape(f32[8,1024]{1,0:T(8,128)} %get-tuple-element.24) | data formatting | bytes 65536 | tf_op jit(solution)/shard_map/stack | solution.py:92
  36.5 1.6 %stack.36 = f32[1,8,64,16]{3,2,1,0:T(8,128)} reshape(f32[8,1024]{1,0:T(8,128)} %get-tuple-element.23) | data formatting | bytes 65536 | tf_op jit(solution)/shard_map/stack | solution.py:92
  38.1 0.8 broadcast_select_fusion.7
  38.9 0.8 stack.35
  39.7 0.8 stack.34
  40.5 1.3 %pad_maximum_fusion = f32[4,8,64,16]{3,2,1,0:T(8,128)S(1)} fusion(f32[1,8,64,16]{3,2,1,0:T(8,128)} %stack.37, f32[1,8,64,16]{3,2,1,0:T(8,128)} %stack.36, f32[1,8,64,16]{3,2,1,0:T(8,128)} %stack.35, f32[1,8,64,16]{3,2,1,0:T(8,128)} %stack.34), kind=kLoop, calls=%fused_computation.22 | loop fusion | flops 98304 | bytes 262144 | tf_op jit(solution)/shard_map/stack | solution.py:92
  41.8 1.3 %stack.39 = f32[32,1024]{1,0:T(8,128)} reshape(f32[4,8,64,16]{3,2,1,0:T(8,128)S(1)} %pad_maximum_fusion) | data formatting | bytes 262144 | tf_op jit(solution)/shard_map/stack | solution.py:92
  43.1 1.6 %scatter_custom_fusion.1 = f32[16,1024]{1,0:T(8,128)S(1)} fusion(f32[16,1024]{1,0:T(8,128)S(1)} %reshape.230, s32[32]{0:T(128)} %fusion.29, f32[32,1024]{1,0:T(8,128)S(1)} %mul.138, f32[32,1024]{1,0:T(8,128)} %copy-done.3, f32[32,1024]{1,0:T(8,128)} %stack.39), kind=kCustom, calls=%fused_computation.33 | custom fusion | flops 98304 | bytes 458752 | tf_op jit(solution)/shard_map/scatter-add | solution.py:94
  44.9 1.3 %gather_fusion.3 = f32[4,1024]{1,0:T(4,128)} fusion(f32[16,1024]{1,0:T(8,128)S(1)} %scatter_custom_fusion.1, s32[1024]{0:T(1024)} %copy-done.8), kind=kCustom, calls=%fused_computation.3 | custom fusion | bytes 32784 | tf_op jit(solution)/shard_map/gather | solution.py:80
  46.2 2.7 %convolution_bitcast_fusion = f32[16,64,16]{1,2,0:T(8,128)} fusion(f32[16,64,16]{2,1,0:T(8,128)S(1)} %reshape.231, f32[1,1,16,64,64]{4,3,2,1,0:T(8,128)} %param.15), kind=kOutput, calls=%fused_computation.14 | convolution fusion | flops 12582912 | bytes 393216 | tf_op jit(solution)/shard_map/bde,bes->bds/dot_general | solution.py:77
  48.8 1.1 %copy.75 = f32[16,64,16]{2,1,0:T(8,128)S(1)} copy(f32[16,64,16]{1,2,0:T(8,128)} %convolution_bitcast_fusion) | data formatting | bytes 131072 | tf_op jit(solution)/shard_map/bde,bes->bds/dot_general | solution.py:77
  50.2 2.0 %all-gather.5 = f32[2,4,1024]{2,1,0:T(4,128)S(1)} all-gather(f32[1,4,1024]{2,1,0:T(4,128)} %bitcast.78), channel_id=3, replica_groups=mesh['dam'=16,'sec'=2] {'sec'}, dimensions={0}, use_global_device_ids=true | all-gather | bytes 49152 | tf_op jit(solution)/shard_map/all_gather | solution.py:81
  53.2 0.8 scatter_fusion.1
  54.0 0.8 gather_fusion.4
  55.0 1.2 %gather_fusion.5 = f32[32,1024]{1,0:T(8,128)} fusion(f32[16,1024]{1,0:T(8,128)S(1)} %scatter_fusion.1, s32[1024]{0:T(1024)S(1)} %pad_clamp_fusion), kind=kCustom, calls=%fused_computation.5 | custom fusion | bytes 262272 | tf_op jit(solution)/shard_map/gather | solution.py:89
  56.2 3.0 %reshape.235 = f32[16,448,16]{2,1,0:T(8,128)} reshape(f32[112,1024]{1,0:T(8,128)S(1)} %gather_fusion.4) | data formatting | bytes 917504 | tf_op jit(solution)/shard_map/reshape | solution.py:38
  59.4 0.8 slice_select_fusion.4
  60.3 1.9 %all-gather.3 = f32[16,1024]{1,0:T(8,128)S(1)} all-gather(f32[8,1024]{1,0:T(8,128)S(1)} %get-tuple-element.13), channel_id=5, replica_groups=mesh['dam'=16,'sec'=2] {'sec'}, dimensions={0}, use_global_device_ids=true | all-gather | bytes 98304 | tf_op jit(solution)/shard_map/all_gather | solution.py:23
  62.1 0.7 collective-permute-start.2
  62.8 4.3 %collective-permute-start.3 = (f32[8,1024]{1,0:T(8,128)S(1)}, f32[8,1024]{1,0:T(8,128)S(1)}, u32[]{:S(2)}, u32[]{:S(2)}) collective-permute-start(f32[8,1024]{1,0:T(8,128)S(1)} %get-tuple-element.12), channel_id=1, source_target_pairs={{0,2},{2,0},{4,6},{6,4},{8,10},{10,8},{12,14},{14,12},{16,18},{18,... | collective-permute-start | bytes 98312 | tf_op jit(solution)/shard_map/ppermute | solution.py:30
  67.1 7.9 %fusion.13 = f32[16,64,16]{1,2,0:T(8,128)S(1)} fusion(f32[16,448,16]{2,1,0:T(8,128)} %reshape.235, f32[1,1,16,64,448]{4,3,2,1,0:T(8,128)S(1)} %copy-done, f32[16,64,16]{1,2,0:T(8,128)S(1)} %copy.78, f32[16,64]{1,0:T(8,128)S(1)} %bitcast.82), kind=kOutput, calls=%fused_computation.19 | convolution fusion | flops 88113152 | bytes 2428928 | tf_op jit(solution)/shard_map/bde,bes->bds/dot_general | solution.py:39
  75.2 0.9 reshape.237
  76.1 0.8 stack.43
  76.9 0.8 stack.42
  77.7 0.8 stack.41
  78.6 0.8 stack.40
  79.4 1.3 %pad_maximum_fusion.1 = f32[4,8,64,16]{3,2,1,0:T(8,128)S(1)} fusion(f32[1,8,64,16]{3,2,1,0:T(8,128)} %stack.43, f32[1,8,64,16]{3,2,1,0:T(8,128)} %stack.42, f32[1,8,64,16]{3,2,1,0:T(8,128)} %stack.41, f32[1,8,64,16]{3,2,1,0:T(8,128)} %stack.40), kind=kLoop, calls=%fused_computation.23 | loop fusion | flops 98304 | bytes 262144 | tf_op jit(solution)/shard_map/stack | solution.py:92
  80.7 1.3 %stack.45 = f32[32,1024]{1,0:T(8,128)} reshape(f32[4,8,64,16]{3,2,1,0:T(8,128)S(1)} %pad_maximum_fusion.1) | data formatting | bytes 262144 | tf_op jit(solution)/shard_map/stack | solution.py:92
  81.9 2.7 %scatter_custom_fusion.3 = f32[16,1024]{1,0:T(8,128)} fusion(f32[16,1024]{1,0:T(8,128)} %reshape.237, s32[32]{0:T(128)} %fusion.29, f32[32,1024]{1,0:T(8,128)S(1)} %mul.138, f32[32,1024]{1,0:T(8,128)} %gather_fusion.5, f32[32,1024]{1,0:T(8,128)} %stack.45), kind=kCustom, calls=%fused_computation.30 | custom fusion | flops 98304 | bytes 458752 | tf_op jit(solution)/shard_map/scatter-add | solution.py:94
  84.7 0.9 multiply_reduce_fusion.3
  86.1 11.7 %all_to_all.6 = f32[32,1,64]{2,1,0:T(1,128)S(1)} all-to-all(f32[32,1,64]{2,1,0:T(1,128)S(1)} %broadcast_in_dim.6), channel_id=1, replica_groups=mesh['dam'=16,'sec'=2] {'dam','sec'}, dimensions={0} | all-to-all | bytes 16384 | tf_op jit(solution)/shard_map/all_to_all | solution.py:12
  98.1 1.5 %add_bitcast_fusion = (f32[1,1,16,1024]{3,2,1,0:T(8,128)}, f32[1,1,16,1024]{3,2,1,0:T(8,128)}) fusion(f32[16,1024]{1,0:T(8,128)} %scatter_custom_fusion.3, f32[16,1024]{1,0:T(8,128)S(1)} %bitcast_multiply_fusion, f32[16,1024]{1,0:T(8,128)S(1)} %scatter_custom_fusion.1, f32[1024]{0:T(1024)S(1)} %mul.159, f32[1024]{0:T(1024)S(1)} %mul.155, ...), kind=kLoop, calls=%fused_computation.37 | loop fusion | flops 114688 | bytes 466944 | tf_op jit(solution)/shard_map/broadcast_in_dim | solution.py:120
  (81 shorter events, 7.4 us)
Async XLA Ops:
  0.6 24.3 %copy-start = (f32[1,1,16,64,448]{4,3,2,1,0:T(8,128)S(1)}, f32[1,1,16,64,448]{4,3,2,1,0:T(8,128)}, u32[]{:S(2)}) copy-start(f32[1,1,16,64,448]{4,3,2,1,0:T(8,128)} %param.12) | copy-start | bytes 5505028
  0.6 5.4 %copy-start.4 = (f32[1,1,16,1024]{3,2,1,0:T(8,128)S(1)}, f32[1,1,16,1024]{3,2,1,0:T(8,128)}, u32[]{:S(2)}) copy-start(f32[1,1,16,1024]{3,2,1,0:T(8,128)} %param.10) | copy-start | bytes 196612
  0.7 8.1 %copy-start.1 = (f32[1,256,512]{2,1,0:T(8,128)S(1)}, f32[1,256,512]{2,1,0:T(8,128)}, u32[]{:S(2)}) copy-start(f32[1,256,512]{2,1,0:T(8,128)} %param.19) | copy-start | bytes 1572868
  0.7 8.9 %copy-start.7 = (s32[1,1,4,8]{3,2,1,0:T(4,128)S(1)}, s32[1,1,4,8]{3,2,1,0:T(4,128)}, u32[]{:S(2)}) copy-start(s32[1,1,4,8]{3,2,1,0:T(4,128)} %param.16) | copy-start | bytes 388
  2.6 15.7 %copy-start.10 = (s32[1,1,16,7]{2,1,3,0:T(1,128)S(1)}, s32[1,1,16,7]{2,1,3,0:T(1,128)}, u32[]{:S(2)}) copy-start(s32[1,1,16,7]{2,1,3,0:T(1,128)} %param.13) | copy-start | bytes 1348
  5.8 13.5 %copy-start.9 = (s32[4]{0:T(128)}, s32[4]{0:T(128)S(1)}, u32[]{:S(2)}) copy-start(s32[4]{0:T(128)S(1)} %fusion.28) | copy-start | bytes 52
  6.1 13.1 %copy-start.8 = (s32[1024]{0:T(1024)}, s32[1024]{0:T(1024)S(1)}, u32[]{:S(2)}) copy-start(s32[1024]{0:T(1024)S(1)} %pad_clamp_fusion.2) | copy-start | bytes 12292
  11.0 1.9 %copy-start.3 = (f32[32,1024]{1,0:T(8,128)}, f32[32,1024]{1,0:T(8,128)S(1)}, u32[]{:S(2)}) copy-start(f32[32,1024]{1,0:T(8,128)S(1)} %gather_fusion.2) | copy-start | bytes 393220
  11.7 26.4 %collective-permute-start = (f32[8,1024]{1,0:T(8,128)}, f32[8,1024]{1,0:T(8,128)}, u32[]{:S(2)}, u32[]{:S(2)}) collective-permute-start(f32[8,1024]{1,0:T(8,128)} %get-tuple-element.14), channel_id=1, source_target_pairs={{2,4},{6,8},{10,12},{14,16},{18,20},{22,24},{26,28},{4,2},{8,6},{1... | collective-permute-start | bytes 98312 | tf_op jit(solution)/shard_map/ppermute | solution.py:31
  12.9 25.2 %collective-permute-start.1 = (f32[8,1024]{1,0:T(8,128)}, f32[8,1024]{1,0:T(8,128)}, u32[]{:S(2)}, u32[]{:S(2)}) collective-permute-start(f32[8,1024]{1,0:T(8,128)} %get-tuple-element.15), channel_id=1, source_target_pairs={{0,2},{2,0},{4,6},{6,4},{8,10},{10,8},{12,14},{14,12},{16,18},{18,... | collective-permute-start | bytes 98312 | tf_op jit(solution)/shard_map/ppermute | solution.py:30
  19.3 5.7 %copy-start.5 = (f32[1,1,16,64]{3,2,1,0:T(8,128)S(1)}, f32[1,1,16,64]{3,2,1,0:T(8,128)}, u32[]{:S(2)}) copy-start(f32[1,1,16,64]{3,2,1,0:T(8,128)} %param.14) | copy-start | bytes 12292
  25.0 8.9 %copy-start.6 = (f32[1,1,4,512]{3,2,1,0:T(4,128)S(1)}, f32[1,1,4,512]{3,2,1,0:T(4,128)}, u32[]{:S(2)}) copy-start(f32[1,1,4,512]{3,2,1,0:T(4,128)} %param.17) | copy-start | bytes 24580
  43.1 9.3 %copy-start.2 = (f32[1,256,512]{2,1,0:T(8,128)S(1)}, f32[1,256,512]{2,1,0:T(8,128)}, u32[]{:S(2)}) copy-start(f32[1,256,512]{2,1,0:T(8,128)} %param.19) | copy-start | bytes 1572868
  62.1 15.6 %collective-permute-start.2 = (f32[8,1024]{1,0:T(8,128)S(1)}, f32[8,1024]{1,0:T(8,128)S(1)}, u32[]{:S(2)}, u32[]{:S(2)}) collective-permute-start(f32[8,1024]{1,0:T(8,128)S(1)} %get-tuple-element.11), channel_id=1, source_target_pairs={{2,4},{6,8},{10,12},{14,16},{18,20},{22,24},{26,28},{4,2},{8,6},{1... | collective-permute-start | bytes 98312 | tf_op jit(solution)/shard_map/ppermute | solution.py:31
  62.8 14.9 %collective-permute-start.3 = (f32[8,1024]{1,0:T(8,128)S(1)}, f32[8,1024]{1,0:T(8,128)S(1)}, u32[]{:S(2)}, u32[]{:S(2)}) collective-permute-start(f32[8,1024]{1,0:T(8,128)S(1)} %get-tuple-element.12), channel_id=1, source_target_pairs={{0,2},{2,0},{4,6},{6,4},{8,10},{10,8},{12,14},{14,12},{16,18},{18,... | collective-permute-start | bytes 98312 | tf_op jit(solution)/shard_map/ppermute | solution.py:30

commit v3 on v0

v3 whole, which is shorter than its diff:
```python
import functools

import jax
import jax.numpy as jnp
from jax import lax
from jax.experimental import pallas as pl
from jax.experimental.pallas import tpu as pltpu
from jax.sharding import PartitionSpec as P

F32 = jnp.float32
BF16 = jnp.bfloat16
VMEM_LIMIT = 24 * 1024 * 1024


def halves(x):
    high = x.astype(BF16)
    return high, (x - high.astype(F32)).astype(BF16)


def dot_t(a, b):
    return lax.dot_general(a, b, (((1,), (1,)), ((), ())), preferred_element_type=F32)


def dot(a, b):
    return lax.dot_general(a, b, (((1,), (0,)), ((), ())), preferred_element_type=F32)


def three_pass(mul, left, high, low):
    rows = left.shape[0] // 2
    first = mul(left, high)
    return first[:rows] + first[rows:] + mul(left[:rows], low)


def corner_kernel(cmap, field, out):
    bdof = field.shape[2]
    for n in range(out.shape[1] // bdof):
        out[:, n * bdof : (n + 1) * bdof] = field[cmap[n]]


def pack_faces(ints, where, ids_at, field, outs):
    bdof = field.shape[2]
    nface = outs[0].shape[1] // bdof
    for i, out in enumerate(outs):
        face = ints[ids_at + i] * nface + where
        for p in range(nface):
            out[:, p * bdof : (p + 1) * bdof] = field[ints[face + p]]


def precondition_kernel(ncorner, nface, ints, field, blocks, rows, corners, zout, *rest):
    *faces, tiles_high, tiles_low, left = rest
    nblk, ncol, bdof = field.shape
    group = tiles_high.shape[1] // bdof
    tiles_high[...] = jnp.zeros_like(tiles_high)
    tiles_low[...] = jnp.zeros_like(tiles_low)
    for b in range(nblk):
        t, j = divmod(b, group)
        high, low = halves(blocks[b])
        here = slice(j * bdof, (j + 1) * bdof)
        tiles_high[t, here, here] = high
        tiles_low[t, here, here] = low
        high, low = halves(field[b])
        left[t, :ncol, here] = high
        left[t, ncol:, here] = low
    for t in range(nblk // group):
        out = three_pass(dot, left[t], tiles_high[t], tiles_low[t])
        for j in range(group):
            zout[t * group + j] = out[:, j * bdof : (j + 1) * bdof]
    wide = ncorner * bdof
    correct = None
    for s in range(corners.shape[0]):
        high, low = halves(rows[:, s * wide : (s + 1) * wide])
        chigh, clow = halves(corners[s])
        term = three_pass(dot_t, jnp.concatenate([chigh, clow], axis=0), high, low)
        correct = term if correct is None else correct + term
    for n in range(ncorner):
        b = ints[n]
        zout[b] = zout[b] + correct[:, n * bdof : (n + 1) * bdof]
    pack_faces(ints, ncorner, ncorner + 4 * nface, zout, faces)


def stack_left(field, left):
    nblk, ncol, bdof = field.shape
    for b in range(nblk):
        high, low = halves(field[b])
        left[:ncol, b * bdof : (b + 1) * bdof] = high
        left[ncol:, b * bdof : (b + 1) * bdof] = low


def build_kernel(nface, ints, cols, field, stiff, capillary, weights, out, high, low, left, diag):
    nblk, ncol, bdof = field.shape
    kept = stiff.shape[2] // bdof
    ncorner = ints.shape[0] - 4 * nface - 8
    for b in range(nblk):
        diag[b] = capillary[b : b + 1, :]
    for f in range(4):
        for p in range(nface):
            b = ints[ncorner + f * nface + p]
            diag[b] = diag[b] + weights[f : f + 1, p * bdof : (p + 1) * bdof]
    eye = lax.broadcasted_iota(jnp.int32, (bdof, bdof), 0) == lax.broadcasted_iota(
        jnp.int32, (bdof, bdof), 1
    )
    high[...] = jnp.zeros_like(high)
    low[...] = jnp.zeros_like(low)
    for b in range(nblk):
        for k in range(kept):
            back = 0 if k == 0 else k + 1 if k % 2 else k - 1
            c = cols[b * kept + k]
            part = stiff[c, :, back * bdof : (back + 1) * bdof]
            if k == 0:
                part = part + jnp.where(eye, diag[b], 0.0)
            phigh, plow = halves(part)
            start = pl.multiple_of(c * bdof, bdof)
            high[pl.ds(start, bdof), b * bdof : (b + 1) * bdof] = phigh
            low[pl.ds(start, bdof), b * bdof : (b + 1) * bdof] = plow
    stack_left(field, left)
    out[...] = three_pass(dot, left[...], high[...], low[...])


def local_kernel(field, high, low, out, left):
    stack_left(field, left)
    out[...] = three_pass(dot, left[...], high[...], low[...])


def couple(ints, ids_at, where, nface, weights, local, besides, field):
    nblk, ncol, bdof = field.shape
    for b in range(nblk):
        field[b] = local[:, b * bdof : (b + 1) * bdof]
    for i, beside in enumerate(besides):
        face = ints[ids_at + i]
        term = weights[pl.ds(face, 1), :] * beside[...]
        for p in range(nface):
            b = ints[where + face * nface + p]
            field[b] = field[b] - term[:, p * bdof : (p + 1) * bdof]


def lanes(first, second):
    return jnp.sum(first[...] * second[...], axis=0)


def image_kernel(ncorner, nface, ints, weights, local, rvec, zvec, *rest):
    *besides, wout, corners, sums = rest
    couple(ints, ncorner + 4 * nface, ncorner, nface, weights, local, besides, wout)
    bdof = zvec.shape[2]
    for n in range(ncorner):
        corners[:, n * bdof : (n + 1) * bdof] = wout[ints[n]]
    sums[0] = lanes(rvec, zvec)
    sums[1] = lanes(zvec, wout)


def last_kernel(ncorner, nface, ints, weights, local, wvec, mvec, sums, *rest):
    *besides, nout, totals = rest
    couple(ints, ncorner + 4 * nface, ncorner, nface, weights, local, besides, nout)
    parts = jnp.concatenate(
        [sums[0], sums[1], lanes(wvec, mvec), lanes(mvec, nout)], axis=0
    )
    totals[...] = lax.dot_general(
        jnp.ones((1, parts.shape[1]), F32),
        parts,
        (((1,), (1,)), ((), ())),
        precision=lax.Precision.HIGHEST,
        preferred_element_type=F32,
    )


def finish_kernel(shares, rvec, zvec, wvec, mvec, nvec, sol, res):
    nblk, ncol, bdof = rvec.shape
    width = shares.shape[1]
    total = jnp.sum(shares[...], axis=0, keepdims=True)
    eye = lax.broadcasted_iota(jnp.int32, (width, width), 0) == lax.broadcasted_iota(
        jnp.int32, (width, width), 1
    )
    column = jnp.sum(jnp.where(eye, total, 0.0), axis=1, keepdims=True)
    gamma, delta, mu, nu = [column[q * ncol : (q + 1) * ncol] for q in range(4)]
    alpha = gamma / delta
    gnew = gamma - 2.0 * alpha * delta + alpha * alpha * mu
    grow = 1.0 + gnew / gamma
    dnew = grow * grow * delta - 2.0 * alpha * grow * mu + alpha * alpha * nu
    anew = gnew / dnew
    both = alpha + anew * grow
    second = anew * alpha
    sol[...] = both * zvec[...] - second * mvec[...]
    res[...] = rvec[...] - both * wvec[...] + second * nvec[...]


def call(kernel, outs, scratch, smem, *args):
    vmem = pl.BlockSpec(memory_space=pltpu.VMEM)
    return pl.pallas_call(
        kernel,
        out_shape=outs,
        in_specs=[pl.BlockSpec(memory_space=pltpu.SMEM)] * smem + [vmem] * (len(args) - smem),
        out_specs=jax.tree.map(lambda _: vmem, outs),
        scratch_shapes=scratch,
        compiler_params=pltpu.CompilerParams(vmem_limit_bytes=VMEM_LIMIT),
    )(*args)


def everywhere(values):
    total = lax.axis_size("dam") * lax.axis_size("sec")
    copies = jnp.broadcast_to(values[None], (total,) + values.shape)
    return lax.all_to_all(copies, ("dam", "sec"), split_axis=0, concat_axis=0)


def partners(axis):
    even = lax.axis_index(axis) % 2 == 0
    near = jnp.where(even, 1, 0)
    return [near] if lax.axis_size(axis) == 2 else [near, 1 - near]


def exchange(sends, axis):
    size = lax.axis_size(axis)
    if size == 2:
        both = lax.all_gather(sends[0], axis)
        return [lax.dynamic_index_in_dim(both, 1 - lax.axis_index(axis), keepdims=False)]
    got = []
    for first, send in enumerate(sends):
        pairs = [(i, i + 1) for i in range(first, size - 1, 2)]
        got.append(lax.ppermute(send, axis, pairs + [(j, i) for i, j in pairs]))
    return got


def shards(
    segment_load,
    segment_mask,
    stiffness,
    block_cols,
    capillary,
    dirichlet_blocks,
    face_map,
    face_weight,
    corner_map,
    coarse_inverse,
):
    nblk, bdof = capillary.shape[2:]
    ncol = segment_load.shape[-1] // bdof
    nface = face_map.shape[3]
    ncorner = corner_map.shape[2]
    size = nblk * bdof
    weights = face_weight[0, 0]
    dam_ids = partners("dam")
    sec_ids = [i + 2 for i in partners("sec")]
    ids = dam_ids + sec_ids
    pad = jnp.zeros((8 - len(ids),), jnp.int32)
    ints = jnp.concatenate(
        [corner_map[0, 0], face_map[0, 0].reshape(-1), jnp.stack(ids).astype(jnp.int32), pad]
    )
    masked = (
        segment_load[0, 0].reshape(nblk, bdof, ncol)
        * segment_mask[0, 0].astype(F32)[:, None, :]
    )
    rvec = jnp.swapaxes(masked, 1, 2)

    field = jax.ShapeDtypeStruct((nblk, ncol, bdof), F32)
    corner = jax.ShapeDtypeStruct((ncol, ncorner * bdof), F32)
    face = jax.ShapeDtypeStruct((ncol, nface * bdof), F32)
    flat = jax.ShapeDtypeStruct((ncol, size), F32)
    dense = jax.ShapeDtypeStruct((size, size), BF16)
    group = ncorner * bdof
    tiles = pltpu.VMEM((size // group, group, group), BF16)

    def precondition(vec, corners):
        return call(
            functools.partial(precondition_kernel, ncorner, nface),
            (field,) + (face,) * len(ids),
            [tiles, tiles, pltpu.VMEM((size // group, 2 * ncol, group), BF16)],
            1,
            ints,
            vec,
            dirichlet_blocks[0, 0],
            coarse_inverse[0],
            lax.all_gather(corners, "sec"),
        )

    def swap(sends):
        dam = exchange(sends[: len(dam_ids)], "dam")
        return dam + exchange(sends[len(dam_ids) :], "sec")

    left = pltpu.VMEM((2 * ncol, size), BF16)
    corners = call(corner_kernel, corner, [], 1, corner_map[0, 0], rvec)
    zvec, *sends = precondition(rvec, corners)
    besides = swap(sends)
    local, high, low = call(
        functools.partial(build_kernel, nface),
        (flat, dense, dense),
        [left, pltpu.VMEM((nblk, 1, bdof), F32)],
        2,
        ints,
        block_cols[0, 0].reshape(-1),
        zvec,
        stiffness[0, 0],
        capillary[0, 0],
        weights,
    )
    wvec, corners, sums = call(
        functools.partial(image_kernel, ncorner, nface),
        (field, corner, jax.ShapeDtypeStruct((2, ncol, bdof), F32)),
        [],
        1,
        ints,
        weights,
        local,
        rvec,
        zvec,
        *besides,
    )
    mvec, *sends = precondition(wvec, corners)
    besides = swap(sends)
    local = call(local_kernel, flat, [left], 0, mvec, high, low)
    nvec, totals = call(
        functools.partial(last_kernel, ncorner, nface),
        (field, jax.ShapeDtypeStruct((1, 4 * ncol), F32)),
        [],
        1,
        ints,
        weights,
        local,
        wvec,
        mvec,
        sums,
        *besides,
    )
    shares = everywhere(totals[0])
    sol, res = call(
        finish_kernel, (field, field), [], 0, shares, rvec, zvec, wvec, mvec, nvec
    )

    def back(vec):
        return jnp.swapaxes(vec, 1, 2).reshape(1, 1, nblk, bdof * ncol)

    return back(sol), back(res)


def solution(mesh):
    placed = (
        P("dam", "sec", None, None),
        P("dam", "sec", None, None),
        P("dam", "sec", None, None, None),
        P("dam", "sec", None, None),
        P("dam", "sec", None, None),
        P("dam", "sec", None, None, None),
        P("dam", "sec", None, None),
        P("dam", "sec", None, None),
        P("dam", "sec", None),
        P("dam", "sec", None),
    )
    return jax.shard_map(
        shards,
        mesh=mesh,
        in_specs=placed,
        out_specs=(P("dam", "sec", None, None), P("dam", "sec", None, None)),
        check_vma=False,
    )
```

time: 220 us -> 51.9 us (0.24)
  blocking collectives: 128 us -> 22.8 us
  local copies, waits for them, and re-layouts: 33.2 us -> 9.27 us
  matrix products: 21.5 us -> 0 us
  starting transfers between devices: 23.1 us -> 8.43 us
  other arithmetic: 12.4 us -> 0.81 us
  Pallas kernels: 0 us -> 9.35 us
    psum x3 -> x0, blocking collectives: 124 us -> none  [global_inner(): return lax.psum(inner(first, second), ('dam', 'sec'))]
    dot_general x6 -> x0, matrix products: 21.5 us -> none  [the longest x2 15.7 us: local_product(): prod = jnp.einsum('bde,bes->bds', stiff, gathered, precision=HIGH)]
    all_to_all x0 -> x1, blocking collectives: none -> 15.2 us  [everywhere(): return lax.all_to_all(copies, ('dam', 'sec'), split_axis=0, concat_axis=0)]
    ppermute x8 -> x4, starting transfers between devices: 23.1 us -> 8.43 us  [exchange(): got.append(lax.ppermute(send, axis, pairs + [(j, i) for i, j in pairs]))]
    another operation x14 -> x3, local copies, waits for them, and re-layouts: 12.3 us -> 1 us  [the longest x1 0.91 us: shards(): face_map[0, 0].reshape(-1)]
    pallas_call x0 -> x8, Pallas kernels: none -> 9.35 us  [call(): pl.pallas_call(kernel, out_shape=outs, in_specs=[pl.BlockSpec(memory_spac...]
    reshape x15 -> x2, local copies, waits for them, and re-layouts: 9.23 us -> 1.81 us  [back(): return jnp.swapaxes(vec, 1, 2).reshape(1, 1, nblk, bdof * ncol)]
    scatter-add x4 -> x0, other arithmetic: 5.56 us -> none  [the longest x2 4.05 us: shards(): image = local.at[flat_faces].add(term)]
  transfers between devices with their start and end apart: 8 -> 4, of which waited for: 0 -> 0; matrix products, arithmetic and copies ran while one was open for 14% -> 3% of each run, Pallas kernels for 0% -> 7%
where the time goes in v3:
time: 51.9 us; the launch traced here: 51.5 us
  blocking collectives  22.8 us (44%)
  Pallas kernels  9.35 us (18%)
  local copies, waits for them, and re-layouts  9.27 us (18%)
  starting transfers between devices  8.43 us (16%)
  other arithmetic  0.81 us (2%)
  between operations  0.81 us (2%)
    all_to_all x1, blocking collectives, everywhere(): return lax.all_to_all(copies, ('dam', 'sec'), split_axis=0, concat_axis=0)  15.2 us
    pallas_call x8, Pallas kernels, call(): pl.pallas_call(kernel, out_shape=outs, in_specs=[pl.BlockSpec(memory_spac...  9.35 us
    ppermute x4, starting transfers between devices, exchange(): got.append(lax.ppermute(send, axis, pairs + [(j, i) for i, j in pairs]))  8.43 us
    all_gather x2, blocking collectives, exchange(): both = lax.all_gather(sends[0], axis)  3.84 us
    all_gather x2, blocking collectives, precondition(): lax.all_gather(corners, 'sec')  3.75 us
    another operation x2, local copies, waits for them, and re-layouts, shards(): segment_load[0, 0].reshape(nblk, bdof, ncol)  3.05 us
    unnamed x13, local copies, waits for them, and re-layouts  2.12 us
    reshape x2, local copies, waits for them, and re-layouts, back(): return jnp.swapaxes(vec, 1, 2).reshape(1, 1, nblk, bdof * ncol)  1.81 us
  transfers between devices with their start and end apart: 4, of which 0 were waited for; matrix products, arithmetic and copies ran while one was open for 3% of the time, Pallas kernels for 7%

profile of v3, /device:TPU:0, one launch (start us, length us, event | category | flops | bytes accessed | tf_op | source)
XLA Modules:
  0.0 51.5 jit_solution(5549365180100604079)
XLA Ops:
  0.6 0.0 copy-start.2
  0.6 0.0 copy-start.1
  0.7 0.0 copy-start.3
  0.7 0.0 copy-start
  0.7 0.9 %reshape_squeeze.9 = s32[32]{0:T(128)S(1)} reshape(s32[1,1,4,8]{3,2,1,0:T(4,128)} %param.16) | data formatting | bytes 256 | tf_op jit(solution)/shard_map/reshape;squeeze | solution.py:244
  1.6 0.7 %convert_bitcast_fusion = f32[16,16]{1,0:T(8,128)S(1)} fusion(s32[1,1,16,16]{3,2,1,0:T(8,128)} %param.11), kind=kLoop, calls=%fused_computation.3 | loop fusion | flops 256 | bytes 2048 | tf_op jit(solution)/shard_map/convert_element_type | solution.py:248
  2.3 1.8 %reshape_squeeze.11 = f32[16,64,16]{2,1,0:T(8,128)} reshape(f32[1,1,16,1024]{3,2,1,0:T(8,128)} %param.10) | data formatting | bytes 131072 | tf_op jit(solution)/shard_map/reshape;squeeze | solution.py:247
  4.1 1.2 %copy.18 = f32[16,64,16]{1,2,0:T(8,128)S(1)} copy(f32[16,64,16]{2,1,0:T(8,128)} %reshape_squeeze.11) | data formatting | bytes 131072 | tf_op jit(solution)/shard_map/reshape;squeeze | solution.py:247
  5.4 0.1 multiply_bitcast_fusion.field.rvec
  5.5 0.0 copy-start.5
  5.5 0.6 %copy-done.5 = s32[1,1,4]{2,1,0:T(1,128)S(1)} copy-done((s32[1,1,4]{2,1,0:T(1,128)S(1)}, s32[1,1,4]{2,1,0:T(1,128)}, u32[]{:S(2)}) %copy-start.5) | copy-done | bytes 40
  6.1 0.6 %shard_map.113 = f32[16,256]{1,0:T(8,128)S(1)} custom-call(s32[4]{0:T(128)S(1)} %bitcast.43, f32[16,16,64]{2,1,0:T(8,128)S(1)} %multiply_bitcast_fusion.field.rvec), custom_call_target="tpu_custom_call" | custom-call | tf_op jit(solution)/shard_map/pallas_call | solution.py:187
  6.8 1.9 %all-gather = f32[32,256]{1,0:T(8,128)S(1)} all-gather(f32[16,256]{1,0:T(8,128)S(1)} %shard_map.113), channel_id=2, replica_groups=mesh['dam'=16,'sec'=2] {'sec'}, dimensions={0}, use_global_device_ids=true | all-gather | bytes 49152 | tf_op jit(solution)/shard_map/all_gather | solution.py:270
  8.7 0.1 concatenate.3.ints
  8.8 0.0 copy-done.2
  8.8 0.0 copy-done.1
  8.8 1.9 %shard_map.114 = (f32[16,16,64]{2,1,0:T(8,128)S(1)}, f32[16,512]{1,0:T(8,128)}, f32[16,512]{1,0:T(8,128)}, f32[16,512]{1,0:T(8,128)S(1)}) custom-call(s32[44]{0:T(128)S(1)} %concatenate.3.ints, f32[16,16,64]{2,1,0:T(8,128)S(1)} %multiply_bitcast_fusion.field.rvec, f32[16,64,64]{2,1,0:T(8,128)S(1)} %bitcast.30, f32[256,512]{1,0:T(8,128)S(1)} %bitcast.32, ...), custom_call_target="tpu_custom_call" | custom-call | tf_op jit(solution)/shard_map/pallas_call | solution.py:187
  10.7 2.8 %collective-permute-start = (f32[16,512]{1,0:T(8,128)}, f32[16,512]{1,0:T(8,128)S(1)}, u32[]{:S(2)}, u32[]{:S(2)}) collective-permute-start(f32[16,512]{1,0:T(8,128)} %get-tuple-element.22), channel_id=1, source_target_pairs={{0,2},{4,6},{8,10},{12,14},{16,18},{20,22},{24,26},{28,30},{2,0},{... | collective-permute-start | bytes 98312 | tf_op jit(solution)/shard_map/ppermute | solution.py:217
  13.6 0.7 %collective-permute-start.1 = (f32[16,512]{1,0:T(8,128)}, f32[16,512]{1,0:T(8,128)S(1)}, u32[]{:S(2)}, u32[]{:S(2)}) collective-permute-start(f32[16,512]{1,0:T(8,128)} %get-tuple-element.23), channel_id=1, source_target_pairs={{2,4},{6,8},{10,12},{14,16},{18,20},{22,24},{26,28},{4,2},{8,6},{1... | collective-permute-start | bytes 98312 | tf_op jit(solution)/shard_map/ppermute | solution.py:217
  14.2 2.0 %all-gather.1 = f32[32,512]{1,0:T(8,128)} all-gather(f32[16,512]{1,0:T(8,128)S(1)} %get-tuple-element.24), channel_id=3, replica_groups=mesh['dam'=16,'sec'=2] {'sec'}, dimensions={0}, use_global_device_ids=true | all-gather | bytes 98304 | tf_op jit(solution)/shard_map/all_gather | solution.py:212
  16.2 0.8 %dynamic-slice_bitcast_fusion.1.rest_2_ = f32[16,512]{1,0:T(8,128)S(1)} fusion(f32[2,16,512]{2,1,0:T(8,128)} %bitcast.46, s32[]{:T(128)S(6)} %select_n.27), kind=kLoop, calls=%fused_computation.2 | loop fusion | bytes 65540 | tf_op jit(solution)/shard_map/jit(dynamic_index_in_dim)/squeeze | solution.py:213
  17.0 0.8 %copy.17 = s32[1,1,16,7]{3,2,1,0:T(8,128)S(1)} copy(s32[1,1,16,7]{2,1,3,0:T(1,128)} %param.13) | data formatting | bytes 896 | tf_op args[3]
  17.7 0.1 reshape_squeeze.10.cols
  17.8 0.0 copy-done.3
  17.8 0.0 copy-done
  17.8 0.0 copy-start.4
  17.8 0.7 %copy-done.4 = f32[1,1,16,64]{3,2,1,0:T(8,128)S(1)} copy-done((f32[1,1,16,64]{3,2,1,0:T(8,128)S(1)}, f32[1,1,16,64]{3,2,1,0:T(8,128)}, u32[]{:S(2)}) %copy-start.4) | copy-done | bytes 4120
  18.5 2.9 %shard_map.115 = (f32[16,1024]{1,0:T(8,128)S(1)}, bf16[1024,1024]{1,0:T(8,128)(2,1)S(1)}, bf16[1024,1024]{1,0:T(8,128)(2,1)S(1)}) custom-call(s32[44]{0:T(128)S(1)} %concatenate.3.ints, s32[112]{0:T(128)S(1)} %reshape_squeeze.10.cols, f32[16,16,64]{2,1,0:T(8,128)S(1)} %get-tuple-element.20.field.zvec, f32[16,64,448]{2,1,0:T(8,128)S(1)} %bitcast.29, ...), custom_call_target="tpu_custom_call" | custom-call | tf_op jit(solution)/shard_map/pallas_call | solution.py:187
  21.4 0.0 collective-permute-done.rest_0_
  21.4 0.0 collective-permute-done.1.rest_1_
  21.5 0.8 %shard_map.116 = (f32[16,16,64]{2,1,0:T(8,128)S(1)}, f32[16,256]{1,0:T(8,128)S(1)}, f32[2,16,64]{2,1,0:T(8,128)S(1)}) custom-call(s32[44]{0:T(128)S(1)} %concatenate.3.ints, f32[4,512]{1,0:T(4,128)S(1)} %bitcast.39, f32[16,1024]{1,0:T(8,128)S(1)} %get-tuple-element.21.local, f32[16,16,64]{2,1,0:T(8,128)S(1)} %multiply_bitcast_fusion.field.rvec, ...), custom_call_target="tpu_custom_call" | custom-call | tf_op jit(solution)/shard_map/pallas_call | solution.py:187
  22.2 1.8 %all-gather.2 = f32[32,256]{1,0:T(8,128)S(1)} all-gather(f32[16,256]{1,0:T(8,128)S(1)} %get-tuple-element.26), channel_id=4, replica_groups=mesh['dam'=16,'sec'=2] {'sec'}, dimensions={0}, use_global_device_ids=true | all-gather | bytes 49152 | tf_op jit(solution)/shard_map/all_gather | solution.py:270
  24.0 1.3 %shard_map.117 = (f32[16,16,64]{2,1,0:T(8,128)S(1)}, f32[16,512]{1,0:T(8,128)S(1)}, f32[16,512]{1,0:T(8,128)S(1)}, f32[16,512]{1,0:T(8,128)S(1)}) custom-call(s32[44]{0:T(128)S(1)} %concatenate.3.ints, f32[16,16,64]{2,1,0:T(8,128)S(1)} %get-tuple-element.25.field.wvec, f32[16,64,64]{2,1,0:T(8,128)S(1)} %bitcast.31, f32[256,512]{1,0:T(8,128)S(1)} %bitcast.33, ...), custom_call_target="tpu_custom_call" | custom-call | tf_op jit(solution)/shard_map/pallas_call | solution.py:187
  25.4 4.3 %collective-permute-start.2 = (f32[16,512]{1,0:T(8,128)S(1)}, f32[16,512]{1,0:T(8,128)S(1)}, u32[]{:S(2)}, u32[]{:S(2)}) collective-permute-start(f32[16,512]{1,0:T(8,128)S(1)} %get-tuple-element.31), channel_id=1, source_target_pairs={{0,2},{4,6},{8,10},{12,14},{16,18},{20,22},{24,26},{28,30},{2,0},{... | collective-permute-start | bytes 98312 | tf_op jit(solution)/shard_map/ppermute | solution.py:217
  29.7 0.7 %collective-permute-start.3 = (f32[16,512]{1,0:T(8,128)S(1)}, f32[16,512]{1,0:T(8,128)S(1)}, u32[]{:S(2)}, u32[]{:S(2)}) collective-permute-start(f32[16,512]{1,0:T(8,128)S(1)} %get-tuple-element.32), channel_id=1, source_target_pairs={{2,4},{6,8},{10,12},{14,16},{18,20},{22,24},{26,28},{4,2},{8,6},{1... | collective-permute-start | bytes 98312 | tf_op jit(solution)/shard_map/ppermute | solution.py:217
  30.3 1.9 %all-gather.3 = f32[32,512]{1,0:T(8,128)S(1)} all-gather(f32[16,512]{1,0:T(8,128)S(1)} %get-tuple-element.33), channel_id=5, replica_groups=mesh['dam'=16,'sec'=2] {'sec'}, dimensions={0}, use_global_device_ids=true | all-gather | bytes 98304 | tf_op jit(solution)/shard_map/all_gather | solution.py:212
  32.2 0.8 %shard_map.118.local = f32[16,1024]{1,0:T(8,128)S(1)} custom-call(f32[16,16,64]{2,1,0:T(8,128)S(1)} %get-tuple-element.27.field.mvec, bf16[1024,1024]{1,0:T(8,128)(2,1)S(1)} %get-tuple-element.28.high, bf16[1024,1024]{1,0:T(8,128)(2,1)S(1)} %get-tuple-element.29.low), custom_call_target="tpu_custom_call" | custom-call | tf_op jit(solution)/shard_map/pallas_call | solution.py:187
  33.0 0.0 collective-permute-done.2.rest_0_
  33.0 0.0 collective-permute-done.3.rest_1_
  33.0 0.9 %shard_map.119 = (f32[16,16,64]{2,1,0:T(8,128)S(1)}, f32[1,64]{1,0:T(1,128)S(1)}) custom-call(s32[44]{0:T(128)S(1)} %concatenate.3.ints, f32[4,512]{1,0:T(4,128)S(1)} %bitcast.40, f32[16,1024]{1,0:T(8,128)S(1)} %shard_map.118.local, f32[16,16,64]{2,1,0:T(8,128)S(1)} %get-tuple-element.25.field.wvec, f32[16,16,64]{2,1,0:T(8,128)S(1)} %get-tuple-element.27.field.mvec, ...), custom_call_target="tpu_custom_call" | custom-call | tf_op jit(solution)/shard_map/pallas_call | solution.py:187
  33.9 15.2 %all_to_all.8 = f32[32,1,64]{2,1,0:T(1,128)S(1)} all-to-all(f32[32,1,64]{2,1,0:T(1,128)S(1)} %broadcast_in_dim.2), channel_id=1, replica_groups=mesh['dam'=16,'sec'=2] {'dam','sec'}, dimensions={0} | all-to-all | bytes 16384 | tf_op jit(solution)/shard_map/all_to_all | solution.py:200
  49.1 0.1 shard_map.120
  49.2 0.2 copy.20
  49.5 0.9 %reshape.23 = f32[1,1,16,1024]{3,2,1,0:T(8,128)} reshape(f32[16,64,16]{2,1,0:T(8,128)S(1)} %copy.20) | data formatting | bytes 131072 | tf_op jit(solution)/shard_map/reshape | solution.py:327
  50.4 0.2 copy.19
  50.6 0.9 %reshape.22 = f32[1,1,16,1024]{3,2,1,0:T(8,128)} reshape(f32[16,64,16]{2,1,0:T(8,128)S(1)} %copy.19) | data formatting | bytes 131072 | tf_op jit(solution)/shard_map/reshape | solution.py:327
  (3 shorter events, 0.0 us)
Async XLA Ops:
  0.6 8.1 %copy-start.2 = (f32[1,256,512]{2,1,0:T(8,128)S(1)}, f32[1,256,512]{2,1,0:T(8,128)}, u32[]{:S(2)}) copy-start(f32[1,256,512]{2,1,0:T(8,128)} %param.19) | copy-start | bytes 1572868
  0.6 8.1 %copy-start.1 = (f32[1,1,16,64,64]{4,3,2,1,0:T(8,128)S(1)}, f32[1,1,16,64,64]{4,3,2,1,0:T(8,128)}, u32[]{:S(2)}) copy-start(f32[1,1,16,64,64]{4,3,2,1,0:T(8,128)} %param.15) | copy-start | bytes 786436
  0.7 17.2 %copy-start.3 = (f32[1,1,4,512]{3,2,1,0:T(4,128)S(1)}, f32[1,1,4,512]{3,2,1,0:T(4,128)}, u32[]{:S(2)}) copy-start(f32[1,1,4,512]{3,2,1,0:T(4,128)} %param.17) | copy-start | bytes 24580
  0.7 17.2 %copy-start = (f32[1,1,16,64,448]{4,3,2,1,0:T(8,128)S(1)}, f32[1,1,16,64,448]{4,3,2,1,0:T(8,128)}, u32[]{:S(2)}) copy-start(f32[1,1,16,64,448]{4,3,2,1,0:T(8,128)} %param.12) | copy-start | bytes 5505028
  5.5 0.7 %copy-start.5 = (s32[1,1,4]{2,1,0:T(1,128)S(1)}, s32[1,1,4]{2,1,0:T(1,128)}, u32[]{:S(2)}) copy-start(s32[1,1,4]{2,1,0:T(1,128)} %param.18) | copy-start | bytes 52
  10.7 10.7 %collective-permute-start = (f32[16,512]{1,0:T(8,128)}, f32[16,512]{1,0:T(8,128)S(1)}, u32[]{:S(2)}, u32[]{:S(2)}) collective-permute-start(f32[16,512]{1,0:T(8,128)} %get-tuple-element.22), channel_id=1, source_target_pairs={{0,2},{4,6},{8,10},{12,14},{16,18},{20,22},{24,26},{28,30},{2,0},{... | collective-permute-start | bytes 98312 | tf_op jit(solution)/shard_map/ppermute | solution.py:217
  13.6 7.9 %collective-permute-start.1 = (f32[16,512]{1,0:T(8,128)}, f32[16,512]{1,0:T(8,128)S(1)}, u32[]{:S(2)}, u32[]{:S(2)}) collective-permute-start(f32[16,512]{1,0:T(8,128)} %get-tuple-element.23), channel_id=1, source_target_pairs={{2,4},{6,8},{10,12},{14,16},{18,20},{22,24},{26,28},{4,2},{8,6},{1... | collective-permute-start | bytes 98312 | tf_op jit(solution)/shard_map/ppermute | solution.py:217
  17.8 0.7 %copy-start.4 = (f32[1,1,16,64]{3,2,1,0:T(8,128)S(1)}, f32[1,1,16,64]{3,2,1,0:T(8,128)}, u32[]{:S(2)}) copy-start(f32[1,1,16,64]{3,2,1,0:T(8,128)} %param.14) | copy-start | bytes 12292
  25.4 7.6 %collective-permute-start.2 = (f32[16,512]{1,0:T(8,128)S(1)}, f32[16,512]{1,0:T(8,128)S(1)}, u32[]{:S(2)}, u32[]{:S(2)}) collective-permute-start(f32[16,512]{1,0:T(8,128)S(1)} %get-tuple-element.31), channel_id=1, source_target_pairs={{0,2},{4,6},{8,10},{12,14},{16,18},{20,22},{24,26},{28,30},{2,0},{... | collective-permute-start | bytes 98312 | tf_op jit(solution)/shard_map/ppermute | solution.py:217
  29.7 3.3 %collective-permute-start.3 = (f32[16,512]{1,0:T(8,128)S(1)}, f32[16,512]{1,0:T(8,128)S(1)}, u32[]{:S(2)}, u32[]{:S(2)}) collective-permute-start(f32[16,512]{1,0:T(8,128)S(1)} %get-tuple-element.32), channel_id=1, source_target_pairs={{2,4},{6,8},{10,12},{14,16},{18,20},{22,24},{26,28},{4,2},{8,6},{1... | collective-permute-start | bytes 98312 | tf_op jit(solution)/shard_map/ppermute | solution.py:217

commit v4 on v3

v4 whole, which is shorter than its diff:
```python
import functools

import jax
import jax.numpy as jnp
from jax import lax
from jax.experimental import pallas as pl
from jax.experimental.pallas import tpu as pltpu
from jax.sharding import PartitionSpec as P

F32 = jnp.float32
BF16 = jnp.bfloat16
VMEM_LIMIT = 16 * 1024 * 1024


def halves(x):
    high = x.astype(BF16)
    return high, (x - high.astype(F32)).astype(BF16)


def dot_t(a, b):
    return lax.dot_general(a, b, (((1,), (1,)), ((), ())), preferred_element_type=F32)


def dot(a, b):
    return lax.dot_general(a, b, (((1,), (0,)), ((), ())), preferred_element_type=F32)


def three_pass(mul, left, high, low):
    rows = left.shape[0] // 2
    first = mul(left, high)
    return first[:rows] + first[rows:] + mul(left[:rows], low)


def near_face():
    return 1 - lax.axis_index("dam") % 2


def sec_face():
    return 3 - lax.axis_index("sec")


def pack_face(face, fmap, field, out):
    bdof = field.shape[2]
    for p in range(fmap.shape[3]):
        out[..., : field.shape[1], p * bdof : (p + 1) * bdof] = field[fmap[0, 0, face, p]]


def scatter_corners(cmap, correct, field):
    bdof = field.shape[2]
    for n in range(cmap.shape[2]):
        b = cmap[0, 0, n]
        field[b] = field[b] + correct[:, n * bdof : (n + 1) * bdof]


def begin(pair, cmap, fmap, field, blocks, rows, base, payload, tiles_high, tiles_low, left):
    nblk, ncol, bdof = field.shape
    ncorner, nface = cmap.shape[2], fmap.shape[3]
    group = tiles_high.shape[1] // bdof
    tiles_high[...] = jnp.zeros_like(tiles_high)
    tiles_low[...] = jnp.zeros_like(tiles_low)
    for b in range(nblk):
        t, j = divmod(b, group)
        here = slice(j * bdof, (j + 1) * bdof)
        tiles_high[t, here, here], tiles_low[t, here, here] = halves(blocks[b])
        left[t, :ncol, here], left[t, ncol:, here] = halves(field[b])
    for t in range(nblk // group):
        out = three_pass(dot, left[t], tiles_high[t], tiles_low[t])
        for j in range(group):
            base[t * group + j] = out[:, j * bdof : (j + 1) * bdof]
    at = nface * bdof if pair else 0
    wide = ncorner * bdof
    for n in range(ncorner):
        payload[:ncol, at + n * bdof : at + (n + 1) * bdof] = field[cmap[0, 0, n]]
    if pair:
        start = pl.multiple_of(lax.axis_index("sec") * wide, wide)
        correct = three_pass(
            dot_t, stack(payload[:ncol, at:]), *halves(rows[:, pl.ds(start, wide)])
        )
        scatter_corners(cmap, correct, base)
        pack_face(sec_face(), fmap, base, payload)
        if payload.shape[0] > ncol:
            payload[ncol:, :] = jnp.zeros_like(payload[ncol:, :])
            for n in range(ncorner):
                for p in range(nface):
                    same = cmap[0, 0, n] == fmap[0, 0, sec_face(), p]
                    payload[ncol + n : ncol + n + 1, p * bdof : (p + 1) * bdof] = jnp.full(
                        (1, bdof), jnp.where(same, 1.0, 0.0), F32
                    )


def stack(x):
    return jnp.concatenate(halves(x), axis=0)


def end_kernel(pair, cmap, fmap, base, rows, shares, marks, zout, *faces):
    nblk, ncol, bdof = base.shape
    ncorner, nface = cmap.shape[2], fmap.shape[3]
    wide = ncorner * bdof
    zout[...] = base[...]
    if pair:
        me = lax.axis_index("sec")
        at = nface * bdof
        start = pl.multiple_of((1 - me) * wide, wide)
        high, low = halves(rows[:, pl.ds(start, wide)])
        own = stack(shares[pl.ds(me, 1), :ncol, at:][0])
        other = stack(shares[pl.ds(1 - me, 1), :ncol, at:][0])
        theirs = three_pass(dot, own, high, low)
        correct = three_pass(dot_t, other, high, low)
        chunk = 2 * bdof
        twice = [
            jnp.concatenate([theirs[:, n * bdof : (n + 1) * bdof]] * 2, axis=1)
            for n in range(ncorner)
        ]
        for j in range(at // chunk):
            here = slice(j * chunk, (j + 1) * chunk)
            value = shares[pl.ds(1 - me, 1), :ncol, here][0]
            for n in range(ncorner):
                mark = marks[pl.ds(1 - me, 1), ncol + n : ncol + n + 1, here][0]
                value = value + mark * twice[n]
            faces[-1][:, here] = value
    else:
        correct = 0.0
        for s in range(shares.shape[0]):
            high, low = halves(rows[:, s * wide : (s + 1) * wide])
            correct = correct + three_pass(dot_t, stack(shares[s]), high, low)
    scatter_corners(cmap, correct, zout)
    near = near_face()
    pack_face(near, fmap, zout, faces[0])
    pack_face(1 - near, fmap, zout, faces[1])
    if not pair:
        near = 3 - lax.axis_index("sec") % 2
        pack_face(near, fmap, zout, faces[2])
        pack_face(5 - near, fmap, zout, faces[3])


def start_kernel(pair, cmap, fmap, load, mask, blocks, rows, rvec, base, payload, *scratch):
    tall, short, *tiles = scratch
    nblk, ncol, bdof = rvec.shape
    lanes_at = 128
    scale = mask[...].astype(F32)
    scale = jnp.concatenate([scale] * (lanes_at // ncol), axis=1)
    for j in range(load.shape[1] // lanes_at):
        here = slice(j * lanes_at, (j + 1) * lanes_at)
        tall[here, :] = (load[:, here] * scale).T
    for c in range(ncol):
        short[c * nblk : (c + 1) * nblk, :] = tall[pl.ds(c, bdof, stride=ncol), :].T
    for b in range(nblk):
        rvec[b] = short[pl.ds(b, ncol, stride=nblk), :]
    begin(pair, cmap, fmap, rvec, blocks, rows, base, payload, *tiles)


def local_kernel(cols, field, stiff, out, left):
    nblk, ncol, bdof = field.shape
    kept = stiff.shape[2] // bdof
    for b in range(nblk):
        left[b] = stack(field[b])
    for b in range(nblk):
        gathered = jnp.concatenate([left[cols[k, 0, b]] for k in range(kept)], axis=1)
        out[b] = three_pass(dot_t, gathered, *halves(stiff[b]))


def couple(fmap, weights, capillary, local, field, besides, out):
    nblk, ncol, bdof = field.shape
    for b in range(nblk):
        out[b] = local[b] + capillary[b : b + 1, :] * field[b]
    near = near_face()
    met = [near, 1 - near]
    if len(besides) == 3:
        met.append(sec_face())
    else:
        first = 3 - lax.axis_index("sec") % 2
        met += [first, 5 - first]
    for face, beside in zip(met, besides):
        weight = weights[pl.ds(face, 1), :]
        term = weight * beside[...]
        for p in range(fmap.shape[3]):
            here = slice(p * bdof, (p + 1) * bdof)
            b = fmap[0, 0, face, p]
            out[b] = out[b] + (weight[:, here] * field[b] - term[:, here])


def lanes(first, second):
    return jnp.sum(first[...] * second[...], axis=0)


def image_kernel(
    pair, cmap, fmap, weights, capillary, local, rvec, zvec, blocks, rows, *rest
):
    count = 3 if pair else 4
    besides, (wout, sums, base, payload, *scratch) = rest[:count], rest[count:]
    couple(fmap, weights, capillary, local, zvec, besides, wout)
    sums[0] = lanes(rvec, zvec)
    sums[1] = lanes(zvec, wout)
    begin(pair, cmap, fmap, wout, blocks, rows, base, payload, *scratch)


def last_kernel(fmap, weights, capillary, local, wvec, mvec, sums, *rest):
    *besides, nout, totals = rest
    couple(fmap, weights, capillary, local, mvec, besides, nout)
    parts = jnp.concatenate(
        [sums[0], sums[1], lanes(wvec, mvec), lanes(mvec, nout)], axis=0
    )
    sides = lax.dot_general(
        jnp.ones(totals.shape[:1] + parts.shape[1:], F32),
        parts,
        (((1,), (1,)), ((), ())),
        precision=lax.Precision.HIGHEST,
        preferred_element_type=F32,
    )
    totals[...] = jnp.concatenate([sides, jnp.zeros_like(sides)], axis=1)


def finish_kernel(shares, rvec, zvec, wvec, mvec, nvec, sol, res, short, tall):
    nblk, ncol, bdof = rvec.shape
    width = 4 * ncol
    total = jnp.sum(shares[:, 0, :], axis=0, keepdims=True)[:, :width]
    eye = lax.broadcasted_iota(jnp.int32, (width, width), 0) == lax.broadcasted_iota(
        jnp.int32, (width, width), 1
    )
    column = jnp.sum(jnp.where(eye, total, 0.0), axis=1, keepdims=True)
    gamma, delta, mu, nu = [column[q * ncol : (q + 1) * ncol] for q in range(4)]
    alpha = gamma / delta
    gnew = gamma - 2.0 * alpha * delta + alpha * alpha * mu
    grow = 1.0 + gnew / gamma
    dnew = grow * grow * delta - 2.0 * alpha * grow * mu + alpha * alpha * nu
    anew = gnew / dnew
    both = alpha + anew * grow
    second = anew * alpha
    both_at = 2 * nblk
    for b in range(nblk):
        short[pl.ds(b, ncol, stride=both_at), :] = both * zvec[b] - second * mvec[b]
        short[pl.ds(nblk + b, ncol, stride=both_at), :] = (
            rvec[b] - both * wvec[b] + second * nvec[b]
        )
    for c in range(ncol):
        tall[pl.ds(c, bdof, stride=ncol), :] = short[c * both_at : (c + 1) * both_at, :].T
    lanes_at = 128
    for j in range(sol.shape[1] // lanes_at):
        here = slice(j * lanes_at, (j + 1) * lanes_at)
        flat = tall[here, :].T
        sol[:, here] = flat[:nblk]
        res[:, here] = flat[nblk:]


def call(kernel, outs, scratch, smem, *args):
    vmem = pl.BlockSpec(memory_space=pltpu.VMEM)
    return pl.pallas_call(
        kernel,
        out_shape=outs,
        in_specs=[pl.BlockSpec(memory_space=pltpu.SMEM)] * smem + [vmem] * (len(args) - smem),
        out_specs=jax.tree.map(lambda _: vmem, outs),
        scratch_shapes=scratch,
        compiler_params=pltpu.CompilerParams(vmem_limit_bytes=VMEM_LIMIT),
    )(*args)


def everywhere(values):
    if lax.axis_size("sec") == 2:
        values = lax.all_gather(values, "sec")[:, :1].sum(axis=0)
    else:
        values = lax.psum(values[:1], "sec")
    copies = jnp.broadcast_to(values[None], (lax.axis_size("dam"),) + values.shape)
    return lax.all_to_all(copies, "dam", split_axis=0, concat_axis=0)


def exchange(sends, axis):
    size = lax.axis_size(axis)
    got = []
    for first, send in enumerate(sends):
        pairs = [(i, i + 1) for i in range(first, size - 1, 2)]
        got.append(lax.ppermute(send, axis, pairs + [(j, i) for i, j in pairs]))
    return got


def shards(
    segment_load,
    segment_mask,
    stiffness,
    block_cols,
    capillary,
    dirichlet_blocks,
    face_map,
    face_weight,
    corner_map,
    coarse_inverse,
):
    nblk, bdof = capillary.shape[2:]
    ncol = segment_load.shape[-1] // bdof
    nface = face_map.shape[3]
    ncorner = corner_map.shape[2]
    size = nblk * bdof
    pair = lax.axis_size("sec") == 2
    cols = jnp.transpose(block_cols[0], (2, 0, 1))
    tang, weights = capillary[0, 0], face_weight[0, 0]
    blocks, rows = dirichlet_blocks[0, 0], coarse_inverse[0]

    def shape(*dims):
        return jax.ShapeDtypeStruct(dims, F32)

    field = shape(nblk, ncol, bdof)
    face = shape(ncol, nface * bdof)
    group = ncorner * bdof
    tiles = pltpu.VMEM((size // group, group, group), BF16)
    splits = [tiles, tiles, pltpu.VMEM((size // group, 2 * ncol, group), BF16)]
    left = pltpu.VMEM((nblk, 2 * ncol, bdof), BF16)
    lane = group + nface * bdof if pair else group
    marked = ncol + 8 if pair else ncol

    def finish(base, shares, marks):
        vec, *faces = call(
            functools.partial(end_kernel, pair),
            (field,) + (face,) * (3 if pair else 4),
            [],
            2,
            corner_map,
            face_map,
            base,
            rows,
            shares,
            marks,
        )
        besides = exchange(faces[:2], "dam")
        besides += faces[2:] if pair else exchange(faces[2:], "sec")
        return vec, besides

    def local(vec):
        return call(local_kernel, field, [left], 1, cols, vec, stiffness[0, 0])

    rvec, base, payload = call(
        functools.partial(start_kernel, pair),
        (field, field, shape(marked, lane)),
        [pltpu.VMEM((size // nblk * ncol, nblk), F32), pltpu.VMEM((ncol * nblk, bdof), F32)]
        + splits,
        2,
        corner_map,
        face_map,
        segment_load[0, 0],
        segment_mask[0, 0],
        blocks,
        rows,
    )
    marks = lax.all_gather(payload, "sec")
    zvec, besides = finish(base, marks, marks)
    wvec, sums, base, payload = call(
        functools.partial(image_kernel, pair),
        (field, shape(2, ncol, bdof), field, shape(ncol, lane)),
        splits,
        2,
        corner_map,
        face_map,
        weights,
        tang,
        local(zvec),
        rvec,
        zvec,
        blocks,
        rows,
        *besides,
    )
    mvec, besides = finish(base, lax.all_gather(payload, "sec"), marks)
    nvec, totals = call(
        last_kernel,
        (field, shape(8, 2 * bdof)),
        [],
        1,
        face_map,
        weights,
        tang,
        local(mvec),
        wvec,
        mvec,
        sums,
        *besides,
    )
    sol, res = call(
        finish_kernel,
        (shape(nblk, bdof * ncol),) * 2,
        [pltpu.VMEM((ncol * 2 * nblk, bdof), F32), pltpu.VMEM((bdof * ncol, 2 * nblk), F32)],
        0,
        everywhere(totals),
        rvec,
        zvec,
        wvec,
        mvec,
        nvec,
    )
    return sol[None, None], res[None, None]


def solution(mesh):
    placed = (
        P("dam", "sec", None, None),
        P("dam", "sec", None, None),
        P("dam", "sec", None, None, None),
        P("dam", "sec", None, None),
        P("dam", "sec", None, None),
        P("dam", "sec", None, None, None),
        P("dam", "sec", None, None),
        P("dam", "sec", None, None),
        P("dam", "sec", None),
        P("dam", "sec", None),
    )
    return jax.shard_map(
        shards,
        mesh=mesh,
        in_specs=placed,
        out_specs=(P("dam", "sec", None, None), P("dam", "sec", None, None)),
        check_vma=False,
    )
```

time: 51.9 us -> 51.6 us (level)
  local copies, waits for them, and re-layouts: 9.27 us -> 6.86 us
  blocking collectives: 22.8 us -> 24.6 us
  Pallas kernels: 9.35 us -> 10.3 us
  other arithmetic: 0.81 us -> 0.02 us
    unnamed x13 -> x32, local copies, waits for them, and re-layouts: 2.12 us -> 6.85 us
    another operation x5 -> x0, local copies, waits for them, and re-layouts: 4.06 us -> none  [the longest x2 3.05 us: shards(): segment_load[0, 0].reshape(nblk, bdof, ncol)]
    all_to_all x1, blocking collectives: 15.2 us -> 18.8 us  [everywhere(): return lax.all_to_all(copies, 'dam', split_axis=0, concat_axis=0)]
    reshape x2 -> x0, local copies, waits for them, and re-layouts: 1.81 us -> none  [back(): return jnp.swapaxes(vec, 1, 2).reshape(1, 1, nblk, bdof * ncol)]
    all_gather x4 -> x3, blocking collectives: 7.59 us -> 5.81 us  [the longest x1 2 us: shards(): mvec, besides = finish(base, lax.all_gather(payload, 'sec'), marks)]
    pallas_call x8, Pallas kernels: 9.35 us -> 10.3 us  [call(): pl.pallas_call(kernel, out_shape=outs, in_specs=[pl.BlockSpec(memory_spac...]
    squeeze x2 -> x0, local copies, waits for them, and re-layouts: 0.76 us -> none  [exchange(): lax.dynamic_index_in_dim(both, 1 - lax.axis_index(axis), keepdims=False)]
    convert_element_type x1 -> x0, other arithmetic: 0.7 us -> none  [shards(): segment_mask[0, 0].astype(F32)[:, None, :]]
  transfers between devices with their start and end apart: 4 -> 4, of which waited for: 0 -> 0; matrix products, arithmetic and copies ran while one was open for 3% -> 0% of each run, Pallas kernels for 7% -> 5%
where the time goes in v4:
time: 51.6 us; the launch traced here: 51.1 us
  blocking collectives  24.6 us (48%)
  Pallas kernels  10.3 us (20%)
  starting transfers between devices  8.5 us (16%)
  local copies, waits for them, and re-layouts  6.86 us (13%)
  between operations  0.78 us (2%)
    all_to_all x1, blocking collectives, everywhere(): return lax.all_to_all(copies, 'dam', split_axis=0, concat_axis=0)  18.8 us
    pallas_call x8, Pallas kernels, call(): pl.pallas_call(kernel, out_shape=outs, in_specs=[pl.BlockSpec(memory_spac...  10.3 us
    ppermute x4, starting transfers between devices, exchange(): got.append(lax.ppermute(send, axis, pairs + [(j, i) for i, j in pairs]))  8.5 us
    unnamed x32, local copies, waits for them, and re-layouts  6.85 us
    all_gather x1, blocking collectives, shards(): mvec, besides = finish(base, lax.all_gather(payload, 'sec'), marks)  2 us
    all_gather x1, blocking collectives, shards(): marks = lax.all_gather(payload, 'sec')  2 us
    all_gather x1, blocking collectives, everywhere(): values = lax.all_gather(values, 'sec')[:, :1].sum(axis=0)  1.81 us
  transfers between devices with their start and end apart: 4, of which 0 were waited for; matrix products, arithmetic and copies ran while one was open for 0% of the time, Pallas kernels for 5%

profile of v4, /device:TPU:0, one launch (start us, length us, event | category | flops | bytes accessed | tf_op | source)
XLA Modules:
  0.0 51.1 jit_solution(4704353989807309705)
XLA Ops:
  0.6 0.0 copy-start
  0.6 0.0 copy-start.1
  0.7 1.2 %copy-done.1 = f32[1,256,512]{2,1,0:T(8,128)S(1)} copy-done((f32[1,256,512]{2,1,0:T(8,128)S(1)}, f32[1,256,512]{2,1,0:T(8,128)}, u32[]{:S(2)}) %copy-start.1) | copy-done | bytes 524312
  1.8 0.0 copy-start.4
  1.8 1.0 %copy-done.4 = f32[1,1,16,64,64]{4,3,2,1,0:T(8,128)S(1)} copy-done((f32[1,1,16,64,64]{4,3,2,1,0:T(8,128)S(1)}, f32[1,1,16,64,64]{4,3,2,1,0:T(8,128)}, u32[]{:S(2)}) %copy-start.4) | copy-done | bytes 262168
  2.9 0.0 copy-start.6
  2.9 0.8 %copy-done.6 = f32[1,1,16,1024]{3,2,1,0:T(8,128)S(1)} copy-done((f32[1,1,16,1024]{3,2,1,0:T(8,128)S(1)}, f32[1,1,16,1024]{3,2,1,0:T(8,128)}, u32[]{:S(2)}) %copy-start.6) | copy-done | bytes 65560
  3.7 0.0 copy-start.7
  3.7 0.7 %copy-done.7 = s32[1,1,4,8]{3,2,1,0:T(4,128)S(1)} copy-done((s32[1,1,4,8]{3,2,1,0:T(4,128)S(1)}, s32[1,1,4,8]{3,2,1,0:T(4,128)}, u32[]{:S(2)}) %copy-start.7) | copy-done | bytes 152
  4.4 0.0 copy-start.13
  4.4 0.7 %copy-done.13 = s32[1,1,4]{2,1,0:T(1,128)S(1)} copy-done((s32[1,1,4]{2,1,0:T(1,128)S(1)}, s32[1,1,4]{2,1,0:T(1,128)}, u32[]{:S(2)}) %copy-start.13) | copy-done | bytes 40
  5.1 0.0 copy-start.15
  5.1 0.7 %copy-done.15 = s32[1,1,16,16]{3,2,1,0:T(8,128)S(1)} copy-done((s32[1,1,16,16]{3,2,1,0:T(8,128)S(1)}, s32[1,1,16,16]{3,2,1,0:T(8,128)}, u32[]{:S(2)}) %copy-start.15) | copy-done | bytes 1048
  5.8 1.7 %shard_map.113 = (f32[16,16,64]{2,1,0:T(8,128)S(1)}, f32[16,16,64]{2,1,0:T(8,128)S(1)}, f32[24,768]{1,0:T(8,128)S(1)}) custom-call(s32[1,1,4]{2,1,0:T(1,128)S(1)} %copy-done.13, s32[1,1,4,8]{3,2,1,0:T(4,128)S(1)} %copy-done.7, f32[16,1024]{1,0:T(8,128)S(1)} %bitcast.27, s32[16,16]{1,0:T(8,128)S(1)} %bitcast.34, f32[16,64,64]{2,1,0:T(8,128)S(1)} %bitcast.24, ...), custom_call_target="tpu_custom_call" | custom-call | tf_op jit(solution)/shard_map/pallas_call | solution.py:247
  7.5 2.0 %all-gather = f32[48,768]{1,0:T(8,128)S(1)} all-gather(f32[24,768]{1,0:T(8,128)S(1)} %get-tuple-element.22), channel_id=2, replica_groups=mesh['dam'=16,'sec'=2] {'sec'}, dimensions={0}, use_global_device_ids=true | all-gather | bytes 221184 | tf_op jit(solution)/shard_map/all_gather | solution.py:342
  9.5 0.0 copy-start.2
  9.5 1.0 %copy-done.2 = f32[1,256,512]{2,1,0:T(8,128)S(1)} copy-done((f32[1,256,512]{2,1,0:T(8,128)S(1)}, f32[1,256,512]{2,1,0:T(8,128)}, u32[]{:S(2)}) %copy-start.2) | copy-done | bytes 524312
  10.5 0.0 copy-start.3
  10.5 0.0 copy-start.5
  10.5 0.0 copy-start.9
  10.5 1.0 %shard_map.114 = (f32[16,16,64]{2,1,0:T(8,128)S(1)}, f32[16,512]{1,0:T(8,128)S(1)}, f32[16,512]{1,0:T(8,128)S(1)}, f32[16,512]{1,0:T(8,128)S(1)}) custom-call(s32[1,1,4]{2,1,0:T(1,128)S(1)} %copy-done.13, s32[1,1,4,8]{3,2,1,0:T(4,128)S(1)} %copy-done.7, f32[16,16,64]{2,1,0:T(8,128)S(1)} %get-tuple-element.21.base, f32[256,512]{1,0:T(8,128)S(1)} %bitcast.18, ...), custom_call_target="tpu_custom_call" | custom-call | tf_op jit(solution)/shard_map/pallas_call | solution.py:247
  11.6 2.9 %collective-permute-start = (f32[16,512]{1,0:T(8,128)S(1)}, f32[16,512]{1,0:T(8,128)S(1)}, u32[]{:S(2)}, u32[]{:S(2)}) collective-permute-start(f32[16,512]{1,0:T(8,128)S(1)} %get-tuple-element.25), channel_id=1, source_target_pairs={{0,2},{4,6},{8,10},{12,14},{16,18},{20,22},{24,26},{28,30},{2,0},{... | collective-permute-start | bytes 98312 | tf_op jit(solution)/shard_map/ppermute | solution.py:271
  14.5 0.7 %collective-permute-start.1 = (f32[16,512]{1,0:T(8,128)S(1)}, f32[16,512]{1,0:T(8,128)S(1)}, u32[]{:S(2)}, u32[]{:S(2)}) collective-permute-start(f32[16,512]{1,0:T(8,128)S(1)} %get-tuple-element.26), channel_id=1, source_target_pairs={{2,4},{6,8},{10,12},{14,16},{18,20},{22,24},{26,28},{4,2},{8,6},{1... | collective-permute-start | bytes 98312 | tf_op jit(solution)/shard_map/ppermute | solution.py:271
  15.1 0.0 copy-done
  15.1 0.0 copy-start.11
  15.1 0.7 %copy-done.11 = s32[1,1,16,7]{2,1,3,0:T(1,128)S(1)} copy-done((s32[1,1,16,7]{2,1,3,0:T(1,128)S(1)}, s32[1,1,16,7]{2,1,3,0:T(1,128)}, u32[]{:S(2)}) %copy-start.11) | copy-done | bytes 472
  15.8 1.3 %shard_map.115.local = f32[16,16,64]{2,1,0:T(8,128)S(1)} custom-call(s32[7,1,16]{2,1,0:T(1,128)S(1)} %bitcast.32, f32[16,16,64]{2,1,0:T(8,128)S(1)} %get-tuple-element.23.field.zvec, f32[16,64,448]{2,1,0:T(8,128)S(1)} %bitcast.15), custom_call_target="tpu_custom_call" | custom-call | tf_op jit(solution)/shard_map/pallas_call | solution.py:247
  17.2 0.0 collective-permute-done.rest_0_
  17.2 0.0 collective-permute-done.1.rest_1_
  17.2 0.0 copy-done.3
  17.2 0.0 copy-done.5
  17.2 0.0 copy-done.9
  17.2 0.0 copy-done.10
  17.2 0.0 copy-done.14
  17.2 1.6 %shard_map.116 = (f32[16,16,64]{2,1,0:T(8,128)S(1)}, f32[2,16,64]{2,1,0:T(8,128)S(1)}, f32[16,16,64]{2,1,0:T(8,128)S(1)}, f32[16,768]{1,0:T(8,128)S(1)}) custom-call(s32[1,1,4]{2,1,0:T(1,128)S(1)} %copy-done.14, s32[1,1,4,8]{3,2,1,0:T(4,128)S(1)} %copy-done.7, f32[4,512]{1,0:T(4,128)S(1)} %bitcast.28, f32[16,64]{1,0:T(8,128)S(1)} %bitcast.30, ...), custom_call_target="tpu_custom_call" | custom-call | tf_op jit(solution)/shard_map/pallas_call | solution.py:247
  18.8 2.0 %all-gather.1 = f32[32,768]{1,0:T(8,128)S(1)} all-gather(f32[16,768]{1,0:T(8,128)S(1)} %get-tuple-element.29), channel_id=3, replica_groups=mesh['dam'=16,'sec'=2] {'sec'}, dimensions={0}, use_global_device_ids=true | all-gather | bytes 147456 | tf_op jit(solution)/shard_map/all_gather | solution.py:360
  20.8 1.0 %shard_map.117 = (f32[16,16,64]{2,1,0:T(8,128)S(1)}, f32[16,512]{1,0:T(8,128)S(1)}, f32[16,512]{1,0:T(8,128)S(1)}, f32[16,512]{1,0:T(8,128)S(1)}) custom-call(s32[1,1,4]{2,1,0:T(1,128)S(1)} %copy-done.14, s32[1,1,4,8]{3,2,1,0:T(4,128)S(1)} %copy-done.7, f32[16,16,64]{2,1,0:T(8,128)S(1)} %get-tuple-element.28.base, f32[256,512]{1,0:T(8,128)S(1)} %bitcast.20, ...), custom_call_target="tpu_custom_call" | custom-call | tf_op jit(solution)/shard_map/pallas_call | solution.py:247
  21.8 4.3 %collective-permute-start.2 = (f32[16,512]{1,0:T(8,128)S(1)}, f32[16,512]{1,0:T(8,128)S(1)}, u32[]{:S(2)}, u32[]{:S(2)}) collective-permute-start(f32[16,512]{1,0:T(8,128)S(1)} %get-tuple-element.33), channel_id=1, source_target_pairs={{0,2},{4,6},{8,10},{12,14},{16,18},{20,22},{24,26},{28,30},{2,0},{... | collective-permute-start | bytes 98312 | tf_op jit(solution)/shard_map/ppermute | solution.py:271
  26.1 0.7 %collective-permute-start.3 = (f32[16,512]{1,0:T(8,128)S(1)}, f32[16,512]{1,0:T(8,128)S(1)}, u32[]{:S(2)}, u32[]{:S(2)}) collective-permute-start(f32[16,512]{1,0:T(8,128)S(1)} %get-tuple-element.34), channel_id=1, source_target_pairs={{2,4},{6,8},{10,12},{14,16},{18,20},{22,24},{26,28},{4,2},{8,6},{1... | collective-permute-start | bytes 98312 | tf_op jit(solution)/shard_map/ppermute | solution.py:271
  26.7 0.0 copy-done.12
  26.7 1.3 %shard_map.118.local = f32[16,16,64]{2,1,0:T(8,128)S(1)} custom-call(s32[7,1,16]{2,1,0:T(1,128)S(1)} %bitcast.33, f32[16,16,64]{2,1,0:T(8,128)S(1)} %get-tuple-element.30.field.mvec, f32[16,64,448]{2,1,0:T(8,128)S(1)} %bitcast.16), custom_call_target="tpu_custom_call" | custom-call | tf_op jit(solution)/shard_map/pallas_call | solution.py:247
  28.1 0.0 collective-permute-done.2.rest_0_
  28.1 0.0 collective-permute-done.3.rest_1_
  28.1 0.0 copy-done.8
  28.1 1.1 %shard_map.119 = (f32[16,16,64]{2,1,0:T(8,128)S(1)}, f32[8,128]{1,0:T(8,128)S(1)}) custom-call(s32[1,1,4,8]{3,2,1,0:T(4,128)S(1)} %copy-done.8, f32[4,512]{1,0:T(4,128)S(1)} %bitcast.29, f32[16,64]{1,0:T(8,128)S(1)} %bitcast.31, f32[16,16,64]{2,1,0:T(8,128)S(1)} %shard_map.118.local, f32[16,16,64]{2,1,0:T(8,128)S(1)} %get-tuple-element.31.wvec, ...), custom_call_target="tpu_custom_call" | custom-call | tf_op jit(solution)/shard_map/pallas_call | solution.py:247
  29.2 1.8 %all-gather.2 = f32[16,128]{1,0:T(8,128)S(1)} all-gather(f32[8,128]{1,0:T(8,128)S(1)} %get-tuple-element.36), channel_id=4, replica_groups=mesh['dam'=16,'sec'=2] {'sec'}, dimensions={0}, use_global_device_ids=true | all-gather | bytes 12288 | tf_op jit(solution)/shard_map/all_gather | solution.py:259
  31.0 18.8 %all_to_all.5.shares = f32[16,1,128]{2,1,0:T(1,128)S(1)} all-to-all(f32[16,1,128]{2,1,0:T(1,128)S(1)} %broadcast_in_dim.12), channel_id=1, replica_groups=mesh['dam'=16,'sec'=2] {'dam'}, dimensions={0} | all-to-all | bytes 16384 | tf_op jit(solution)/shard_map/all_to_all | solution.py:263
  49.8 1.3 %shard_map.120 = (f32[16,1024]{1,0:T(8,128)}, f32[16,1024]{1,0:T(8,128)}) custom-call(f32[16,1,128]{2,1,0:T(1,128)S(1)} %all_to_all.5.shares, f32[16,16,64]{2,1,0:T(8,128)S(1)} %get-tuple-element.24.rvec, f32[16,16,64]{2,1,0:T(8,128)S(1)} %get-tuple-element.23.field.zvec, f32[16,16,64]{2,1,0:T(8,128)S(1)} %get-tuple-element.31.wvec, ...), custom_call_target="tpu_custom_call" | custom-call | tf_op jit(solution)/shard_map/pallas_call | solution.py:247
  (6 shorter events, 0.0 us)
Async XLA Ops:
  0.6 14.5 %copy-start = (f32[1,1,16,64,448]{4,3,2,1,0:T(8,128)S(1)}, f32[1,1,16,64,448]{4,3,2,1,0:T(8,128)}, u32[]{:S(2)}) copy-start(f32[1,1,16,64,448]{4,3,2,1,0:T(8,128)} %param.12) | copy-start | bytes 5505028
  0.6 1.2 %copy-start.1 = (f32[1,256,512]{2,1,0:T(8,128)S(1)}, f32[1,256,512]{2,1,0:T(8,128)}, u32[]{:S(2)}) copy-start(f32[1,256,512]{2,1,0:T(8,128)} %param.19) | copy-start | bytes 1572868
  1.8 1.0 %copy-start.4 = (f32[1,1,16,64,64]{4,3,2,1,0:T(8,128)S(1)}, f32[1,1,16,64,64]{4,3,2,1,0:T(8,128)}, u32[]{:S(2)}) copy-start(f32[1,1,16,64,64]{4,3,2,1,0:T(8,128)} %param.15) | copy-start | bytes 786436
  2.9 0.8 %copy-start.6 = (f32[1,1,16,1024]{3,2,1,0:T(8,128)S(1)}, f32[1,1,16,1024]{3,2,1,0:T(8,128)}, u32[]{:S(2)}) copy-start(f32[1,1,16,1024]{3,2,1,0:T(8,128)} %param.10) | copy-start | bytes 196612
  3.7 0.7 %copy-start.7 = (s32[1,1,4,8]{3,2,1,0:T(4,128)S(1)}, s32[1,1,4,8]{3,2,1,0:T(4,128)}, u32[]{:S(2)}) copy-start(s32[1,1,4,8]{3,2,1,0:T(4,128)} %fmap.9) | copy-start | bytes 388
  4.4 0.7 %copy-start.13 = (s32[1,1,4]{2,1,0:T(1,128)S(1)}, s32[1,1,4]{2,1,0:T(1,128)}, u32[]{:S(2)}) copy-start(s32[1,1,4]{2,1,0:T(1,128)} %cmap.7) | copy-start | bytes 52
  5.1 0.7 %copy-start.15 = (s32[1,1,16,16]{3,2,1,0:T(8,128)S(1)}, s32[1,1,16,16]{3,2,1,0:T(8,128)}, u32[]{:S(2)}) copy-start(s32[1,1,16,16]{3,2,1,0:T(8,128)} %param.11) | copy-start | bytes 3076
  9.5 1.0 %copy-start.2 = (f32[1,256,512]{2,1,0:T(8,128)S(1)}, f32[1,256,512]{2,1,0:T(8,128)}, u32[]{:S(2)}) copy-start(f32[1,256,512]{2,1,0:T(8,128)} %param.19) | copy-start | bytes 1572868
  10.5 6.6 %copy-start.3 = (f32[1,256,512]{2,1,0:T(8,128)S(1)}, f32[1,256,512]{2,1,0:T(8,128)}, u32[]{:S(2)}) copy-start(f32[1,256,512]{2,1,0:T(8,128)} %param.19) | copy-start | bytes 1572868
  10.5 6.7 %copy-start.5 = (f32[1,1,16,64,64]{4,3,2,1,0:T(8,128)S(1)}, f32[1,1,16,64,64]{4,3,2,1,0:T(8,128)}, u32[]{:S(2)}) copy-start(f32[1,1,16,64,64]{4,3,2,1,0:T(8,128)} %param.15) | copy-start | bytes 786436
  10.5 6.7 %copy-start.9 = (f32[1,1,4,512]{3,2,1,0:T(4,128)S(1)}, f32[1,1,4,512]{3,2,1,0:T(4,128)}, u32[]{:S(2)}) copy-start(f32[1,1,4,512]{3,2,1,0:T(4,128)} %param.17) | copy-start | bytes 24580
  10.5 6.7 %copy-start.10 = (f32[1,1,16,64]{3,2,1,0:T(8,128)S(1)}, f32[1,1,16,64]{3,2,1,0:T(8,128)}, u32[]{:S(2)}) copy-start(f32[1,1,16,64]{3,2,1,0:T(8,128)} %param.14) | copy-start | bytes 12292
  11.6 5.6 %collective-permute-start = (f32[16,512]{1,0:T(8,128)S(1)}, f32[16,512]{1,0:T(8,128)S(1)}, u32[]{:S(2)}, u32[]{:S(2)}) collective-permute-start(f32[16,512]{1,0:T(8,128)S(1)} %get-tuple-element.25), channel_id=1, source_target_pairs={{0,2},{4,6},{8,10},{12,14},{16,18},{20,22},{24,26},{28,30},{2,0},{... | collective-permute-start | bytes 98312 | tf_op jit(solution)/shard_map/ppermute | solution.py:271
  14.5 2.7 %collective-permute-start.1 = (f32[16,512]{1,0:T(8,128)S(1)}, f32[16,512]{1,0:T(8,128)S(1)}, u32[]{:S(2)}, u32[]{:S(2)}) collective-permute-start(f32[16,512]{1,0:T(8,128)S(1)} %get-tuple-element.26), channel_id=1, source_target_pairs={{2,4},{6,8},{10,12},{14,16},{18,20},{22,24},{26,28},{4,2},{8,6},{1... | collective-permute-start | bytes 98312 | tf_op jit(solution)/shard_map/ppermute | solution.py:271
  15.1 0.7 %copy-start.11 = (s32[1,1,16,7]{2,1,3,0:T(1,128)S(1)}, s32[1,1,16,7]{2,1,3,0:T(1,128)}, u32[]{:S(2)}) copy-start(s32[1,1,16,7]{2,1,3,0:T(1,128)} %param.13) | copy-start | bytes 1348
  15.8 1.4 %copy-start.14 = (s32[1,1,4]{2,1,0:T(1,128)S(1)}, s32[1,1,4]{2,1,0:T(1,128)}, u32[]{:S(2)}) copy-start(s32[1,1,4]{2,1,0:T(1,128)} %cmap.7) | copy-start | bytes 52
  15.8 10.9 %copy-start.12 = (s32[1,1,16,7]{2,1,3,0:T(1,128)S(1)}, s32[1,1,16,7]{2,1,3,0:T(1,128)}, u32[]{:S(2)}) copy-start(s32[1,1,16,7]{2,1,3,0:T(1,128)} %param.13) | copy-start | bytes 1348
  18.8 9.3 %copy-start.8 = (s32[1,1,4,8]{3,2,1,0:T(4,128)S(1)}, s32[1,1,4,8]{3,2,1,0:T(4,128)}, u32[]{:S(2)}) copy-start(s32[1,1,4,8]{3,2,1,0:T(4,128)} %fmap.9) | copy-start | bytes 388
  21.8 6.3 %collective-permute-start.2 = (f32[16,512]{1,0:T(8,128)S(1)}, f32[16,512]{1,0:T(8,128)S(1)}, u32[]{:S(2)}, u32[]{:S(2)}) collective-permute-start(f32[16,512]{1,0:T(8,128)S(1)} %get-tuple-element.33), channel_id=1, source_target_pairs={{0,2},{4,6},{8,10},{12,14},{16,18},{20,22},{24,26},{28,30},{2,0},{... | collective-permute-start | bytes 98312 | tf_op jit(solution)/shard_map/ppermute | solution.py:271
  26.1 2.0 %collective-permute-start.3 = (f32[16,512]{1,0:T(8,128)S(1)}, f32[16,512]{1,0:T(8,128)S(1)}, u32[]{:S(2)}, u32[]{:S(2)}) collective-permute-start(f32[16,512]{1,0:T(8,128)S(1)} %get-tuple-element.34), channel_id=1, source_target_pairs={{2,4},{6,8},{10,12},{14,16},{18,20},{22,24},{26,28},{4,2},{8,6},{1... | collective-permute-start | bytes 98312 | tf_op jit(solution)/shard_map/ppermute | solution.py:271

commit v5 on v4

v5 whole, which is shorter than its diff:
```python
import functools

import jax
import jax.numpy as jnp
from jax import lax
from jax.experimental import pallas as pl
from jax.experimental.pallas import tpu as pltpu
from jax.sharding import PartitionSpec as P

F32 = jnp.float32
BF16 = jnp.bfloat16
VMEM_LIMIT = 16 * 1024 * 1024


def halves(x):
    high = x.astype(BF16)
    return high, (x - high.astype(F32)).astype(BF16)


def dot_t(a, b):
    return lax.dot_general(a, b, (((1,), (1,)), ((), ())), preferred_element_type=F32)


def dot(a, b):
    return lax.dot_general(a, b, (((1,), (0,)), ((), ())), preferred_element_type=F32)


def three_pass(mul, left, high, low):
    rows = left.shape[0] // 2
    first = mul(left, high)
    return first[:rows] + first[rows:] + mul(left[:rows], low)


def near_face():
    return 1 - lax.axis_index("dam") % 2


def sec_face():
    return 3 - lax.axis_index("sec")


def pack_face(face, fmap, field, out):
    bdof = field.shape[2]
    for p in range(fmap.shape[3]):
        out[..., : field.shape[1], p * bdof : (p + 1) * bdof] = field[fmap[0, 0, face, p]]


def scatter_corners(cmap, correct, field):
    bdof = field.shape[2]
    where = [cmap[0, 0, n] for n in range(cmap.shape[2])]
    new = [
        field[b] + correct[:, n * bdof : (n + 1) * bdof] for n, b in enumerate(where)
    ]
    for b, value in zip(where, new):
        field[b] = value


def split_blocks(blocks, tiles_high, tiles_low):
    nblk, bdof = blocks.shape[:2]
    group = tiles_high.shape[1] // bdof
    tiles_high[...] = jnp.zeros_like(tiles_high)
    tiles_low[...] = jnp.zeros_like(tiles_low)
    for b in range(nblk):
        t, j = divmod(b, group)
        here = slice(j * bdof, (j + 1) * bdof)
        tiles_high[t, here, here], tiles_low[t, here, here] = halves(blocks[b])


def apply_blocks(field, tiles_high, tiles_low, left, base):
    nblk, ncol, bdof = field.shape
    group = tiles_high.shape[1] // bdof
    for b in range(nblk):
        t, j = divmod(b, group)
        here = slice(j * bdof, (j + 1) * bdof)
        left[t, :ncol, here], left[t, ncol:, here] = halves(field[b])
    for t in range(nblk // group):
        out = three_pass(dot, left[t], tiles_high[t], tiles_low[t])
        for j in range(group):
            base[t * group + j] = out[:, j * bdof : (j + 1) * bdof]


def pack_corners(pair, cmap, fmap, field, payload):
    ncol, bdof = field.shape[1:]
    at = fmap.shape[3] * bdof if pair else 0
    for n in range(cmap.shape[2]):
        payload[:ncol, at + n * bdof : at + (n + 1) * bdof] = field[cmap[0, 0, n]]


def own_correction(cmap, fmap, rows, base, payload):
    ncol, bdof = base.shape[1:]
    wide = cmap.shape[2] * bdof
    start = pl.multiple_of(lax.axis_index("sec") * wide, wide)
    own = stack(payload[:ncol, fmap.shape[3] * bdof :])
    correct = three_pass(dot_t, own, *halves(rows[:, pl.ds(start, wide)]))
    scatter_corners(cmap, correct, base)
    pack_face(sec_face(), fmap, base, payload)


def mark_corners(cmap, fmap, ncol, bdof, payload):
    payload[ncol:, :] = jnp.zeros_like(payload[ncol:, :])
    for n in range(cmap.shape[2]):
        for p in range(fmap.shape[3]):
            same = cmap[0, 0, n] == fmap[0, 0, sec_face(), p]
            payload[ncol + n : ncol + n + 1, p * bdof : (p + 1) * bdof] = jnp.full(
                (1, bdof), jnp.where(same, 1.0, 0.0), F32
            )


def stack(x):
    return jnp.concatenate(halves(x), axis=0)


def fetch(pairs, sems):
    copies = [
        pltpu.make_async_copy(source, target, sems.at[i])
        for i, (source, target) in enumerate(pairs)
    ]
    for copy in copies:
        copy.start()
    return [copy.wait for copy in copies]


def end_kernel(pair, cmap_in, fmap_in, base, rows, shares, marks, zout, *rest):
    *faces, cmap, fmap, sems = rest
    waits = fetch([(cmap_in, cmap), (fmap_in, fmap)], sems)
    nblk, ncol, bdof = base.shape
    ncorner, nface = cmap.shape[2], fmap.shape[3]
    wide = ncorner * bdof
    zout[...] = base[...]
    if pair:
        me = lax.axis_index("sec")
        at = nface * bdof
        start = pl.multiple_of((1 - me) * wide, wide)
        high, low = halves(rows[:, pl.ds(start, wide)])
        own = stack(shares[pl.ds(me, 1), :ncol, at:][0])
        other = stack(shares[pl.ds(1 - me, 1), :ncol, at:][0])
        theirs = three_pass(dot, own, high, low)
        correct = three_pass(dot_t, other, high, low)
        chunk = 2 * bdof
        twice = [
            jnp.concatenate([theirs[:, n * bdof : (n + 1) * bdof]] * 2, axis=1)
            for n in range(ncorner)
        ]
        for j in range(at // chunk):
            here = slice(j * chunk, (j + 1) * chunk)
            value = shares[pl.ds(1 - me, 1), :ncol, here][0]
            for n in range(ncorner):
                mark = marks[pl.ds(1 - me, 1), ncol + n : ncol + n + 1, here][0]
                value = value + mark * twice[n]
            faces[-1][:, here] = value
    else:
        correct = 0.0
        for s in range(shares.shape[0]):
            high, low = halves(rows[:, s * wide : (s + 1) * wide])
            correct = correct + three_pass(dot_t, stack(shares[s]), high, low)
    for wait in waits:
        wait()
    scatter_corners(cmap, correct, zout)
    near = near_face()
    pack_face(1 - near, fmap, zout, faces[0])
    pack_face(near, fmap, zout, faces[1])
    if not pair:
        near = 3 - lax.axis_index("sec") % 2
        pack_face(5 - near, fmap, zout, faces[2])
        pack_face(near, fmap, zout, faces[3])


def start_kernel(pair, *refs):
    load_in, mask_in, cmap_in, fmap_in, blocks_in, *others = refs[:9]
    rvec, base, payload, tiles_high, tiles_low, *copied = refs[9:20]
    load, mask, blocks, cmap, fmap, tall, short, left, sems = refs[20:]
    rows = copied[2]
    waits = fetch(
        [
            (load_in, load),
            (mask_in, mask),
            (blocks_in, blocks),
            (cmap_in, cmap),
            (fmap_in, fmap),
        ]
        + list(zip([cmap_in, fmap_in] + others, copied)),
        sems,
    )
    nblk, ncol, bdof = rvec.shape
    lanes_at = 128
    waits[0]()
    waits[1]()
    scale = mask[...].astype(F32)
    scale = jnp.concatenate([scale] * (lanes_at // ncol), axis=1)
    for j in range(load.shape[1] // lanes_at):
        here = slice(j * lanes_at, (j + 1) * lanes_at)
        tall[here, :] = (load[:, here] * scale).T
    for c in range(ncol):
        short[c * nblk : (c + 1) * nblk, :] = tall[pl.ds(c, bdof, stride=ncol), :].T
    for b in range(nblk):
        rvec[b] = short[pl.ds(b, ncol, stride=nblk), :]
    waits[2]()
    split_blocks(blocks, tiles_high, tiles_low)
    apply_blocks(rvec, tiles_high, tiles_low, left, base)
    waits[3]()
    waits[4]()
    pack_corners(pair, cmap, fmap, rvec, payload)
    for wait in waits[5:]:
        wait()
    if pair:
        own_correction(cmap, fmap, rows, base, payload)
        mark_corners(cmap, fmap, ncol, bdof, payload)


def local_kernel(cols_in, fmap_in, weights, capillary, field, stiff, out, left, cols, fmap, sems):
    nblk, ncol, bdof = field.shape
    waits = fetch([(cols_in, cols), (fmap_in, fmap)], sems)
    kept = stiff.shape[2] // bdof
    for b in range(nblk):
        left[b] = stack(field[b])
    waits[0]()
    group = 4
    for t in range(0, nblk, group):
        gathered = [
            jnp.concatenate([left[cols[k, 0, t + j]] for k in range(kept)], axis=1)
            for j in range(group)
        ]
        firsts = [g[:ncol] for g in gathered]
        seconds = [g[ncol:] for g in gathered]
        rows = stiff[t : t + group].reshape(group * bdof, kept * bdof)
        prod = three_pass(dot_t, jnp.concatenate(firsts + seconds, axis=0), *halves(rows))
        for j in range(group):
            out[t + j] = (
                prod[j * ncol : (j + 1) * ncol, j * bdof : (j + 1) * bdof]
                + capillary[t + j : t + j + 1, :] * field[t + j]
            )
    waits[1]()
    for face in range(4):
        where = [fmap[0, 0, face, p] for p in range(fmap.shape[3])]
        new = [
            out[b] + weights[face : face + 1, p * bdof : (p + 1) * bdof] * field[b]
            for p, b in enumerate(where)
        ]
        for b, value in zip(where, new):
            out[b] = value


def couple(fmap, weights, local, besides, out):
    bdof = local.shape[2]
    out[...] = local[...]
    near = near_face()
    met = [1 - near, near]
    if len(besides) == 3:
        met.append(sec_face())
    else:
        first = 3 - lax.axis_index("sec") % 2
        met += [5 - first, first]
    for face, beside in zip(met, besides):
        term = weights[pl.ds(face, 1), :] * beside[...]
        where = [fmap[0, 0, face, p] for p in range(fmap.shape[3])]
        new = [out[b] - term[:, p * bdof : (p + 1) * bdof] for p, b in enumerate(where)]
        for b, value in zip(where, new):
            out[b] = value


def lanes(first, second):
    return jnp.sum(first[...] * second[...], axis=0)


def image_kernel(
    pair, cmap_in, fmap_in, weights, local, rvec, zvec, tiles_high, tiles_low, rows, *rest
):
    count = 3 if pair else 4
    besides, rest = rest[:count], rest[count:]
    wout, sums, base, payload, cmap, fmap, left, sems = rest
    waits = fetch([(fmap_in, fmap), (cmap_in, cmap)], sems)
    sums[0] = lanes(rvec, zvec)
    waits[0]()
    couple(fmap, weights, local, besides, wout)
    sums[1] = lanes(zvec, wout)
    apply_blocks(wout, tiles_high, tiles_low, left, base)
    waits[1]()
    pack_corners(pair, cmap, fmap, wout, payload)
    if pair:
        own_correction(cmap, fmap, rows, base, payload)


def last_kernel(fmap_in, weights, local, wvec, mvec, sums, *rest):
    *besides, nout, totals, fmap, sems = rest
    (wait,) = fetch([(fmap_in, fmap)], sems)
    third = lanes(wvec, mvec)
    wait()
    couple(fmap, weights, local, besides, nout)
    parts = jnp.concatenate([sums[0], sums[1], third, lanes(mvec, nout)], axis=0)
    totals[...] = lax.dot_general(
        jnp.ones((1, parts.shape[1]), F32),
        parts,
        (((1,), (1,)), ((), ())),
        precision=lax.Precision.HIGHEST,
        preferred_element_type=F32,
    )


def finish_kernel(shares, rvec, zvec, wvec, mvec, nvec, sol, res, short, tall):
    nblk, ncol, bdof = rvec.shape
    width = 4 * ncol
    total = jnp.sum(shares[...], axis=0, keepdims=True)
    eye = lax.broadcasted_iota(jnp.int32, (width, width), 0) == lax.broadcasted_iota(
        jnp.int32, (width, width), 1
    )
    column = jnp.sum(jnp.where(eye, total, 0.0), axis=1, keepdims=True)
    gamma, delta, mu, nu = [column[q * ncol : (q + 1) * ncol] for q in range(4)]
    alpha = gamma / delta
    gnew = gamma - 2.0 * alpha * delta + alpha * alpha * mu
    grow = 1.0 + gnew / gamma
    dnew = grow * grow * delta - 2.0 * alpha * grow * mu + alpha * alpha * nu
    anew = gnew / dnew
    both = alpha + anew * grow
    second = anew * alpha
    both_at = 2 * nblk
    for b in range(nblk):
        short[pl.ds(b, ncol, stride=both_at), :] = both * zvec[b] - second * mvec[b]
        short[pl.ds(nblk + b, ncol, stride=both_at), :] = (
            rvec[b] - both * wvec[b] + second * nvec[b]
        )
    for c in range(ncol):
        tall[pl.ds(c, bdof, stride=ncol), :] = short[c * both_at : (c + 1) * both_at, :].T
    lanes_at = 128
    for j in range(sol.shape[1] // lanes_at):
        here = slice(j * lanes_at, (j + 1) * lanes_at)
        flat = tall[here, :].T
        sol[:, here] = flat[:nblk]
        res[:, here] = flat[nblk:]


def call(kernel, outs, scratch, args, space=pltpu.VMEM):
    vmem = pl.BlockSpec(memory_space=pltpu.VMEM)
    if space != pltpu.VMEM:
        args = [pltpu.with_memory_space_constraint(arg, space) for arg in args]
    return pl.pallas_call(
        kernel,
        out_shape=outs,
        in_specs=[pl.BlockSpec(memory_space=space)] * len(args),
        out_specs=jax.tree.map(lambda _: vmem, outs),
        scratch_shapes=scratch,
        compiler_params=pltpu.CompilerParams(vmem_limit_bytes=VMEM_LIMIT),
    )(*args)


def everywhere(values):
    total = lax.axis_size("dam") * lax.axis_size("sec")
    copies = jnp.broadcast_to(values[None], (total,) + values.shape)
    return lax.all_to_all(copies, ("dam", "sec"), split_axis=0, concat_axis=0)


def exchange(sends, axis):
    size = lax.axis_size(axis)
    got = []
    for first, send in zip((1, 0), sends):
        pairs = [(i, i + 1) for i in range(first, size - 1, 2)]
        got.append(lax.ppermute(send, axis, pairs + [(j, i) for i, j in pairs]))
    return got


def shards(
    segment_load,
    segment_mask,
    stiffness,
    block_cols,
    capillary,
    dirichlet_blocks,
    face_map,
    face_weight,
    corner_map,
    coarse_inverse,
):
    nblk, bdof = capillary.shape[2:]
    ncol = segment_load.shape[-1] // bdof
    nface = face_map.shape[3]
    ncorner = corner_map.shape[2]
    size = nblk * bdof
    pair = lax.axis_size("sec") == 2
    cols = jnp.transpose(block_cols[0], (2, 0, 1))
    tang, weights = capillary[0, 0], face_weight[0, 0]
    blocks, rows = dirichlet_blocks[0, 0], coarse_inverse[0]

    def shape(*dims, dtype=F32):
        return jax.ShapeDtypeStruct(dims, dtype)

    def like(array):
        return shape(*array.shape, dtype=array.dtype)

    def index(array):
        return pltpu.SMEM(array.shape, array.dtype)

    def sems(count):
        return pltpu.SemaphoreType.DMA((count,))

    field = shape(nblk, ncol, bdof)
    face = shape(ncol, nface * bdof)
    group = ncorner * bdof
    tiles = shape(size // group, group, group, dtype=BF16)
    halved = pltpu.VMEM((size // group, 2 * ncol, group), BF16)
    lane = group + nface * bdof if pair else group
    marked = ncol + 8 if pair else ncol
    faces_met = 3 if pair else 4

    load, mask = segment_load[0, 0], segment_mask[0, 0]
    copied = (corner_map, face_map, rows, cols, weights, tang)
    rvec, base, payload, high, low, cmap, fmap, rows, cols, weights, tang = call(
        functools.partial(start_kernel, pair),
        (field, field, shape(marked, lane), tiles, tiles)
        + tuple(like(a) for a in copied),
        [
            pltpu.VMEM(load.shape, load.dtype),
            pltpu.VMEM(mask.shape, mask.dtype),
            pltpu.VMEM(blocks.shape, blocks.dtype),
            index(corner_map),
            index(face_map),
            pltpu.VMEM((bdof * ncol, nblk), F32),
            pltpu.VMEM((ncol * nblk, bdof), F32),
            halved,
            sems(11),
        ],
        (load, mask, corner_map, face_map, blocks) + copied[2:],
        pltpu.HBM,
    )
    maps = [index(cmap), index(fmap)]

    def finish(base, shares, marks):
        vec, *faces = call(
            functools.partial(end_kernel, pair),
            (field,) + (face,) * faces_met,
            maps + [sems(2)],
            (cmap, fmap, base, rows, shares, marks),
        )
        besides = exchange(faces[:2], "dam")
        besides += faces[2:] if pair else exchange(faces[2:], "sec")
        return vec, besides

    def local(vec):
        return call(
            local_kernel,
            field,
            [pltpu.VMEM((nblk, 2 * ncol, bdof), BF16), index(cols), index(fmap), sems(2)],
            (cols, fmap, weights, tang, vec, stiffness[0, 0]),
        )

    marks = lax.all_gather(payload, "sec")
    zvec, besides = finish(base, marks, marks)
    wvec, sums, base, payload = call(
        functools.partial(image_kernel, pair),
        (field, shape(2, ncol, bdof), field, shape(ncol, lane)),
        maps + [halved, sems(2)],
        (cmap, fmap, weights, local(zvec), rvec, zvec, high, low, rows, *besides),
    )
    mvec, besides = finish(base, lax.all_gather(payload, "sec"), marks)
    nvec, totals = call(
        last_kernel,
        (field, shape(1, 4 * ncol)),
        [index(fmap), sems(1)],
        (fmap, weights, local(mvec), wvec, mvec, sums, *besides),
    )
    sol, res = call(
        finish_kernel,
        (shape(nblk, bdof * ncol),) * 2,
        [pltpu.VMEM((ncol * 2 * nblk, bdof), F32), pltpu.VMEM((bdof * ncol, 2 * nblk), F32)],
        (everywhere(totals[0]), rvec, zvec, wvec, mvec, nvec),
    )
    return sol[None, None], res[None, None]


def solution(mesh):
    placed = (
        P("dam", "sec", None, None),
        P("dam", "sec", None, None),
        P("dam", "sec", None, None, None),
        P("dam", "sec", None, None),
        P("dam", "sec", None, None),
        P("dam", "sec", None, None, None),
        P("dam", "sec", None, None),
        P("dam", "sec", None, None),
        P("dam", "sec", None),
        P("dam", "sec", None),
    )
    return jax.shard_map(
        shards,
        mesh=mesh,
        in_specs=placed,
        out_specs=(P("dam", "sec", None, None), P("dam", "sec", None, None)),
        check_vma=False,
    )
```

time: 51.6 us -> 41.3 us (0.80)
  blocking collectives: 24.6 us -> 16.8 us
  local copies, waits for them, and re-layouts: 6.86 us -> 0.01 us
  starting transfers between devices: 8.5 us -> 11.5 us
  waiting for transfers between devices: 0.03 us -> 0.91 us
  Pallas kernels: 10.3 us -> 11.1 us
    unnamed x32 -> x2, local copies, waits for them, and re-layouts: 6.85 us -> 0.01 us
    all_to_all x1, blocking collectives: 18.8 us -> 13 us  [everywhere(): return lax.all_to_all(copies, ('dam', 'sec'), split_axis=0, concat_axis=0)]
    ppermute x4, starting transfers between devices: 8.5 us -> 11.5 us  [exchange(): got.append(lax.ppermute(send, axis, pairs + [(j, i) for i, j in pairs]))]
    all_gather x1 -> x0, blocking collectives: 1.81 us -> none  [everywhere(): values = lax.all_gather(values, 'sec')[:, :1].sum(axis=0)]
    ppermute x4, waiting for transfers between devices: 0.03 us -> 0.91 us  [exchange(): got.append(lax.ppermute(send, axis, pairs + [(j, i) for i, j in pairs]))]
    pallas_call x8, Pallas kernels: 10.3 us -> 11.1 us  [call(): pl.pallas_call(kernel, out_shape=outs, in_specs=[pl.BlockSpec(memory_spac...]
  transfers between devices with their start and end apart: 4 -> 4, of which waited for: 0 -> 2; matrix products, arithmetic and copies ran while one was open for 0% -> 0% of each run, Pallas kernels for 5% -> 8%
where the time goes in v5:
time: 41.3 us; the launch traced here: 41.1 us
  blocking collectives  16.8 us (41%)
  starting transfers between devices  11.5 us (28%)
  Pallas kernels  11.1 us (27%)
  waiting for transfers between devices  0.91 us (2%)
  between operations  0.74 us (2%)
    all_to_all x1, blocking collectives, everywhere(): return lax.all_to_all(copies, ('dam', 'sec'), split_axis=0, concat_axis=0)  13 us
    ppermute x4, starting transfers between devices, exchange(): got.append(lax.ppermute(send, axis, pairs + [(j, i) for i, j in pairs]))  11.5 us
    pallas_call x8, Pallas kernels, call(): pl.pallas_call(kernel, out_shape=outs, in_specs=[pl.BlockSpec(memory_spac...  11.1 us
    all_gather x1, blocking collectives, shards(): marks = lax.all_gather(payload, 'sec')  2.01 us
    all_gather x1, blocking collectives, shards(): mvec, besides = finish(base, lax.all_gather(payload, 'sec'), marks)  1.88 us
    ppermute x4, waiting for transfers between devices, exchange(): got.append(lax.ppermute(send, axis, pairs + [(j, i) for i, j in pairs]))  0.91 us
  transfers between devices with their start and end apart: 4, of which 2 were waited for; matrix products, arithmetic and copies ran while one was open for 0% of the time, Pallas kernels for 8%

profile of v5, /device:TPU:0, one launch (start us, length us, event | category | flops | bytes accessed | tf_op | source)
XLA Modules:
  0.0 41.1 jit_solution(1974458059584024152)
XLA Ops:
  0.6 0.0 copy-start
  0.6 2.6 %shard_map.113 = (f32[16,16,64]{2,1,0:T(8,128)S(1)}, f32[16,16,64]{2,1,0:T(8,128)S(1)}, f32[24,768]{1,0:T(8,128)S(1)}, bf16[4,256,256]{2,1,0:T(8,128)(2,1)S(1)},...) custom-call(f32[16,1024]{1,0:T(8,128)} %bitcast.26, ...), custom_call_target="tpu_custom_call" | custom-call | tf_op jit(solution)/shard_map/pallas_call | solution.py:335
  3.3 2.0 %all-gather = f32[48,768]{1,0:T(8,128)S(1)} all-gather(f32[24,768]{1,0:T(8,128)S(1)} %get-tuple-element.36), channel_id=2, replica_groups=mesh['dam'=16,'sec'=2] {'sec'}, dimensions={0}, use_global_device_ids=true | all-gather | bytes 221184 | tf_op jit(solution)/shard_map/all_gather | solution.py:444
  5.3 0.7 %shard_map.114 = (f32[16,16,64]{2,1,0:T(8,128)S(1)}, f32[16,512]{1,0:T(8,128)S(1)}, f32[16,512]{1,0:T(8,128)S(1)}, f32[16,512]{1,0:T(8,128)S(1)}) custom-call(s32[1,1,4]{2,1,0:T(1,128)S(1)} %get-tuple-element.33.cmap_in, s32[1,1,4,8]{3,2,1,0:T(4,128)S(1)} %get-tuple-element.29.fmap_in, f32[16,16,64]{2,1,0:T(8,128)S(1)} %get-tuple-element.34.base, ...), custom_call_target="tpu_custom_call" | custom-call | tf_op jit(solution)/shard_map/pallas_call | solution.py:335
  6.0 0.7 %collective-permute-start = (f32[16,512]{1,0:T(8,128)S(1)}, f32[16,512]{1,0:T(8,128)S(1)}, u32[]{:S(2)}, u32[]{:S(2)}) collective-permute-start(f32[16,512]{1,0:T(8,128)S(1)} %get-tuple-element.41), channel_id=1, source_target_pairs={{2,4},{6,8},{10,12},{14,16},{18,20},{22,24},{26,28},{4,2},{8,6},{1... | collective-permute-start | bytes 98312 | tf_op jit(solution)/shard_map/ppermute | solution.py:356
  6.7 5.6 %collective-permute-start.1 = (f32[16,512]{1,0:T(8,128)S(1)}, f32[16,512]{1,0:T(8,128)S(1)}, u32[]{:S(2)}, u32[]{:S(2)}) collective-permute-start(f32[16,512]{1,0:T(8,128)S(1)} %get-tuple-element.42), channel_id=1, source_target_pairs={{0,2},{4,6},{8,10},{12,14},{16,18},{20,22},{24,26},{28,30},{2,0},{... | collective-permute-start | bytes 98312 | tf_op jit(solution)/shard_map/ppermute | solution.py:356
  12.3 0.0 copy-done
  12.3 1.7 %shard_map.115.local = f32[16,16,64]{2,1,0:T(8,128)S(1)} custom-call(s32[7,1,16]{2,1,0:T(1,128)S(1)} %get-tuple-element.31.cols_in, s32[1,1,4,8]{3,2,1,0:T(4,128)S(1)} %get-tuple-element.29.fmap_in, f32[4,512]{1,0:T(4,128)S(1)} %get-tuple-element.30.weights, f32[16,64]{1,0:T(8,128)S(1)} %get-tuple-element.32.capillary, ...), custom_call_target="tpu_custom_call" | custom-call | tf_op jit(solution)/shard_map/pallas_call | solution.py:335
  14.0 0.0 collective-permute-done.rest_0_
  14.0 0.5 %collective-permute-done.1.rest_1_ = f32[16,512]{1,0:T(8,128)S(1)} collective-permute-done((f32[16,512]{1,0:T(8,128)S(1)}, f32[16,512]{1,0:T(8,128)S(1)}, u32[]{:S(2)}, u32[]{:S(2)}) %collective-permute-start.1) | collective-permute-done | bytes 32800 | tf_op jit(solution)/shard_map/ppermute | solution.py:356
  14.5 1.5 %shard_map.116 = (f32[16,16,64]{2,1,0:T(8,128)S(1)}, f32[2,16,64]{2,1,0:T(8,128)S(1)}, f32[16,16,64]{2,1,0:T(8,128)S(1)}, f32[16,768]{1,0:T(8,128)S(1)}) custom-call(s32[1,1,4]{2,1,0:T(1,128)S(1)} %get-tuple-element.33.cmap_in, s32[1,1,4,8]{3,2,1,0:T(4,128)S(1)} %get-tuple-element.29.fmap_in, f32[4,512]{1,0:T(4,128)S(1)} %get-tuple-element.30.weights, ...), custom_call_target="tpu_custom_call" | custom-call | tf_op jit(solution)/shard_map/pallas_call | solution.py:335
  16.0 1.9 %all-gather.1 = f32[32,768]{1,0:T(8,128)S(1)} all-gather(f32[16,768]{1,0:T(8,128)S(1)} %get-tuple-element.45), channel_id=3, replica_groups=mesh['dam'=16,'sec'=2] {'sec'}, dimensions={0}, use_global_device_ids=true | all-gather | bytes 147456 | tf_op jit(solution)/shard_map/all_gather | solution.py:452
  17.8 0.7 %shard_map.117 = (f32[16,16,64]{2,1,0:T(8,128)S(1)}, f32[16,512]{1,0:T(8,128)S(1)}, f32[16,512]{1,0:T(8,128)S(1)}, f32[16,512]{1,0:T(8,128)S(1)}) custom-call(s32[1,1,4]{2,1,0:T(1,128)S(1)} %get-tuple-element.33.cmap_in, s32[1,1,4,8]{3,2,1,0:T(4,128)S(1)} %get-tuple-element.29.fmap_in, f32[16,16,64]{2,1,0:T(8,128)S(1)} %get-tuple-element.44.base, ...), custom_call_target="tpu_custom_call" | custom-call | tf_op jit(solution)/shard_map/pallas_call | solution.py:335
  18.6 0.7 %collective-permute-start.2 = (f32[16,512]{1,0:T(8,128)S(1)}, f32[16,512]{1,0:T(8,128)S(1)}, u32[]{:S(2)}, u32[]{:S(2)}) collective-permute-start(f32[16,512]{1,0:T(8,128)S(1)} %get-tuple-element.49), channel_id=1, source_target_pairs={{2,4},{6,8},{10,12},{14,16},{18,20},{22,24},{26,28},{4,2},{8,6},{1... | collective-permute-start | bytes 98312 | tf_op jit(solution)/shard_map/ppermute | solution.py:356
  19.3 4.5 %collective-permute-start.3 = (f32[16,512]{1,0:T(8,128)S(1)}, f32[16,512]{1,0:T(8,128)S(1)}, u32[]{:S(2)}, u32[]{:S(2)}) collective-permute-start(f32[16,512]{1,0:T(8,128)S(1)} %get-tuple-element.50), channel_id=1, source_target_pairs={{0,2},{4,6},{8,10},{12,14},{16,18},{20,22},{24,26},{28,30},{2,0},{... | collective-permute-start | bytes 98312 | tf_op jit(solution)/shard_map/ppermute | solution.py:356
  23.8 1.7 %shard_map.118.local = f32[16,16,64]{2,1,0:T(8,128)S(1)} custom-call(s32[7,1,16]{2,1,0:T(1,128)S(1)} %get-tuple-element.31.cols_in, s32[1,1,4,8]{3,2,1,0:T(4,128)S(1)} %get-tuple-element.29.fmap_in, f32[4,512]{1,0:T(4,128)S(1)} %get-tuple-element.30.weights, f32[16,64]{1,0:T(8,128)S(1)} %get-tuple-element.32.capillary, ...), custom_call_target="tpu_custom_call" | custom-call | tf_op jit(solution)/shard_map/pallas_call | solution.py:335
  25.5 0.0 collective-permute-done.2.rest_0_
  25.5 0.5 %collective-permute-done.3.rest_1_ = f32[16,512]{1,0:T(8,128)S(1)} collective-permute-done((f32[16,512]{1,0:T(8,128)S(1)}, f32[16,512]{1,0:T(8,128)S(1)}, u32[]{:S(2)}, u32[]{:S(2)}) %collective-permute-start.3) | collective-permute-done | bytes 32800 | tf_op jit(solution)/shard_map/ppermute | solution.py:356
  25.9 0.9 %shard_map.119 = (f32[16,16,64]{2,1,0:T(8,128)S(1)}, f32[1,64]{1,0:T(1,128)S(1)}) custom-call(s32[1,1,4,8]{3,2,1,0:T(4,128)S(1)} %get-tuple-element.29.fmap_in, f32[4,512]{1,0:T(4,128)S(1)} %get-tuple-element.30.weights, f32[16,16,64]{2,1,0:T(8,128)S(1)} %shard_map.118.local, f32[16,16,64]{2,1,0:T(8,128)S(1)} %get-tuple-element.47.wvec, ...), custom_call_target="tpu_custom_call" | custom-call | tf_op jit(solution)/shard_map/pallas_call | solution.py:335
  26.8 13.0 %all_to_all.8 = f32[32,1,64]{2,1,0:T(1,128)S(1)} all-to-all(f32[32,1,64]{2,1,0:T(1,128)S(1)} %broadcast_in_dim.11), channel_id=1, replica_groups=mesh['dam'=16,'sec'=2] {'dam','sec'}, dimensions={0} | all-to-all | bytes 16384 | tf_op jit(solution)/shard_map/all_to_all | solution.py:348
  39.8 1.3 %shard_map.120 = (f32[16,1024]{1,0:T(8,128)}, f32[16,1024]{1,0:T(8,128)}) custom-call(f32[32,64]{1,0:T(8,128)S(1)} %bitcast.22, f32[16,16,64]{2,1,0:T(8,128)S(1)} %get-tuple-element.38.rvec, f32[16,16,64]{2,1,0:T(8,128)S(1)} %get-tuple-element.37.field.zvec, f32[16,16,64]{2,1,0:T(8,128)S(1)} %get-tuple-element.47.wvec, ...), custom_call_target="tpu_custom_call" | custom-call | tf_op jit(solution)/shard_map/pallas_call | solution.py:335
  (1 shorter events, 0.0 us)
Async XLA Ops:
  0.6 11.7 %copy-start = (f32[1,1,16,64,448]{4,3,2,1,0:T(8,128)S(1)}, f32[1,1,16,64,448]{4,3,2,1,0:T(8,128)}, u32[]{:S(2)}) copy-start(f32[1,1,16,64,448]{4,3,2,1,0:T(8,128)} %param.12) | copy-start | bytes 5505028
  6.0 8.0 %collective-permute-start = (f32[16,512]{1,0:T(8,128)S(1)}, f32[16,512]{1,0:T(8,128)S(1)}, u32[]{:S(2)}, u32[]{:S(2)}) collective-permute-start(f32[16,512]{1,0:T(8,128)S(1)} %get-tuple-element.41), channel_id=1, source_target_pairs={{2,4},{6,8},{10,12},{14,16},{18,20},{22,24},{26,28},{4,2},{8,6},{1... | collective-permute-start | bytes 98312 | tf_op jit(solution)/shard_map/ppermute | solution.py:356
  6.7 7.8 %collective-permute-start.1 = (f32[16,512]{1,0:T(8,128)S(1)}, f32[16,512]{1,0:T(8,128)S(1)}, u32[]{:S(2)}, u32[]{:S(2)}) collective-permute-start(f32[16,512]{1,0:T(8,128)S(1)} %get-tuple-element.42), channel_id=1, source_target_pairs={{0,2},{4,6},{8,10},{12,14},{16,18},{20,22},{24,26},{28,30},{2,0},{... | collective-permute-start | bytes 98312 | tf_op jit(solution)/shard_map/ppermute | solution.py:356
  18.6 6.9 %collective-permute-start.2 = (f32[16,512]{1,0:T(8,128)S(1)}, f32[16,512]{1,0:T(8,128)S(1)}, u32[]{:S(2)}, u32[]{:S(2)}) collective-permute-start(f32[16,512]{1,0:T(8,128)S(1)} %get-tuple-element.49), channel_id=1, source_target_pairs={{2,4},{6,8},{10,12},{14,16},{18,20},{22,24},{26,28},{4,2},{8,6},{1... | collective-permute-start | bytes 98312 | tf_op jit(solution)/shard_map/ppermute | solution.py:356
  19.3 6.7 %collective-permute-start.3 = (f32[16,512]{1,0:T(8,128)S(1)}, f32[16,512]{1,0:T(8,128)S(1)}, u32[]{:S(2)}, u32[]{:S(2)}) collective-permute-start(f32[16,512]{1,0:T(8,128)S(1)} %get-tuple-element.50), channel_id=1, source_target_pairs={{0,2},{4,6},{8,10},{12,14},{16,18},{20,22},{24,26},{28,30},{2,0},{... | collective-permute-start | bytes 98312 | tf_op jit(solution)/shard_map/ppermute | solution.py:356

commit v6 on v5

v6 whole, which is shorter than its diff:
```python
import functools

import jax
import jax.numpy as jnp
from jax import lax
from jax.experimental import pallas as pl
from jax.experimental.pallas import tpu as pltpu
from jax.sharding import PartitionSpec as P

F32 = jnp.float32
BF16 = jnp.bfloat16
VMEM_LIMIT = 16 * 1024 * 1024
LANES = 128


def halves(x):
    high = x.astype(BF16)
    return high, (x - high.astype(F32)).astype(BF16)


def stack(x):
    return jnp.concatenate(halves(x), axis=0)


def dot_t(a, b):
    return lax.dot_general(a, b, (((1,), (1,)), ((), ())), preferred_element_type=F32)


def dot(a, b):
    return lax.dot_general(a, b, (((1,), (0,)), ((), ())), preferred_element_type=F32)


def three_pass(mul, left, high, low):
    rows = left.shape[0] // 2
    first = mul(left, high)
    return first[:rows] + first[rows:] + mul(left[:rows], low)


def fetch(pairs, sems):
    copies = [
        pltpu.make_async_copy(source, target, sems.at[i])
        for i, (source, target) in enumerate(pairs)
    ]
    for copy in copies:
        copy.start()
    return [copy.wait for copy in copies]


def face_order(pair):
    near = 1 - lax.axis_index("dam") % 2
    across = 3 - lax.axis_index("sec") % 2
    return [1 - near, near] + ([across, 5 - across] if pair else [5 - across, across])


def listed(index):
    value = index[...]
    return [[value[i, j] for j in range(value.shape[1])] for i in range(value.shape[0])]


def pack(field, where, out, at=0):
    ncol, bdof = field.shape[1:]
    for p, b in enumerate(where):
        out[:ncol, at + p * bdof : at + (p + 1) * bdof] = field[b]


def add_pieces(field, where, piece):
    new = [field[b] + piece(p, b) for p, b in enumerate(where)]
    for b, value in zip(where, new):
        field[b] = value


def lane_piece(x, p, bdof):
    return x[:, p * bdof : (p + 1) * bdof]


def split_blocks(blocks, tiles_high, tiles_low):
    nblk, bdof = blocks.shape[:2]
    group = tiles_high.shape[1] // bdof
    for b in range(nblk):
        t, j = divmod(b, group)
        here = slice(j * bdof, (j + 1) * bdof)
        tiles_high[t, here, here], tiles_low[t, here, here] = halves(blocks[b])


def apply_blocks(field, tiles_high, tiles_low, left, base):
    nblk, ncol, bdof = field.shape
    group = tiles_high.shape[1] // bdof
    for b in range(nblk):
        t, j = divmod(b, group)
        here = slice(j * bdof, (j + 1) * bdof)
        left[t, :ncol, here], left[t, ncol:, here] = halves(field[b])
    for t in range(nblk // group):
        out = three_pass(dot, left[t], tiles_high[t], tiles_low[t])
        for j in range(group):
            base[t * group + j] = lane_piece(out, j, bdof)


def offer(pair, corners, across, field, rows, base, payload):
    bdof = field.shape[2]
    if not pair:
        pack(field, corners, payload)
        return
    wide = len(corners) * bdof
    at = payload.shape[1] - wide
    me = lax.axis_index("sec")
    own = stack(jnp.concatenate([field[b] for b in corners], axis=1))
    mine = pl.multiple_of(me * wide, wide)
    other = pl.multiple_of((1 - me) * wide, wide)
    correct = three_pass(dot_t, own, *halves(rows[:, pl.ds(mine, wide)]))
    payload[: field.shape[1], at:] = three_pass(dot, own, *halves(rows[:, pl.ds(other, wide)]))
    add_pieces(base, corners, lambda n, b: lane_piece(correct, n, bdof))
    pack(base, across, payload)


def end_kernel(pair, cmap, met, base, rows, shares, marks, zout, *faces):
    nblk, ncol, bdof = base.shape
    (corners,) = listed(cmap)
    where = listed(met)
    wide = len(corners) * bdof
    zout[...] = base[...]
    if pair:
        me = lax.axis_index("sec")
        at = len(where[0]) * bdof
        correct = shares[pl.ds(1 - me, 1), :ncol, at:][0]
        theirs = shares[pl.ds(me, 1), :ncol, at:][0]
        chunk = 2 * bdof
        twice = [
            jnp.concatenate([lane_piece(theirs, n, bdof)] * 2, axis=1)
            for n in range(len(corners))
        ]
        for j in range(at // chunk):
            here = slice(j * chunk, (j + 1) * chunk)
            value = shares[pl.ds(1 - me, 1), :ncol, here][0]
            for n in range(len(corners)):
                mark = marks[pl.ds(1 - me, 1), ncol + n : ncol + n + 1, here][0]
                value = value + mark * twice[n]
            faces[-1][:, here] = value
    else:
        correct = 0.0
        for s in range(shares.shape[0]):
            high, low = halves(rows[:, s * wide : (s + 1) * wide])
            correct = correct + three_pass(dot_t, stack(shares[s]), high, low)
    add_pieces(zout, corners, lambda n, b: lane_piece(correct, n, bdof))
    for blocks, out in zip(where, faces[: 2 if pair else 4]):
        pack(zout, blocks, out)


def start_kernel(pair, *refs):
    load_in, mask_in, cmap_in, fmap_in, blocks_in, rows_in, cols_in, weights_in, tang_in = refs[:9]
    rvec, base, payload, tiles_high, tiles_low, cmap_out, met, wmet, rows, cols, tang = refs[9:20]
    load, mask, blocks, cmap, cmap_row, fmap, fmap_rows, weights, tall, short, left, sems = refs[20:]
    waits = fetch(
        [
            (load_in, load),
            (mask_in, mask),
            (cmap_in, cmap),
            (fmap_in, fmap),
            (blocks_in, blocks),
            (rows_in, rows),
            (cmap_in, cmap_row),
            (fmap_in, fmap_rows),
            (weights_in, weights),
            (cols_in, cols),
            (tang_in, tang),
        ],
        sems,
    )
    nblk, ncol, bdof = rvec.shape
    order = face_order(pair)
    tiles_high[...] = jnp.zeros_like(tiles_high)
    tiles_low[...] = jnp.zeros_like(tiles_low)
    waits[2]()
    waits[3]()
    corners = [cmap[0, 0, n] for n in range(cmap.shape[2])]
    across = [fmap[0, 0, order[2], p] for p in range(fmap.shape[3])]
    if pair:
        payload[ncol:, :] = jnp.zeros_like(payload[ncol:, :])
        for n, corner in enumerate(corners):
            for p, b in enumerate(across):
                payload[ncol + n : ncol + n + 1, p * bdof : (p + 1) * bdof] = jnp.full(
                    (1, bdof), jnp.where(corner == b, 1.0, 0.0), F32
                )
    waits[0]()
    waits[1]()
    scale = mask[...].astype(F32)
    scale = jnp.concatenate([scale] * (LANES // ncol), axis=1)
    for j in range(load.shape[1] // LANES):
        here = slice(j * LANES, (j + 1) * LANES)
        tall[here, :] = (load[:, here] * scale).T
    for c in range(ncol):
        short[c * nblk : (c + 1) * nblk, :] = tall[pl.ds(c, bdof, stride=ncol), :].T
    for b in range(nblk):
        rvec[b] = short[pl.ds(b, ncol, stride=nblk), :]
    waits[4]()
    split_blocks(blocks, tiles_high, tiles_low)
    apply_blocks(rvec, tiles_high, tiles_low, left, base)
    for wait in waits[5:]:
        wait()
    offer(pair, corners, across, rvec, rows, base, payload)
    cmap_out[...] = cmap_row[0]
    for i, face in enumerate(order):
        met[i : i + 1, :] = fmap_rows[0, 0, pl.ds(face, 1), :]
        wmet[i : i + 1, :] = weights[pl.ds(face, 1), :]


def flatten(block, nblk, ncol, bdof, short, tall, out):
    for b in range(nblk):
        short[pl.ds(b, ncol, stride=nblk), :] = block(b)
    for c in range(ncol):
        tall[pl.ds(c, bdof, stride=ncol), :] = short[c * nblk : (c + 1) * nblk, :].T
    for j in range(out.shape[1] // LANES):
        here = slice(j * LANES, (j + 1) * LANES)
        out[:, here] = tall[here, :].T


def local_kernel(cols_in, met, weights, capillary, field, stiff, out, flat, *scratch):
    left, short, tall, cols, sems = scratch
    nblk, ncol, bdof = field.shape
    (wait,) = fetch([(cols_in, cols)], sems)
    where = listed(met)
    flatten(lambda b: field[b], nblk, ncol, bdof, short, tall, flat)
    kept = stiff.shape[2] // bdof
    for b in range(nblk):
        left[b] = stack(field[b])
    wait()
    group = 4
    for t in range(0, nblk, group):
        gathered = [
            jnp.concatenate([left[cols[k, 0, t + j]] for k in range(kept)], axis=1)
            for j in range(group)
        ]
        firsts = [g[:ncol] for g in gathered]
        seconds = [g[ncol:] for g in gathered]
        rows = stiff[t : t + group].reshape(group * bdof, kept * bdof)
        prod = three_pass(dot_t, jnp.concatenate(firsts + seconds, axis=0), *halves(rows))
        for j in range(group):
            out[t + j] = (
                lane_piece(prod[j * ncol : (j + 1) * ncol], j, bdof)
                + capillary[t + j : t + j + 1, :] * field[t + j]
            )
    for i, blocks in enumerate(where):
        row = weights[i : i + 1, :]
        add_pieces(out, blocks, lambda p, b: lane_piece(row, p, bdof) * field[b])


def couple(met, weights, local, besides, out):
    bdof = local.shape[2]
    where = listed(met)
    out[...] = local[...]
    for i, beside in enumerate(besides):
        term = weights[i : i + 1, :] * beside[...]
        add_pieces(out, where[i], lambda p, b: -lane_piece(term, p, bdof))
    return where


def lanes(first, second):
    return jnp.sum(first[...] * second[...], axis=0)


def image_kernel(
    pair, cmap, met, weights, local, rvec, zvec, tiles_high, tiles_low, rows, *rest
):
    count = 3 if pair else 4
    besides, (wout, sums, base, payload, left) = rest[:count], rest[count:]
    (corners,) = listed(cmap)
    where = couple(met, weights, local, besides, wout)
    apply_blocks(wout, tiles_high, tiles_low, left, base)
    offer(pair, corners, where[2], wout, rows, base, payload)
    sums[0] = lanes(rvec, zvec)
    sums[1] = lanes(zvec, wout)


def last_kernel(met, weights, local, wvec, mvec, sums, *rest):
    *besides, nout, totals = rest
    couple(met, weights, local, besides, nout)
    parts = jnp.concatenate(
        [sums[0], sums[1], lanes(wvec, mvec), lanes(mvec, nout)], axis=0
    )
    totals[...] = lax.dot_general(
        jnp.ones((1, parts.shape[1]), F32),
        parts,
        (((1,), (1,)), ((), ())),
        precision=lax.Precision.HIGHEST,
        preferred_element_type=F32,
    )


def finish_kernel(shares, rvec, wvec, nvec, zflat, mflat, sol, res, short, tall):
    nblk, ncol, bdof = rvec.shape
    total = jnp.sum(shares[...], axis=0, keepdims=True)
    gamma, delta, mu, nu = [total[:, q * ncol : (q + 1) * ncol] for q in range(4)]
    alpha = gamma / delta
    gnew = gamma - 2.0 * alpha * delta + alpha * alpha * mu
    grow = 1.0 + gnew / gamma
    dnew = grow * grow * delta - 2.0 * alpha * grow * mu + alpha * alpha * nu
    anew = gnew / dnew
    both = alpha + anew * grow
    second = anew * alpha
    eye = lax.broadcasted_iota(jnp.int32, (ncol, ncol), 0) == lax.broadcasted_iota(
        jnp.int32, (ncol, ncol), 1
    )
    down = [
        jnp.sum(jnp.where(eye, x, 0.0), axis=1, keepdims=True) for x in (both, second)
    ]
    flatten(
        lambda b: rvec[b] - down[0] * wvec[b] + down[1] * nvec[b],
        nblk,
        ncol,
        bdof,
        short,
        tall,
        res,
    )
    along = [jnp.concatenate([x] * (LANES // ncol), axis=1) for x in (both, second)]
    for j in range(sol.shape[1] // LANES):
        here = slice(j * LANES, (j + 1) * LANES)
        sol[:, here] = along[0] * zflat[:, here] - along[1] * mflat[:, here]


def call(kernel, outs, scratch, args, space=pltpu.VMEM):
    vmem = pl.BlockSpec(memory_space=pltpu.VMEM)
    if space != pltpu.VMEM:
        args = [pltpu.with_memory_space_constraint(arg, space) for arg in args]
    return pl.pallas_call(
        kernel,
        out_shape=outs,
        in_specs=[pl.BlockSpec(memory_space=space)] * len(args),
        out_specs=jax.tree.map(lambda _: vmem, outs),
        scratch_shapes=scratch,
        compiler_params=pltpu.CompilerParams(vmem_limit_bytes=VMEM_LIMIT),
    )(*args)


def everywhere(values):
    total = lax.axis_size("dam") * lax.axis_size("sec")
    copies = jnp.broadcast_to(values[None], (total,) + values.shape)
    return lax.all_to_all(copies, ("dam", "sec"), split_axis=0, concat_axis=0)


def exchange(sends, axis):
    size = lax.axis_size(axis)
    got = []
    for first, send in zip((1, 0), sends):
        pairs = [(i, i + 1) for i in range(first, size - 1, 2)]
        got.append(lax.ppermute(send, axis, pairs + [(j, i) for i, j in pairs]))
    return got


def shards(
    segment_load,
    segment_mask,
    stiffness,
    block_cols,
    capillary,
    dirichlet_blocks,
    face_map,
    face_weight,
    corner_map,
    coarse_inverse,
):
    nblk, bdof = capillary.shape[2:]
    ncol = segment_load.shape[-1] // bdof
    nface = face_map.shape[3]
    ncorner = corner_map.shape[2]
    size = nblk * bdof
    pair = lax.axis_size("sec") == 2
    load, mask = segment_load[0, 0], segment_mask[0, 0]
    cols = jnp.transpose(block_cols[0], (2, 0, 1))
    tang, weights = capillary[0, 0], face_weight[0, 0]
    blocks, rows = dirichlet_blocks[0, 0], coarse_inverse[0]

    def shape(*dims, dtype=F32):
        return jax.ShapeDtypeStruct(dims, dtype)

    def like(array):
        return shape(*array.shape, dtype=array.dtype)

    def hold(array):
        return pltpu.VMEM(array.shape, array.dtype)

    def index(array):
        return pltpu.SMEM(array.shape, array.dtype)

    def sems(count):
        return pltpu.SemaphoreType.DMA((count,))

    field = shape(nblk, ncol, bdof)
    flat = shape(nblk, bdof * ncol)
    face = shape(ncol, nface * bdof)
    group = ncorner * bdof
    tiles = shape(size // group, group, group, dtype=BF16)
    halved = pltpu.VMEM((size // group, 2 * ncol, group), BF16)
    relayout = [pltpu.VMEM((ncol * nblk, bdof), F32), pltpu.VMEM((bdof * ncol, nblk), F32)]
    lane = group + nface * bdof if pair else group
    marked = ncol + 8 if pair else ncol

    rvec, base, payload, high, low, cmap, met, weights, rows, cols, tang = call(
        functools.partial(start_kernel, pair),
        (field, field, shape(marked, lane), tiles, tiles)
        + (shape(1, ncorner, dtype=jnp.int32), shape(4, nface, dtype=jnp.int32))
        + tuple(like(a) for a in (weights, rows, cols, tang)),
        [
            hold(load),
            hold(mask),
            hold(blocks),
            index(corner_map),
            hold(corner_map),
            index(face_map),
            hold(face_map),
            hold(weights),
            relayout[1],
            relayout[0],
            halved,
            sems(11),
        ],
        (load, mask, corner_map, face_map, blocks, rows, cols, weights, tang),
        pltpu.HBM,
    )

    def finish(base, shares, marks):
        vec, *faces = call(
            functools.partial(end_kernel, pair),
            (field,) + (face,) * (3 if pair else 4),
            [],
            (cmap, met, base, rows, shares, marks),
        )
        besides = exchange(faces[:2], "dam")
        besides += faces[2:] if pair else exchange(faces[2:], "sec")
        return vec, besides

    def local(vec):
        return call(
            local_kernel,
            (field, flat),
            [pltpu.VMEM((nblk, 2 * ncol, bdof), BF16)] + relayout + [index(cols), sems(1)],
            (cols, met, weights, tang, vec, stiffness[0, 0]),
        )

    marks = lax.all_gather(payload, "sec")
    zvec, besides = finish(base, marks, marks)
    part, zflat = local(zvec)
    wvec, sums, base, payload = call(
        functools.partial(image_kernel, pair),
        (field, shape(2, ncol, bdof), field, shape(ncol, lane)),
        [halved],
        (cmap, met, weights, part, rvec, zvec, high, low, rows, *besides),
    )
    mvec, besides = finish(base, lax.all_gather(payload, "sec"), marks)
    part, mflat = local(mvec)
    nvec, totals = call(
        last_kernel,
        (field, shape(1, 4 * ncol)),
        [],
        (met, weights, part, wvec, mvec, sums, *besides),
    )
    sol, res = call(
        finish_kernel,
        (flat, flat),
        relayout,
        (everywhere(totals[0]), rvec, wvec, nvec, zflat, mflat),
    )
    return sol[None, None], res[None, None]


def solution(mesh):
    placed = (
        P("dam", "sec", None, None),
        P("dam", "sec", None, None),
        P("dam", "sec", None, None, None),
        P("dam", "sec", None, None),
        P("dam", "sec", None, None),
        P("dam", "sec", None, None, None),
        P("dam", "sec", None, None),
        P("dam", "sec", None, None),
        P("dam", "sec", None),
        P("dam", "sec", None),
    )
    return jax.shard_map(
        shards,
        mesh=mesh,
        in_specs=placed,
        out_specs=(P("dam", "sec", None, None), P("dam", "sec", None, None)),
        check_vma=False,
    )
```

time: 41.3 us -> 38.8 us (0.939)
  Pallas kernels: 11.1 us -> 8.42 us
    pallas_call x8, Pallas kernels: 11.1 us -> 8.42 us  [call(): pl.pallas_call(kernel, out_shape=outs, in_specs=[pl.BlockSpec(memory_spac...]
where the time goes in v6:
time: 38.8 us; the launch traced here: 38.6 us
  blocking collectives  16.8 us (43%)
  starting transfers between devices  11.5 us (30%)
  Pallas kernels  8.42 us (22%)
  waiting for transfers between devices  1.09 us (3%)
  between operations  0.71 us (2%)
    all_to_all x1, blocking collectives, everywhere(): return lax.all_to_all(copies, ('dam', 'sec'), split_axis=0, concat_axis=0)  13 us
    ppermute x4, starting transfers between devices, exchange(): got.append(lax.ppermute(send, axis, pairs + [(j, i) for i, j in pairs]))  11.5 us
    pallas_call x8, Pallas kernels, call(): pl.pallas_call(kernel, out_shape=outs, in_specs=[pl.BlockSpec(memory_spac...  8.42 us
    all_gather x1, blocking collectives, shards(): marks = lax.all_gather(payload, 'sec')  2.01 us
    all_gather x1, blocking collectives, shards(): mvec, besides = finish(base, lax.all_gather(payload, 'sec'), marks)  1.87 us
    ppermute x4, waiting for transfers between devices, exchange(): got.append(lax.ppermute(send, axis, pairs + [(j, i) for i, j in pairs]))  1.09 us
  transfers between devices with their start and end apart: 4, of which 2 were waited for; matrix products, arithmetic and copies ran while one was open for 0% of the time, Pallas kernels for 8%

profile of v6, /device:TPU:0, one launch (start us, length us, event | category | flops | bytes accessed | tf_op | source)
XLA Modules:
  0.0 38.6 jit_solution(5995834536569543206)
XLA Ops:
  0.6 0.0 copy-start
  0.6 2.5 %shard_map.113 = (f32[16,16,64]{2,1,0:T(8,128)S(1)}, f32[16,16,64]{2,1,0:T(8,128)S(1)}, f32[24,768]{1,0:T(8,128)S(1)}, bf16[4,256,256]{2,1,0:T(8,128)(2,1)S(1)},...) custom-call(f32[16,1024]{1,0:T(8,128)} %bitcast.26, ...), custom_call_target="tpu_custom_call" | custom-call | tf_op jit(solution)/shard_map/pallas_call | solution.py:324
  3.2 2.0 %all-gather = f32[48,768]{1,0:T(8,128)S(1)} all-gather(f32[24,768]{1,0:T(8,128)S(1)} %get-tuple-element.40), channel_id=2, replica_groups=mesh['dam'=16,'sec'=2] {'sec'}, dimensions={0}, use_global_device_ids=true | all-gather | bytes 221184 | tf_op jit(solution)/shard_map/all_gather | solution.py:439
  5.2 0.2 shard_map.114
  5.4 0.7 %collective-permute-start = (f32[16,512]{1,0:T(8,128)S(1)}, f32[16,512]{1,0:T(8,128)S(1)}, u32[]{:S(2)}, u32[]{:S(2)}) collective-permute-start(f32[16,512]{1,0:T(8,128)S(1)} %get-tuple-element.46), channel_id=1, source_target_pairs={{2,4},{6,8},{10,12},{14,16},{18,20},{22,24},{26,28},{4,2},{8,6},{1... | collective-permute-start | bytes 98312 | tf_op jit(solution)/shard_map/ppermute | solution.py:345
  6.1 5.6 %collective-permute-start.1 = (f32[16,512]{1,0:T(8,128)S(1)}, f32[16,512]{1,0:T(8,128)S(1)}, u32[]{:S(2)}, u32[]{:S(2)}) collective-permute-start(f32[16,512]{1,0:T(8,128)S(1)} %get-tuple-element.47), channel_id=1, source_target_pairs={{0,2},{4,6},{8,10},{12,14},{16,18},{20,22},{24,26},{28,30},{2,0},{... | collective-permute-start | bytes 98312 | tf_op jit(solution)/shard_map/ppermute | solution.py:345
  11.7 0.0 copy-done
  11.7 1.6 %shard_map.115 = (f32[16,16,64]{2,1,0:T(8,128)S(1)}, f32[16,1024]{1,0:T(8,128)S(1)}) custom-call(s32[7,1,16]{2,1,0:T(1,128)S(1)} %get-tuple-element.35.cols_in, s32[4,8]{1,0:T(4,128)S(1)} %get-tuple-element.33.met, f32[4,512]{1,0:T(4,128)S(1)} %get-tuple-element.34.weights, f32[16,64]{1,0:T(8,128)S(1)} %get-tuple-element.36.capillary, ...), custom_call_target="tpu_custom_call" | custom-call | tf_op jit(solution)/shard_map/pallas_call | solution.py:324
  13.3 0.0 collective-permute-done.rest_0_
  13.3 0.5 %collective-permute-done.1.rest_1_ = f32[16,512]{1,0:T(8,128)S(1)} collective-permute-done((f32[16,512]{1,0:T(8,128)S(1)}, f32[16,512]{1,0:T(8,128)S(1)}, u32[]{:S(2)}, u32[]{:S(2)}) %collective-permute-start.1) | collective-permute-done | bytes 32800 | tf_op jit(solution)/shard_map/ppermute | solution.py:345
  13.9 0.7 %shard_map.116 = (f32[16,16,64]{2,1,0:T(8,128)S(1)}, f32[2,16,64]{2,1,0:T(8,128)S(1)}, f32[16,16,64]{2,1,0:T(8,128)S(1)}, f32[16,768]{1,0:T(8,128)S(1)}) custom-call(s32[1,4]{1,0:T(1,128)S(1)} %get-tuple-element.37.cmap, s32[4,8]{1,0:T(4,128)S(1)} %get-tuple-element.33.met, f32[4,512]{1,0:T(4,128)S(1)} %get-tuple-element.34.weights, ...), custom_call_target="tpu_custom_call" | custom-call | tf_op jit(solution)/shard_map/pallas_call | solution.py:324
  14.6 1.9 %all-gather.1 = f32[32,768]{1,0:T(8,128)S(1)} all-gather(f32[16,768]{1,0:T(8,128)S(1)} %get-tuple-element.50), channel_id=3, replica_groups=mesh['dam'=16,'sec'=2] {'sec'}, dimensions={0}, use_global_device_ids=true | all-gather | bytes 147456 | tf_op jit(solution)/shard_map/all_gather | solution.py:448
  16.4 0.2 shard_map.117
  16.6 0.7 %collective-permute-start.2 = (f32[16,512]{1,0:T(8,128)S(1)}, f32[16,512]{1,0:T(8,128)S(1)}, u32[]{:S(2)}, u32[]{:S(2)}) collective-permute-start(f32[16,512]{1,0:T(8,128)S(1)} %get-tuple-element.55), channel_id=1, source_target_pairs={{2,4},{6,8},{10,12},{14,16},{18,20},{22,24},{26,28},{4,2},{8,6},{1... | collective-permute-start | bytes 98312 | tf_op jit(solution)/shard_map/ppermute | solution.py:345
  17.3 4.5 %collective-permute-start.3 = (f32[16,512]{1,0:T(8,128)S(1)}, f32[16,512]{1,0:T(8,128)S(1)}, u32[]{:S(2)}, u32[]{:S(2)}) collective-permute-start(f32[16,512]{1,0:T(8,128)S(1)} %get-tuple-element.56), channel_id=1, source_target_pairs={{0,2},{4,6},{8,10},{12,14},{16,18},{20,22},{24,26},{28,30},{2,0},{... | collective-permute-start | bytes 98312 | tf_op jit(solution)/shard_map/ppermute | solution.py:345
  21.8 1.6 %shard_map.118 = (f32[16,16,64]{2,1,0:T(8,128)S(1)}, f32[16,1024]{1,0:T(8,128)S(1)}) custom-call(s32[7,1,16]{2,1,0:T(1,128)S(1)} %get-tuple-element.35.cols_in, s32[4,8]{1,0:T(4,128)S(1)} %get-tuple-element.33.met, f32[4,512]{1,0:T(4,128)S(1)} %get-tuple-element.34.weights, f32[16,64]{1,0:T(8,128)S(1)} %get-tuple-element.36.capillary, ...), custom_call_target="tpu_custom_call" | custom-call | tf_op jit(solution)/shard_map/pallas_call | solution.py:324
  23.4 0.0 collective-permute-done.2.rest_0_
  23.4 0.5 %collective-permute-done.3.rest_1_ = f32[16,512]{1,0:T(8,128)S(1)} collective-permute-done((f32[16,512]{1,0:T(8,128)S(1)}, f32[16,512]{1,0:T(8,128)S(1)}, u32[]{:S(2)}, u32[]{:S(2)}) %collective-permute-start.3) | collective-permute-done | bytes 32800 | tf_op jit(solution)/shard_map/ppermute | solution.py:345
  24.0 0.3 shard_map.119
  24.3 13.0 %all_to_all.8 = f32[32,1,64]{2,1,0:T(1,128)S(1)} all-to-all(f32[32,1,64]{2,1,0:T(1,128)S(1)} %broadcast_in_dim.11), channel_id=1, replica_groups=mesh['dam'=16,'sec'=2] {'dam','sec'}, dimensions={0} | all-to-all | bytes 16384 | tf_op jit(solution)/shard_map/all_to_all | solution.py:337
  37.3 1.3 %shard_map.120 = (f32[16,1024]{1,0:T(8,128)}, f32[16,1024]{1,0:T(8,128)}) custom-call(f32[32,64]{1,0:T(8,128)S(1)} %bitcast.22, f32[16,16,64]{2,1,0:T(8,128)S(1)} %get-tuple-element.43.rvec, f32[16,16,64]{2,1,0:T(8,128)S(1)} %get-tuple-element.53.wvec, f32[16,16,64]{2,1,0:T(8,128)S(1)} %get-tuple-element.59.nvec, f32[16,1024]{1,0:T(8,128)S(1)} %get-tuple-element.60.zflat, ...), custom_call_target="tpu_custom_call" | custom-call | tf_op jit(solution)/shard_map/pallas_call | solution.py:324
  (1 shorter events, 0.0 us)
Async XLA Ops:
  0.6 11.1 %copy-start = (f32[1,1,16,64,448]{4,3,2,1,0:T(8,128)S(1)}, f32[1,1,16,64,448]{4,3,2,1,0:T(8,128)}, u32[]{:S(2)}) copy-start(f32[1,1,16,64,448]{4,3,2,1,0:T(8,128)} %param.12) | copy-start | bytes 5505028
  5.4 7.9 %collective-permute-start = (f32[16,512]{1,0:T(8,128)S(1)}, f32[16,512]{1,0:T(8,128)S(1)}, u32[]{:S(2)}, u32[]{:S(2)}) collective-permute-start(f32[16,512]{1,0:T(8,128)S(1)} %get-tuple-element.46), channel_id=1, source_target_pairs={{2,4},{6,8},{10,12},{14,16},{18,20},{22,24},{26,28},{4,2},{8,6},{1... | collective-permute-start | bytes 98312 | tf_op jit(solution)/shard_map/ppermute | solution.py:345
  6.1 7.8 %collective-permute-start.1 = (f32[16,512]{1,0:T(8,128)S(1)}, f32[16,512]{1,0:T(8,128)S(1)}, u32[]{:S(2)}, u32[]{:S(2)}) collective-permute-start(f32[16,512]{1,0:T(8,128)S(1)} %get-tuple-element.47), channel_id=1, source_target_pairs={{0,2},{4,6},{8,10},{12,14},{16,18},{20,22},{24,26},{28,30},{2,0},{... | collective-permute-start | bytes 98312 | tf_op jit(solution)/shard_map/ppermute | solution.py:345
  16.6 6.8 %collective-permute-start.2 = (f32[16,512]{1,0:T(8,128)S(1)}, f32[16,512]{1,0:T(8,128)S(1)}, u32[]{:S(2)}, u32[]{:S(2)}) collective-permute-start(f32[16,512]{1,0:T(8,128)S(1)} %get-tuple-element.55), channel_id=1, source_target_pairs={{2,4},{6,8},{10,12},{14,16},{18,20},{22,24},{26,28},{4,2},{8,6},{1... | collective-permute-start | bytes 98312 | tf_op jit(solution)/shard_map/ppermute | solution.py:345
  17.3 6.7 %collective-permute-start.3 = (f32[16,512]{1,0:T(8,128)S(1)}, f32[16,512]{1,0:T(8,128)S(1)}, u32[]{:S(2)}, u32[]{:S(2)}) collective-permute-start(f32[16,512]{1,0:T(8,128)S(1)} %get-tuple-element.56), channel_id=1, source_target_pairs={{0,2},{4,6},{8,10},{12,14},{16,18},{20,22},{24,26},{28,30},{2,0},{... | collective-permute-start | bytes 98312 | tf_op jit(solution)/shard_map/ppermute | solution.py:345

commit v7 on v6

--- a/solution.py
+++ b/solution.py
@@ -203,26 +203,42 @@
         wmet[i : i + 1, :] = weights[pl.ds(face, 1), :]
 
 
-def flatten(block, nblk, ncol, bdof, short, tall, out):
-    for b in range(nblk):
-        short[pl.ds(b, ncol, stride=nblk), :] = block(b)
-    for c in range(ncol):
-        tall[pl.ds(c, bdof, stride=ncol), :] = short[c * nblk : (c + 1) * nblk, :].T
-    for j in range(out.shape[1] // LANES):
-        here = slice(j * LANES, (j + 1) * LANES)
-        out[:, here] = tall[here, :].T
-
-
-def local_kernel(cols_in, met, weights, capillary, field, stiff, out, flat, *scratch):
-    left, short, tall, cols, sems = scratch
+def flatten(block, nblk, ncol, bdof, out):
+    both = jnp.concatenate([stack(block(b)) for b in range(nblk)], axis=0)
+    rows, span = 2 * nblk * ncol, 2 * LANES
+
+    def iota(shape, dim):
+        return lax.broadcasted_iota(jnp.int32, shape, dim)
+
+    first = iota((nblk, rows), 0) * (2 * ncol)
+    offset = iota((nblk, rows), 1) - first
+    gather = jnp.where((offset >= 0) & (offset < 2 * ncol), 1.0, 0.0).astype(BF16)
+    column = iota((ncol, span), 1) & (ncol - 1)
+    keep = column == iota((ncol, span), 0)
+    keep = jnp.concatenate([keep] * (2 * nblk), axis=0)
+    for j in range(out.shape[1] // span):
+        here = slice(j * span, (j + 1) * span)
+        offset = iota((bdof, span), 1) + j * span - iota((bdof, span), 0) * ncol
+        spread = jnp.where((offset >= 0) & (offset < ncol), 1.0, 0.0).astype(BF16)
+        wide = jnp.where(keep, dot(both, spread), 0.0).astype(BF16)
+        out[:, here] = dot(gather, wide)
+
+
+def local_kernel(first, cols_in, met, weights, capillary, field, stiff, out, flat, *scratch):
+    copies = [(cols_in, scratch[-2])]
+    if first:
+        copies.append((stiff, scratch[0]))
+        stiff = scratch[0]
+    left, cols, sems = scratch[-3:]
     nblk, ncol, bdof = field.shape
-    (wait,) = fetch([(cols_in, cols)], sems)
+    waits = fetch(copies, sems)
     where = listed(met)
-    flatten(lambda b: field[b], nblk, ncol, bdof, short, tall, flat)
+    flatten(lambda b: field[b], nblk, ncol, bdof, flat)
     kept = stiff.shape[2] // bdof
     for b in range(nblk):
         left[b] = stack(field[b])
-    wait()
+    for wait in waits:
+        wait()
     group = 4
     for t in range(0, nblk, group):
         gathered = [
@@ -285,7 +301,7 @@
     )
 
 
-def finish_kernel(shares, rvec, wvec, nvec, zflat, mflat, sol, res, short, tall):
+def finish_kernel(shares, rvec, wvec, nvec, zflat, mflat, sol, res):
     nblk, ncol, bdof = rvec.shape
     total = jnp.sum(shares[...], axis=0, keepdims=True)
     gamma, delta, mu, nu = [total[:, q * ncol : (q + 1) * ncol] for q in range(4)]
@@ -307,8 +323,6 @@
         nblk,
         ncol,
         bdof,
-        short,
-        tall,
         res,
     )
     along = [jnp.concatenate([x] * (LANES // ncol), axis=1) for x in (both, second)]
@@ -317,18 +331,18 @@
         sol[:, here] = along[0] * zflat[:, here] - along[1] * mflat[:, here]
 
 
-def call(kernel, outs, scratch, args, space=pltpu.VMEM):
+def call(kernel, outs, scratch, args, far=()):
     vmem = pl.BlockSpec(memory_space=pltpu.VMEM)
-    if space != pltpu.VMEM:
-        args = [pltpu.with_memory_space_constraint(arg, space) for arg in args]
+    hbm = pl.BlockSpec(memory_space=pltpu.HBM)
+    far = [pltpu.with_memory_space_constraint(arg, pltpu.HBM) for arg in far]
     return pl.pallas_call(
         kernel,
         out_shape=outs,
-        in_specs=[pl.BlockSpec(memory_space=space)] * len(args),
+        in_specs=[vmem] * len(args) + [hbm] * len(far),
         out_specs=jax.tree.map(lambda _: vmem, outs),
         scratch_shapes=scratch,
         compiler_params=pltpu.CompilerParams(vmem_limit_bytes=VMEM_LIMIT),
-    )(*args)
+    )(*args, *far)
 
 
 def everywhere(values):
@@ -390,7 +404,6 @@
     group = ncorner * bdof
     tiles = shape(size // group, group, group, dtype=BF16)
     halved = pltpu.VMEM((size // group, 2 * ncol, group), BF16)
-    relayout = [pltpu.VMEM((ncol * nblk, bdof), F32), pltpu.VMEM((bdof * ncol, nblk), F32)]
     lane = group + nface * bdof if pair else group
     marked = ncol + 8 if pair else ncol
 
@@ -408,13 +421,13 @@
             index(face_map),
             hold(face_map),
             hold(weights),
-            relayout[1],
-            relayout[0],
+            pltpu.VMEM((bdof * ncol, nblk), F32),
+            pltpu.VMEM((ncol * nblk, bdof), F32),
             halved,
             sems(11),
         ],
+        (),
         (load, mask, corner_map, face_map, blocks, rows, cols, weights, tang),
-        pltpu.HBM,
     )
 
     def finish(base, shares, marks):
@@ -428,17 +441,18 @@
         besides += faces[2:] if pair else exchange(faces[2:], "sec")
         return vec, besides
 
-    def local(vec):
+    def local(vec, near, far):
         return call(
-            local_kernel,
-            (field, flat),
-            [pltpu.VMEM((nblk, 2 * ncol, bdof), BF16)] + relayout + [index(cols), sems(1)],
-            (cols, met, weights, tang, vec, stiffness[0, 0]),
+            functools.partial(local_kernel, bool(far)),
+            (field, flat) + tuple(like(a) for a in far),
+            [pltpu.VMEM((nblk, 2 * ncol, bdof), BF16), index(cols), sems(2)],
+            (cols, met, weights, tang, vec) + near,
+            far,
         )
 
     marks = lax.all_gather(payload, "sec")
     zvec, besides = finish(base, marks, marks)
-    part, zflat = local(zvec)
+    part, zflat, stiff = local(zvec, (), (stiffness[0, 0],))
     wvec, sums, base, payload = call(
         functools.partial(image_kernel, pair),
         (field, shape(2, ncol, bdof), field, shape(ncol, lane)),
@@ -446,7 +460,7 @@
         (cmap, met, weights, part, rvec, zvec, high, low, rows, *besides),
     )
     mvec, besides = finish(base, lax.all_gather(payload, "sec"), marks)
-    part, mflat = local(mvec)
+    part, mflat = local(mvec, (stiff,), ())
     nvec, totals = call(
         last_kernel,
         (field, shape(1, 4 * ncol)),
@@ -456,7 +470,7 @@
     sol, res = call(
         finish_kernel,
         (flat, flat),
-        relayout,
+        [],
         (everywhere(totals[0]), rvec, wvec, nvec, zflat, mflat),
     )
     return sol[None, None], res[None, None]

time: 38.8 us -> 39.9 us (1.028)
  Pallas kernels: 8.42 us -> 12.1 us
  blocking collectives: 16.8 us -> 15.6 us
  waiting for transfers between devices: 1.09 us -> 0.01 us
    pallas_call x8, Pallas kernels: 8.42 us -> 12.1 us  [call(): pl.pallas_call(kernel, out_shape=outs, in_specs=[vmem] * len(args) + [hbm...]
    all_to_all x1, blocking collectives: 13 us -> 11.7 us  [everywhere(): return lax.all_to_all(copies, ('dam', 'sec'), split_axis=0, concat_axis=0)]
    ppermute x4, waiting for transfers between devices: 1.09 us -> 0.01 us  [exchange(): got.append(lax.ppermute(send, axis, pairs + [(j, i) for i, j in pairs]))]
  transfers between devices with their start and end apart: 4 -> 4, of which waited for: 2 -> 0; matrix products, arithmetic and copies ran while one was open for 0% -> 0% of each run, Pallas kernels for 8% -> 16%
where the time goes in v7:
time: 39.9 us; the launch traced here: 39.7 us
  blocking collectives  15.6 us (39%)
  Pallas kernels  12.1 us (30%)
  starting transfers between devices  11.2 us (28%)
  between operations  0.72 us (2%)
    pallas_call x8, Pallas kernels, call(): pl.pallas_call(kernel, out_shape=outs, in_specs=[vmem] * len(args) + [hbm...  12.1 us
    all_to_all x1, blocking collectives, everywhere(): return lax.all_to_all(copies, ('dam', 'sec'), split_axis=0, concat_axis=0)  11.7 us
    ppermute x4, starting transfers between devices, exchange(): got.append(lax.ppermute(send, axis, pairs + [(j, i) for i, j in pairs]))  11.2 us
    all_gather x1, blocking collectives, shards(): marks = lax.all_gather(payload, 'sec')  2 us
    all_gather x1, blocking collectives, shards(): mvec, besides = finish(base, lax.all_gather(payload, 'sec'), marks)  1.87 us
  transfers between devices with their start and end apart: 4, of which 0 were waited for; matrix products, arithmetic and copies ran while one was open for 0% of the time, Pallas kernels for 16%

profile of v7, /device:TPU:0, one launch (start us, length us, event | category | flops | bytes accessed | tf_op | source)
XLA Modules:
  0.0 39.7 jit_solution(9762567082756465463)
XLA Ops:
  0.6 2.4 %shard_map.113 = (f32[16,16,64]{2,1,0:T(8,128)S(1)}, f32[16,16,64]{2,1,0:T(8,128)S(1)}, f32[24,768]{1,0:T(8,128)S(1)}, bf16[4,256,256]{2,1,0:T(8,128)(2,1)S(1)},...) custom-call(f32[16,1024]{1,0:T(8,128)} %bitcast.25, ...), custom_call_target="tpu_custom_call" | custom-call | tf_op jit(solution)/shard_map/pallas_call | solution.py:338
  3.1 2.0 %all-gather = f32[48,768]{1,0:T(8,128)S(1)} all-gather(f32[24,768]{1,0:T(8,128)S(1)} %get-tuple-element.41), channel_id=2, replica_groups=mesh['dam'=16,'sec'=2] {'sec'}, dimensions={0}, use_global_device_ids=true | all-gather | bytes 221184 | tf_op jit(solution)/shard_map/all_gather | solution.py:453
  5.1 0.2 shard_map.114
  5.3 0.7 %collective-permute-start = (f32[16,512]{1,0:T(8,128)S(1)}, f32[16,512]{1,0:T(8,128)S(1)}, u32[]{:S(2)}, u32[]{:S(2)}) collective-permute-start(f32[16,512]{1,0:T(8,128)S(1)} %get-tuple-element.47), channel_id=1, source_target_pairs={{2,4},{6,8},{10,12},{14,16},{18,20},{22,24},{26,28},{4,2},{8,6},{1... | collective-permute-start | bytes 98312 | tf_op jit(solution)/shard_map/ppermute | solution.py:359
  5.9 5.6 %collective-permute-start.1 = (f32[16,512]{1,0:T(8,128)S(1)}, f32[16,512]{1,0:T(8,128)S(1)}, u32[]{:S(2)}, u32[]{:S(2)}) collective-permute-start(f32[16,512]{1,0:T(8,128)S(1)} %get-tuple-element.48), channel_id=1, source_target_pairs={{0,2},{4,6},{8,10},{12,14},{16,18},{20,22},{24,26},{28,30},{2,0},{... | collective-permute-start | bytes 98312 | tf_op jit(solution)/shard_map/ppermute | solution.py:359
  11.6 3.7 %shard_map.115 = (f32[16,16,64]{2,1,0:T(8,128)S(1)}, f32[16,1024]{1,0:T(8,128)S(1)}, f32[16,64,448]{2,1,0:T(8,128)S(1)}) custom-call(s32[7,1,16]{2,1,0:T(1,128)S(1)} %get-tuple-element.36.cols_in, s32[4,8]{1,0:T(4,128)S(1)} %get-tuple-element.34.met, f32[4,512]{1,0:T(4,128)S(1)} %get-tuple-element.35.weights, f32[16,64]{1,0:T(8,128)S(1)} %get-tuple-element.37.capillary, ...), custom_call_target="tpu_custom_call" | custom-call | tf_op jit(solution)/shard_map/pallas_call | solution.py:338
  15.2 0.0 collective-permute-done.rest_0_
  15.3 0.0 collective-permute-done.1.rest_1_
  15.3 0.7 %shard_map.116 = (f32[16,16,64]{2,1,0:T(8,128)S(1)}, f32[2,16,64]{2,1,0:T(8,128)S(1)}, f32[16,16,64]{2,1,0:T(8,128)S(1)}, f32[16,768]{1,0:T(8,128)S(1)}) custom-call(s32[1,4]{1,0:T(1,128)S(1)} %get-tuple-element.38.cmap, s32[4,8]{1,0:T(4,128)S(1)} %get-tuple-element.34.met, f32[4,512]{1,0:T(4,128)S(1)} %get-tuple-element.35.weights, ...), custom_call_target="tpu_custom_call" | custom-call | tf_op jit(solution)/shard_map/pallas_call | solution.py:338
  16.0 1.9 %all-gather.1 = f32[32,768]{1,0:T(8,128)S(1)} all-gather(f32[16,768]{1,0:T(8,128)S(1)} %get-tuple-element.51), channel_id=3, replica_groups=mesh['dam'=16,'sec'=2] {'sec'}, dimensions={0}, use_global_device_ids=true | all-gather | bytes 147456 | tf_op jit(solution)/shard_map/all_gather | solution.py:462
  17.9 0.2 shard_map.117
  18.0 0.7 %collective-permute-start.2 = (f32[16,512]{1,0:T(8,128)S(1)}, f32[16,512]{1,0:T(8,128)S(1)}, u32[]{:S(2)}, u32[]{:S(2)}) collective-permute-start(f32[16,512]{1,0:T(8,128)S(1)} %get-tuple-element.57), channel_id=1, source_target_pairs={{2,4},{6,8},{10,12},{14,16},{18,20},{22,24},{26,28},{4,2},{8,6},{1... | collective-permute-start | bytes 98312 | tf_op jit(solution)/shard_map/ppermute | solution.py:359
  18.7 4.3 %collective-permute-start.3 = (f32[16,512]{1,0:T(8,128)S(1)}, f32[16,512]{1,0:T(8,128)S(1)}, u32[]{:S(2)}, u32[]{:S(2)}) collective-permute-start(f32[16,512]{1,0:T(8,128)S(1)} %get-tuple-element.58), channel_id=1, source_target_pairs={{0,2},{4,6},{8,10},{12,14},{16,18},{20,22},{24,26},{28,30},{2,0},{... | collective-permute-start | bytes 98312 | tf_op jit(solution)/shard_map/ppermute | solution.py:359
  23.0 2.7 %shard_map.118 = (f32[16,16,64]{2,1,0:T(8,128)S(1)}, f32[16,1024]{1,0:T(8,128)S(1)}) custom-call(s32[7,1,16]{2,1,0:T(1,128)S(1)} %get-tuple-element.36.cols_in, s32[4,8]{1,0:T(4,128)S(1)} %get-tuple-element.34.met, f32[4,512]{1,0:T(4,128)S(1)} %get-tuple-element.35.weights, f32[16,64]{1,0:T(8,128)S(1)} %get-tuple-element.37.capillary, ...), custom_call_target="tpu_custom_call" | custom-call | tf_op jit(solution)/shard_map/pallas_call | solution.py:338
  25.7 0.0 collective-permute-done.2.rest_0_
  25.7 0.0 collective-permute-done.3.rest_1_
  25.7 0.3 shard_map.119
  26.0 11.7 %all_to_all.8 = f32[32,1,64]{2,1,0:T(1,128)S(1)} all-to-all(f32[32,1,64]{2,1,0:T(1,128)S(1)} %broadcast_in_dim.11), channel_id=1, replica_groups=mesh['dam'=16,'sec'=2] {'dam','sec'}, dimensions={0} | all-to-all | bytes 16384 | tf_op jit(solution)/shard_map/all_to_all | solution.py:351
  37.7 2.0 %shard_map.120 = (f32[16,1024]{1,0:T(8,128)}, f32[16,1024]{1,0:T(8,128)}) custom-call(f32[32,64]{1,0:T(8,128)S(1)} %bitcast.20, f32[16,16,64]{2,1,0:T(8,128)S(1)} %get-tuple-element.44.rvec, f32[16,16,64]{2,1,0:T(8,128)S(1)} %get-tuple-element.55.wvec, f32[16,16,64]{2,1,0:T(8,128)S(1)} %get-tuple-element.61.nvec, f32[16,1024]{1,0:T(8,128)S(1)} %get-tuple-element.62.zflat, ...), custom_call_target="tpu_custom_call" | custom-call | tf_op jit(solution)/shard_map/pallas_call | solution.py:338
  (1 shorter events, 0.0 us)
Async XLA Ops:
  5.3 10.0 %collective-permute-start = (f32[16,512]{1,0:T(8,128)S(1)}, f32[16,512]{1,0:T(8,128)S(1)}, u32[]{:S(2)}, u32[]{:S(2)}) collective-permute-start(f32[16,512]{1,0:T(8,128)S(1)} %get-tuple-element.47), channel_id=1, source_target_pairs={{2,4},{6,8},{10,12},{14,16},{18,20},{22,24},{26,28},{4,2},{8,6},{1... | collective-permute-start | bytes 98312 | tf_op jit(solution)/shard_map/ppermute | solution.py:359
  5.9 9.3 %collective-permute-start.1 = (f32[16,512]{1,0:T(8,128)S(1)}, f32[16,512]{1,0:T(8,128)S(1)}, u32[]{:S(2)}, u32[]{:S(2)}) collective-permute-start(f32[16,512]{1,0:T(8,128)S(1)} %get-tuple-element.48), channel_id=1, source_target_pairs={{0,2},{4,6},{8,10},{12,14},{16,18},{20,22},{24,26},{28,30},{2,0},{... | collective-permute-start | bytes 98312 | tf_op jit(solution)/shard_map/ppermute | solution.py:359
  18.0 7.6 %collective-permute-start.2 = (f32[16,512]{1,0:T(8,128)S(1)}, f32[16,512]{1,0:T(8,128)S(1)}, u32[]{:S(2)}, u32[]{:S(2)}) collective-permute-start(f32[16,512]{1,0:T(8,128)S(1)} %get-tuple-element.57), channel_id=1, source_target_pairs={{2,4},{6,8},{10,12},{14,16},{18,20},{22,24},{26,28},{4,2},{8,6},{1... | collective-permute-start | bytes 98312 | tf_op jit(solution)/shard_map/ppermute | solution.py:359
  18.7 7.0 %collective-permute-start.3 = (f32[16,512]{1,0:T(8,128)S(1)}, f32[16,512]{1,0:T(8,128)S(1)}, u32[]{:S(2)}, u32[]{:S(2)}) collective-permute-start(f32[16,512]{1,0:T(8,128)S(1)} %get-tuple-element.58), channel_id=1, source_target_pairs={{0,2},{4,6},{8,10},{12,14},{16,18},{20,22},{24,26},{28,30},{2,0},{... | collective-permute-start | bytes 98312 | tf_op jit(solution)/shard_map/ppermute | solution.py:359

commit v8 on v6

--- a/solution.py
+++ b/solution.py
@@ -145,10 +145,44 @@
         pack(zout, blocks, out)
 
 
+def swap_groups(x, ncol):
+    subs, lanes_at = x.shape[1:]
+    sub = lax.broadcasted_iota(jnp.int32, x.shape, 1)
+    lane = lax.broadcasted_iota(jnp.int32, x.shape, 2)
+    step = 1
+    while step < subs:
+        move = step * ncol
+        low, left = (sub & step) == 0, (lane & move) == 0
+        up = pltpu.roll(pltpu.roll(x, subs - step, 1), move, 2)
+        down = pltpu.roll(pltpu.roll(x, step, 1), lanes_at - move, 2)
+        x = jnp.where(low == left, x, jnp.where(low, up, down))
+        step *= 2
+    return x
+
+
+def flatten(part, shape, out):
+    nblk, ncol, bdof = shape
+    subs = LANES // ncol
+    for first in range(0, nblk, subs):
+        tall = part(first, first + subs).reshape(LANES, bdof).T
+        tall = swap_groups(tall.reshape(bdof // subs, subs, LANES), ncol)
+        for j in range(bdof // subs):
+            out[first : first + subs, j * LANES : (j + 1) * LANES] = tall[j]
+
+
+def unflatten(part, shape, out):
+    nblk, ncol, bdof = shape
+    subs = LANES // ncol
+    for first in range(0, nblk, subs):
+        parts = [part(first, first + subs, j)[None] for j in range(bdof // subs)]
+        tall = swap_groups(jnp.concatenate(parts, axis=0), ncol).reshape(bdof, LANES)
+        out[first : first + subs] = tall.T.reshape(subs, ncol, bdof)
+
+
 def start_kernel(pair, *refs):
     load_in, mask_in, cmap_in, fmap_in, blocks_in, rows_in, cols_in, weights_in, tang_in = refs[:9]
     rvec, base, payload, tiles_high, tiles_low, cmap_out, met, wmet, rows, cols, tang = refs[9:20]
-    load, mask, blocks, cmap, cmap_row, fmap, fmap_rows, weights, tall, short, left, sems = refs[20:]
+    load, mask, blocks, cmap, cmap_row, fmap, fmap_rows, weights, left, sems = refs[20:]
     waits = fetch(
         [
             (load_in, load),
@@ -184,13 +218,12 @@
     waits[1]()
     scale = mask[...].astype(F32)
     scale = jnp.concatenate([scale] * (LANES // ncol), axis=1)
-    for j in range(load.shape[1] // LANES):
-        here = slice(j * LANES, (j + 1) * LANES)
-        tall[here, :] = (load[:, here] * scale).T
-    for c in range(ncol):
-        short[c * nblk : (c + 1) * nblk, :] = tall[pl.ds(c, bdof, stride=ncol), :].T
-    for b in range(nblk):
-        rvec[b] = short[pl.ds(b, ncol, stride=nblk), :]
+    unflatten(
+        lambda first, last, j: load[first:last, j * LANES : (j + 1) * LANES]
+        * scale[first:last],
+        rvec.shape,
+        rvec,
+    )
     waits[4]()
     split_blocks(blocks, tiles_high, tiles_low)
     apply_blocks(rvec, tiles_high, tiles_low, left, base)
@@ -203,22 +236,12 @@
         wmet[i : i + 1, :] = weights[pl.ds(face, 1), :]
 
 
-def flatten(block, nblk, ncol, bdof, short, tall, out):
-    for b in range(nblk):
-        short[pl.ds(b, ncol, stride=nblk), :] = block(b)
-    for c in range(ncol):
-        tall[pl.ds(c, bdof, stride=ncol), :] = short[c * nblk : (c + 1) * nblk, :].T
-    for j in range(out.shape[1] // LANES):
-        here = slice(j * LANES, (j + 1) * LANES)
-        out[:, here] = tall[here, :].T
-
-
 def local_kernel(cols_in, met, weights, capillary, field, stiff, out, flat, *scratch):
-    left, short, tall, cols, sems = scratch
+    left, cols, sems = scratch
     nblk, ncol, bdof = field.shape
     (wait,) = fetch([(cols_in, cols)], sems)
     where = listed(met)
-    flatten(lambda b: field[b], nblk, ncol, bdof, short, tall, flat)
+    flatten(lambda first, last: field[first:last], field.shape, flat)
     kept = stiff.shape[2] // bdof
     for b in range(nblk):
         left[b] = stack(field[b])
@@ -285,7 +308,7 @@
     )
 
 
-def finish_kernel(shares, rvec, wvec, nvec, zflat, mflat, sol, res, short, tall):
+def finish_kernel(shares, rvec, wvec, nvec, zflat, mflat, sol, res):
     nblk, ncol, bdof = rvec.shape
     total = jnp.sum(shares[...], axis=0, keepdims=True)
     gamma, delta, mu, nu = [total[:, q * ncol : (q + 1) * ncol] for q in range(4)]
@@ -303,12 +326,10 @@
         jnp.sum(jnp.where(eye, x, 0.0), axis=1, keepdims=True) for x in (both, second)
     ]
     flatten(
-        lambda b: rvec[b] - down[0] * wvec[b] + down[1] * nvec[b],
-        nblk,
-        ncol,
-        bdof,
-        short,
-        tall,
+        lambda first, last: rvec[first:last]
+        - down[0] * wvec[first:last]
+        + down[1] * nvec[first:last],
+        rvec.shape,
         res,
     )
     along = [jnp.concatenate([x] * (LANES // ncol), axis=1) for x in (both, second)]
@@ -390,7 +411,6 @@
     group = ncorner * bdof
     tiles = shape(size // group, group, group, dtype=BF16)
     halved = pltpu.VMEM((size // group, 2 * ncol, group), BF16)
-    relayout = [pltpu.VMEM((ncol * nblk, bdof), F32), pltpu.VMEM((bdof * ncol, nblk), F32)]
     lane = group + nface * bdof if pair else group
     marked = ncol + 8 if pair else ncol
 
@@ -408,8 +428,6 @@
             index(face_map),
             hold(face_map),
             hold(weights),
-            relayout[1],
-            relayout[0],
             halved,
             sems(11),
         ],
@@ -432,7 +450,7 @@
         return call(
             local_kernel,
             (field, flat),
-            [pltpu.VMEM((nblk, 2 * ncol, bdof), BF16)] + relayout + [index(cols), sems(1)],
+            [pltpu.VMEM((nblk, 2 * ncol, bdof), BF16), index(cols), sems(1)],
             (cols, met, weights, tang, vec, stiffness[0, 0]),
         )
 
@@ -456,7 +474,7 @@
     sol, res = call(
         finish_kernel,
         (flat, flat),
-        relayout,
+        [],
         (everywhere(totals[0]), rvec, wvec, nvec, zflat, mflat),
     )
     return sol[None, None], res[None, None]

time: 38.8 us -> 38.4 us (0.990)
  waiting for transfers between devices: 1.09 us -> 0.58 us
    ppermute x4, waiting for transfers between devices: 1.09 us -> 0.58 us  [exchange(): got.append(lax.ppermute(send, axis, pairs + [(j, i) for i, j in pairs]))]
  transfers between devices with their start and end apart: 4 -> 4, of which waited for: 2 -> 2; matrix products, arithmetic and copies ran while one was open for 0% -> 0% of each run, Pallas kernels for 8% -> 10%
where the time goes in v8:
time: 38.4 us; the launch traced here: 38.3 us
  blocking collectives  16.8 us (44%)
  starting transfers between devices  11.5 us (30%)
  Pallas kernels  8.64 us (22%)
  between operations  0.71 us (2%)
  waiting for transfers between devices  0.58 us (2%)
    all_to_all x1, blocking collectives, everywhere(): return lax.all_to_all(copies, ('dam', 'sec'), split_axis=0, concat_axis=0)  13 us
    ppermute x4, starting transfers between devices, exchange(): got.append(lax.ppermute(send, axis, pairs + [(j, i) for i, j in pairs]))  11.5 us
    pallas_call x8, Pallas kernels, call(): pl.pallas_call(kernel, out_shape=outs, in_specs=[pl.BlockSpec(memory_spac...  8.64 us
    all_gather x1, blocking collectives, shards(): marks = lax.all_gather(payload, 'sec')  2.01 us
    all_gather x1, blocking collectives, shards(): mvec, besides = finish(base, lax.all_gather(payload, 'sec'), marks)  1.87 us
  transfers between devices with their start and end apart: 4, of which 2 were waited for; matrix products, arithmetic and copies ran while one was open for 0% of the time, Pallas kernels for 10%

profile of v8, /device:TPU:0, one launch (start us, length us, event | category | flops | bytes accessed | tf_op | source)
XLA Modules:
  0.0 38.3 jit_solution(6358872031387578715)
XLA Ops:
  0.6 0.0 copy-start
  0.6 2.4 %shard_map.113 = (f32[16,16,64]{2,1,0:T(8,128)S(1)}, f32[16,16,64]{2,1,0:T(8,128)S(1)}, f32[24,768]{1,0:T(8,128)S(1)}, bf16[4,256,256]{2,1,0:T(8,128)(2,1)S(1)},...) custom-call(f32[16,1024]{1,0:T(8,128)} %bitcast.26, ...), custom_call_target="tpu_custom_call" | custom-call | tf_op jit(solution)/shard_map/pallas_call | solution.py:345
  3.1 2.0 %all-gather = f32[48,768]{1,0:T(8,128)S(1)} all-gather(f32[24,768]{1,0:T(8,128)S(1)} %get-tuple-element.40), channel_id=2, replica_groups=mesh['dam'=16,'sec'=2] {'sec'}, dimensions={0}, use_global_device_ids=true | all-gather | bytes 221184 | tf_op jit(solution)/shard_map/all_gather | solution.py:457
  5.1 0.2 shard_map.114
  5.3 0.7 %collective-permute-start = (f32[16,512]{1,0:T(8,128)S(1)}, f32[16,512]{1,0:T(8,128)S(1)}, u32[]{:S(2)}, u32[]{:S(2)}) collective-permute-start(f32[16,512]{1,0:T(8,128)S(1)} %get-tuple-element.46), channel_id=1, source_target_pairs={{2,4},{6,8},{10,12},{14,16},{18,20},{22,24},{26,28},{4,2},{8,6},{1... | collective-permute-start | bytes 98312 | tf_op jit(solution)/shard_map/ppermute | solution.py:366
  5.9 5.6 %collective-permute-start.1 = (f32[16,512]{1,0:T(8,128)S(1)}, f32[16,512]{1,0:T(8,128)S(1)}, u32[]{:S(2)}, u32[]{:S(2)}) collective-permute-start(f32[16,512]{1,0:T(8,128)S(1)} %get-tuple-element.47), channel_id=1, source_target_pairs={{0,2},{4,6},{8,10},{12,14},{16,18},{20,22},{24,26},{28,30},{2,0},{... | collective-permute-start | bytes 98312 | tf_op jit(solution)/shard_map/ppermute | solution.py:366
  11.6 0.0 copy-done
  11.6 1.8 %shard_map.115 = (f32[16,16,64]{2,1,0:T(8,128)S(1)}, f32[16,1024]{1,0:T(8,128)S(1)}) custom-call(s32[7,1,16]{2,1,0:T(1,128)S(1)} %get-tuple-element.35.cols_in, s32[4,8]{1,0:T(4,128)S(1)} %get-tuple-element.33.met, f32[4,512]{1,0:T(4,128)S(1)} %get-tuple-element.34.weights, f32[16,64]{1,0:T(8,128)S(1)} %get-tuple-element.36.capillary, ...), custom_call_target="tpu_custom_call" | custom-call | tf_op jit(solution)/shard_map/pallas_call | solution.py:345
  13.4 0.0 collective-permute-done.rest_0_
  13.5 0.3 collective-permute-done.1.rest_1_
  13.7 0.7 %shard_map.116 = (f32[16,16,64]{2,1,0:T(8,128)S(1)}, f32[2,16,64]{2,1,0:T(8,128)S(1)}, f32[16,16,64]{2,1,0:T(8,128)S(1)}, f32[16,768]{1,0:T(8,128)S(1)}) custom-call(s32[1,4]{1,0:T(1,128)S(1)} %get-tuple-element.37.cmap, s32[4,8]{1,0:T(4,128)S(1)} %get-tuple-element.33.met, f32[4,512]{1,0:T(4,128)S(1)} %get-tuple-element.34.weights, ...), custom_call_target="tpu_custom_call" | custom-call | tf_op jit(solution)/shard_map/pallas_call | solution.py:345
  14.5 1.9 %all-gather.1 = f32[32,768]{1,0:T(8,128)S(1)} all-gather(f32[16,768]{1,0:T(8,128)S(1)} %get-tuple-element.50), channel_id=3, replica_groups=mesh['dam'=16,'sec'=2] {'sec'}, dimensions={0}, use_global_device_ids=true | all-gather | bytes 147456 | tf_op jit(solution)/shard_map/all_gather | solution.py:466
  16.3 0.2 shard_map.117
  16.5 0.7 %collective-permute-start.2 = (f32[16,512]{1,0:T(8,128)S(1)}, f32[16,512]{1,0:T(8,128)S(1)}, u32[]{:S(2)}, u32[]{:S(2)}) collective-permute-start(f32[16,512]{1,0:T(8,128)S(1)} %get-tuple-element.55), channel_id=1, source_target_pairs={{2,4},{6,8},{10,12},{14,16},{18,20},{22,24},{26,28},{4,2},{8,6},{1... | collective-permute-start | bytes 98312 | tf_op jit(solution)/shard_map/ppermute | solution.py:366
  17.2 4.5 %collective-permute-start.3 = (f32[16,512]{1,0:T(8,128)S(1)}, f32[16,512]{1,0:T(8,128)S(1)}, u32[]{:S(2)}, u32[]{:S(2)}) collective-permute-start(f32[16,512]{1,0:T(8,128)S(1)} %get-tuple-element.56), channel_id=1, source_target_pairs={{0,2},{4,6},{8,10},{12,14},{16,18},{20,22},{24,26},{28,30},{2,0},{... | collective-permute-start | bytes 98312 | tf_op jit(solution)/shard_map/ppermute | solution.py:366
  21.7 1.8 %shard_map.118 = (f32[16,16,64]{2,1,0:T(8,128)S(1)}, f32[16,1024]{1,0:T(8,128)S(1)}) custom-call(s32[7,1,16]{2,1,0:T(1,128)S(1)} %get-tuple-element.35.cols_in, s32[4,8]{1,0:T(4,128)S(1)} %get-tuple-element.33.met, f32[4,512]{1,0:T(4,128)S(1)} %get-tuple-element.34.weights, f32[16,64]{1,0:T(8,128)S(1)} %get-tuple-element.36.capillary, ...), custom_call_target="tpu_custom_call" | custom-call | tf_op jit(solution)/shard_map/pallas_call | solution.py:345
  23.5 0.0 collective-permute-done.2.rest_0_
  23.5 0.3 collective-permute-done.3.rest_1_
  23.8 0.3 shard_map.119
  24.2 13.0 %all_to_all.8 = f32[32,1,64]{2,1,0:T(1,128)S(1)} all-to-all(f32[32,1,64]{2,1,0:T(1,128)S(1)} %broadcast_in_dim.11), channel_id=1, replica_groups=mesh['dam'=16,'sec'=2] {'dam','sec'}, dimensions={0} | all-to-all | bytes 16384 | tf_op jit(solution)/shard_map/all_to_all | solution.py:358
  37.1 1.1 %shard_map.120 = (f32[16,1024]{1,0:T(8,128)}, f32[16,1024]{1,0:T(8,128)}) custom-call(f32[32,64]{1,0:T(8,128)S(1)} %bitcast.22, f32[16,16,64]{2,1,0:T(8,128)S(1)} %get-tuple-element.43.rvec, f32[16,16,64]{2,1,0:T(8,128)S(1)} %get-tuple-element.53.wvec, f32[16,16,64]{2,1,0:T(8,128)S(1)} %get-tuple-element.59.nvec, f32[16,1024]{1,0:T(8,128)S(1)} %get-tuple-element.60.zflat, ...), custom_call_target="tpu_custom_call" | custom-call | tf_op jit(solution)/shard_map/pallas_call | solution.py:345
  (1 shorter events, 0.0 us)
Async XLA Ops:
  0.6 11.0 %copy-start = (f32[1,1,16,64,448]{4,3,2,1,0:T(8,128)S(1)}, f32[1,1,16,64,448]{4,3,2,1,0:T(8,128)}, u32[]{:S(2)}) copy-start(f32[1,1,16,64,448]{4,3,2,1,0:T(8,128)} %param.12) | copy-start | bytes 5505028
  5.3 8.2 %collective-permute-start = (f32[16,512]{1,0:T(8,128)S(1)}, f32[16,512]{1,0:T(8,128)S(1)}, u32[]{:S(2)}, u32[]{:S(2)}) collective-permute-start(f32[16,512]{1,0:T(8,128)S(1)} %get-tuple-element.46), channel_id=1, source_target_pairs={{2,4},{6,8},{10,12},{14,16},{18,20},{22,24},{26,28},{4,2},{8,6},{1... | collective-permute-start | bytes 98312 | tf_op jit(solution)/shard_map/ppermute | solution.py:366
  5.9 7.8 %collective-permute-start.1 = (f32[16,512]{1,0:T(8,128)S(1)}, f32[16,512]{1,0:T(8,128)S(1)}, u32[]{:S(2)}, u32[]{:S(2)}) collective-permute-start(f32[16,512]{1,0:T(8,128)S(1)} %get-tuple-element.47), channel_id=1, source_target_pairs={{0,2},{4,6},{8,10},{12,14},{16,18},{20,22},{24,26},{28,30},{2,0},{... | collective-permute-start | bytes 98312 | tf_op jit(solution)/shard_map/ppermute | solution.py:366
  16.5 7.0 %collective-permute-start.2 = (f32[16,512]{1,0:T(8,128)S(1)}, f32[16,512]{1,0:T(8,128)S(1)}, u32[]{:S(2)}, u32[]{:S(2)}) collective-permute-start(f32[16,512]{1,0:T(8,128)S(1)} %get-tuple-element.55), channel_id=1, source_target_pairs={{2,4},{6,8},{10,12},{14,16},{18,20},{22,24},{26,28},{4,2},{8,6},{1... | collective-permute-start | bytes 98312 | tf_op jit(solution)/shard_map/ppermute | solution.py:366
  17.2 6.7 %collective-permute-start.3 = (f32[16,512]{1,0:T(8,128)S(1)}, f32[16,512]{1,0:T(8,128)S(1)}, u32[]{:S(2)}, u32[]{:S(2)}) collective-permute-start(f32[16,512]{1,0:T(8,128)S(1)} %get-tuple-element.56), channel_id=1, source_target_pairs={{0,2},{4,6},{8,10},{12,14},{16,18},{20,22},{24,26},{28,30},{2,0},{... | collective-permute-start | bytes 98312 | tf_op jit(solution)/shard_map/ppermute | solution.py:366

commit v9 on v8

--- a/solution.py
+++ b/solution.py
@@ -236,12 +236,15 @@
         wmet[i : i + 1, :] = weights[pl.ds(face, 1), :]
 
 
-def local_kernel(cols_in, met, weights, capillary, field, stiff, out, flat, *scratch):
+def local_kernel(
+    cols_in, met, weights, capillary, field, other, stiff, out, flat, other_flat, *scratch
+):
     left, cols, sems = scratch
     nblk, ncol, bdof = field.shape
     (wait,) = fetch([(cols_in, cols)], sems)
     where = listed(met)
     flatten(lambda first, last: field[first:last], field.shape, flat)
+    flatten(lambda first, last: other[first:last], field.shape, other_flat)
     kept = stiff.shape[2] // bdof
     for b in range(nblk):
         left[b] = stack(field[b])
@@ -299,43 +302,35 @@
     parts = jnp.concatenate(
         [sums[0], sums[1], lanes(wvec, mvec), lanes(mvec, nout)], axis=0
     )
-    totals[...] = lax.dot_general(
-        jnp.ones((1, parts.shape[1]), F32),
+    sides = lax.dot_general(
+        jnp.ones((totals.shape[0], parts.shape[1]), F32),
         parts,
         (((1,), (1,)), ((), ())),
         precision=lax.Precision.HIGHEST,
         preferred_element_type=F32,
     )
-
-
-def finish_kernel(shares, rvec, wvec, nvec, zflat, mflat, sol, res):
-    nblk, ncol, bdof = rvec.shape
-    total = jnp.sum(shares[...], axis=0, keepdims=True)
+    rest = totals.shape[1] - sides.shape[1]
+    totals[...] = jnp.concatenate([sides, jnp.zeros((sides.shape[0], rest), F32)], axis=1)
+
+
+def finish_kernel(shares, nvec, rflat, zflat, wflat, mflat, sol, res):
+    nblk, ncol, bdof = nvec.shape
+    flatten(lambda first, last: nvec[first:last], nvec.shape, res)
+    total = jnp.sum(shares[...], axis=0)[:1]
     gamma, delta, mu, nu = [total[:, q * ncol : (q + 1) * ncol] for q in range(4)]
     alpha = gamma / delta
     gnew = gamma - 2.0 * alpha * delta + alpha * alpha * mu
     grow = 1.0 + gnew / gamma
     dnew = grow * grow * delta - 2.0 * alpha * grow * mu + alpha * alpha * nu
     anew = gnew / dnew
-    both = alpha + anew * grow
-    second = anew * alpha
-    eye = lax.broadcasted_iota(jnp.int32, (ncol, ncol), 0) == lax.broadcasted_iota(
-        jnp.int32, (ncol, ncol), 1
-    )
-    down = [
-        jnp.sum(jnp.where(eye, x, 0.0), axis=1, keepdims=True) for x in (both, second)
+    both, second = [
+        jnp.concatenate([x] * (LANES // ncol), axis=1)
+        for x in (alpha + anew * grow, anew * alpha)
     ]
-    flatten(
-        lambda first, last: rvec[first:last]
-        - down[0] * wvec[first:last]
-        + down[1] * nvec[first:last],
-        rvec.shape,
-        res,
-    )
-    along = [jnp.concatenate([x] * (LANES // ncol), axis=1) for x in (both, second)]
     for j in range(sol.shape[1] // LANES):
         here = slice(j * LANES, (j + 1) * LANES)
-        sol[:, here] = along[0] * zflat[:, here] - along[1] * mflat[:, here]
+        sol[:, here] = both * zflat[:, here] - second * mflat[:, here]
+        res[:, here] = rflat[:, here] - both * wflat[:, here] + second * res[:, here]
 
 
 def call(kernel, outs, scratch, args, space=pltpu.VMEM):
@@ -353,9 +348,7 @@
 
 
 def everywhere(values):
-    total = lax.axis_size("dam") * lax.axis_size("sec")
-    copies = jnp.broadcast_to(values[None], (total,) + values.shape)
-    return lax.all_to_all(copies, ("dam", "sec"), split_axis=0, concat_axis=0)
+    return lax.all_gather(values, ("dam", "sec"))
 
 
 def exchange(sends, axis):
@@ -446,17 +439,17 @@
         besides += faces[2:] if pair else exchange(faces[2:], "sec")
         return vec, besides
 
-    def local(vec):
+    def local(vec, other):
         return call(
             local_kernel,
-            (field, flat),
+            (field, flat, flat),
             [pltpu.VMEM((nblk, 2 * ncol, bdof), BF16), index(cols), sems(1)],
-            (cols, met, weights, tang, vec, stiffness[0, 0]),
+            (cols, met, weights, tang, vec, other, stiffness[0, 0]),
         )
 
     marks = lax.all_gather(payload, "sec")
     zvec, besides = finish(base, marks, marks)
-    part, zflat = local(zvec)
+    part, zflat, rflat = local(zvec, rvec)
     wvec, sums, base, payload = call(
         functools.partial(image_kernel, pair),
         (field, shape(2, ncol, bdof), field, shape(ncol, lane)),
@@ -464,10 +457,10 @@
         (cmap, met, weights, part, rvec, zvec, high, low, rows, *besides),
     )
     mvec, besides = finish(base, lax.all_gather(payload, "sec"), marks)
-    part, mflat = local(mvec)
+    part, mflat, wflat = local(mvec, wvec)
     nvec, totals = call(
         last_kernel,
-        (field, shape(1, 4 * ncol)),
+        (field, shape(8, LANES)),
         [],
         (met, weights, part, wvec, mvec, sums, *besides),
     )
@@ -475,7 +468,7 @@
         finish_kernel,
         (flat, flat),
         [],
-        (everywhere(totals[0]), rvec, wvec, nvec, zflat, mflat),
+        (everywhere(totals), nvec, rflat, zflat, wflat, mflat),
     )
     return sol[None, None], res[None, None]
 

time: 38.4 us -> 66.5 us (1.73)
  blocking collectives: 16.8 us -> 45 us
    all_gather x0 -> x1, blocking collectives: none -> 41.2 us  [everywhere(): return lax.all_gather(values, ('dam', 'sec'))]
    all_to_all x1 -> x0, blocking collectives: 13 us -> none  [everywhere(): return lax.all_to_all(copies, ('dam', 'sec'), split_axis=0, concat_axis=0)]
  transfers between devices with their start and end apart: 4 -> 4, of which waited for: 2 -> 2; matrix products, arithmetic and copies ran while one was open for 0% -> 0% of each run, Pallas kernels for 10% -> 6%
where the time goes in v9:
time: 66.5 us; the launch traced here: 66.3 us
  blocking collectives  45 us (68%)
  starting transfers between devices  11.5 us (17%)
  Pallas kernels  8.91 us (13%)
  between operations  0.7 us (1%)
    all_gather x1, blocking collectives, everywhere(): return lax.all_gather(values, ('dam', 'sec'))  41.2 us
    ppermute x4, starting transfers between devices, exchange(): got.append(lax.ppermute(send, axis, pairs + [(j, i) for i, j in pairs]))  11.5 us
    pallas_call x8, Pallas kernels, call(): pl.pallas_call(kernel, out_shape=outs, in_specs=[pl.BlockSpec(memory_spac...  8.91 us
    all_gather x1, blocking collectives, shards(): marks = lax.all_gather(payload, 'sec')  2.01 us
    all_gather x1, blocking collectives, shards(): mvec, besides = finish(base, lax.all_gather(payload, 'sec'), marks)  1.87 us
  transfers between devices with their start and end apart: 4, of which 2 were waited for; matrix products, arithmetic and copies ran while one was open for 0% of the time, Pallas kernels for 6%

profile of v9, /device:TPU:0, one launch (start us, length us, event | category | flops | bytes accessed | tf_op | source)
XLA Modules:
  0.0 66.3 jit_solution(4768960064125305192)
XLA Ops:
  0.6 0.0 copy-start
  0.6 2.4 %shard_map.113 = (f32[16,16,64]{2,1,0:T(8,128)S(1)}, f32[16,16,64]{2,1,0:T(8,128)S(1)}, f32[24,768]{1,0:T(8,128)S(1)}, bf16[4,256,256]{2,1,0:T(8,128)(2,1)S(1)},...) custom-call(f32[16,1024]{1,0:T(8,128)} %bitcast.24, ...), custom_call_target="tpu_custom_call" | custom-call | tf_op jit(solution)/shard_map/pallas_call | solution.py:340
  3.1 2.0 %all-gather = f32[48,768]{1,0:T(8,128)S(1)} all-gather(f32[24,768]{1,0:T(8,128)S(1)} %get-tuple-element.42), channel_id=2, replica_groups=mesh['dam'=16,'sec'=2] {'sec'}, dimensions={0}, use_global_device_ids=true | all-gather | bytes 221184 | tf_op jit(solution)/shard_map/all_gather | solution.py:450
  5.1 0.2 shard_map.114
  5.3 0.7 collective-permute-start
  5.9 5.6 %collective-permute-start.1 = (f32[16,512]{1,0:T(8,128)S(1)}, f32[16,512]{1,0:T(8,128)S(1)}, u32[]{:S(2)}, u32[]{:S(2)}) collective-permute-start(f32[16,512]{1,0:T(8,128)S(1)} %get-tuple-element.49), channel_id=1, source_target_pairs={{0,2},{4,6},{8,10},{12,14},{16,18},{20,22},{24,26},{28,30},{2,0},{... | collective-permute-start | bytes 98312 | tf_op jit(solution)/shard_map/ppermute | solution.py:359
  11.6 0.0 copy-done
  11.6 2.0 %shard_map.115 = (f32[16,16,64]{2,1,0:T(8,128)S(1)}, f32[16,1024]{1,0:T(8,128)S(1)}, f32[16,1024]{1,0:T(8,128)S(1)}) custom-call(s32[7,1,16]{2,1,0:T(1,128)S(1)} %get-tuple-element.37.cols_in, s32[4,8]{1,0:T(4,128)S(1)} %get-tuple-element.35.met, f32[4,512]{1,0:T(4,128)S(1)} %get-tuple-element.36.weights, f32[16,64]{1,0:T(8,128)S(1)} %get-tuple-element.38.capillary, ...), custom_call_target="tpu_custom_call" | custom-call | tf_op jit(solution)/shard_map/pallas_call | solution.py:340
  13.6 0.0 collective-permute-done.rest_0_
  13.6 0.1 collective-permute-done.1.rest_1_
  13.7 0.7 %shard_map.116 = (f32[16,16,64]{2,1,0:T(8,128)S(1)}, f32[2,16,64]{2,1,0:T(8,128)S(1)}, f32[16,16,64]{2,1,0:T(8,128)S(1)}, f32[16,768]{1,0:T(8,128)S(1)}) custom-call(s32[1,4]{1,0:T(1,128)S(1)} %get-tuple-element.39.cmap, s32[4,8]{1,0:T(4,128)S(1)} %get-tuple-element.35.met, f32[4,512]{1,0:T(4,128)S(1)} %get-tuple-element.36.weights, ...), custom_call_target="tpu_custom_call" | custom-call | tf_op jit(solution)/shard_map/pallas_call | solution.py:340
  14.5 1.9 %all-gather.1 = f32[32,768]{1,0:T(8,128)S(1)} all-gather(f32[16,768]{1,0:T(8,128)S(1)} %get-tuple-element.52), channel_id=3, replica_groups=mesh['dam'=16,'sec'=2] {'sec'}, dimensions={0}, use_global_device_ids=true | all-gather | bytes 147456 | tf_op jit(solution)/shard_map/all_gather | solution.py:459
  16.3 0.2 shard_map.117
  16.5 0.7 collective-permute-start.2
  17.2 4.5 %collective-permute-start.3 = (f32[16,512]{1,0:T(8,128)S(1)}, f32[16,512]{1,0:T(8,128)S(1)}, u32[]{:S(2)}, u32[]{:S(2)}) collective-permute-start(f32[16,512]{1,0:T(8,128)S(1)} %get-tuple-element.58), channel_id=1, source_target_pairs={{0,2},{4,6},{8,10},{12,14},{16,18},{20,22},{24,26},{28,30},{2,0},{... | collective-permute-start | bytes 98312 | tf_op jit(solution)/shard_map/ppermute | solution.py:359
  21.7 2.0 %shard_map.118 = (f32[16,16,64]{2,1,0:T(8,128)S(1)}, f32[16,1024]{1,0:T(8,128)S(1)}, f32[16,1024]{1,0:T(8,128)S(1)}) custom-call(s32[7,1,16]{2,1,0:T(1,128)S(1)} %get-tuple-element.37.cols_in, s32[4,8]{1,0:T(4,128)S(1)} %get-tuple-element.35.met, f32[4,512]{1,0:T(4,128)S(1)} %get-tuple-element.36.weights, f32[16,64]{1,0:T(8,128)S(1)} %get-tuple-element.38.capillary, ...), custom_call_target="tpu_custom_call" | custom-call | tf_op jit(solution)/shard_map/pallas_call | solution.py:340
  23.7 0.0 collective-permute-done.2.rest_0_
  23.7 0.1 collective-permute-done.3.rest_1_
  23.8 0.3 shard_map.119
  24.1 41.2 %all-gather.2 = f32[256,128]{1,0:T(8,128)S(1)} all-gather(f32[8,128]{1,0:T(8,128)S(1)} %get-tuple-element.60), channel_id=4, replica_groups=mesh['dam'=16,'sec'=2] {'dam','sec'}, dimensions={0}, use_global_device_ids=true | all-gather | bytes 135168 | tf_op jit(solution)/shard_map/all_gather | solution.py:351
  65.3 1.0 %shard_map.120 = (f32[16,1024]{1,0:T(8,128)}, f32[16,1024]{1,0:T(8,128)}) custom-call(f32[32,8,128]{2,1,0:T(8,128)S(1)} %bitcast.20, f32[16,16,64]{2,1,0:T(8,128)S(1)} %get-tuple-element.61.nvec, f32[16,1024]{1,0:T(8,128)S(1)} %get-tuple-element.62.rflat, f32[16,1024]{1,0:T(8,128)S(1)} %get-tuple-element.63.zflat, f32[16,1024]{1,0:T(8,128)S(1)} %get-tuple-element.64.wflat, ...), custom_call_target="tpu_custom_call" | custom-call | tf_op jit(solution)/shard_map/pallas_call | solution.py:340
Async XLA Ops:
  0.6 11.0 %copy-start = (f32[1,1,16,64,448]{4,3,2,1,0:T(8,128)S(1)}, f32[1,1,16,64,448]{4,3,2,1,0:T(8,128)}, u32[]{:S(2)}) copy-start(f32[1,1,16,64,448]{4,3,2,1,0:T(8,128)} %param.12) | copy-start | bytes 5505028
  5.3 8.4 %collective-permute-start = (f32[16,512]{1,0:T(8,128)S(1)}, f32[16,512]{1,0:T(8,128)S(1)}, u32[]{:S(2)}, u32[]{:S(2)}) collective-permute-start(f32[16,512]{1,0:T(8,128)S(1)} %get-tuple-element.48), channel_id=1, source_target_pairs={{2,4},{6,8},{10,12},{14,16},{18,20},{22,24},{26,28},{4,2},{8,6},{1... | collective-permute-start | bytes 98312 | tf_op jit(solution)/shard_map/ppermute | solution.py:359
  5.9 7.8 %collective-permute-start.1 = (f32[16,512]{1,0:T(8,128)S(1)}, f32[16,512]{1,0:T(8,128)S(1)}, u32[]{:S(2)}, u32[]{:S(2)}) collective-permute-start(f32[16,512]{1,0:T(8,128)S(1)} %get-tuple-element.49), channel_id=1, source_target_pairs={{0,2},{4,6},{8,10},{12,14},{16,18},{20,22},{24,26},{28,30},{2,0},{... | collective-permute-start | bytes 98312 | tf_op jit(solution)/shard_map/ppermute | solution.py:359
  16.5 7.2 %collective-permute-start.2 = (f32[16,512]{1,0:T(8,128)S(1)}, f32[16,512]{1,0:T(8,128)S(1)}, u32[]{:S(2)}, u32[]{:S(2)}) collective-permute-start(f32[16,512]{1,0:T(8,128)S(1)} %get-tuple-element.57), channel_id=1, source_target_pairs={{2,4},{6,8},{10,12},{14,16},{18,20},{22,24},{26,28},{4,2},{8,6},{1... | collective-permute-start | bytes 98312 | tf_op jit(solution)/shard_map/ppermute | solution.py:359
  17.2 6.7 %collective-permute-start.3 = (f32[16,512]{1,0:T(8,128)S(1)}, f32[16,512]{1,0:T(8,128)S(1)}, u32[]{:S(2)}, u32[]{:S(2)}) collective-permute-start(f32[16,512]{1,0:T(8,128)S(1)} %get-tuple-element.58), channel_id=1, source_target_pairs={{0,2},{4,6},{8,10},{12,14},{16,18},{20,22},{24,26},{28,30},{2,0},{... | collective-permute-start | bytes 98312 | tf_op jit(solution)/shard_map/ppermute | solution.py:359

commit v10 on v9

--- a/solution.py
+++ b/solution.py
@@ -214,8 +214,8 @@
                 payload[ncol + n : ncol + n + 1, p * bdof : (p + 1) * bdof] = jnp.full(
                     (1, bdof), jnp.where(corner == b, 1.0, 0.0), F32
                 )
-    waits[0]()
-    waits[1]()
+    for wait in waits[:2] + waits[4:]:
+        wait()
     scale = mask[...].astype(F32)
     scale = jnp.concatenate([scale] * (LANES // ncol), axis=1)
     unflatten(
@@ -224,11 +224,8 @@
         rvec.shape,
         rvec,
     )
-    waits[4]()
     split_blocks(blocks, tiles_high, tiles_low)
     apply_blocks(rvec, tiles_high, tiles_low, left, base)
-    for wait in waits[5:]:
-        wait()
     offer(pair, corners, across, rvec, rows, base, payload)
     cmap_out[...] = cmap_row[0]
     for i, face in enumerate(order):
@@ -302,21 +299,19 @@
     parts = jnp.concatenate(
         [sums[0], sums[1], lanes(wvec, mvec), lanes(mvec, nout)], axis=0
     )
-    sides = lax.dot_general(
-        jnp.ones((totals.shape[0], parts.shape[1]), F32),
+    totals[...] = lax.dot_general(
+        jnp.ones((1, parts.shape[1]), F32),
         parts,
         (((1,), (1,)), ((), ())),
         precision=lax.Precision.HIGHEST,
         preferred_element_type=F32,
     )
-    rest = totals.shape[1] - sides.shape[1]
-    totals[...] = jnp.concatenate([sides, jnp.zeros((sides.shape[0], rest), F32)], axis=1)
 
 
 def finish_kernel(shares, nvec, rflat, zflat, wflat, mflat, sol, res):
     nblk, ncol, bdof = nvec.shape
     flatten(lambda first, last: nvec[first:last], nvec.shape, res)
-    total = jnp.sum(shares[...], axis=0)[:1]
+    total = jnp.sum(shares[...], axis=0, keepdims=True)
     gamma, delta, mu, nu = [total[:, q * ncol : (q + 1) * ncol] for q in range(4)]
     alpha = gamma / delta
     gnew = gamma - 2.0 * alpha * delta + alpha * alpha * mu
@@ -348,7 +343,9 @@
 
 
 def everywhere(values):
-    return lax.all_gather(values, ("dam", "sec"))
+    total = lax.axis_size("dam") * lax.axis_size("sec")
+    copies = jnp.broadcast_to(values[None], (total,) + values.shape)
+    return lax.all_to_all(copies, ("dam", "sec"), split_axis=0, concat_axis=0)
 
 
 def exchange(sends, axis):
@@ -460,7 +457,7 @@
     part, mflat, wflat = local(mvec, wvec)
     nvec, totals = call(
         last_kernel,
-        (field, shape(8, LANES)),
+        (field, shape(1, 4 * ncol)),
         [],
         (met, weights, part, wvec, mvec, sums, *besides),
     )
@@ -468,7 +465,7 @@
         finish_kernel,
         (flat, flat),
         [],
-        (everywhere(totals), nvec, rflat, zflat, wflat, mflat),
+        (everywhere(totals[0]), nvec, rflat, zflat, wflat, mflat),
     )
     return sol[None, None], res[None, None]
 

time: 66.5 us -> 38.5 us (0.58)
  blocking collectives: 45 us -> 16.9 us
    all_gather x1 -> x0, blocking collectives: 41.2 us -> none  [everywhere(): return lax.all_gather(values, ('dam', 'sec'))]
    all_to_all x0 -> x1, blocking collectives: none -> 13 us  [everywhere(): return lax.all_to_all(copies, ('dam', 'sec'), split_axis=0, concat_axis=0)]
  transfers between devices with their start and end apart: 4 -> 4, of which waited for: 2 -> 2; matrix products, arithmetic and copies ran while one was open for 0% -> 0% of each run, Pallas kernels for 6% -> 11%
where the time goes in v10:
time: 38.5 us; the launch traced here: 38.3 us
  blocking collectives  16.9 us (44%)
  starting transfers between devices  11.5 us (30%)
  Pallas kernels  9.04 us (23%)
  between operations  0.71 us (2%)
    all_to_all x1, blocking collectives, everywhere(): return lax.all_to_all(copies, ('dam', 'sec'), split_axis=0, concat_axis=0)  13 us
    ppermute x4, starting transfers between devices, exchange(): got.append(lax.ppermute(send, axis, pairs + [(j, i) for i, j in pairs]))  11.5 us
    pallas_call x8, Pallas kernels, call(): pl.pallas_call(kernel, out_shape=outs, in_specs=[pl.BlockSpec(memory_spac...  9.04 us
    all_gather x1, blocking collectives, shards(): marks = lax.all_gather(payload, 'sec')  2.02 us
    all_gather x1, blocking collectives, shards(): mvec, besides = finish(base, lax.all_gather(payload, 'sec'), marks)  1.87 us
  transfers between devices with their start and end apart: 4, of which 2 were waited for; matrix products, arithmetic and copies ran while one was open for 0% of the time, Pallas kernels for 11%

profile of v10, /device:TPU:0, one launch (start us, length us, event | category | flops | bytes accessed | tf_op | source)
XLA Modules:
  0.0 38.3 jit_solution(7322361623259270120)
XLA Ops:
  0.6 0.0 copy-start
  0.6 2.6 %shard_map.113 = (f32[16,16,64]{2,1,0:T(8,128)S(1)}, f32[16,16,64]{2,1,0:T(8,128)S(1)}, f32[24,768]{1,0:T(8,128)S(1)}, bf16[4,256,256]{2,1,0:T(8,128)(2,1)S(1)},...) custom-call(f32[16,1024]{1,0:T(8,128)} %bitcast.26, ...), custom_call_target="tpu_custom_call" | custom-call | tf_op jit(solution)/shard_map/pallas_call | solution.py:335
  3.2 2.0 %all-gather = f32[48,768]{1,0:T(8,128)S(1)} all-gather(f32[24,768]{1,0:T(8,128)S(1)} %get-tuple-element.42), channel_id=2, replica_groups=mesh['dam'=16,'sec'=2] {'sec'}, dimensions={0}, use_global_device_ids=true | all-gather | bytes 221184 | tf_op jit(solution)/shard_map/all_gather | solution.py:447
  5.2 0.2 shard_map.114
  5.4 0.7 %collective-permute-start = (f32[16,512]{1,0:T(8,128)S(1)}, f32[16,512]{1,0:T(8,128)S(1)}, u32[]{:S(2)}, u32[]{:S(2)}) collective-permute-start(f32[16,512]{1,0:T(8,128)S(1)} %get-tuple-element.48), channel_id=1, source_target_pairs={{2,4},{6,8},{10,12},{14,16},{18,20},{22,24},{26,28},{4,2},{8,6},{1... | collective-permute-start | bytes 98312 | tf_op jit(solution)/shard_map/ppermute | solution.py:356
  6.1 5.6 %collective-permute-start.1 = (f32[16,512]{1,0:T(8,128)S(1)}, f32[16,512]{1,0:T(8,128)S(1)}, u32[]{:S(2)}, u32[]{:S(2)}) collective-permute-start(f32[16,512]{1,0:T(8,128)S(1)} %get-tuple-element.49), channel_id=1, source_target_pairs={{0,2},{4,6},{8,10},{12,14},{16,18},{20,22},{24,26},{28,30},{2,0},{... | collective-permute-start | bytes 98312 | tf_op jit(solution)/shard_map/ppermute | solution.py:356
  11.7 0.0 copy-done
  11.7 2.0 %shard_map.115 = (f32[16,16,64]{2,1,0:T(8,128)S(1)}, f32[16,1024]{1,0:T(8,128)S(1)}, f32[16,1024]{1,0:T(8,128)S(1)}) custom-call(s32[7,1,16]{2,1,0:T(1,128)S(1)} %get-tuple-element.37.cols_in, s32[4,8]{1,0:T(4,128)S(1)} %get-tuple-element.35.met, f32[4,512]{1,0:T(4,128)S(1)} %get-tuple-element.36.weights, f32[16,64]{1,0:T(8,128)S(1)} %get-tuple-element.38.capillary, ...), custom_call_target="tpu_custom_call" | custom-call | tf_op jit(solution)/shard_map/pallas_call | solution.py:335
  13.8 0.0 collective-permute-done.rest_0_
  13.8 0.1 collective-permute-done.1.rest_1_
  13.9 0.7 %shard_map.116 = (f32[16,16,64]{2,1,0:T(8,128)S(1)}, f32[2,16,64]{2,1,0:T(8,128)S(1)}, f32[16,16,64]{2,1,0:T(8,128)S(1)}, f32[16,768]{1,0:T(8,128)S(1)}) custom-call(s32[1,4]{1,0:T(1,128)S(1)} %get-tuple-element.39.cmap, s32[4,8]{1,0:T(4,128)S(1)} %get-tuple-element.35.met, f32[4,512]{1,0:T(4,128)S(1)} %get-tuple-element.36.weights, ...), custom_call_target="tpu_custom_call" | custom-call | tf_op jit(solution)/shard_map/pallas_call | solution.py:335
  14.6 1.9 %all-gather.1 = f32[32,768]{1,0:T(8,128)S(1)} all-gather(f32[16,768]{1,0:T(8,128)S(1)} %get-tuple-element.52), channel_id=3, replica_groups=mesh['dam'=16,'sec'=2] {'sec'}, dimensions={0}, use_global_device_ids=true | all-gather | bytes 147456 | tf_op jit(solution)/shard_map/all_gather | solution.py:456
  16.5 0.2 shard_map.117
  16.6 0.7 %collective-permute-start.2 = (f32[16,512]{1,0:T(8,128)S(1)}, f32[16,512]{1,0:T(8,128)S(1)}, u32[]{:S(2)}, u32[]{:S(2)}) collective-permute-start(f32[16,512]{1,0:T(8,128)S(1)} %get-tuple-element.57), channel_id=1, source_target_pairs={{2,4},{6,8},{10,12},{14,16},{18,20},{22,24},{26,28},{4,2},{8,6},{1... | collective-permute-start | bytes 98312 | tf_op jit(solution)/shard_map/ppermute | solution.py:356
  17.3 4.5 %collective-permute-start.3 = (f32[16,512]{1,0:T(8,128)S(1)}, f32[16,512]{1,0:T(8,128)S(1)}, u32[]{:S(2)}, u32[]{:S(2)}) collective-permute-start(f32[16,512]{1,0:T(8,128)S(1)} %get-tuple-element.58), channel_id=1, source_target_pairs={{0,2},{4,6},{8,10},{12,14},{16,18},{20,22},{24,26},{28,30},{2,0},{... | collective-permute-start | bytes 98312 | tf_op jit(solution)/shard_map/ppermute | solution.py:356
  21.8 2.0 %shard_map.118 = (f32[16,16,64]{2,1,0:T(8,128)S(1)}, f32[16,1024]{1,0:T(8,128)S(1)}, f32[16,1024]{1,0:T(8,128)S(1)}) custom-call(s32[7,1,16]{2,1,0:T(1,128)S(1)} %get-tuple-element.37.cols_in, s32[4,8]{1,0:T(4,128)S(1)} %get-tuple-element.35.met, f32[4,512]{1,0:T(4,128)S(1)} %get-tuple-element.36.weights, f32[16,64]{1,0:T(8,128)S(1)} %get-tuple-element.38.capillary, ...), custom_call_target="tpu_custom_call" | custom-call | tf_op jit(solution)/shard_map/pallas_call | solution.py:335
  23.9 0.0 collective-permute-done.2.rest_0_
  23.9 0.1 collective-permute-done.3.rest_1_
  24.0 0.3 shard_map.119
  24.3 13.0 %all_to_all.8 = f32[32,1,64]{2,1,0:T(1,128)S(1)} all-to-all(f32[32,1,64]{2,1,0:T(1,128)S(1)} %broadcast_in_dim.11), channel_id=1, replica_groups=mesh['dam'=16,'sec'=2] {'dam','sec'}, dimensions={0} | all-to-all | bytes 16384 | tf_op jit(solution)/shard_map/all_to_all | solution.py:348
  37.3 1.0 %shard_map.120 = (f32[16,1024]{1,0:T(8,128)}, f32[16,1024]{1,0:T(8,128)}) custom-call(f32[32,64]{1,0:T(8,128)S(1)} %bitcast.22, f32[16,16,64]{2,1,0:T(8,128)S(1)} %get-tuple-element.61.nvec, f32[16,1024]{1,0:T(8,128)S(1)} %get-tuple-element.62.rflat, f32[16,1024]{1,0:T(8,128)S(1)} %get-tuple-element.63.zflat, f32[16,1024]{1,0:T(8,128)S(1)} %get-tuple-element.64.wflat, ...), custom_call_target="tpu_custom_call" | custom-call | tf_op jit(solution)/shard_map/pallas_call | solution.py:335
  (1 shorter events, 0.0 us)
Async XLA Ops:
  0.6 11.1 %copy-start = (f32[1,1,16,64,448]{4,3,2,1,0:T(8,128)S(1)}, f32[1,1,16,64,448]{4,3,2,1,0:T(8,128)}, u32[]{:S(2)}) copy-start(f32[1,1,16,64,448]{4,3,2,1,0:T(8,128)} %param.12) | copy-start | bytes 5505028
  5.4 8.4 %collective-permute-start = (f32[16,512]{1,0:T(8,128)S(1)}, f32[16,512]{1,0:T(8,128)S(1)}, u32[]{:S(2)}, u32[]{:S(2)}) collective-permute-start(f32[16,512]{1,0:T(8,128)S(1)} %get-tuple-element.48), channel_id=1, source_target_pairs={{2,4},{6,8},{10,12},{14,16},{18,20},{22,24},{26,28},{4,2},{8,6},{1... | collective-permute-start | bytes 98312 | tf_op jit(solution)/shard_map/ppermute | solution.py:356
  6.1 7.8 %collective-permute-start.1 = (f32[16,512]{1,0:T(8,128)S(1)}, f32[16,512]{1,0:T(8,128)S(1)}, u32[]{:S(2)}, u32[]{:S(2)}) collective-permute-start(f32[16,512]{1,0:T(8,128)S(1)} %get-tuple-element.49), channel_id=1, source_target_pairs={{0,2},{4,6},{8,10},{12,14},{16,18},{20,22},{24,26},{28,30},{2,0},{... | collective-permute-start | bytes 98312 | tf_op jit(solution)/shard_map/ppermute | solution.py:356
  16.6 7.2 %collective-permute-start.2 = (f32[16,512]{1,0:T(8,128)S(1)}, f32[16,512]{1,0:T(8,128)S(1)}, u32[]{:S(2)}, u32[]{:S(2)}) collective-permute-start(f32[16,512]{1,0:T(8,128)S(1)} %get-tuple-element.57), channel_id=1, source_target_pairs={{2,4},{6,8},{10,12},{14,16},{18,20},{22,24},{26,28},{4,2},{8,6},{1... | collective-permute-start | bytes 98312 | tf_op jit(solution)/shard_map/ppermute | solution.py:356
  17.3 6.7 %collective-permute-start.3 = (f32[16,512]{1,0:T(8,128)S(1)}, f32[16,512]{1,0:T(8,128)S(1)}, u32[]{:S(2)}, u32[]{:S(2)}) collective-permute-start(f32[16,512]{1,0:T(8,128)S(1)} %get-tuple-element.58), channel_id=1, source_target_pairs={{0,2},{4,6},{8,10},{12,14},{16,18},{20,22},{24,26},{28,30},{2,0},{... | collective-permute-start | bytes 98312 | tf_op jit(solution)/shard_map/ppermute | solution.py:356

commit v11 on v10

--- a/solution.py
+++ b/solution.py
@@ -11,6 +11,7 @@
 BF16 = jnp.bfloat16
 VMEM_LIMIT = 16 * 1024 * 1024
 LANES = 128
+PIECES = 4
 
 
 def halves(x):
@@ -44,6 +45,14 @@
     for copy in copies:
         copy.start()
     return [copy.wait for copy in copies]
+
+
+def pieces(source, target, count):
+    step = source.shape[0] // count
+    return [
+        (source.at[i * step : (i + 1) * step], target.at[i * step : (i + 1) * step])
+        for i in range(count)
+    ]
 
 
 def face_order(pair):
@@ -189,14 +198,14 @@
             (mask_in, mask),
             (cmap_in, cmap),
             (fmap_in, fmap),
-            (blocks_in, blocks),
-            (rows_in, rows),
             (cmap_in, cmap_row),
             (fmap_in, fmap_rows),
             (weights_in, weights),
             (cols_in, cols),
             (tang_in, tang),
-        ],
+        ]
+        + pieces(blocks_in, blocks, PIECES)
+        + pieces(rows_in, rows, PIECES),
         sems,
     )
     nblk, ncol, bdof = rvec.shape
@@ -214,7 +223,7 @@
                 payload[ncol + n : ncol + n + 1, p * bdof : (p + 1) * bdof] = jnp.full(
                     (1, bdof), jnp.where(corner == b, 1.0, 0.0), F32
                 )
-    for wait in waits[:2] + waits[4:]:
+    for wait in waits[:2]:
         wait()
     scale = mask[...].astype(F32)
     scale = jnp.concatenate([scale] * (LANES // ncol), axis=1)
@@ -224,8 +233,12 @@
         rvec.shape,
         rvec,
     )
+    for wait in waits[9 : 9 + PIECES]:
+        wait()
     split_blocks(blocks, tiles_high, tiles_low)
     apply_blocks(rvec, tiles_high, tiles_low, left, base)
+    for wait in waits[9 + PIECES :] + waits[4:9]:
+        wait()
     offer(pair, corners, across, rvec, rows, base, payload)
     cmap_out[...] = cmap_row[0]
     for i, face in enumerate(order):
@@ -234,20 +247,27 @@
 
 
 def local_kernel(
-    cols_in, met, weights, capillary, field, other, stiff, out, flat, other_flat, *scratch
+    first, cols_in, met, weights, capillary, field, other, stiff, out, flat, other_flat, *scratch
 ):
-    left, cols, sems = scratch
+    left, cols, sems = scratch[-3:]
+    copies = [(cols_in, cols)]
+    if first:
+        copies += pieces(stiff, scratch[0], 2 * PIECES)
+        stiff = scratch[0]
     nblk, ncol, bdof = field.shape
-    (wait,) = fetch([(cols_in, cols)], sems)
+    waits = fetch(copies, sems)
     where = listed(met)
     flatten(lambda first, last: field[first:last], field.shape, flat)
     flatten(lambda first, last: other[first:last], field.shape, other_flat)
     kept = stiff.shape[2] // bdof
     for b in range(nblk):
         left[b] = stack(field[b])
-    wait()
-    group = 4
+    waits.pop(0)()
+    group = nblk // PIECES
     for t in range(0, nblk, group):
+        for wait in waits[:2]:
+            wait()
+        waits = waits[2:]
         gathered = [
             jnp.concatenate([left[cols[k, 0, t + j]] for k in range(kept)], axis=1)
             for j in range(group)
@@ -328,18 +348,18 @@
         res[:, here] = rflat[:, here] - both * wflat[:, here] + second * res[:, here]
 
 
-def call(kernel, outs, scratch, args, space=pltpu.VMEM):
+def call(kernel, outs, scratch, args, far=()):
     vmem = pl.BlockSpec(memory_space=pltpu.VMEM)
-    if space != pltpu.VMEM:
-        args = [pltpu.with_memory_space_constraint(arg, space) for arg in args]
+    hbm = pl.BlockSpec(memory_space=pltpu.HBM)
+    far = [pltpu.with_memory_space_constraint(arg, pltpu.HBM) for arg in far]
     return pl.pallas_call(
         kernel,
         out_shape=outs,
-        in_specs=[pl.BlockSpec(memory_space=space)] * len(args),
+        in_specs=[vmem] * len(args) + [hbm] * len(far),
         out_specs=jax.tree.map(lambda _: vmem, outs),
         scratch_shapes=scratch,
         compiler_params=pltpu.CompilerParams(vmem_limit_bytes=VMEM_LIMIT),
-    )(*args)
+    )(*args, *far)
 
 
 def everywhere(values):
@@ -419,10 +439,10 @@
             hold(face_map),
             hold(weights),
             halved,
-            sems(11),
+            sems(9 + 2 * PIECES),
         ],
+        (),
         (load, mask, corner_map, face_map, blocks, rows, cols, weights, tang),
-        pltpu.HBM,
     )
 
     def finish(base, shares, marks):
@@ -436,17 +456,18 @@
         besides += faces[2:] if pair else exchange(faces[2:], "sec")
         return vec, besides
 
-    def local(vec, other):
+    def local(vec, other, near, far):
         return call(
-            local_kernel,
-            (field, flat, flat),
-            [pltpu.VMEM((nblk, 2 * ncol, bdof), BF16), index(cols), sems(1)],
-            (cols, met, weights, tang, vec, other, stiffness[0, 0]),
+            functools.partial(local_kernel, bool(far)),
+            (field, flat, flat) + tuple(like(a) for a in far),
+            [pltpu.VMEM((nblk, 2 * ncol, bdof), BF16), index(cols), sems(1 + 2 * PIECES)],
+            (cols, met, weights, tang, vec, other) + near,
+            far,
         )
 
     marks = lax.all_gather(payload, "sec")
     zvec, besides = finish(base, marks, marks)
-    part, zflat, rflat = local(zvec, rvec)
+    part, zflat, rflat, stiff = local(zvec, rvec, (), (stiffness[0, 0],))
     wvec, sums, base, payload = call(
         functools.partial(image_kernel, pair),
         (field, shape(2, ncol, bdof), field, shape(ncol, lane)),
@@ -454,7 +475,7 @@
         (cmap, met, weights, part, rvec, zvec, high, low, rows, *besides),
     )
     mvec, besides = finish(base, lax.all_gather(payload, "sec"), marks)
-    part, mflat, wflat = local(mvec, wvec)
+    part, mflat, wflat = local(mvec, wvec, (stiff,), ())
     nvec, totals = call(
         last_kernel,
         (field, shape(1, 4 * ncol)),

time: 38.5 us -> 38.3 us (level)
  Pallas kernels: 9.04 us -> 10 us
  blocking collectives: 16.9 us -> 16.1 us
    pallas_call x8, Pallas kernels: 9.04 us -> 10 us  [call(): pl.pallas_call(kernel, out_shape=outs, in_specs=[vmem] * len(args) + [hbm...]
    all_to_all x1, blocking collectives: 13 us -> 12.2 us  [everywhere(): return lax.all_to_all(copies, ('dam', 'sec'), split_axis=0, concat_axis=0)]
  transfers between devices with their start and end apart: 4 -> 4, of which waited for: 2 -> 0; matrix products, arithmetic and copies ran while one was open for 0% -> 0% of each run, Pallas kernels for 11% -> 14%
where the time goes in v11:
time: 38.3 us; the launch traced here: 38.1 us
  blocking collectives  16.1 us (42%)
  starting transfers between devices  11.2 us (29%)
  Pallas kernels  10 us (26%)
  between operations  0.71 us (2%)
    all_to_all x1, blocking collectives, everywhere(): return lax.all_to_all(copies, ('dam', 'sec'), split_axis=0, concat_axis=0)  12.2 us
    ppermute x4, starting transfers between devices, exchange(): got.append(lax.ppermute(send, axis, pairs + [(j, i) for i, j in pairs]))  11.2 us
    pallas_call x8, Pallas kernels, call(): pl.pallas_call(kernel, out_shape=outs, in_specs=[vmem] * len(args) + [hbm...  10 us
    all_gather x1, blocking collectives, shards(): marks = lax.all_gather(payload, 'sec')  2.01 us
    all_gather x1, blocking collectives, shards(): mvec, besides = finish(base, lax.all_gather(payload, 'sec'), marks)  1.87 us
  transfers between devices with their start and end apart: 4, of which 0 were waited for; matrix products, arithmetic and copies ran while one was open for 0% of the time, Pallas kernels for 14%

profile of v11, /device:TPU:0, one launch (start us, length us, event | category | flops | bytes accessed | tf_op | source)
XLA Modules:
  0.0 38.1 jit_solution(15259009410236195314)
XLA Ops:
  0.6 2.4 %shard_map.113 = (f32[16,16,64]{2,1,0:T(8,128)S(1)}, f32[16,16,64]{2,1,0:T(8,128)S(1)}, f32[24,768]{1,0:T(8,128)S(1)}, bf16[4,256,256]{2,1,0:T(8,128)(2,1)S(1)},...) custom-call(f32[16,1024]{1,0:T(8,128)} %bitcast.25, ...), custom_call_target="tpu_custom_call" | custom-call | tf_op jit(solution)/shard_map/pallas_call | solution.py:355
  3.0 2.0 %all-gather = f32[48,768]{1,0:T(8,128)S(1)} all-gather(f32[24,768]{1,0:T(8,128)S(1)} %get-tuple-element.43), channel_id=2, replica_groups=mesh['dam'=16,'sec'=2] {'sec'}, dimensions={0}, use_global_device_ids=true | all-gather | bytes 221184 | tf_op jit(solution)/shard_map/all_gather | solution.py:468
  5.0 0.2 shard_map.114
  5.2 0.7 %collective-permute-start = (f32[16,512]{1,0:T(8,128)S(1)}, f32[16,512]{1,0:T(8,128)S(1)}, u32[]{:S(2)}, u32[]{:S(2)}) collective-permute-start(f32[16,512]{1,0:T(8,128)S(1)} %get-tuple-element.49), channel_id=1, source_target_pairs={{2,4},{6,8},{10,12},{14,16},{18,20},{22,24},{26,28},{4,2},{8,6},{1... | collective-permute-start | bytes 98312 | tf_op jit(solution)/shard_map/ppermute | solution.py:376
  5.9 5.6 %collective-permute-start.1 = (f32[16,512]{1,0:T(8,128)S(1)}, f32[16,512]{1,0:T(8,128)S(1)}, u32[]{:S(2)}, u32[]{:S(2)}) collective-permute-start(f32[16,512]{1,0:T(8,128)S(1)} %get-tuple-element.50), channel_id=1, source_target_pairs={{0,2},{4,6},{8,10},{12,14},{16,18},{20,22},{24,26},{28,30},{2,0},{... | collective-permute-start | bytes 98312 | tf_op jit(solution)/shard_map/ppermute | solution.py:376
  11.5 3.1 %shard_map.115 = (f32[16,16,64]{2,1,0:T(8,128)S(1)}, f32[16,1024]{1,0:T(8,128)S(1)}, f32[16,1024]{1,0:T(8,128)S(1)}, f32[16,64,448]{2,1,0:T(8,128)S(1)}) custom-call(s32[7,1,16]{2,1,0:T(1,128)S(1)} %get-tuple-element.38.cols_in, s32[4,8]{1,0:T(4,128)S(1)} %get-tuple-element.36.met, f32[4,512]{1,0:T(4,128)S(1)} %get-tuple-element.37.weights, ...), custom_call_target="tpu_custom_call" | custom-call | tf_op jit(solution)/shard_map/pallas_call | solution.py:355
  14.6 0.0 collective-permute-done.rest_0_
  14.7 0.0 collective-permute-done.1.rest_1_
  14.7 0.7 %shard_map.116 = (f32[16,16,64]{2,1,0:T(8,128)S(1)}, f32[2,16,64]{2,1,0:T(8,128)S(1)}, f32[16,16,64]{2,1,0:T(8,128)S(1)}, f32[16,768]{1,0:T(8,128)S(1)}) custom-call(s32[1,4]{1,0:T(1,128)S(1)} %get-tuple-element.40.cmap, s32[4,8]{1,0:T(4,128)S(1)} %get-tuple-element.36.met, f32[4,512]{1,0:T(4,128)S(1)} %get-tuple-element.37.weights, ...), custom_call_target="tpu_custom_call" | custom-call | tf_op jit(solution)/shard_map/pallas_call | solution.py:355
  15.4 1.9 %all-gather.1 = f32[32,768]{1,0:T(8,128)S(1)} all-gather(f32[16,768]{1,0:T(8,128)S(1)} %get-tuple-element.53), channel_id=3, replica_groups=mesh['dam'=16,'sec'=2] {'sec'}, dimensions={0}, use_global_device_ids=true | all-gather | bytes 147456 | tf_op jit(solution)/shard_map/all_gather | solution.py:477
  17.3 0.2 shard_map.117
  17.4 0.7 %collective-permute-start.2 = (f32[16,512]{1,0:T(8,128)S(1)}, f32[16,512]{1,0:T(8,128)S(1)}, u32[]{:S(2)}, u32[]{:S(2)}) collective-permute-start(f32[16,512]{1,0:T(8,128)S(1)} %get-tuple-element.59), channel_id=1, source_target_pairs={{2,4},{6,8},{10,12},{14,16},{18,20},{22,24},{26,28},{4,2},{8,6},{1... | collective-permute-start | bytes 98312 | tf_op jit(solution)/shard_map/ppermute | solution.py:376
  18.1 4.3 %collective-permute-start.3 = (f32[16,512]{1,0:T(8,128)S(1)}, f32[16,512]{1,0:T(8,128)S(1)}, u32[]{:S(2)}, u32[]{:S(2)}) collective-permute-start(f32[16,512]{1,0:T(8,128)S(1)} %get-tuple-element.60), channel_id=1, source_target_pairs={{0,2},{4,6},{8,10},{12,14},{16,18},{20,22},{24,26},{28,30},{2,0},{... | collective-permute-start | bytes 98312 | tf_op jit(solution)/shard_map/ppermute | solution.py:376
  22.4 2.1 %shard_map.118 = (f32[16,16,64]{2,1,0:T(8,128)S(1)}, f32[16,1024]{1,0:T(8,128)S(1)}, f32[16,1024]{1,0:T(8,128)S(1)}) custom-call(s32[7,1,16]{2,1,0:T(1,128)S(1)} %get-tuple-element.38.cols_in, s32[4,8]{1,0:T(4,128)S(1)} %get-tuple-element.36.met, f32[4,512]{1,0:T(4,128)S(1)} %get-tuple-element.37.weights, f32[16,64]{1,0:T(8,128)S(1)} %get-tuple-element.39.capillary, ...), custom_call_target="tpu_custom_call" | custom-call | tf_op jit(solution)/shard_map/pallas_call | solution.py:355
  24.5 0.0 collective-permute-done.2.rest_0_
  24.5 0.0 collective-permute-done.3.rest_1_
  24.6 0.3 shard_map.119
  24.9 12.2 %all_to_all.8 = f32[32,1,64]{2,1,0:T(1,128)S(1)} all-to-all(f32[32,1,64]{2,1,0:T(1,128)S(1)} %broadcast_in_dim.11), channel_id=1, replica_groups=mesh['dam'=16,'sec'=2] {'dam','sec'}, dimensions={0} | all-to-all | bytes 16384 | tf_op jit(solution)/shard_map/all_to_all | solution.py:368
  37.1 1.0 %shard_map.120 = (f32[16,1024]{1,0:T(8,128)}, f32[16,1024]{1,0:T(8,128)}) custom-call(f32[32,64]{1,0:T(8,128)S(1)} %bitcast.20, f32[16,16,64]{2,1,0:T(8,128)S(1)} %get-tuple-element.63.nvec, f32[16,1024]{1,0:T(8,128)S(1)} %get-tuple-element.64.rflat, f32[16,1024]{1,0:T(8,128)S(1)} %get-tuple-element.65.zflat, f32[16,1024]{1,0:T(8,128)S(1)} %get-tuple-element.66.wflat, ...), custom_call_target="tpu_custom_call" | custom-call | tf_op jit(solution)/shard_map/pallas_call | solution.py:355
  (1 shorter events, 0.0 us)
Async XLA Ops:
  5.2 9.4 %collective-permute-start = (f32[16,512]{1,0:T(8,128)S(1)}, f32[16,512]{1,0:T(8,128)S(1)}, u32[]{:S(2)}, u32[]{:S(2)}) collective-permute-start(f32[16,512]{1,0:T(8,128)S(1)} %get-tuple-element.49), channel_id=1, source_target_pairs={{2,4},{6,8},{10,12},{14,16},{18,20},{22,24},{26,28},{4,2},{8,6},{1... | collective-permute-start | bytes 98312 | tf_op jit(solution)/shard_map/ppermute | solution.py:376
  5.9 8.8 %collective-permute-start.1 = (f32[16,512]{1,0:T(8,128)S(1)}, f32[16,512]{1,0:T(8,128)S(1)}, u32[]{:S(2)}, u32[]{:S(2)}) collective-permute-start(f32[16,512]{1,0:T(8,128)S(1)} %get-tuple-element.50), channel_id=1, source_target_pairs={{0,2},{4,6},{8,10},{12,14},{16,18},{20,22},{24,26},{28,30},{2,0},{... | collective-permute-start | bytes 98312 | tf_op jit(solution)/shard_map/ppermute | solution.py:376
  17.4 7.1 %collective-permute-start.2 = (f32[16,512]{1,0:T(8,128)S(1)}, f32[16,512]{1,0:T(8,128)S(1)}, u32[]{:S(2)}, u32[]{:S(2)}) collective-permute-start(f32[16,512]{1,0:T(8,128)S(1)} %get-tuple-element.59), channel_id=1, source_target_pairs={{2,4},{6,8},{10,12},{14,16},{18,20},{22,24},{26,28},{4,2},{8,6},{1... | collective-permute-start | bytes 98312 | tf_op jit(solution)/shard_map/ppermute | solution.py:376
  18.1 6.4 %collective-permute-start.3 = (f32[16,512]{1,0:T(8,128)S(1)}, f32[16,512]{1,0:T(8,128)S(1)}, u32[]{:S(2)}, u32[]{:S(2)}) collective-permute-start(f32[16,512]{1,0:T(8,128)S(1)} %get-tuple-element.60), channel_id=1, source_target_pairs={{0,2},{4,6},{8,10},{12,14},{16,18},{20,22},{24,26},{28,30},{2,0},{... | collective-permute-start | bytes 98312 | tf_op jit(solution)/shard_map/ppermute | solution.py:376

commit v12 on v11

--- a/solution.py
+++ b/solution.py
@@ -121,37 +121,37 @@
     pack(base, across, payload)
 
 
-def end_kernel(pair, cmap, met, base, rows, shares, marks, zout, *faces):
+def end_kernel(pair, cmap, met, base, rows, shares, zout, *faces):
     nblk, ncol, bdof = base.shape
     (corners,) = listed(cmap)
     where = listed(met)
     wide = len(corners) * bdof
     zout[...] = base[...]
     if pair:
-        me = lax.axis_index("sec")
         at = len(where[0]) * bdof
-        correct = shares[pl.ds(1 - me, 1), :ncol, at:][0]
-        theirs = shares[pl.ds(me, 1), :ncol, at:][0]
-        chunk = 2 * bdof
-        twice = [
-            jnp.concatenate([lane_piece(theirs, n, bdof)] * 2, axis=1)
-            for n in range(len(corners))
-        ]
-        for j in range(at // chunk):
-            here = slice(j * chunk, (j + 1) * chunk)
-            value = shares[pl.ds(1 - me, 1), :ncol, here][0]
-            for n in range(len(corners)):
-                mark = marks[pl.ds(1 - me, 1), ncol + n : ncol + n + 1, here][0]
-                value = value + mark * twice[n]
-            faces[-1][:, here] = value
+        correct = shares[pl.ds(1 - lax.axis_index("sec"), 1), :ncol, at:][0]
     else:
         correct = 0.0
         for s in range(shares.shape[0]):
             high, low = halves(rows[:, s * wide : (s + 1) * wide])
             correct = correct + three_pass(dot_t, stack(shares[s]), high, low)
     add_pieces(zout, corners, lambda n, b: lane_piece(correct, n, bdof))
-    for blocks, out in zip(where, faces[: 2 if pair else 4]):
+    for blocks, out in zip(where, faces):
         pack(zout, blocks, out)
+
+
+def face_across(shares, labels, nface, shape, out):
+    nblk, ncol, bdof = shape
+    at = nface * bdof
+    me = lax.axis_index("sec")
+    names = labels[pl.ds(1 - me, 1), ncol : ncol + 2, : LANES][0]
+    for p in range(nface):
+        value = shares[pl.ds(1 - me, 1), :ncol, p * bdof : (p + 1) * bdof][0]
+        for n in range((shares.shape[2] - at) // bdof):
+            here = slice(at + n * bdof, at + (n + 1) * bdof)
+            same = jnp.where(names[0, n] == names[1, p], 1.0, 0.0)
+            value = value + same * shares[pl.ds(me, 1), :ncol, here][0]
+        out[:, p * bdof : (p + 1) * bdof] = value
 
 
 def swap_groups(x, ncol):
@@ -216,13 +216,6 @@
     waits[3]()
     corners = [cmap[0, 0, n] for n in range(cmap.shape[2])]
     across = [fmap[0, 0, order[2], p] for p in range(fmap.shape[3])]
-    if pair:
-        payload[ncol:, :] = jnp.zeros_like(payload[ncol:, :])
-        for n, corner in enumerate(corners):
-            for p, b in enumerate(across):
-                payload[ncol + n : ncol + n + 1, p * bdof : (p + 1) * bdof] = jnp.full(
-                    (1, bdof), jnp.where(corner == b, 1.0, 0.0), F32
-                )
     for wait in waits[:2]:
         wait()
     scale = mask[...].astype(F32)
@@ -241,33 +234,35 @@
         wait()
     offer(pair, corners, across, rvec, rows, base, payload)
     cmap_out[...] = cmap_row[0]
+    if pair:
+        payload[ncol:, :] = jnp.zeros_like(payload[ncol:, :])
+        payload[ncol : ncol + 1, : len(corners)] = cmap_row[0].astype(F32)
+        payload[ncol + 1 : ncol + 2, : len(across)] = fmap_rows[
+            0, 0, pl.ds(order[2], 1), :
+        ].astype(F32)
     for i, face in enumerate(order):
         met[i : i + 1, :] = fmap_rows[0, 0, pl.ds(face, 1), :]
         wmet[i : i + 1, :] = weights[pl.ds(face, 1), :]
 
 
 def local_kernel(
-    first, cols_in, met, weights, capillary, field, other, stiff, out, flat, other_flat, *scratch
+    pair, cols_in, met, weights, capillary, field, other, stiff, shares, labels, *rest
 ):
-    left, cols, sems = scratch[-3:]
-    copies = [(cols_in, cols)]
-    if first:
-        copies += pieces(stiff, scratch[0], 2 * PIECES)
-        stiff = scratch[0]
+    out, sums, flat, other_flat, *across, left, cols, sems = rest
     nblk, ncol, bdof = field.shape
-    waits = fetch(copies, sems)
+    (wait,) = fetch([(cols_in, cols)], sems)
     where = listed(met)
+    if pair:
+        face_across(shares, labels, len(where[2]), field.shape, across[0])
+    sums[...] = lanes(field, other)
     flatten(lambda first, last: field[first:last], field.shape, flat)
     flatten(lambda first, last: other[first:last], field.shape, other_flat)
     kept = stiff.shape[2] // bdof
     for b in range(nblk):
         left[b] = stack(field[b])
-    waits.pop(0)()
-    group = nblk // PIECES
+    wait()
+    group = 4
     for t in range(0, nblk, group):
-        for wait in waits[:2]:
-            wait()
-        waits = waits[2:]
         gathered = [
             jnp.concatenate([left[cols[k, 0, t + j]] for k in range(kept)], axis=1)
             for j in range(group)
@@ -301,7 +296,7 @@
 
 
 def image_kernel(
-    pair, cmap, met, weights, local, rvec, zvec, tiles_high, tiles_low, rows, *rest
+    pair, cmap, met, weights, local, zvec, tiles_high, tiles_low, rows, *rest
 ):
     count = 3 if pair else 4
     besides, (wout, sums, base, payload, left) = rest[:count], rest[count:]
@@ -309,16 +304,15 @@
     where = couple(met, weights, local, besides, wout)
     apply_blocks(wout, tiles_high, tiles_low, left, base)
     offer(pair, corners, where[2], wout, rows, base, payload)
-    sums[0] = lanes(rvec, zvec)
-    sums[1] = lanes(zvec, wout)
-
-
-def last_kernel(met, weights, local, wvec, mvec, sums, *rest):
+    sums[...] = lanes(zvec, wout)
+
+
+def last_kernel(met, weights, local, rvec, zvec, mvec, gamma, delta, mu, *rest):
     *besides, nout, totals = rest
+    rm = lanes(rvec, mvec)
     couple(met, weights, local, besides, nout)
-    parts = jnp.concatenate(
-        [sums[0], sums[1], lanes(wvec, mvec), lanes(mvec, nout)], axis=0
-    )
+    parts = [gamma[...], delta[...], mu[...], rm, lanes(mvec, nout), lanes(zvec, nout)]
+    parts = jnp.concatenate(parts, axis=0)
     totals[...] = lax.dot_general(
         jnp.ones((1, parts.shape[1]), F32),
         parts,
@@ -332,11 +326,11 @@
     nblk, ncol, bdof = nvec.shape
     flatten(lambda first, last: nvec[first:last], nvec.shape, res)
     total = jnp.sum(shares[...], axis=0, keepdims=True)
-    gamma, delta, mu, nu = [total[:, q * ncol : (q + 1) * ncol] for q in range(4)]
+    gamma, delta, mu, rm, nu, zn = [total[:, q * ncol : (q + 1) * ncol] for q in range(6)]
     alpha = gamma / delta
-    gnew = gamma - 2.0 * alpha * delta + alpha * alpha * mu
+    gnew = gamma - alpha * (delta + rm) + alpha * alpha * mu
     grow = 1.0 + gnew / gamma
-    dnew = grow * grow * delta - 2.0 * alpha * grow * mu + alpha * alpha * nu
+    dnew = grow * grow * delta - alpha * grow * (mu + zn) + alpha * alpha * nu
     anew = gnew / dnew
     both, second = [
         jnp.concatenate([x] * (LANES // ncol), axis=1)
@@ -445,42 +439,41 @@
         (load, mask, corner_map, face_map, blocks, rows, cols, weights, tang),
     )
 
-    def finish(base, shares, marks):
+    def finish(base, shares):
         vec, *faces = call(
             functools.partial(end_kernel, pair),
-            (field,) + (face,) * (3 if pair else 4),
+            (field,) + (face,) * (2 if pair else 4),
             [],
-            (cmap, met, base, rows, shares, marks),
+            (cmap, met, base, rows, shares),
         )
-        besides = exchange(faces[:2], "dam")
-        besides += faces[2:] if pair else exchange(faces[2:], "sec")
-        return vec, besides
-
-    def local(vec, other, near, far):
-        return call(
-            functools.partial(local_kernel, bool(far)),
-            (field, flat, flat) + tuple(like(a) for a in far),
-            [pltpu.VMEM((nblk, 2 * ncol, bdof), BF16), index(cols), sems(1 + 2 * PIECES)],
-            (cols, met, weights, tang, vec, other) + near,
-            far,
+        return vec, exchange(faces[:2], "dam"), exchange(faces[2:], "sec")
+
+    def local(vec, other, shares, labels):
+        part, sums, *rest = call(
+            functools.partial(local_kernel, pair),
+            (field, shape(ncol, bdof), flat, flat) + ((face,) if pair else ()),
+            [pltpu.VMEM((nblk, 2 * ncol, bdof), BF16), index(cols), sems(1)],
+            (cols, met, weights, tang, vec, other, stiffness[0, 0], shares, labels),
         )
-
-    marks = lax.all_gather(payload, "sec")
-    zvec, besides = finish(base, marks, marks)
-    part, zflat, rflat, stiff = local(zvec, rvec, (), (stiffness[0, 0],))
-    wvec, sums, base, payload = call(
+        return part, sums, *rest[:2], rest[2:]
+
+    shares = labels = lax.all_gather(payload, "sec")
+    zvec, besides, beyond = finish(base, shares)
+    part, gamma, zflat, rflat, across = local(zvec, rvec, shares, labels)
+    wvec, delta, base, payload = call(
         functools.partial(image_kernel, pair),
-        (field, shape(2, ncol, bdof), field, shape(ncol, lane)),
+        (field, shape(ncol, bdof), field, shape(ncol, lane)),
         [halved],
-        (cmap, met, weights, part, rvec, zvec, high, low, rows, *besides),
-    )
-    mvec, besides = finish(base, lax.all_gather(payload, "sec"), marks)
-    part, mflat, wflat = local(mvec, wvec, (stiff,), ())
+        (cmap, met, weights, part, zvec, high, low, rows, *besides, *beyond, *across),
+    )
+    shares = lax.all_gather(payload, "sec")
+    mvec, besides, beyond = finish(base, shares)
+    part, mu, mflat, wflat, across = local(mvec, wvec, shares, labels)
     nvec, totals = call(
         last_kernel,
-        (field, shape(1, 4 * ncol)),
+        (field, shape(1, 6 * ncol)),
         [],
-        (met, weights, part, wvec, mvec, sums, *besides),
+        (met, weights, part, rvec, zvec, mvec, gamma, delta, mu, *besides, *beyond, *across),
     )
     sol, res = call(
         finish_kernel,

time: 38.3 us -> 38.5 us (level)
  Pallas kernels: 10 us -> 8.56 us
  blocking collectives: 16.1 us -> 16.8 us
  waiting for transfers between devices: 0.04 us -> 0.61 us
    pallas_call x8, Pallas kernels: 10 us -> 8.56 us  [call(): pl.pallas_call(kernel, out_shape=outs, in_specs=[vmem] * len(args) + [hbm...]
    all_to_all x1, blocking collectives: 12.2 us -> 13 us  [everywhere(): return lax.all_to_all(copies, ('dam', 'sec'), split_axis=0, concat_axis=0)]
    ppermute x4, waiting for transfers between devices: 0.04 us -> 0.61 us  [exchange(): got.append(lax.ppermute(send, axis, pairs + [(j, i) for i, j in pairs]))]
  transfers between devices with their start and end apart: 4 -> 4, of which waited for: 0 -> 2; matrix products, arithmetic and copies ran while one was open for 0% -> 0% of each run, Pallas kernels for 14% -> 10%
where the time goes in v12:
time: 38.5 us; the launch traced here: 38.2 us
  blocking collectives  16.8 us (44%)
  starting transfers between devices  11.5 us (30%)
  Pallas kernels  8.56 us (22%)
  between operations  0.71 us (2%)
  waiting for transfers between devices  0.61 us (2%)
    all_to_all x1, blocking collectives, everywhere(): return lax.all_to_all(copies, ('dam', 'sec'), split_axis=0, concat_axis=0)  13 us
    ppermute x4, starting transfers between devices, exchange(): got.append(lax.ppermute(send, axis, pairs + [(j, i) for i, j in pairs]))  11.5 us
    pallas_call x8, Pallas kernels, call(): pl.pallas_call(kernel, out_shape=outs, in_specs=[vmem] * len(args) + [hbm...  8.56 us
    all_gather x1, blocking collectives, shards(): shares = labels = lax.all_gather(payload, 'sec')  2.01 us
    all_gather x1, blocking collectives, shards(): shares = lax.all_gather(payload, 'sec')  1.87 us
  transfers between devices with their start and end apart: 4, of which 2 were waited for; matrix products, arithmetic and copies ran while one was open for 0% of the time, Pallas kernels for 10%

profile of v12, /device:TPU:0, one launch (start us, length us, event | category | flops | bytes accessed | tf_op | source)
XLA Modules:
  0.0 38.2 jit_solution(4650641501844679248)
XLA Ops:
  0.6 0.0 copy-start
  0.6 2.5 %shard_map.113 = (f32[16,16,64]{2,1,0:T(8,128)S(1)}, f32[16,16,64]{2,1,0:T(8,128)S(1)}, f32[24,768]{1,0:T(8,128)S(1)}, bf16[4,256,256]{2,1,0:T(8,128)(2,1)S(1)},...) custom-call(f32[16,1024]{1,0:T(8,128)} %bitcast.28, ...), custom_call_target="tpu_custom_call" | custom-call | tf_op jit(solution)/shard_map/pallas_call | solution.py:349
  3.1 2.0 %all-gather = f32[48,768]{1,0:T(8,128)S(1)} all-gather(f32[24,768]{1,0:T(8,128)S(1)} %get-tuple-element.44), channel_id=2, replica_groups=mesh['dam'=16,'sec'=2] {'sec'}, dimensions={0}, use_global_device_ids=true | all-gather | bytes 221184 | tf_op jit(solution)/shard_map/all_gather | solution.py:460
  5.2 0.2 shard_map.114
  5.3 0.7 %collective-permute-start = (f32[16,512]{1,0:T(8,128)S(1)}, f32[16,512]{1,0:T(8,128)S(1)}, u32[]{:S(2)}, u32[]{:S(2)}) collective-permute-start(f32[16,512]{1,0:T(8,128)S(1)} %get-tuple-element.50), channel_id=1, source_target_pairs={{2,4},{6,8},{10,12},{14,16},{18,20},{22,24},{26,28},{4,2},{8,6},{1... | collective-permute-start | bytes 98312 | tf_op jit(solution)/shard_map/ppermute | solution.py:370
  6.0 5.6 %collective-permute-start.1 = (f32[16,512]{1,0:T(8,128)S(1)}, f32[16,512]{1,0:T(8,128)S(1)}, u32[]{:S(2)}, u32[]{:S(2)}) collective-permute-start(f32[16,512]{1,0:T(8,128)S(1)} %get-tuple-element.51), channel_id=1, source_target_pairs={{0,2},{4,6},{8,10},{12,14},{16,18},{20,22},{24,26},{28,30},{2,0},{... | collective-permute-start | bytes 98312 | tf_op jit(solution)/shard_map/ppermute | solution.py:370
  11.7 0.0 copy-done
  11.7 1.8 %shard_map.115 = (f32[16,16,64]{2,1,0:T(8,128)S(1)}, f32[16,64]{1,0:T(8,128)S(1)}, f32[16,1024]{1,0:T(8,128)S(1)}, f32[16,1024]{1,0:T(8,128)S(1)}, f32[16,512]{1,0:T(8,128)S(1)}) custom-call(s32[7,1,16]{2,1,0:T(1,128)S(1)} %get-tuple-element.39.cols_in, s32[4,8]{1,0:T(4,128)S(1)} %get-tuple-element.37.met, f32[4,512]{1,0:T(4,128)S(1)} %get-tuple-element.38.weights, ...), custom_call_target="tpu_custom_call" | custom-call | tf_op jit(solution)/shard_map/pallas_call | solution.py:349
  13.5 0.0 collective-permute-done.rest_0_
  13.5 0.3 collective-permute-done.1.rest_1_
  13.8 0.7 %shard_map.116 = (f32[16,16,64]{2,1,0:T(8,128)S(1)}, f32[16,64]{1,0:T(8,128)S(1)}, f32[16,16,64]{2,1,0:T(8,128)S(1)}, f32[16,768]{1,0:T(8,128)S(1)}) custom-call(s32[1,4]{1,0:T(1,128)S(1)} %get-tuple-element.41.cmap, s32[4,8]{1,0:T(4,128)S(1)} %get-tuple-element.37.met, f32[4,512]{1,0:T(4,128)S(1)} %get-tuple-element.38.weights, ...), custom_call_target="tpu_custom_call" | custom-call | tf_op jit(solution)/shard_map/pallas_call | solution.py:349
  14.5 1.9 %all-gather.1 = f32[32,768]{1,0:T(8,128)S(1)} all-gather(f32[16,768]{1,0:T(8,128)S(1)} %get-tuple-element.54), channel_id=3, replica_groups=mesh['dam'=16,'sec'=2] {'sec'}, dimensions={0}, use_global_device_ids=true | all-gather | bytes 147456 | tf_op jit(solution)/shard_map/all_gather | solution.py:469
  16.4 0.2 shard_map.117
  16.6 0.7 %collective-permute-start.2 = (f32[16,512]{1,0:T(8,128)S(1)}, f32[16,512]{1,0:T(8,128)S(1)}, u32[]{:S(2)}, u32[]{:S(2)}) collective-permute-start(f32[16,512]{1,0:T(8,128)S(1)} %get-tuple-element.61), channel_id=1, source_target_pairs={{2,4},{6,8},{10,12},{14,16},{18,20},{22,24},{26,28},{4,2},{8,6},{1... | collective-permute-start | bytes 98312 | tf_op jit(solution)/shard_map/ppermute | solution.py:370
  17.2 4.5 %collective-permute-start.3 = (f32[16,512]{1,0:T(8,128)S(1)}, f32[16,512]{1,0:T(8,128)S(1)}, u32[]{:S(2)}, u32[]{:S(2)}) collective-permute-start(f32[16,512]{1,0:T(8,128)S(1)} %get-tuple-element.62), channel_id=1, source_target_pairs={{0,2},{4,6},{8,10},{12,14},{16,18},{20,22},{24,26},{28,30},{2,0},{... | collective-permute-start | bytes 98312 | tf_op jit(solution)/shard_map/ppermute | solution.py:370
  21.7 1.8 %shard_map.118 = (f32[16,16,64]{2,1,0:T(8,128)S(1)}, f32[16,64]{1,0:T(8,128)S(1)}, f32[16,1024]{1,0:T(8,128)S(1)}, f32[16,1024]{1,0:T(8,128)S(1)}, f32[16,512]{1,0:T(8,128)S(1)}) custom-call(s32[7,1,16]{2,1,0:T(1,128)S(1)} %get-tuple-element.39.cols_in, s32[4,8]{1,0:T(4,128)S(1)} %get-tuple-element.37.met, f32[4,512]{1,0:T(4,128)S(1)} %get-tuple-element.38.weights, ...), custom_call_target="tpu_custom_call" | custom-call | tf_op jit(solution)/shard_map/pallas_call | solution.py:349
  23.6 0.0 collective-permute-done.2.rest_0_
  23.6 0.3 collective-permute-done.3.rest_1_
  23.9 0.3 shard_map.119
  24.3 13.0 %all_to_all.8 = f32[32,1,96]{2,1,0:T(1,128)S(1)} all-to-all(f32[32,1,96]{2,1,0:T(1,128)S(1)} %broadcast_in_dim.11), channel_id=1, replica_groups=mesh['dam'=16,'sec'=2] {'dam','sec'}, dimensions={0} | all-to-all | bytes 24576 | tf_op jit(solution)/shard_map/all_to_all | solution.py:362
  37.2 1.0 %shard_map.120 = (f32[16,1024]{1,0:T(8,128)}, f32[16,1024]{1,0:T(8,128)}) custom-call(f32[32,96]{1,0:T(8,128)S(1)} %bitcast.24, f32[16,16,64]{2,1,0:T(8,128)S(1)} %get-tuple-element.65.nvec, f32[16,1024]{1,0:T(8,128)S(1)} %get-tuple-element.66.rflat, f32[16,1024]{1,0:T(8,128)S(1)} %get-tuple-element.67.zflat, f32[16,1024]{1,0:T(8,128)S(1)} %get-tuple-element.68.wflat, ...), custom_call_target="tpu_custom_call" | custom-call | tf_op jit(solution)/shard_map/pallas_call | solution.py:349
  (1 shorter events, 0.0 us)
Async XLA Ops:
  0.6 11.0 %copy-start = (f32[1,1,16,64,448]{4,3,2,1,0:T(8,128)S(1)}, f32[1,1,16,64,448]{4,3,2,1,0:T(8,128)}, u32[]{:S(2)}) copy-start(f32[1,1,16,64,448]{4,3,2,1,0:T(8,128)} %param.12) | copy-start | bytes 5505028
  5.3 8.1 %collective-permute-start = (f32[16,512]{1,0:T(8,128)S(1)}, f32[16,512]{1,0:T(8,128)S(1)}, u32[]{:S(2)}, u32[]{:S(2)}) collective-permute-start(f32[16,512]{1,0:T(8,128)S(1)} %get-tuple-element.50), channel_id=1, source_target_pairs={{2,4},{6,8},{10,12},{14,16},{18,20},{22,24},{26,28},{4,2},{8,6},{1... | collective-permute-start | bytes 98312 | tf_op jit(solution)/shard_map/ppermute | solution.py:370
  6.0 7.8 %collective-permute-start.1 = (f32[16,512]{1,0:T(8,128)S(1)}, f32[16,512]{1,0:T(8,128)S(1)}, u32[]{:S(2)}, u32[]{:S(2)}) collective-permute-start(f32[16,512]{1,0:T(8,128)S(1)} %get-tuple-element.51), channel_id=1, source_target_pairs={{0,2},{4,6},{8,10},{12,14},{16,18},{20,22},{24,26},{28,30},{2,0},{... | collective-permute-start | bytes 98312 | tf_op jit(solution)/shard_map/ppermute | solution.py:370
  16.6 7.0 %collective-permute-start.2 = (f32[16,512]{1,0:T(8,128)S(1)}, f32[16,512]{1,0:T(8,128)S(1)}, u32[]{:S(2)}, u32[]{:S(2)}) collective-permute-start(f32[16,512]{1,0:T(8,128)S(1)} %get-tuple-element.61), channel_id=1, source_target_pairs={{2,4},{6,8},{10,12},{14,16},{18,20},{22,24},{26,28},{4,2},{8,6},{1... | collective-permute-start | bytes 98312 | tf_op jit(solution)/shard_map/ppermute | solution.py:370
  17.2 6.7 %collective-permute-start.3 = (f32[16,512]{1,0:T(8,128)S(1)}, f32[16,512]{1,0:T(8,128)S(1)}, u32[]{:S(2)}, u32[]{:S(2)}) collective-permute-start(f32[16,512]{1,0:T(8,128)S(1)} %get-tuple-element.62), channel_id=1, source_target_pairs={{0,2},{4,6},{8,10},{12,14},{16,18},{20,22},{24,26},{28,30},{2,0},{... | collective-permute-start | bytes 98312 | tf_op jit(solution)/shard_map/ppermute | solution.py:370

commit v13 on v12

--- a/solution.py
+++ b/solution.py
@@ -104,10 +104,11 @@
             base[t * group + j] = lane_piece(out, j, bdof)
 
 
-def offer(pair, corners, across, field, rows, base, payload):
+def offer(pair, corners, across, field, rows, tiles, left, base, payload):
     bdof = field.shape[2]
     if not pair:
         pack(field, corners, payload)
+        apply_blocks(field, *tiles, left, base)
         return
     wide = len(corners) * bdof
     at = payload.shape[1] - wide
@@ -117,6 +118,7 @@
     other = pl.multiple_of((1 - me) * wide, wide)
     correct = three_pass(dot_t, own, *halves(rows[:, pl.ds(mine, wide)]))
     payload[: field.shape[1], at:] = three_pass(dot, own, *halves(rows[:, pl.ds(other, wide)]))
+    apply_blocks(field, *tiles, left, base)
     add_pieces(base, corners, lambda n, b: lane_piece(correct, n, bdof))
     pack(base, across, payload)
 
@@ -229,10 +231,10 @@
     for wait in waits[9 : 9 + PIECES]:
         wait()
     split_blocks(blocks, tiles_high, tiles_low)
-    apply_blocks(rvec, tiles_high, tiles_low, left, base)
     for wait in waits[9 + PIECES :] + waits[4:9]:
         wait()
-    offer(pair, corners, across, rvec, rows, base, payload)
+    tiles = (tiles_high, tiles_low)
+    offer(pair, corners, across, rvec, rows, tiles, left, base, payload)
     cmap_out[...] = cmap_row[0]
     if pair:
         payload[ncol:, :] = jnp.zeros_like(payload[ncol:, :])
@@ -302,8 +304,8 @@
     besides, (wout, sums, base, payload, left) = rest[:count], rest[count:]
     (corners,) = listed(cmap)
     where = couple(met, weights, local, besides, wout)
-    apply_blocks(wout, tiles_high, tiles_low, left, base)
-    offer(pair, corners, where[2], wout, rows, base, payload)
+    tiles = (tiles_high, tiles_low)
+    offer(pair, corners, where[2], wout, rows, tiles, left, base, payload)
     sums[...] = lanes(zvec, wout)
 
 

time: 38.5 us -> 38.4 us (level)
  no operation moved by 1% of the time
where the time goes in v13:
time: 38.4 us; the launch traced here: 38.2 us
  blocking collectives  16.9 us (44%)
  starting transfers between devices  11.5 us (30%)
  Pallas kernels  8.48 us (22%)
  between operations  0.71 us (2%)
  waiting for transfers between devices  0.62 us (2%)
    all_to_all x1, blocking collectives, everywhere(): return lax.all_to_all(copies, ('dam', 'sec'), split_axis=0, concat_axis=0)  13 us
    ppermute x4, starting transfers between devices, exchange(): got.append(lax.ppermute(send, axis, pairs + [(j, i) for i, j in pairs]))  11.5 us
    pallas_call x8, Pallas kernels, call(): pl.pallas_call(kernel, out_shape=outs, in_specs=[vmem] * len(args) + [hbm...  8.48 us
    all_gather x1, blocking collectives, shards(): shares = labels = lax.all_gather(payload, 'sec')  2.02 us
    all_gather x1, blocking collectives, shards(): shares = lax.all_gather(payload, 'sec')  1.87 us
  transfers between devices with their start and end apart: 4, of which 2 were waited for; matrix products, arithmetic and copies ran while one was open for 0% of the time, Pallas kernels for 10%

profile of v13, /device:TPU:0, one launch (start us, length us, event | category | flops | bytes accessed | tf_op | source)
XLA Modules:
  0.0 38.2 jit_solution(4504099990173884773)
XLA Ops:
  0.6 0.0 copy-start
  0.6 2.4 %shard_map.113 = (f32[16,16,64]{2,1,0:T(8,128)S(1)}, f32[16,16,64]{2,1,0:T(8,128)S(1)}, f32[24,768]{1,0:T(8,128)S(1)}, bf16[4,256,256]{2,1,0:T(8,128)(2,1)S(1)},...) custom-call(f32[16,1024]{1,0:T(8,128)} %bitcast.28, ...), custom_call_target="tpu_custom_call" | custom-call | tf_op jit(solution)/shard_map/pallas_call | solution.py:351
  3.1 2.0 %all-gather = f32[48,768]{1,0:T(8,128)S(1)} all-gather(f32[24,768]{1,0:T(8,128)S(1)} %get-tuple-element.44), channel_id=2, replica_groups=mesh['dam'=16,'sec'=2] {'sec'}, dimensions={0}, use_global_device_ids=true | all-gather | bytes 221184 | tf_op jit(solution)/shard_map/all_gather | solution.py:462
  5.1 0.2 shard_map.114
  5.3 0.7 %collective-permute-start = (f32[16,512]{1,0:T(8,128)S(1)}, f32[16,512]{1,0:T(8,128)S(1)}, u32[]{:S(2)}, u32[]{:S(2)}) collective-permute-start(f32[16,512]{1,0:T(8,128)S(1)} %get-tuple-element.50), channel_id=1, source_target_pairs={{2,4},{6,8},{10,12},{14,16},{18,20},{22,24},{26,28},{4,2},{8,6},{1... | collective-permute-start | bytes 98312 | tf_op jit(solution)/shard_map/ppermute | solution.py:372
  5.9 5.6 %collective-permute-start.1 = (f32[16,512]{1,0:T(8,128)S(1)}, f32[16,512]{1,0:T(8,128)S(1)}, u32[]{:S(2)}, u32[]{:S(2)}) collective-permute-start(f32[16,512]{1,0:T(8,128)S(1)} %get-tuple-element.51), channel_id=1, source_target_pairs={{0,2},{4,6},{8,10},{12,14},{16,18},{20,22},{24,26},{28,30},{2,0},{... | collective-permute-start | bytes 98312 | tf_op jit(solution)/shard_map/ppermute | solution.py:372
  11.6 0.0 copy-done
  11.6 1.8 %shard_map.115 = (f32[16,16,64]{2,1,0:T(8,128)S(1)}, f32[16,64]{1,0:T(8,128)S(1)}, f32[16,1024]{1,0:T(8,128)S(1)}, f32[16,1024]{1,0:T(8,128)S(1)}, f32[16,512]{1,0:T(8,128)S(1)}) custom-call(s32[7,1,16]{2,1,0:T(1,128)S(1)} %get-tuple-element.39.cols_in, s32[4,8]{1,0:T(4,128)S(1)} %get-tuple-element.37.met, f32[4,512]{1,0:T(4,128)S(1)} %get-tuple-element.38.weights, ...), custom_call_target="tpu_custom_call" | custom-call | tf_op jit(solution)/shard_map/pallas_call | solution.py:351
  13.4 0.0 collective-permute-done.rest_0_
  13.4 0.3 collective-permute-done.1.rest_1_
  13.7 0.7 %shard_map.116 = (f32[16,16,64]{2,1,0:T(8,128)S(1)}, f32[16,64]{1,0:T(8,128)S(1)}, f32[16,16,64]{2,1,0:T(8,128)S(1)}, f32[16,768]{1,0:T(8,128)S(1)}) custom-call(s32[1,4]{1,0:T(1,128)S(1)} %get-tuple-element.41.cmap, s32[4,8]{1,0:T(4,128)S(1)} %get-tuple-element.37.met, f32[4,512]{1,0:T(4,128)S(1)} %get-tuple-element.38.weights, ...), custom_call_target="tpu_custom_call" | custom-call | tf_op jit(solution)/shard_map/pallas_call | solution.py:351
  14.4 1.9 %all-gather.1 = f32[32,768]{1,0:T(8,128)S(1)} all-gather(f32[16,768]{1,0:T(8,128)S(1)} %get-tuple-element.54), channel_id=3, replica_groups=mesh['dam'=16,'sec'=2] {'sec'}, dimensions={0}, use_global_device_ids=true | all-gather | bytes 147456 | tf_op jit(solution)/shard_map/all_gather | solution.py:471
  16.3 0.2 shard_map.117
  16.5 0.7 %collective-permute-start.2 = (f32[16,512]{1,0:T(8,128)S(1)}, f32[16,512]{1,0:T(8,128)S(1)}, u32[]{:S(2)}, u32[]{:S(2)}) collective-permute-start(f32[16,512]{1,0:T(8,128)S(1)} %get-tuple-element.61), channel_id=1, source_target_pairs={{2,4},{6,8},{10,12},{14,16},{18,20},{22,24},{26,28},{4,2},{8,6},{1... | collective-permute-start | bytes 98312 | tf_op jit(solution)/shard_map/ppermute | solution.py:372
  17.2 4.5 %collective-permute-start.3 = (f32[16,512]{1,0:T(8,128)S(1)}, f32[16,512]{1,0:T(8,128)S(1)}, u32[]{:S(2)}, u32[]{:S(2)}) collective-permute-start(f32[16,512]{1,0:T(8,128)S(1)} %get-tuple-element.62), channel_id=1, source_target_pairs={{0,2},{4,6},{8,10},{12,14},{16,18},{20,22},{24,26},{28,30},{2,0},{... | collective-permute-start | bytes 98312 | tf_op jit(solution)/shard_map/ppermute | solution.py:372
  21.7 1.8 %shard_map.118 = (f32[16,16,64]{2,1,0:T(8,128)S(1)}, f32[16,64]{1,0:T(8,128)S(1)}, f32[16,1024]{1,0:T(8,128)S(1)}, f32[16,1024]{1,0:T(8,128)S(1)}, f32[16,512]{1,0:T(8,128)S(1)}) custom-call(s32[7,1,16]{2,1,0:T(1,128)S(1)} %get-tuple-element.39.cols_in, s32[4,8]{1,0:T(4,128)S(1)} %get-tuple-element.37.met, f32[4,512]{1,0:T(4,128)S(1)} %get-tuple-element.38.weights, ...), custom_call_target="tpu_custom_call" | custom-call | tf_op jit(solution)/shard_map/pallas_call | solution.py:351
  23.5 0.0 collective-permute-done.2.rest_0_
  23.5 0.3 collective-permute-done.3.rest_1_
  23.8 0.3 shard_map.119
  24.2 13.0 %all_to_all.8 = f32[32,1,96]{2,1,0:T(1,128)S(1)} all-to-all(f32[32,1,96]{2,1,0:T(1,128)S(1)} %broadcast_in_dim.11), channel_id=1, replica_groups=mesh['dam'=16,'sec'=2] {'dam','sec'}, dimensions={0} | all-to-all | bytes 24576 | tf_op jit(solution)/shard_map/all_to_all | solution.py:364
  37.1 1.0 %shard_map.120 = (f32[16,1024]{1,0:T(8,128)}, f32[16,1024]{1,0:T(8,128)}) custom-call(f32[32,96]{1,0:T(8,128)S(1)} %bitcast.24, f32[16,16,64]{2,1,0:T(8,128)S(1)} %get-tuple-element.65.nvec, f32[16,1024]{1,0:T(8,128)S(1)} %get-tuple-element.66.rflat, f32[16,1024]{1,0:T(8,128)S(1)} %get-tuple-element.67.zflat, f32[16,1024]{1,0:T(8,128)S(1)} %get-tuple-element.68.wflat, ...), custom_call_target="tpu_custom_call" | custom-call | tf_op jit(solution)/shard_map/pallas_call | solution.py:351
  (1 shorter events, 0.0 us)
Async XLA Ops:
  0.6 10.9 %copy-start = (f32[1,1,16,64,448]{4,3,2,1,0:T(8,128)S(1)}, f32[1,1,16,64,448]{4,3,2,1,0:T(8,128)}, u32[]{:S(2)}) copy-start(f32[1,1,16,64,448]{4,3,2,1,0:T(8,128)} %param.12) | copy-start | bytes 5505028
  5.3 8.1 %collective-permute-start = (f32[16,512]{1,0:T(8,128)S(1)}, f32[16,512]{1,0:T(8,128)S(1)}, u32[]{:S(2)}, u32[]{:S(2)}) collective-permute-start(f32[16,512]{1,0:T(8,128)S(1)} %get-tuple-element.50), channel_id=1, source_target_pairs={{2,4},{6,8},{10,12},{14,16},{18,20},{22,24},{26,28},{4,2},{8,6},{1... | collective-permute-start | bytes 98312 | tf_op jit(solution)/shard_map/ppermute | solution.py:372
  5.9 7.8 %collective-permute-start.1 = (f32[16,512]{1,0:T(8,128)S(1)}, f32[16,512]{1,0:T(8,128)S(1)}, u32[]{:S(2)}, u32[]{:S(2)}) collective-permute-start(f32[16,512]{1,0:T(8,128)S(1)} %get-tuple-element.51), channel_id=1, source_target_pairs={{0,2},{4,6},{8,10},{12,14},{16,18},{20,22},{24,26},{28,30},{2,0},{... | collective-permute-start | bytes 98312 | tf_op jit(solution)/shard_map/ppermute | solution.py:372
  16.5 7.0 %collective-permute-start.2 = (f32[16,512]{1,0:T(8,128)S(1)}, f32[16,512]{1,0:T(8,128)S(1)}, u32[]{:S(2)}, u32[]{:S(2)}) collective-permute-start(f32[16,512]{1,0:T(8,128)S(1)} %get-tuple-element.61), channel_id=1, source_target_pairs={{2,4},{6,8},{10,12},{14,16},{18,20},{22,24},{26,28},{4,2},{8,6},{1... | collective-permute-start | bytes 98312 | tf_op jit(solution)/shard_map/ppermute | solution.py:372
  17.2 6.7 %collective-permute-start.3 = (f32[16,512]{1,0:T(8,128)S(1)}, f32[16,512]{1,0:T(8,128)S(1)}, u32[]{:S(2)}, u32[]{:S(2)}) collective-permute-start(f32[16,512]{1,0:T(8,128)S(1)} %get-tuple-element.62), channel_id=1, source_target_pairs={{0,2},{4,6},{8,10},{12,14},{16,18},{20,22},{24,26},{28,30},{2,0},{... | collective-permute-start | bytes 98312 | tf_op jit(solution)/shard_map/ppermute | solution.py:372

commit v14 on v13

--- a/solution.py
+++ b/solution.py
@@ -196,29 +196,27 @@
     load, mask, blocks, cmap, cmap_row, fmap, fmap_rows, weights, left, sems = refs[20:]
     waits = fetch(
         [
-            (load_in, load),
             (mask_in, mask),
+            *pieces(load_in, load, load.shape[0] // (LANES // rvec.shape[1])),
+            *pieces(blocks_in, blocks, PIECES),
             (cmap_in, cmap),
             (fmap_in, fmap),
+            *pieces(rows_in, rows, PIECES),
             (cmap_in, cmap_row),
             (fmap_in, fmap_rows),
             (weights_in, weights),
             (cols_in, cols),
             (tang_in, tang),
-        ]
-        + pieces(blocks_in, blocks, PIECES)
-        + pieces(rows_in, rows, PIECES),
+        ],
         sems,
     )
+    loads = waits[: load.shape[0] // (LANES // rvec.shape[1]) + 1]
+    waits = waits[len(loads) :]
     nblk, ncol, bdof = rvec.shape
     order = face_order(pair)
     tiles_high[...] = jnp.zeros_like(tiles_high)
     tiles_low[...] = jnp.zeros_like(tiles_low)
-    waits[2]()
-    waits[3]()
-    corners = [cmap[0, 0, n] for n in range(cmap.shape[2])]
-    across = [fmap[0, 0, order[2], p] for p in range(fmap.shape[3])]
-    for wait in waits[:2]:
+    for wait in loads:
         wait()
     scale = mask[...].astype(F32)
     scale = jnp.concatenate([scale] * (LANES // ncol), axis=1)
@@ -228,11 +226,13 @@
         rvec.shape,
         rvec,
     )
-    for wait in waits[9 : 9 + PIECES]:
+    for wait in waits[:PIECES]:
         wait()
     split_blocks(blocks, tiles_high, tiles_low)
-    for wait in waits[9 + PIECES :] + waits[4:9]:
+    for wait in waits[PIECES:]:
         wait()
+    corners = [cmap[0, 0, n] for n in range(cmap.shape[2])]
+    across = [fmap[0, 0, order[2], p] for p in range(fmap.shape[3])]
     tiles = (tiles_high, tiles_low)
     offer(pair, corners, across, rvec, rows, tiles, left, base, payload)
     cmap_out[...] = cmap_row[0]
@@ -315,13 +315,14 @@
     couple(met, weights, local, besides, nout)
     parts = [gamma[...], delta[...], mu[...], rm, lanes(mvec, nout), lanes(zvec, nout)]
     parts = jnp.concatenate(parts, axis=0)
-    totals[...] = lax.dot_general(
+    sides = lax.dot_general(
         jnp.ones((1, parts.shape[1]), F32),
         parts,
         (((1,), (1,)), ((), ())),
         precision=lax.Precision.HIGHEST,
         preferred_element_type=F32,
     )
+    totals[...] = jnp.broadcast_to(sides[None], totals.shape)
 
 
 def finish_kernel(shares, nvec, rflat, zflat, wflat, mflat, sol, res):
@@ -358,9 +359,7 @@
     )(*args, *far)
 
 
-def everywhere(values):
-    total = lax.axis_size("dam") * lax.axis_size("sec")
-    copies = jnp.broadcast_to(values[None], (total,) + values.shape)
+def everywhere(copies):
     return lax.all_to_all(copies, ("dam", "sec"), split_axis=0, concat_axis=0)
 
 
@@ -435,7 +434,7 @@
             hold(face_map),
             hold(weights),
             halved,
-            sems(9 + 2 * PIECES),
+            sems(8 + nblk * ncol // LANES + 2 * PIECES),
         ],
         (),
         (load, mask, corner_map, face_map, blocks, rows, cols, weights, tang),
@@ -473,7 +472,7 @@
     part, mu, mflat, wflat, across = local(mvec, wvec, shares, labels)
     nvec, totals = call(
         last_kernel,
-        (field, shape(1, 6 * ncol)),
+        (field, shape(lax.axis_size("dam") * lax.axis_size("sec"), 1, 6 * ncol)),
         [],
         (met, weights, part, rvec, zvec, mvec, gamma, delta, mu, *besides, *beyond, *across),
     )
@@ -481,7 +480,7 @@
         finish_kernel,
         (flat, flat),
         [],
-        (everywhere(totals[0]), nvec, rflat, zflat, wflat, mflat),
+        (everywhere(totals)[:, 0], nvec, rflat, zflat, wflat, mflat),
     )
     return sol[None, None], res[None, None]
 

time: 38.4 us -> 38.3 us (level)
  no operation moved by 1% of the time
where the time goes in v14:
time: 38.3 us; the launch traced here: 38.1 us
  blocking collectives  16.9 us (44%)
  starting transfers between devices  11.5 us (30%)
  Pallas kernels  8.48 us (22%)
  between operations  0.73 us (2%)
  waiting for transfers between devices  0.61 us (2%)
    all_to_all x1, blocking collectives, everywhere(): return lax.all_to_all(copies, ('dam', 'sec'), split_axis=0, concat_axis=0)  13 us
    ppermute x4, starting transfers between devices, exchange(): got.append(lax.ppermute(send, axis, pairs + [(j, i) for i, j in pairs]))  11.5 us
    pallas_call x8, Pallas kernels, call(): pl.pallas_call(kernel, out_shape=outs, in_specs=[vmem] * len(args) + [hbm...  8.48 us
    all_gather x1, blocking collectives, shards(): shares = labels = lax.all_gather(payload, 'sec')  2.02 us
    all_gather x1, blocking collectives, shards(): shares = lax.all_gather(payload, 'sec')  1.87 us
  transfers between devices with their start and end apart: 4, of which 2 were waited for; matrix products, arithmetic and copies ran while one was open for 0% of the time, Pallas kernels for 10%

profile of v14, /device:TPU:0, one launch (start us, length us, event | category | flops | bytes accessed | tf_op | source)
XLA Modules:
  0.0 38.1 jit_solution(4767371082419242215)
XLA Ops:
  0.6 0.0 copy-start
  0.6 2.4 %shard_map.113 = (f32[16,16,64]{2,1,0:T(8,128)S(1)}, f32[16,16,64]{2,1,0:T(8,128)S(1)}, f32[24,768]{1,0:T(8,128)S(1)}, bf16[4,256,256]{2,1,0:T(8,128)(2,1)S(1)},...) custom-call(f32[16,1024]{1,0:T(8,128)} %bitcast.26, ...), custom_call_target="tpu_custom_call" | custom-call | tf_op jit(solution)/shard_map/pallas_call | solution.py:352
  3.0 2.0 %all-gather = f32[48,768]{1,0:T(8,128)S(1)} all-gather(f32[24,768]{1,0:T(8,128)S(1)} %get-tuple-element.44), channel_id=2, replica_groups=mesh['dam'=16,'sec'=2] {'sec'}, dimensions={0}, use_global_device_ids=true | all-gather | bytes 221184 | tf_op jit(solution)/shard_map/all_gather | solution.py:461
  5.0 0.2 shard_map.114
  5.2 0.7 %collective-permute-start = (f32[16,512]{1,0:T(8,128)S(1)}, f32[16,512]{1,0:T(8,128)S(1)}, u32[]{:S(2)}, u32[]{:S(2)}) collective-permute-start(f32[16,512]{1,0:T(8,128)S(1)} %get-tuple-element.50), channel_id=1, source_target_pairs={{2,4},{6,8},{10,12},{14,16},{18,20},{22,24},{26,28},{4,2},{8,6},{1... | collective-permute-start | bytes 98312 | tf_op jit(solution)/shard_map/ppermute | solution.py:371
  5.9 5.6 %collective-permute-start.1 = (f32[16,512]{1,0:T(8,128)S(1)}, f32[16,512]{1,0:T(8,128)S(1)}, u32[]{:S(2)}, u32[]{:S(2)}) collective-permute-start(f32[16,512]{1,0:T(8,128)S(1)} %get-tuple-element.51), channel_id=1, source_target_pairs={{0,2},{4,6},{8,10},{12,14},{16,18},{20,22},{24,26},{28,30},{2,0},{... | collective-permute-start | bytes 98312 | tf_op jit(solution)/shard_map/ppermute | solution.py:371
  11.5 0.0 copy-done
  11.5 1.8 %shard_map.115 = (f32[16,16,64]{2,1,0:T(8,128)S(1)}, f32[16,64]{1,0:T(8,128)S(1)}, f32[16,1024]{1,0:T(8,128)S(1)}, f32[16,1024]{1,0:T(8,128)S(1)}, f32[16,512]{1,0:T(8,128)S(1)}) custom-call(s32[7,1,16]{2,1,0:T(1,128)S(1)} %get-tuple-element.39.cols_in, s32[4,8]{1,0:T(4,128)S(1)} %get-tuple-element.37.met, f32[4,512]{1,0:T(4,128)S(1)} %get-tuple-element.38.weights, ...), custom_call_target="tpu_custom_call" | custom-call | tf_op jit(solution)/shard_map/pallas_call | solution.py:352
  13.4 0.0 collective-permute-done.rest_0_
  13.4 0.3 collective-permute-done.1.rest_1_
  13.7 0.7 %shard_map.116 = (f32[16,16,64]{2,1,0:T(8,128)S(1)}, f32[16,64]{1,0:T(8,128)S(1)}, f32[16,16,64]{2,1,0:T(8,128)S(1)}, f32[16,768]{1,0:T(8,128)S(1)}) custom-call(s32[1,4]{1,0:T(1,128)S(1)} %get-tuple-element.41.cmap, s32[4,8]{1,0:T(4,128)S(1)} %get-tuple-element.37.met, f32[4,512]{1,0:T(4,128)S(1)} %get-tuple-element.38.weights, ...), custom_call_target="tpu_custom_call" | custom-call | tf_op jit(solution)/shard_map/pallas_call | solution.py:352
  14.4 1.9 %all-gather.1 = f32[32,768]{1,0:T(8,128)S(1)} all-gather(f32[16,768]{1,0:T(8,128)S(1)} %get-tuple-element.54), channel_id=3, replica_groups=mesh['dam'=16,'sec'=2] {'sec'}, dimensions={0}, use_global_device_ids=true | all-gather | bytes 147456 | tf_op jit(solution)/shard_map/all_gather | solution.py:470
  16.3 0.2 shard_map.117
  16.5 0.7 %collective-permute-start.2 = (f32[16,512]{1,0:T(8,128)S(1)}, f32[16,512]{1,0:T(8,128)S(1)}, u32[]{:S(2)}, u32[]{:S(2)}) collective-permute-start(f32[16,512]{1,0:T(8,128)S(1)} %get-tuple-element.61), channel_id=1, source_target_pairs={{2,4},{6,8},{10,12},{14,16},{18,20},{22,24},{26,28},{4,2},{8,6},{1... | collective-permute-start | bytes 98312 | tf_op jit(solution)/shard_map/ppermute | solution.py:371
  17.1 4.5 %collective-permute-start.3 = (f32[16,512]{1,0:T(8,128)S(1)}, f32[16,512]{1,0:T(8,128)S(1)}, u32[]{:S(2)}, u32[]{:S(2)}) collective-permute-start(f32[16,512]{1,0:T(8,128)S(1)} %get-tuple-element.62), channel_id=1, source_target_pairs={{0,2},{4,6},{8,10},{12,14},{16,18},{20,22},{24,26},{28,30},{2,0},{... | collective-permute-start | bytes 98312 | tf_op jit(solution)/shard_map/ppermute | solution.py:371
  21.6 1.8 %shard_map.118 = (f32[16,16,64]{2,1,0:T(8,128)S(1)}, f32[16,64]{1,0:T(8,128)S(1)}, f32[16,1024]{1,0:T(8,128)S(1)}, f32[16,1024]{1,0:T(8,128)S(1)}, f32[16,512]{1,0:T(8,128)S(1)}) custom-call(s32[7,1,16]{2,1,0:T(1,128)S(1)} %get-tuple-element.39.cols_in, s32[4,8]{1,0:T(4,128)S(1)} %get-tuple-element.37.met, f32[4,512]{1,0:T(4,128)S(1)} %get-tuple-element.38.weights, ...), custom_call_target="tpu_custom_call" | custom-call | tf_op jit(solution)/shard_map/pallas_call | solution.py:352
  23.5 0.0 collective-permute-done.2.rest_0_
  23.5 0.3 collective-permute-done.3.rest_1_
  23.8 0.3 shard_map.119
  24.1 13.0 %all_to_all.5 = f32[32,1,96]{2,1,0:T(1,128)S(1)} all-to-all(f32[32,1,96]{2,1,0:T(1,128)S(1)} %get-tuple-element.64), channel_id=1, replica_groups=mesh['dam'=16,'sec'=2] {'dam','sec'}, dimensions={0} | all-to-all | bytes 24576 | tf_op jit(solution)/shard_map/all_to_all | solution.py:363
  37.1 1.0 %shard_map.120 = (f32[16,1024]{1,0:T(8,128)}, f32[16,1024]{1,0:T(8,128)}) custom-call(f32[32,96]{1,0:T(8,128)S(1)} %bitcast.23, f32[16,16,64]{2,1,0:T(8,128)S(1)} %get-tuple-element.65.nvec, f32[16,1024]{1,0:T(8,128)S(1)} %get-tuple-element.66.rflat, f32[16,1024]{1,0:T(8,128)S(1)} %get-tuple-element.67.zflat, f32[16,1024]{1,0:T(8,128)S(1)} %get-tuple-element.68.wflat, ...), custom_call_target="tpu_custom_call" | custom-call | tf_op jit(solution)/shard_map/pallas_call | solution.py:352
Async XLA Ops:
  0.6 10.9 %copy-start = (f32[1,1,16,64,448]{4,3,2,1,0:T(8,128)S(1)}, f32[1,1,16,64,448]{4,3,2,1,0:T(8,128)}, u32[]{:S(2)}) copy-start(f32[1,1,16,64,448]{4,3,2,1,0:T(8,128)} %param.12) | copy-start | bytes 5505028
  5.2 8.1 %collective-permute-start = (f32[16,512]{1,0:T(8,128)S(1)}, f32[16,512]{1,0:T(8,128)S(1)}, u32[]{:S(2)}, u32[]{:S(2)}) collective-permute-start(f32[16,512]{1,0:T(8,128)S(1)} %get-tuple-element.50), channel_id=1, source_target_pairs={{2,4},{6,8},{10,12},{14,16},{18,20},{22,24},{26,28},{4,2},{8,6},{1... | collective-permute-start | bytes 98312 | tf_op jit(solution)/shard_map/ppermute | solution.py:371
  5.9 7.8 %collective-permute-start.1 = (f32[16,512]{1,0:T(8,128)S(1)}, f32[16,512]{1,0:T(8,128)S(1)}, u32[]{:S(2)}, u32[]{:S(2)}) collective-permute-start(f32[16,512]{1,0:T(8,128)S(1)} %get-tuple-element.51), channel_id=1, source_target_pairs={{0,2},{4,6},{8,10},{12,14},{16,18},{20,22},{24,26},{28,30},{2,0},{... | collective-permute-start | bytes 98312 | tf_op jit(solution)/shard_map/ppermute | solution.py:371
  16.5 7.0 %collective-permute-start.2 = (f32[16,512]{1,0:T(8,128)S(1)}, f32[16,512]{1,0:T(8,128)S(1)}, u32[]{:S(2)}, u32[]{:S(2)}) collective-permute-start(f32[16,512]{1,0:T(8,128)S(1)} %get-tuple-element.61), channel_id=1, source_target_pairs={{2,4},{6,8},{10,12},{14,16},{18,20},{22,24},{26,28},{4,2},{8,6},{1... | collective-permute-start | bytes 98312 | tf_op jit(solution)/shard_map/ppermute | solution.py:371
  17.1 6.7 %collective-permute-start.3 = (f32[16,512]{1,0:T(8,128)S(1)}, f32[16,512]{1,0:T(8,128)S(1)}, u32[]{:S(2)}, u32[]{:S(2)}) collective-permute-start(f32[16,512]{1,0:T(8,128)S(1)} %get-tuple-element.62), channel_id=1, source_target_pairs={{0,2},{4,6},{8,10},{12,14},{16,18},{20,22},{24,26},{28,30},{2,0},{... | collective-permute-start | bytes 98312 | tf_op jit(solution)/shard_map/ppermute | solution.py:371

commit v15 on v14

--- a/solution.py
+++ b/solution.py
@@ -216,8 +216,9 @@
     order = face_order(pair)
     tiles_high[...] = jnp.zeros_like(tiles_high)
     tiles_low[...] = jnp.zeros_like(tiles_low)
-    for wait in loads:
+    for wait in loads + waits[:PIECES]:
         wait()
+    split_blocks(blocks, tiles_high, tiles_low)
     scale = mask[...].astype(F32)
     scale = jnp.concatenate([scale] * (LANES // ncol), axis=1)
     unflatten(
@@ -226,9 +227,6 @@
         rvec.shape,
         rvec,
     )
-    for wait in waits[:PIECES]:
-        wait()
-    split_blocks(blocks, tiles_high, tiles_low)
     for wait in waits[PIECES:]:
         wait()
     corners = [cmap[0, 0, n] for n in range(cmap.shape[2])]
@@ -325,7 +323,7 @@
     totals[...] = jnp.broadcast_to(sides[None], totals.shape)
 
 
-def finish_kernel(shares, nvec, rflat, zflat, wflat, mflat, sol, res):
+def finish_kernel(shares, nvec, rflat, zflat, wflat, mflat, sol_out, res_out, sol, res, sems):
     nblk, ncol, bdof = nvec.shape
     flatten(lambda first, last: nvec[first:last], nvec.shape, res)
     total = jnp.sum(shares[...], axis=0, keepdims=True)
@@ -339,13 +337,22 @@
         jnp.concatenate([x] * (LANES // ncol), axis=1)
         for x in (alpha + anew * grow, anew * alpha)
     ]
-    for j in range(sol.shape[1] // LANES):
-        here = slice(j * LANES, (j + 1) * LANES)
+    spans = [slice(j * LANES, (j + 1) * LANES) for j in range(sol.shape[1] // LANES)]
+    for here in spans:
         sol[:, here] = both * zflat[:, here] - second * mflat[:, here]
-        res[:, here] = rflat[:, here] - both * wflat[:, here] + second * res[:, here]
-
-
-def call(kernel, outs, scratch, args, far=()):
+    waits = fetch([(sol, sol_out)], sems.at[pl.ds(0, 1)])
+    half = nblk // 2
+    for i, rows in enumerate((slice(0, half), slice(half, nblk))):
+        for here in spans:
+            res[rows, here] = (
+                rflat[rows, here] - both * wflat[rows, here] + second * res[rows, here]
+            )
+        waits += fetch([(res.at[rows], res_out.at[rows])], sems.at[pl.ds(i + 1, 1)])
+    for wait in waits:
+        wait()
+
+
+def call(kernel, outs, scratch, args, far=(), near=True):
     vmem = pl.BlockSpec(memory_space=pltpu.VMEM)
     hbm = pl.BlockSpec(memory_space=pltpu.HBM)
     far = [pltpu.with_memory_space_constraint(arg, pltpu.HBM) for arg in far]
@@ -353,7 +360,7 @@
         kernel,
         out_shape=outs,
         in_specs=[vmem] * len(args) + [hbm] * len(far),
-        out_specs=jax.tree.map(lambda _: vmem, outs),
+        out_specs=jax.tree.map(lambda _: vmem if near else hbm, outs),
         scratch_shapes=scratch,
         compiler_params=pltpu.CompilerParams(vmem_limit_bytes=VMEM_LIMIT),
     )(*args, *far)
@@ -479,8 +486,10 @@
     sol, res = call(
         finish_kernel,
         (flat, flat),
-        [],
+        [hold(flat), hold(flat), sems(3)],
         (everywhere(totals)[:, 0], nvec, rflat, zflat, wflat, mflat),
+        (),
+        False,
     )
     return sol[None, None], res[None, None]
 

time: 38.3 us -> 38.6 us (level)
  no operation moved by 1% of the time
where the time goes in v15:
time: 38.6 us; the launch traced here: 38.4 us
  blocking collectives  16.9 us (44%)
  starting transfers between devices  11.5 us (30%)
  Pallas kernels  8.72 us (23%)
  between operations  0.73 us (2%)
  waiting for transfers between devices  0.61 us (2%)
    all_to_all x1, blocking collectives, everywhere(): return lax.all_to_all(copies, ('dam', 'sec'), split_axis=0, concat_axis=0)  13 us
    ppermute x4, starting transfers between devices, exchange(): got.append(lax.ppermute(send, axis, pairs + [(j, i) for i, j in pairs]))  11.5 us
    pallas_call x8, Pallas kernels, call(): pl.pallas_call(kernel, out_shape=outs, in_specs=[vmem] * len(args) + [hbm...  8.72 us
    all_gather x1, blocking collectives, shards(): shares = labels = lax.all_gather(payload, 'sec')  2.02 us
    all_gather x1, blocking collectives, shards(): shares = lax.all_gather(payload, 'sec')  1.87 us
  transfers between devices with their start and end apart: 4, of which 2 were waited for; matrix products, arithmetic and copies ran while one was open for 0% of the time, Pallas kernels for 10%

profile of v15, /device:TPU:0, one launch (start us, length us, event | category | flops | bytes accessed | tf_op | source)
XLA Modules:
  0.0 38.4 jit_solution(14779324789743172400)
XLA Ops:
  0.6 0.0 copy-start
  0.6 2.6 %shard_map.113 = (f32[16,16,64]{2,1,0:T(8,128)S(1)}, f32[16,16,64]{2,1,0:T(8,128)S(1)}, f32[24,768]{1,0:T(8,128)S(1)}, bf16[4,256,256]{2,1,0:T(8,128)(2,1)S(1)},...) custom-call(f32[16,1024]{1,0:T(8,128)} %bitcast.26, ...), custom_call_target="tpu_custom_call" | custom-call | tf_op jit(solution)/shard_map/pallas_call | solution.py:359
  3.3 2.0 %all-gather = f32[48,768]{1,0:T(8,128)S(1)} all-gather(f32[24,768]{1,0:T(8,128)S(1)} %get-tuple-element.44), channel_id=2, replica_groups=mesh['dam'=16,'sec'=2] {'sec'}, dimensions={0}, use_global_device_ids=true | all-gather | bytes 221184 | tf_op jit(solution)/shard_map/all_gather | solution.py:468
  5.3 0.2 shard_map.114
  5.5 0.7 %collective-permute-start = (f32[16,512]{1,0:T(8,128)S(1)}, f32[16,512]{1,0:T(8,128)S(1)}, u32[]{:S(2)}, u32[]{:S(2)}) collective-permute-start(f32[16,512]{1,0:T(8,128)S(1)} %get-tuple-element.50), channel_id=1, source_target_pairs={{2,4},{6,8},{10,12},{14,16},{18,20},{22,24},{26,28},{4,2},{8,6},{1... | collective-permute-start | bytes 98312 | tf_op jit(solution)/shard_map/ppermute | solution.py:378
  6.1 5.6 %collective-permute-start.1 = (f32[16,512]{1,0:T(8,128)S(1)}, f32[16,512]{1,0:T(8,128)S(1)}, u32[]{:S(2)}, u32[]{:S(2)}) collective-permute-start(f32[16,512]{1,0:T(8,128)S(1)} %get-tuple-element.51), channel_id=1, source_target_pairs={{0,2},{4,6},{8,10},{12,14},{16,18},{20,22},{24,26},{28,30},{2,0},{... | collective-permute-start | bytes 98312 | tf_op jit(solution)/shard_map/ppermute | solution.py:378
  11.8 0.0 copy-done
  11.8 1.8 %shard_map.115 = (f32[16,16,64]{2,1,0:T(8,128)S(1)}, f32[16,64]{1,0:T(8,128)S(1)}, f32[16,1024]{1,0:T(8,128)S(1)}, f32[16,1024]{1,0:T(8,128)S(1)}, f32[16,512]{1,0:T(8,128)S(1)}) custom-call(s32[7,1,16]{2,1,0:T(1,128)S(1)} %get-tuple-element.39.cols_in, s32[4,8]{1,0:T(4,128)S(1)} %get-tuple-element.37.met, f32[4,512]{1,0:T(4,128)S(1)} %get-tuple-element.38.weights, ...), custom_call_target="tpu_custom_call" | custom-call | tf_op jit(solution)/shard_map/pallas_call | solution.py:359
  13.6 0.0 collective-permute-done.rest_0_
  13.6 0.3 collective-permute-done.1.rest_1_
  13.9 0.7 %shard_map.116 = (f32[16,16,64]{2,1,0:T(8,128)S(1)}, f32[16,64]{1,0:T(8,128)S(1)}, f32[16,16,64]{2,1,0:T(8,128)S(1)}, f32[16,768]{1,0:T(8,128)S(1)}) custom-call(s32[1,4]{1,0:T(1,128)S(1)} %get-tuple-element.41.cmap, s32[4,8]{1,0:T(4,128)S(1)} %get-tuple-element.37.met, f32[4,512]{1,0:T(4,128)S(1)} %get-tuple-element.38.weights, ...), custom_call_target="tpu_custom_call" | custom-call | tf_op jit(solution)/shard_map/pallas_call | solution.py:359
  14.6 1.9 %all-gather.1 = f32[32,768]{1,0:T(8,128)S(1)} all-gather(f32[16,768]{1,0:T(8,128)S(1)} %get-tuple-element.54), channel_id=3, replica_groups=mesh['dam'=16,'sec'=2] {'sec'}, dimensions={0}, use_global_device_ids=true | all-gather | bytes 147456 | tf_op jit(solution)/shard_map/all_gather | solution.py:477
  16.5 0.2 shard_map.117
  16.7 0.7 %collective-permute-start.2 = (f32[16,512]{1,0:T(8,128)S(1)}, f32[16,512]{1,0:T(8,128)S(1)}, u32[]{:S(2)}, u32[]{:S(2)}) collective-permute-start(f32[16,512]{1,0:T(8,128)S(1)} %get-tuple-element.61), channel_id=1, source_target_pairs={{2,4},{6,8},{10,12},{14,16},{18,20},{22,24},{26,28},{4,2},{8,6},{1... | collective-permute-start | bytes 98312 | tf_op jit(solution)/shard_map/ppermute | solution.py:378
  17.4 4.5 %collective-permute-start.3 = (f32[16,512]{1,0:T(8,128)S(1)}, f32[16,512]{1,0:T(8,128)S(1)}, u32[]{:S(2)}, u32[]{:S(2)}) collective-permute-start(f32[16,512]{1,0:T(8,128)S(1)} %get-tuple-element.62), channel_id=1, source_target_pairs={{0,2},{4,6},{8,10},{12,14},{16,18},{20,22},{24,26},{28,30},{2,0},{... | collective-permute-start | bytes 98312 | tf_op jit(solution)/shard_map/ppermute | solution.py:378
  21.9 1.8 %shard_map.118 = (f32[16,16,64]{2,1,0:T(8,128)S(1)}, f32[16,64]{1,0:T(8,128)S(1)}, f32[16,1024]{1,0:T(8,128)S(1)}, f32[16,1024]{1,0:T(8,128)S(1)}, f32[16,512]{1,0:T(8,128)S(1)}) custom-call(s32[7,1,16]{2,1,0:T(1,128)S(1)} %get-tuple-element.39.cols_in, s32[4,8]{1,0:T(4,128)S(1)} %get-tuple-element.37.met, f32[4,512]{1,0:T(4,128)S(1)} %get-tuple-element.38.weights, ...), custom_call_target="tpu_custom_call" | custom-call | tf_op jit(solution)/shard_map/pallas_call | solution.py:359
  23.7 0.0 collective-permute-done.2.rest_0_
  23.7 0.3 collective-permute-done.3.rest_1_
  24.0 0.3 shard_map.119
  24.4 13.0 %all_to_all.5 = f32[32,1,96]{2,1,0:T(1,128)S(1)} all-to-all(f32[32,1,96]{2,1,0:T(1,128)S(1)} %get-tuple-element.64), channel_id=1, replica_groups=mesh['dam'=16,'sec'=2] {'dam','sec'}, dimensions={0} | all-to-all | bytes 24576 | tf_op jit(solution)/shard_map/all_to_all | solution.py:370
  37.4 1.0 %shard_map.120 = (f32[16,1024]{1,0:T(8,128)}, f32[16,1024]{1,0:T(8,128)}) custom-call(f32[32,96]{1,0:T(8,128)S(1)} %bitcast.23, f32[16,16,64]{2,1,0:T(8,128)S(1)} %get-tuple-element.65.nvec, f32[16,1024]{1,0:T(8,128)S(1)} %get-tuple-element.66.rflat, f32[16,1024]{1,0:T(8,128)S(1)} %get-tuple-element.67.zflat, f32[16,1024]{1,0:T(8,128)S(1)} %get-tuple-element.68.wflat, ...), custom_call_target="tpu_custom_call" | custom-call | tf_op jit(solution)/shard_map/pallas_call | solution.py:359
Async XLA Ops:
  0.6 11.1 %copy-start = (f32[1,1,16,64,448]{4,3,2,1,0:T(8,128)S(1)}, f32[1,1,16,64,448]{4,3,2,1,0:T(8,128)}, u32[]{:S(2)}) copy-start(f32[1,1,16,64,448]{4,3,2,1,0:T(8,128)} %param.12) | copy-start | bytes 5505028
  5.5 8.1 %collective-permute-start = (f32[16,512]{1,0:T(8,128)S(1)}, f32[16,512]{1,0:T(8,128)S(1)}, u32[]{:S(2)}, u32[]{:S(2)}) collective-permute-start(f32[16,512]{1,0:T(8,128)S(1)} %get-tuple-element.50), channel_id=1, source_target_pairs={{2,4},{6,8},{10,12},{14,16},{18,20},{22,24},{26,28},{4,2},{8,6},{1... | collective-permute-start | bytes 98312 | tf_op jit(solution)/shard_map/ppermute | solution.py:378
  6.1 7.8 %collective-permute-start.1 = (f32[16,512]{1,0:T(8,128)S(1)}, f32[16,512]{1,0:T(8,128)S(1)}, u32[]{:S(2)}, u32[]{:S(2)}) collective-permute-start(f32[16,512]{1,0:T(8,128)S(1)} %get-tuple-element.51), channel_id=1, source_target_pairs={{0,2},{4,6},{8,10},{12,14},{16,18},{20,22},{24,26},{28,30},{2,0},{... | collective-permute-start | bytes 98312 | tf_op jit(solution)/shard_map/ppermute | solution.py:378
  16.7 7.0 %collective-permute-start.2 = (f32[16,512]{1,0:T(8,128)S(1)}, f32[16,512]{1,0:T(8,128)S(1)}, u32[]{:S(2)}, u32[]{:S(2)}) collective-permute-start(f32[16,512]{1,0:T(8,128)S(1)} %get-tuple-element.61), channel_id=1, source_target_pairs={{2,4},{6,8},{10,12},{14,16},{18,20},{22,24},{26,28},{4,2},{8,6},{1... | collective-permute-start | bytes 98312 | tf_op jit(solution)/shard_map/ppermute | solution.py:378
  17.4 6.7 %collective-permute-start.3 = (f32[16,512]{1,0:T(8,128)S(1)}, f32[16,512]{1,0:T(8,128)S(1)}, u32[]{:S(2)}, u32[]{:S(2)}) collective-permute-start(f32[16,512]{1,0:T(8,128)S(1)} %get-tuple-element.62), channel_id=1, source_target_pairs={{0,2},{4,6},{8,10},{12,14},{16,18},{20,22},{24,26},{28,30},{2,0},{... | collective-permute-start | bytes 98312 | tf_op jit(solution)/shard_map/ppermute | solution.py:378

commit v16 on v14

--- a/solution.py
+++ b/solution.py
@@ -82,33 +82,23 @@
     return x[:, p * bdof : (p + 1) * bdof]
 
 
-def split_blocks(blocks, tiles_high, tiles_low):
-    nblk, bdof = blocks.shape[:2]
-    group = tiles_high.shape[1] // bdof
-    for b in range(nblk):
-        t, j = divmod(b, group)
-        here = slice(j * bdof, (j + 1) * bdof)
-        tiles_high[t, here, here], tiles_low[t, here, here] = halves(blocks[b])
-
-
-def apply_blocks(field, tiles_high, tiles_low, left, base):
+def apply_blocks(field, high, low, base):
     nblk, ncol, bdof = field.shape
-    group = tiles_high.shape[1] // bdof
-    for b in range(nblk):
-        t, j = divmod(b, group)
-        here = slice(j * bdof, (j + 1) * bdof)
-        left[t, :ncol, here], left[t, ncol:, here] = halves(field[b])
-    for t in range(nblk // group):
-        out = three_pass(dot, left[t], tiles_high[t], tiles_low[t])
+    group = 4
+    for t in range(0, nblk, group):
+        parts = [halves(field[t + j]) for j in range(group)]
+        left = jnp.concatenate([p[0] for p in parts] + [p[1] for p in parts], axis=0)
+        rows = [x[t : t + group].reshape(group * bdof, bdof) for x in (high, low)]
+        prod = three_pass(dot_t, left, *rows)
         for j in range(group):
-            base[t * group + j] = lane_piece(out, j, bdof)
-
-
-def offer(pair, corners, across, field, rows, tiles, left, base, payload):
+            base[t + j] = lane_piece(prod[j * ncol : (j + 1) * ncol], j, bdof)
+
+
+def offer(pair, corners, across, field, rows, split, base, payload):
     bdof = field.shape[2]
     if not pair:
         pack(field, corners, payload)
-        apply_blocks(field, *tiles, left, base)
+        apply_blocks(field, *split, base)
         return
     wide = len(corners) * bdof
     at = payload.shape[1] - wide
@@ -118,7 +108,7 @@
     other = pl.multiple_of((1 - me) * wide, wide)
     correct = three_pass(dot_t, own, *halves(rows[:, pl.ds(mine, wide)]))
     payload[: field.shape[1], at:] = three_pass(dot, own, *halves(rows[:, pl.ds(other, wide)]))
-    apply_blocks(field, *tiles, left, base)
+    apply_blocks(field, *split, base)
     add_pieces(base, corners, lambda n, b: lane_piece(correct, n, bdof))
     pack(base, across, payload)
 
@@ -192,8 +182,8 @@
 
 def start_kernel(pair, *refs):
     load_in, mask_in, cmap_in, fmap_in, blocks_in, rows_in, cols_in, weights_in, tang_in = refs[:9]
-    rvec, base, payload, tiles_high, tiles_low, cmap_out, met, wmet, rows, cols, tang = refs[9:20]
-    load, mask, blocks, cmap, cmap_row, fmap, fmap_rows, weights, left, sems = refs[20:]
+    rvec, base, payload, high, low, cmap_out, met, wmet, rows, cols, tang = refs[9:20]
+    load, mask, blocks, cmap, cmap_row, fmap, fmap_rows, weights, sems = refs[20:]
     waits = fetch(
         [
             (mask_in, mask),
@@ -214,8 +204,6 @@
     waits = waits[len(loads) :]
     nblk, ncol, bdof = rvec.shape
     order = face_order(pair)
-    tiles_high[...] = jnp.zeros_like(tiles_high)
-    tiles_low[...] = jnp.zeros_like(tiles_low)
     for wait in loads:
         wait()
     scale = mask[...].astype(F32)
@@ -228,13 +216,12 @@
     )
     for wait in waits[:PIECES]:
         wait()
-    split_blocks(blocks, tiles_high, tiles_low)
+    high[...], low[...] = halves(blocks[...])
     for wait in waits[PIECES:]:
         wait()
     corners = [cmap[0, 0, n] for n in range(cmap.shape[2])]
     across = [fmap[0, 0, order[2], p] for p in range(fmap.shape[3])]
-    tiles = (tiles_high, tiles_low)
-    offer(pair, corners, across, rvec, rows, tiles, left, base, payload)
+    offer(pair, corners, across, rvec, rows, (high, low), base, payload)
     cmap_out[...] = cmap_row[0]
     if pair:
         payload[ncol:, :] = jnp.zeros_like(payload[ncol:, :])
@@ -298,14 +285,13 @@
 
 
 def image_kernel(
-    pair, cmap, met, weights, local, zvec, tiles_high, tiles_low, rows, *rest
+    pair, cmap, met, weights, local, zvec, high, low, rows, *rest
 ):
     count = 3 if pair else 4
-    besides, (wout, sums, base, payload, left) = rest[:count], rest[count:]
+    besides, (wout, sums, base, payload) = rest[:count], rest[count:]
     (corners,) = listed(cmap)
     where = couple(met, weights, local, besides, wout)
-    tiles = (tiles_high, tiles_low)
-    offer(pair, corners, where[2], wout, rows, tiles, left, base, payload)
+    offer(pair, corners, where[2], wout, rows, (high, low), base, payload)
     sums[...] = lanes(zvec, wout)
 
 
@@ -388,7 +374,6 @@
     ncol = segment_load.shape[-1] // bdof
     nface = face_map.shape[3]
     ncorner = corner_map.shape[2]
-    size = nblk * bdof
     pair = lax.axis_size("sec") == 2
     load, mask = segment_load[0, 0], segment_mask[0, 0]
     cols = jnp.transpose(block_cols[0], (2, 0, 1))
@@ -414,14 +399,13 @@
     flat = shape(nblk, bdof * ncol)
     face = shape(ncol, nface * bdof)
     group = ncorner * bdof
-    tiles = shape(size // group, group, group, dtype=BF16)
-    halved = pltpu.VMEM((size // group, 2 * ncol, group), BF16)
+    half = shape(nblk, bdof, bdof, dtype=BF16)
     lane = group + nface * bdof if pair else group
     marked = ncol + 8 if pair else ncol
 
     rvec, base, payload, high, low, cmap, met, weights, rows, cols, tang = call(
         functools.partial(start_kernel, pair),
-        (field, field, shape(marked, lane), tiles, tiles)
+        (field, field, shape(marked, lane), half, half)
         + (shape(1, ncorner, dtype=jnp.int32), shape(4, nface, dtype=jnp.int32))
         + tuple(like(a) for a in (weights, rows, cols, tang)),
         [
@@ -433,7 +417,6 @@
             index(face_map),
             hold(face_map),
             hold(weights),
-            halved,
             sems(8 + nblk * ncol // LANES + 2 * PIECES),
         ],
         (),
@@ -464,7 +447,7 @@
     wvec, delta, base, payload = call(
         functools.partial(image_kernel, pair),
         (field, shape(ncol, bdof), field, shape(ncol, lane)),
-        [halved],
+        [],
         (cmap, met, weights, part, zvec, high, low, rows, *besides, *beyond, *across),
     )
     shares = lax.all_gather(payload, "sec")

time: 38.3 us -> 38.3 us (level)
  no operation moved by 1% of the time
where the time goes in v16:
time: 38.3 us; the launch traced here: 38.1 us
  blocking collectives  16.8 us (44%)
  starting transfers between devices  11.5 us (30%)
  Pallas kernels  8.41 us (22%)
  between operations  0.73 us (2%)
  waiting for transfers between devices  0.61 us (2%)
    all_to_all x1, blocking collectives, everywhere(): return lax.all_to_all(copies, ('dam', 'sec'), split_axis=0, concat_axis=0)  13 us
    ppermute x4, starting transfers between devices, exchange(): got.append(lax.ppermute(send, axis, pairs + [(j, i) for i, j in pairs]))  11.5 us
    pallas_call x8, Pallas kernels, call(): pl.pallas_call(kernel, out_shape=outs, in_specs=[vmem] * len(args) + [hbm...  8.41 us
    all_gather x1, blocking collectives, shards(): shares = labels = lax.all_gather(payload, 'sec')  2.01 us
    all_gather x1, blocking collectives, shards(): shares = lax.all_gather(payload, 'sec')  1.87 us
  transfers between devices with their start and end apart: 4, of which 2 were waited for; matrix products, arithmetic and copies ran while one was open for 0% of the time, Pallas kernels for 10%

profile of v16, /device:TPU:0, one launch (start us, length us, event | category | flops | bytes accessed | tf_op | source)
XLA Modules:
  0.0 38.1 jit_solution(10686924419408669717)
XLA Ops:
  0.6 0.0 copy-start
  0.6 2.3 %shard_map.113 = (f32[16,16,64]{2,1,0:T(8,128)S(1)}, f32[16,16,64]{2,1,0:T(8,128)S(1)}, f32[24,768]{1,0:T(8,128)S(1)}, bf16[16,64,64]{2,1,0:T(8,128)(2,1)S(1)}, ...) custom-call(f32[16,1024]{1,0:T(8,128)} %bitcast.26, ...), custom_call_target="tpu_custom_call" | custom-call | tf_op jit(solution)/shard_map/pallas_call | solution.py:338
  2.9 2.0 %all-gather = f32[48,768]{1,0:T(8,128)S(1)} all-gather(f32[24,768]{1,0:T(8,128)S(1)} %get-tuple-element.44), channel_id=2, replica_groups=mesh['dam'=16,'sec'=2] {'sec'}, dimensions={0}, use_global_device_ids=true | all-gather | bytes 221184 | tf_op jit(solution)/shard_map/all_gather | solution.py:444
  4.9 0.2 shard_map.114
  5.1 0.7 %collective-permute-start = (f32[16,512]{1,0:T(8,128)S(1)}, f32[16,512]{1,0:T(8,128)S(1)}, u32[]{:S(2)}, u32[]{:S(2)}) collective-permute-start(f32[16,512]{1,0:T(8,128)S(1)} %get-tuple-element.50), channel_id=1, source_target_pairs={{2,4},{6,8},{10,12},{14,16},{18,20},{22,24},{26,28},{4,2},{8,6},{1... | collective-permute-start | bytes 98312 | tf_op jit(solution)/shard_map/ppermute | solution.py:357
  5.8 5.6 %collective-permute-start.1 = (f32[16,512]{1,0:T(8,128)S(1)}, f32[16,512]{1,0:T(8,128)S(1)}, u32[]{:S(2)}, u32[]{:S(2)}) collective-permute-start(f32[16,512]{1,0:T(8,128)S(1)} %get-tuple-element.51), channel_id=1, source_target_pairs={{0,2},{4,6},{8,10},{12,14},{16,18},{20,22},{24,26},{28,30},{2,0},{... | collective-permute-start | bytes 98312 | tf_op jit(solution)/shard_map/ppermute | solution.py:357
  11.4 0.0 copy-done
  11.4 1.8 %shard_map.115 = (f32[16,16,64]{2,1,0:T(8,128)S(1)}, f32[16,64]{1,0:T(8,128)S(1)}, f32[16,1024]{1,0:T(8,128)S(1)}, f32[16,1024]{1,0:T(8,128)S(1)}, f32[16,512]{1,0:T(8,128)S(1)}) custom-call(s32[7,1,16]{2,1,0:T(1,128)S(1)} %get-tuple-element.39.cols_in, s32[4,8]{1,0:T(4,128)S(1)} %get-tuple-element.37.met, f32[4,512]{1,0:T(4,128)S(1)} %get-tuple-element.38.weights, ...), custom_call_target="tpu_custom_call" | custom-call | tf_op jit(solution)/shard_map/pallas_call | solution.py:338
  13.3 0.0 collective-permute-done.rest_0_
  13.3 0.3 collective-permute-done.1.rest_1_
  13.6 0.7 %shard_map.116 = (f32[16,16,64]{2,1,0:T(8,128)S(1)}, f32[16,64]{1,0:T(8,128)S(1)}, f32[16,16,64]{2,1,0:T(8,128)S(1)}, f32[16,768]{1,0:T(8,128)S(1)}) custom-call(s32[1,4]{1,0:T(1,128)S(1)} %get-tuple-element.41.cmap, s32[4,8]{1,0:T(4,128)S(1)} %get-tuple-element.37.met, f32[4,512]{1,0:T(4,128)S(1)} %get-tuple-element.38.weights, ...), custom_call_target="tpu_custom_call" | custom-call | tf_op jit(solution)/shard_map/pallas_call | solution.py:338
  14.3 1.9 %all-gather.1 = f32[32,768]{1,0:T(8,128)S(1)} all-gather(f32[16,768]{1,0:T(8,128)S(1)} %get-tuple-element.54), channel_id=3, replica_groups=mesh['dam'=16,'sec'=2] {'sec'}, dimensions={0}, use_global_device_ids=true | all-gather | bytes 147456 | tf_op jit(solution)/shard_map/all_gather | solution.py:453
  16.2 0.2 shard_map.117
  16.4 0.7 %collective-permute-start.2 = (f32[16,512]{1,0:T(8,128)S(1)}, f32[16,512]{1,0:T(8,128)S(1)}, u32[]{:S(2)}, u32[]{:S(2)}) collective-permute-start(f32[16,512]{1,0:T(8,128)S(1)} %get-tuple-element.61), channel_id=1, source_target_pairs={{2,4},{6,8},{10,12},{14,16},{18,20},{22,24},{26,28},{4,2},{8,6},{1... | collective-permute-start | bytes 98312 | tf_op jit(solution)/shard_map/ppermute | solution.py:357
  17.1 4.5 %collective-permute-start.3 = (f32[16,512]{1,0:T(8,128)S(1)}, f32[16,512]{1,0:T(8,128)S(1)}, u32[]{:S(2)}, u32[]{:S(2)}) collective-permute-start(f32[16,512]{1,0:T(8,128)S(1)} %get-tuple-element.62), channel_id=1, source_target_pairs={{0,2},{4,6},{8,10},{12,14},{16,18},{20,22},{24,26},{28,30},{2,0},{... | collective-permute-start | bytes 98312 | tf_op jit(solution)/shard_map/ppermute | solution.py:357
  21.6 1.8 %shard_map.118 = (f32[16,16,64]{2,1,0:T(8,128)S(1)}, f32[16,64]{1,0:T(8,128)S(1)}, f32[16,1024]{1,0:T(8,128)S(1)}, f32[16,1024]{1,0:T(8,128)S(1)}, f32[16,512]{1,0:T(8,128)S(1)}) custom-call(s32[7,1,16]{2,1,0:T(1,128)S(1)} %get-tuple-element.39.cols_in, s32[4,8]{1,0:T(4,128)S(1)} %get-tuple-element.37.met, f32[4,512]{1,0:T(4,128)S(1)} %get-tuple-element.38.weights, ...), custom_call_target="tpu_custom_call" | custom-call | tf_op jit(solution)/shard_map/pallas_call | solution.py:338
  23.4 0.0 collective-permute-done.2.rest_0_
  23.4 0.3 collective-permute-done.3.rest_1_
  23.7 0.3 shard_map.119
  24.1 13.0 %all_to_all.5 = f32[32,1,96]{2,1,0:T(1,128)S(1)} all-to-all(f32[32,1,96]{2,1,0:T(1,128)S(1)} %get-tuple-element.64), channel_id=1, replica_groups=mesh['dam'=16,'sec'=2] {'dam','sec'}, dimensions={0} | all-to-all | bytes 24576 | tf_op jit(solution)/shard_map/all_to_all | solution.py:349
  37.0 1.0 %shard_map.120 = (f32[16,1024]{1,0:T(8,128)}, f32[16,1024]{1,0:T(8,128)}) custom-call(f32[32,96]{1,0:T(8,128)S(1)} %bitcast.23, f32[16,16,64]{2,1,0:T(8,128)S(1)} %get-tuple-element.65.nvec, f32[16,1024]{1,0:T(8,128)S(1)} %get-tuple-element.66.rflat, f32[16,1024]{1,0:T(8,128)S(1)} %get-tuple-element.67.zflat, f32[16,1024]{1,0:T(8,128)S(1)} %get-tuple-element.68.wflat, ...), custom_call_target="tpu_custom_call" | custom-call | tf_op jit(solution)/shard_map/pallas_call | solution.py:338
Async XLA Ops:
  0.6 10.8 %copy-start = (f32[1,1,16,64,448]{4,3,2,1,0:T(8,128)S(1)}, f32[1,1,16,64,448]{4,3,2,1,0:T(8,128)}, u32[]{:S(2)}) copy-start(f32[1,1,16,64,448]{4,3,2,1,0:T(8,128)} %param.12) | copy-start | bytes 5505028
  5.1 8.2 %collective-permute-start = (f32[16,512]{1,0:T(8,128)S(1)}, f32[16,512]{1,0:T(8,128)S(1)}, u32[]{:S(2)}, u32[]{:S(2)}) collective-permute-start(f32[16,512]{1,0:T(8,128)S(1)} %get-tuple-element.50), channel_id=1, source_target_pairs={{2,4},{6,8},{10,12},{14,16},{18,20},{22,24},{26,28},{4,2},{8,6},{1... | collective-permute-start | bytes 98312 | tf_op jit(solution)/shard_map/ppermute | solution.py:357
  5.8 7.8 %collective-permute-start.1 = (f32[16,512]{1,0:T(8,128)S(1)}, f32[16,512]{1,0:T(8,128)S(1)}, u32[]{:S(2)}, u32[]{:S(2)}) collective-permute-start(f32[16,512]{1,0:T(8,128)S(1)} %get-tuple-element.51), channel_id=1, source_target_pairs={{0,2},{4,6},{8,10},{12,14},{16,18},{20,22},{24,26},{28,30},{2,0},{... | collective-permute-start | bytes 98312 | tf_op jit(solution)/shard_map/ppermute | solution.py:357
  16.4 7.0 %collective-permute-start.2 = (f32[16,512]{1,0:T(8,128)S(1)}, f32[16,512]{1,0:T(8,128)S(1)}, u32[]{:S(2)}, u32[]{:S(2)}) collective-permute-start(f32[16,512]{1,0:T(8,128)S(1)} %get-tuple-element.61), channel_id=1, source_target_pairs={{2,4},{6,8},{10,12},{14,16},{18,20},{22,24},{26,28},{4,2},{8,6},{1... | collective-permute-start | bytes 98312 | tf_op jit(solution)/shard_map/ppermute | solution.py:357
  17.1 6.7 %collective-permute-start.3 = (f32[16,512]{1,0:T(8,128)S(1)}, f32[16,512]{1,0:T(8,128)S(1)}, u32[]{:S(2)}, u32[]{:S(2)}) collective-permute-start(f32[16,512]{1,0:T(8,128)S(1)} %get-tuple-element.62), channel_id=1, source_target_pairs={{0,2},{4,6},{8,10},{12,14},{16,18},{20,22},{24,26},{28,30},{2,0},{... | collective-permute-start | bytes 98312 | tf_op jit(solution)/shard_map/ppermute | solution.py:357

commit v17 on v16

--- a/solution.py
+++ b/solution.py
@@ -268,6 +268,9 @@
     for i, blocks in enumerate(where):
         row = weights[i : i + 1, :]
         add_pieces(out, blocks, lambda p, b: lane_piece(row, p, bdof) * field[b])
+    if pair:
+        term = weights[2:3, :] * across[0][...]
+        add_pieces(out, where[2], lambda p, b: -lane_piece(term, p, bdof))
 
 
 def couple(met, weights, local, besides, out):
@@ -287,7 +290,7 @@
 def image_kernel(
     pair, cmap, met, weights, local, zvec, high, low, rows, *rest
 ):
-    count = 3 if pair else 4
+    count = 2 if pair else 4
     besides, (wout, sums, base, payload) = rest[:count], rest[count:]
     (corners,) = listed(cmap)
     where = couple(met, weights, local, besides, wout)
@@ -433,31 +436,31 @@
         return vec, exchange(faces[:2], "dam"), exchange(faces[2:], "sec")
 
     def local(vec, other, shares, labels):
-        part, sums, *rest = call(
+        return call(
             functools.partial(local_kernel, pair),
-            (field, shape(ncol, bdof), flat, flat) + ((face,) if pair else ()),
-            [pltpu.VMEM((nblk, 2 * ncol, bdof), BF16), index(cols), sems(1)],
+            (field, shape(ncol, bdof), flat, flat),
+            ([hold(face)] if pair else [])
+            + [pltpu.VMEM((nblk, 2 * ncol, bdof), BF16), index(cols), sems(1)],
             (cols, met, weights, tang, vec, other, stiffness[0, 0], shares, labels),
         )
-        return part, sums, *rest[:2], rest[2:]
 
     shares = labels = lax.all_gather(payload, "sec")
     zvec, besides, beyond = finish(base, shares)
-    part, gamma, zflat, rflat, across = local(zvec, rvec, shares, labels)
+    part, gamma, zflat, rflat = local(zvec, rvec, shares, labels)
     wvec, delta, base, payload = call(
         functools.partial(image_kernel, pair),
         (field, shape(ncol, bdof), field, shape(ncol, lane)),
         [],
-        (cmap, met, weights, part, zvec, high, low, rows, *besides, *beyond, *across),
+        (cmap, met, weights, part, zvec, high, low, rows, *besides, *beyond),
     )
     shares = lax.all_gather(payload, "sec")
     mvec, besides, beyond = finish(base, shares)
-    part, mu, mflat, wflat, across = local(mvec, wvec, shares, labels)
+    part, mu, mflat, wflat = local(mvec, wvec, shares, labels)
     nvec, totals = call(
         last_kernel,
         (field, shape(lax.axis_size("dam") * lax.axis_size("sec"), 1, 6 * ncol)),
         [],
-        (met, weights, part, rvec, zvec, mvec, gamma, delta, mu, *besides, *beyond, *across),
+        (met, weights, part, rvec, zvec, mvec, gamma, delta, mu, *besides, *beyond),
     )
     sol, res = call(
         finish_kernel,

time: 38.3 us -> 38.2 us (level)
  no operation moved by 1% of the time
where the time goes in v17:
time: 38.2 us; the launch traced here: 38 us
  blocking collectives  16.8 us (44%)
  starting transfers between devices  11.5 us (30%)
  Pallas kernels  8.39 us (22%)
  between operations  0.73 us (2%)
  waiting for transfers between devices  0.6 us (2%)
    all_to_all x1, blocking collectives, everywhere(): return lax.all_to_all(copies, ('dam', 'sec'), split_axis=0, concat_axis=0)  13 us
    ppermute x4, starting transfers between devices, exchange(): got.append(lax.ppermute(send, axis, pairs + [(j, i) for i, j in pairs]))  11.5 us
    pallas_call x8, Pallas kernels, call(): pl.pallas_call(kernel, out_shape=outs, in_specs=[vmem] * len(args) + [hbm...  8.39 us
    all_gather x1, blocking collectives, shards(): shares = labels = lax.all_gather(payload, 'sec')  2.01 us
    all_gather x1, blocking collectives, shards(): shares = lax.all_gather(payload, 'sec')  1.87 us
  transfers between devices with their start and end apart: 4, of which 2 were waited for; matrix products, arithmetic and copies ran while one was open for 0% of the time, Pallas kernels for 10%

profile of v17, /device:TPU:0, one launch (start us, length us, event | category | flops | bytes accessed | tf_op | source)
XLA Modules:
  0.0 38.0 jit_solution(7507781693605795495)
XLA Ops:
  0.6 0.0 copy-start
  0.6 2.3 %shard_map.113 = (f32[16,16,64]{2,1,0:T(8,128)S(1)}, f32[16,16,64]{2,1,0:T(8,128)S(1)}, f32[24,768]{1,0:T(8,128)S(1)}, bf16[16,64,64]{2,1,0:T(8,128)(2,1)S(1)}, ...) custom-call(f32[16,1024]{1,0:T(8,128)} %bitcast.26, ...), custom_call_target="tpu_custom_call" | custom-call | tf_op jit(solution)/shard_map/pallas_call | solution.py:341
  2.9 2.0 %all-gather = f32[48,768]{1,0:T(8,128)S(1)} all-gather(f32[24,768]{1,0:T(8,128)S(1)} %get-tuple-element.42), channel_id=2, replica_groups=mesh['dam'=16,'sec'=2] {'sec'}, dimensions={0}, use_global_device_ids=true | all-gather | bytes 221184 | tf_op jit(solution)/shard_map/all_gather | solution.py:447
  4.9 0.2 shard_map.114
  5.1 0.7 %collective-permute-start = (f32[16,512]{1,0:T(8,128)S(1)}, f32[16,512]{1,0:T(8,128)S(1)}, u32[]{:S(2)}, u32[]{:S(2)}) collective-permute-start(f32[16,512]{1,0:T(8,128)S(1)} %get-tuple-element.48), channel_id=1, source_target_pairs={{2,4},{6,8},{10,12},{14,16},{18,20},{22,24},{26,28},{4,2},{8,6},{1... | collective-permute-start | bytes 98312 | tf_op jit(solution)/shard_map/ppermute | solution.py:360
  5.8 5.6 %collective-permute-start.1 = (f32[16,512]{1,0:T(8,128)S(1)}, f32[16,512]{1,0:T(8,128)S(1)}, u32[]{:S(2)}, u32[]{:S(2)}) collective-permute-start(f32[16,512]{1,0:T(8,128)S(1)} %get-tuple-element.49), channel_id=1, source_target_pairs={{0,2},{4,6},{8,10},{12,14},{16,18},{20,22},{24,26},{28,30},{2,0},{... | collective-permute-start | bytes 98312 | tf_op jit(solution)/shard_map/ppermute | solution.py:360
  11.4 0.0 copy-done
  11.4 1.8 %shard_map.115 = (f32[16,16,64]{2,1,0:T(8,128)S(1)}, f32[16,64]{1,0:T(8,128)S(1)}, f32[16,1024]{1,0:T(8,128)S(1)}, f32[16,1024]{1,0:T(8,128)S(1)}) custom-call(s32[7,1,16]{2,1,0:T(1,128)S(1)} %get-tuple-element.37.cols_in, s32[4,8]{1,0:T(4,128)S(1)} %get-tuple-element.35.met, f32[4,512]{1,0:T(4,128)S(1)} %get-tuple-element.36.weights, ...), custom_call_target="tpu_custom_call" | custom-call | tf_op jit(solution)/shard_map/pallas_call | solution.py:341
  13.3 0.0 collective-permute-done.rest_0_
  13.3 0.3 collective-permute-done.1.rest_1_
  13.6 0.7 %shard_map.116 = (f32[16,16,64]{2,1,0:T(8,128)S(1)}, f32[16,64]{1,0:T(8,128)S(1)}, f32[16,16,64]{2,1,0:T(8,128)S(1)}, f32[16,768]{1,0:T(8,128)S(1)}) custom-call(s32[1,4]{1,0:T(1,128)S(1)} %get-tuple-element.39.cmap, s32[4,8]{1,0:T(4,128)S(1)} %get-tuple-element.35.met, f32[4,512]{1,0:T(4,128)S(1)} %get-tuple-element.36.weights, ...), custom_call_target="tpu_custom_call" | custom-call | tf_op jit(solution)/shard_map/pallas_call | solution.py:341
  14.3 1.9 %all-gather.1 = f32[32,768]{1,0:T(8,128)S(1)} all-gather(f32[16,768]{1,0:T(8,128)S(1)} %get-tuple-element.51), channel_id=3, replica_groups=mesh['dam'=16,'sec'=2] {'sec'}, dimensions={0}, use_global_device_ids=true | all-gather | bytes 147456 | tf_op jit(solution)/shard_map/all_gather | solution.py:456
  16.2 0.2 shard_map.117
  16.4 0.7 %collective-permute-start.2 = (f32[16,512]{1,0:T(8,128)S(1)}, f32[16,512]{1,0:T(8,128)S(1)}, u32[]{:S(2)}, u32[]{:S(2)}) collective-permute-start(f32[16,512]{1,0:T(8,128)S(1)} %get-tuple-element.58), channel_id=1, source_target_pairs={{2,4},{6,8},{10,12},{14,16},{18,20},{22,24},{26,28},{4,2},{8,6},{1... | collective-permute-start | bytes 98312 | tf_op jit(solution)/shard_map/ppermute | solution.py:360
  17.1 4.5 %collective-permute-start.3 = (f32[16,512]{1,0:T(8,128)S(1)}, f32[16,512]{1,0:T(8,128)S(1)}, u32[]{:S(2)}, u32[]{:S(2)}) collective-permute-start(f32[16,512]{1,0:T(8,128)S(1)} %get-tuple-element.59), channel_id=1, source_target_pairs={{0,2},{4,6},{8,10},{12,14},{16,18},{20,22},{24,26},{28,30},{2,0},{... | collective-permute-start | bytes 98312 | tf_op jit(solution)/shard_map/ppermute | solution.py:360
  21.6 1.8 %shard_map.118 = (f32[16,16,64]{2,1,0:T(8,128)S(1)}, f32[16,64]{1,0:T(8,128)S(1)}, f32[16,1024]{1,0:T(8,128)S(1)}, f32[16,1024]{1,0:T(8,128)S(1)}) custom-call(s32[7,1,16]{2,1,0:T(1,128)S(1)} %get-tuple-element.37.cols_in, s32[4,8]{1,0:T(4,128)S(1)} %get-tuple-element.35.met, f32[4,512]{1,0:T(4,128)S(1)} %get-tuple-element.36.weights, ...), custom_call_target="tpu_custom_call" | custom-call | tf_op jit(solution)/shard_map/pallas_call | solution.py:341
  23.4 0.0 collective-permute-done.2.rest_0_
  23.4 0.3 collective-permute-done.3.rest_1_
  23.7 0.3 shard_map.119
  24.1 13.0 %all_to_all.5 = f32[32,1,96]{2,1,0:T(1,128)S(1)} all-to-all(f32[32,1,96]{2,1,0:T(1,128)S(1)} %get-tuple-element.60), channel_id=1, replica_groups=mesh['dam'=16,'sec'=2] {'dam','sec'}, dimensions={0} | all-to-all | bytes 24576 | tf_op jit(solution)/shard_map/all_to_all | solution.py:352
  37.0 1.0 %shard_map.120 = (f32[16,1024]{1,0:T(8,128)}, f32[16,1024]{1,0:T(8,128)}) custom-call(f32[32,96]{1,0:T(8,128)S(1)} %bitcast.23, f32[16,16,64]{2,1,0:T(8,128)S(1)} %get-tuple-element.61.nvec, f32[16,1024]{1,0:T(8,128)S(1)} %get-tuple-element.62.rflat, f32[16,1024]{1,0:T(8,128)S(1)} %get-tuple-element.63.zflat, f32[16,1024]{1,0:T(8,128)S(1)} %get-tuple-element.64.wflat, ...), custom_call_target="tpu_custom_call" | custom-call | tf_op jit(solution)/shard_map/pallas_call | solution.py:341
Async XLA Ops:
  0.6 10.8 %copy-start = (f32[1,1,16,64,448]{4,3,2,1,0:T(8,128)S(1)}, f32[1,1,16,64,448]{4,3,2,1,0:T(8,128)}, u32[]{:S(2)}) copy-start(f32[1,1,16,64,448]{4,3,2,1,0:T(8,128)} %param.12) | copy-start | bytes 5505028
  5.1 8.2 %collective-permute-start = (f32[16,512]{1,0:T(8,128)S(1)}, f32[16,512]{1,0:T(8,128)S(1)}, u32[]{:S(2)}, u32[]{:S(2)}) collective-permute-start(f32[16,512]{1,0:T(8,128)S(1)} %get-tuple-element.48), channel_id=1, source_target_pairs={{2,4},{6,8},{10,12},{14,16},{18,20},{22,24},{26,28},{4,2},{8,6},{1... | collective-permute-start | bytes 98312 | tf_op jit(solution)/shard_map/ppermute | solution.py:360
  5.8 7.8 %collective-permute-start.1 = (f32[16,512]{1,0:T(8,128)S(1)}, f32[16,512]{1,0:T(8,128)S(1)}, u32[]{:S(2)}, u32[]{:S(2)}) collective-permute-start(f32[16,512]{1,0:T(8,128)S(1)} %get-tuple-element.49), channel_id=1, source_target_pairs={{0,2},{4,6},{8,10},{12,14},{16,18},{20,22},{24,26},{28,30},{2,0},{... | collective-permute-start | bytes 98312 | tf_op jit(solution)/shard_map/ppermute | solution.py:360
  16.4 7.0 %collective-permute-start.2 = (f32[16,512]{1,0:T(8,128)S(1)}, f32[16,512]{1,0:T(8,128)S(1)}, u32[]{:S(2)}, u32[]{:S(2)}) collective-permute-start(f32[16,512]{1,0:T(8,128)S(1)} %get-tuple-element.58), channel_id=1, source_target_pairs={{2,4},{6,8},{10,12},{14,16},{18,20},{22,24},{26,28},{4,2},{8,6},{1... | collective-permute-start | bytes 98312 | tf_op jit(solution)/shard_map/ppermute | solution.py:360
  17.1 6.7 %collective-permute-start.3 = (f32[16,512]{1,0:T(8,128)S(1)}, f32[16,512]{1,0:T(8,128)S(1)}, u32[]{:S(2)}, u32[]{:S(2)}) collective-permute-start(f32[16,512]{1,0:T(8,128)S(1)} %get-tuple-element.59), channel_id=1, source_target_pairs={{0,2},{4,6},{8,10},{12,14},{16,18},{20,22},{24,26},{28,30},{2,0},{... | collective-permute-start | bytes 98312 | tf_op jit(solution)/shard_map/ppermute | solution.py:360
